TPU v7x, 128 devices: a whole 4x4x4 slice. The times are simulated.
128 devices in a mesh: prow: 64 (over z, y, x), pcol: 2 (over core).
Axes of the slice: x: 4, y: 4, z: 4, core: 2. Of those that a mesh axis runs over, the one named last changes fastest.
Arguments:
- hist_factor: bfloat16 [3, 4096, 65536], P(None, 'pcol', 'prow'), may hold values from -0.013671875 to 0.013671875
- hist_solution: bfloat16 [3, 1024, 65536], P(None, None, 'prow'), may hold values from -16 to 16
- diag_factor: bfloat16 [4096, 4096], P('pcol', 'prow'), may hold values from -2 to 2, as said below
- samples: bfloat16 [1024, 4096], P('prow', 'pcol'), may hold values from -6 to 6
Outputs:
- solution: float32 [1024, 4096], P('prow', 'pcol')
Inputs may be any that keep to these rules, and one draw needn't show every extreme that they name: `diag_factor`: only the lower triangle with the diagonal is read; the diagonal entries are positive.
All inputs are finite; a program needn't handle non-finite values.
Results may differ from a plain program's by a relative error of at most 0.0003.
Values may be sent and summed in bfloat16 or wider, within the bound.
No kernel may reach another device: no remote copies, remote signals or barrier semaphores. Data moves between devices by JAX's collectives and lax.ppermute only.
A program may use at most 192 MiB of HBM per device.

v0:
```python
import jax
import jax.numpy as jnp
from jax import lax
from jax.sharding import PartitionSpec as P


def spread(value, axis, source):
    kept = jnp.where(lax.axis_index(axis) == source, value, 0).astype(value.dtype)
    return lax.psum(kept, axis)


def per_device(hist_factor, hist_solution, diag_factor, samples):
    total_rhs = hist_solution.shape[1]
    share = total_rhs // lax.axis_size("prow")
    slab = hist_factor.shape[1]
    window = lax.all_gather(diag_factor, "prow", axis=1, tiled=True)
    mine = lax.psum_scatter(
        jnp.einsum("brc,bsc->rs", hist_solution, hist_factor, preferred_element_type=jnp.float32),
        "prow",
        scatter_dimension=0,
        tiled=True,
    )
    pending = samples.astype(jnp.float32) - mine
    column = lax.axis_index("pcol")
    solved = jnp.zeros((share, slab), jnp.float32)
    for owner in range(lax.axis_size("pcol")):
        tile = window[:, owner * slab : (owner + 1) * slab].astype(jnp.float32)
        candidate = lax.linalg.triangular_solve(
            jnp.tril(tile), pending, left_side=False, lower=True, transpose_a=True
        )
        received = spread(candidate, "pcol", owner)
        solved = jnp.where(column == owner, received, solved)
        update = lax.dot_general(
            received,
            tile,
            (((1,), (1,)), ((), ())),
            precision=lax.Precision.HIGHEST,
            preferred_element_type=jnp.float32,
        )
        pending = jnp.where(column > owner, pending - update, pending)
    return solved


def solution(mesh):
    return jax.shard_map(
        per_device,
        mesh=mesh,
        in_specs=(
            P(None, "pcol", "prow"),
            P(None, None, "prow"),
            P("pcol", "prow"),
            P("prow", "pcol"),
        ),
        out_specs=P("prow", "pcol"),
        check_vma=False,
    )
```

profile of v0, /device:TPU:1, one launch (start us, length us, event | category | flops | bytes accessed | tf_op | source)
XLA Modules:
  0.0 1015.6 jit_solution(924688981476371951)
XLA Ops:
  6.5 19.0 %convolution_bitcast_fusion = f32[1024,2048]{1,0:T(8,128)} fusion(bf16[3,1024,1024]{2,1,0:T(8,128)(2,1)} %param.7, bf16[3,2048,1024]{2,1,0:T(8,128)(2,1)} %param.6), kind=kOutput, calls=%fused_computation.9 | convolution fusion | flops 12884901888 | bytes 27262976 | tf_op jit(solution)/shard_map/brc,bsc->rs/dot_general | solution.py:18
  26.6 321.9 %reduce-scatter.2.cloned.1.call-done = f32[16,2048]{1,0:T(8,128)} async-done(((f32[1024,2048]{1,0:T(8,128)}), f32[16,2048]{1,0:T(8,128)}) %reduce-scatter.2.cloned.1.call-update) | async-done | bytes 131088 | tf_op jit(solution)/shard_map/reduce_scatter | solution.py:17
  349.4 149.6 %all-gather.2.cloned.1.call-done = bf16[2048,4096]{0,1:T(8,128)(2,1)} async-done(((bf16[2048,64]{0,1:T(8,128)(2,1)}), bf16[2048,4096]{0,1:T(8,128)(2,1)}) %all-gather.2.cloned.1.call-update) | async-done | bytes 16777232 | tf_op jit(solution)/shard_map/all_gather | solution.py:16
  499.0 17.7 %select_select_fusion = (f32[2048,2048]{0,1:T(8,128)}, f32[2048,2048]{0,1:T(8,128)}) fusion(bf16[2048,4096]{0,1:T(8,128)(2,1)} %all-gather.2.cloned.1.call-done), kind=kLoop, calls=%fused_computation.4 | loop fusion | flops 29360128 | bytes 50331648 | tf_op jit(solution)/shard_map/triangular_solve/select.1 | solution.py:28
  516.7 46.3 %while.4 = (s32[]{:T(128)}, f32[2048,2048]{0,1:T(8,128)}, s32[16,2]{0,1:T(2,128)S(1)}, f32[16,128,128]{2,1,0:T(8,128)S(1)}, s32[]{:T(128)}) while((s32[]{:T(128)}, f32[2048,2048]{0,1:T(8,128)}, s32[16,2]{0,1:T(2,128)S(1)}, f32[16,128,128]{2,1,0:T(8,128)S(1)}, s32[]{:T(128)}) %tuple.266), condition=%wide.while_cond, body=%wide.while_body.sunk | while | flops 2 | bytes 393329 | solution.py:28
  517.3 2.2 dynamic-slice.12
  520.2 2.2 dynamic-slice.12
  523.1 2.2 dynamic-slice.12
  526.0 2.2 dynamic-slice.12
  528.9 2.2 dynamic-slice.12
  531.8 2.2 dynamic-slice.12
  534.7 2.2 dynamic-slice.12
  537.6 2.2 dynamic-slice.12
  540.5 2.2 dynamic-slice.12
  543.4 2.2 dynamic-slice.12
  546.4 2.2 dynamic-slice.12
  549.3 2.2 dynamic-slice.12
  552.2 2.2 dynamic-slice.12
  555.1 2.2 dynamic-slice.12
  558.0 2.2 dynamic-slice.12
  560.9 2.1 dynamic-slice.12
  563.1 157.2 %custom-call.4 = f32[16,128,128]{1,2,0:T(8,128)S(1)} custom-call(f32[16,128,128]{2,1,0:T(8,128)S(1)} %get-tuple-element.20), custom_call_target="InvertDiagBlocksLowerTriangular" | custom-call | tf_op jit(solution)/shard_map/triangular_solve/custom-call.1 | solution.py:28
  727.1 1.3 convolution_subtract_fusion.28
  728.6 1.4 convolution_subtract_fusion.27
  730.1 1.4 convolution_subtract_fusion.26
  731.7 1.5 convolution_subtract_fusion.17
  733.4 1.5 convolution_subtract_fusion.16
  735.1 1.6 convolution_subtract_fusion.15
  736.9 1.6 convolution_subtract_fusion.14
  738.7 1.7 convolution_subtract_fusion.13
  740.6 1.8 convolution_subtract_fusion.12
  742.5 1.8 convolution_subtract_fusion.11
  745.6 49.4 %while.5 = (s32[]{:T(128)}, f32[2048,2048]{0,1:T(8,128)}, s32[16,2]{0,1:T(2,128)S(1)}, f32[16,128,128]{2,1,0:T(8,128)S(1)}, s32[]{:T(128)}) while((s32[]{:T(128)}, f32[2048,2048]{0,1:T(8,128)}, s32[16,2]{0,1:T(2,128)S(1)}, f32[16,128,128]{2,1,0:T(8,128)S(1)}, s32[]{:T(128)}) %tuple.280), condition=%wide.while_cond.clone, body=%wide.while_body.clone.sunk | while | flops 2 | bytes 393329 | solution.py:28
  746.2 2.3 dynamic-slice.14
  749.3 2.3 dynamic-slice.14
  752.4 2.3 dynamic-slice.14
  755.5 2.3 dynamic-slice.14
  758.6 2.3 dynamic-slice.14
  761.7 2.3 dynamic-slice.14
  764.8 2.3 dynamic-slice.14
  767.9 2.3 dynamic-slice.14
  771.0 2.3 dynamic-slice.14
  774.1 2.3 dynamic-slice.14
  777.2 2.3 dynamic-slice.14
  780.3 2.3 dynamic-slice.14
  783.4 2.3 dynamic-slice.14
  786.4 2.3 dynamic-slice.14
  789.5 2.3 dynamic-slice.14
  792.6 2.2 dynamic-slice.14
  795.0 157.2 %custom-call.5 = f32[16,128,128]{1,2,0:T(8,128)S(1)} custom-call(f32[16,128,128]{2,1,0:T(8,128)S(1)} %get-tuple-element.21), custom_call_target="InvertDiagBlocksLowerTriangular" | custom-call | tf_op jit(solution)/shard_map/triangular_solve/custom-call.1 | solution.py:28
  952.2 6.7 fusion.5
  964.3 1.3 convolution_subtract_fusion.25
  965.7 1.3 convolution_subtract_fusion.24
  967.2 1.4 convolution_subtract_fusion.23
  968.8 1.4 convolution_subtract_fusion.22
  970.4 1.5 convolution_subtract_fusion.6
  972.0 1.5 convolution_subtract_fusion.5
  973.7 1.6 convolution_subtract_fusion.4
  975.5 1.6 convolution_subtract_fusion.3
  977.3 1.7 convolution_subtract_fusion.2
  979.2 1.8 convolution_subtract_fusion.1
  981.1 1.8 convolution_subtract_fusion
  983.8 23.6 %all-reduce.5.cloned.1.call-done = f32[16,2048]{1,0:T(8,128)} async-done(((f32[16,2048]{1,0:T(8,128)}), f32[16,2048]{1,0:T(8,128)}) %all-reduce.5.cloned.1.call-update) | async-done | bytes 131088 | tf_op jit(solution)/shard_map/psum | solution.py:9
  1007.5 1.6 select_select_fusion.2
  (189 shorter events, 42.8 us)
Async XLA Ops:
  6.5 341.9 %copy-start.1 = (bf16[16,2048]{1,0:T(8,128)(2,1)S(1)}, bf16[16,2048]{1,0:T(8,128)(2,1)}, u32[]{:S(2)}) copy-start(bf16[16,2048]{1,0:T(8,128)(2,1)} %param.9) | copy-start | bytes 196612
  6.5 341.9 %reduce-scatter.2.cloned.1.call-start = ((), (), s32[]{:S(2)}) async-start(), calls=%async_computation.2 | async-start | bytes 8519680 | tf_op jit(solution)/shard_map/reduce_scatter | solution.py:17
  25.6 473.4 %all-gather.2.cloned.1.call-start = ((), (), s32[]{:S(2)}) async-start(), calls=%async_computation.1 | async-start | bytes 17039360 | tf_op jit(solution)/shard_map/all_gather | solution.py:16
  26.3 925.8 %all-reduce.3.cloned.1.call-start = ((), (), s32[]{:S(2)}) async-start(), calls=%async_computation.3 | async-start | bytes 262144 | tf_op jit(solution)/shard_map/psum | solution.py:9
  745.2 262.3 %all-reduce.5.cloned.1.call-start = ((), (), s32[]{:S(2)}) async-start(), calls=%async_computation.4 | async-start | bytes 262144 | tf_op jit(solution)/shard_map/psum | solution.py:9
  952.2 55.3 %copy-start = (f32[16,2048]{1,0:T(8,128)S(1)}, f32[16,2048]{1,0:T(8,128)}, u32[]{:S(2)}) copy-start(f32[16,2048]{1,0:T(8,128)} %all-reduce.3.cloned.1.call-done) | copy-start | bytes 393220
Sparse Core Ops, SparseCore 0:
  25.7 322.7 reduce-scatter.1
  351.4 147.5 all-gather.1
  745.3 23.4 all-reduce.2
  984.0 23.4 all-reduce.4
where the time goes:
time: 1020 us
  waiting for transfers between devices  496 us (49%)
  other arithmetic  336 us (33%)
  local copies, waits for them, and re-layouts  94.8 us (9%)
  matrix products  73.9 us (7%)
  between operations  13.5 us (1%)
    another operation x4, other arithmetic, per_device(): lax.linalg.triangular_solve(jnp.tril(tile), pending, left_side=False, low...  332 us
    reduce_scatter x1, waiting for transfers between devices, per_device(): lax.psum_scatter(jnp.einsum('brc,bsc->rs', hist_solution, hist_factor, pr...  322 us
    all_gather x1, waiting for transfers between devices, per_device(): window = lax.all_gather(diag_factor, 'prow', axis=1, tiled=True)  150 us
    another operation x162, local copies, waits for them, and re-layouts, per_device(): lax.linalg.triangular_solve(jnp.tril(tile), pending, left_side=False, low...  94.8 us
    another operation x62, matrix products, per_device(): lax.linalg.triangular_solve(jnp.tril(tile), pending, left_side=False, low...  48.2 us
    psum x2, waiting for transfers between devices, spread(): return lax.psum(kept, axis)  23.7 us
  transfers between devices with their start and end apart: 4, of which 3 were waited for; matrix products, arithmetic and copies ran while one was open for 20% of the time, Pallas kernels for 0%

commit v1 on v0

v1 whole, which is shorter than its diff:
```python
import functools

import jax
import jax.numpy as jnp
import numpy as np
from jax import lax
from jax.experimental import pallas as pl
from jax.experimental.pallas import tpu as pltpu
from jax.sharding import Mesh
from jax.sharding import PartitionSpec as P

F32 = jnp.float32
BF16 = jnp.bfloat16
SIDE = 4
ROWS = 16
STRIP = 64
BLOCK = 512
AXES = ("z", "y", "x")
EVERY = ("z", "y", "x", "pcol")
PARTS = ((0, 768, "xyz"), (768, 768, "yzx"), (1536, 512, "zxy"))
MB = 1 << 20


def split2(value):
    high = value.astype(BF16)
    return high, (value - high.astype(F32)).astype(BF16)


def dot(a, b):
    return jnp.dot(a, b, preferred_element_type=F32)


def dot_exact(a, b):
    high, low = split2(a)
    rows = a.shape[0]
    both = dot(jnp.concatenate([high, low], axis=0), b)
    return both[:rows] + both[rows:]


def dot_pair(a, b_high, b_low):
    high, low = split2(a)
    rows = a.shape[0]
    both = dot(jnp.concatenate([high, low], axis=0), b_high)
    return both[:rows] + both[rows:] + dot(high, b_low)


def pack_kernel(info, strip, out):
    out[:, : strip.shape[1]] = strip[...]
    block = strip[:, pl.ds(pl.multiple_of(info[0] * 128, 128), 128)].astype(F32)
    odd = info[1] > 0
    block = jnp.where(odd, pltpu.roll(block, 64, 1), block)
    rows = lax.broadcasted_iota(jnp.int32, block.shape, 0)
    lanes = lax.broadcasted_iota(jnp.int32, block.shape, 1)
    upper = jnp.where((lanes > rows) & (lanes < STRIP), block, 0.0)
    diagonal = jnp.sum(jnp.where(lanes == rows, block, 0.0), axis=1, keepdims=True)
    scale = jnp.broadcast_to(1.0 / diagonal, block.shape)
    todo = jnp.where(lanes == rows, 1.0, 0.0)
    for k in range(STRIP - 1, 0, -1):
        row = todo[k : k + 1, :] * scale[k : k + 1, :]
        todo = todo - upper[:, k : k + 1] * row
    inverse = todo * scale
    inverse = jnp.where(odd, pltpu.roll(inverse, 64, 1), inverse)
    high, low = split2(inverse)
    width = strip.shape[1]
    out[:, width : width + 128] = high
    out[:, width + 128 : width + 256] = low


def pack(info, strip):
    rows, width = strip.shape
    return pl.pallas_call(
        pack_kernel,
        out_shape=jax.ShapeDtypeStruct((rows, width + 256), BF16),
        in_specs=[
            pl.BlockSpec(memory_space=pltpu.SMEM),
            pl.BlockSpec(memory_space=pltpu.VMEM),
        ],
        out_specs=pl.BlockSpec(memory_space=pltpu.VMEM),
        compiler_params=pltpu.CompilerParams(vmem_limit_bytes=16 * MB),
        name="pack_inverse",
    )(info, strip)


def grow_kernel(core, window, out_high, out_low):
    width = window.shape[0]
    rows = lax.broadcasted_iota(jnp.int32, (128, 128), 0)
    lanes = lax.broadcasted_iota(jnp.int32, (128, 128), 1)
    corner = (rows < STRIP) & (lanes >= STRIP)
    level = []
    for start in range(0, width, 128):
        rng = slice(start, start + 128)
        high = window[rng, width : width + 128]
        low = window[rng, width + 128 : width + 256]
        both = high.astype(F32) + low.astype(F32)
        off = jnp.where(corner, window[rng, rng].astype(F32), 0.0).astype(BF16)
        level.append(both - dot_pair(dot_exact(both, off), high, low))
    size = 128
    while size < BLOCK:
        grown = []
        for n in range(0, len(level), 2):
            start = n * size
            off = window[start : start + size, start + size : start + 2 * size]
            high, low = split2(level[n + 1])
            corner_block = -dot_pair(dot_exact(level[n], off), high, low)
            if 2 * size < BLOCK:
                top = jnp.concatenate([level[n], corner_block], axis=1)
                bottom = jnp.concatenate([jnp.zeros_like(corner_block), level[n + 1]], axis=1)
                grown.append(jnp.concatenate([top, bottom], axis=0))
            else:
                b = n // 2
                corner_high, corner_low = split2(corner_block)
                first_high, first_low = split2(level[n])
                zero = jnp.zeros((size, size), BF16)
                for ref, first, mixed, second in (
                    (out_high, first_high, corner_high, high),
                    (out_low, first_low, corner_low, low),
                ):
                    ref[b, :size, :size] = first
                    ref[b, :size, size:] = mixed
                    ref[b, size:, :size] = zero
                    ref[b, size:, size:] = second
        level = grown
        size *= 2


def grow(core, window, slab):
    shape = jax.ShapeDtypeStruct((slab // BLOCK, BLOCK, BLOCK), BF16)
    return pl.pallas_call(
        grow_kernel,
        out_shape=(shape, shape),
        grid_spec=pltpu.PrefetchScalarGridSpec(
            num_scalar_prefetch=1,
            grid=(1,),
            in_specs=[pl.BlockSpec((slab, window.shape[1]), lambda i, core: (core[0], 0))],
            out_specs=[pl.BlockSpec(shape.shape, lambda i, core: (0, 0, 0))] * 2,
        ),
        compiler_params=pltpu.CompilerParams(vmem_limit_bytes=48 * MB),
        name="grow_inverse",
    )(core, window)


def solve_block(blocks, pending, factor, high, low, out, wait):
    for b in range(blocks):
        cols = slice(b * BLOCK, (b + 1) * BLOCK)
        wait(b)
        y = dot_pair(pending[:, cols], high[b], low[b])
        out[:, cols] = y
        if b + 1 < blocks:
            rest = slice((b + 1) * BLOCK, blocks * BLOCK)
            pending[:, rest] = pending[:, rest] - dot_exact(y, factor[cols, rest])


def solve_copies(base, slab, window, inv_high, inv_low, factor, high, low, sems):
    copies = []
    for b in range(slab // BLOCK):
        rows = pl.ds(pl.multiple_of(base + b * BLOCK, BLOCK), BLOCK)
        group = [
            pltpu.make_async_copy(inv_high.at[b], high.at[b], sems.at[0, b]),
            pltpu.make_async_copy(inv_low.at[b], low.at[b], sems.at[1, b]),
        ]
        if (b + 1) * BLOCK < slab:
            rest = pl.ds((b + 1) * BLOCK, slab - (b + 1) * BLOCK)
            group.append(
                pltpu.make_async_copy(
                    window.at[rows, rest],
                    factor.at[pl.ds(b * BLOCK, BLOCK), rest],
                    sems.at[2, b],
                )
            )
        copies.append(group)
    return copies


def first_kernel(core, right, window, inv_high, inv_low, out, factor, high, low, pending, sems):
    slab = right.shape[1]

    @pl.when(core[0] == 0)
    def _():
        copies = solve_copies(0, slab, window, inv_high, inv_low, factor, high, low, sems)
        for group in copies:
            for copy in group:
                copy.start()
        pending[...] = right[...]

        def wait(b):
            for copy in copies[b]:
                copy.wait()

        solve_block(slab // BLOCK, pending, factor, high, low, out, wait)

    @pl.when(core[0] != 0)
    def _():
        out[...] = jnp.zeros_like(out)


def second_kernel(
    core, right, own, other, window, inv_high, inv_low, out, factor, high, low, pending, below, sems, below_sems
):
    slab = right.shape[1]

    @pl.when(core[0] != 0)
    def _():
        belows = []
        for b in range(slab // BLOCK):
            rows = pl.ds(b * BLOCK, BLOCK)
            belows.append(
                pltpu.make_async_copy(window.at[rows, pl.ds(0, slab)], below.at[rows], below_sems.at[b])
            )
        copies = solve_copies(slab, slab, window, inv_high, inv_low, factor, high, low, sems)
        for copy in belows:
            copy.start()
        for group in copies:
            for copy in group:
                copy.start()
        pending[...] = right[...]
        for b in range(slab // BLOCK):
            cols = slice(b * BLOCK, (b + 1) * BLOCK)
            belows[b].wait()
            pending[...] = pending[...] - dot_exact(other[:, cols], below[cols, :])

        def wait(b):
            for copy in copies[b]:
                copy.wait()

        solve_block(slab // BLOCK, pending, factor, high, low, out, wait)

    @pl.when(core[0] == 0)
    def _():
        out[...] = own[...]


def solve_call(kernel, core, dense, window, inv_high, inv_low, extra, name):
    rows, slab = dense[0].shape
    blocks = slab // BLOCK
    vmem = pl.BlockSpec(memory_space=pltpu.VMEM)
    hbm = pl.BlockSpec(memory_space=pl.ANY)
    return pl.pallas_call(
        kernel,
        out_shape=jax.ShapeDtypeStruct((rows, slab), F32),
        in_specs=[pl.BlockSpec(memory_space=pltpu.SMEM)] + [vmem] * len(dense) + [hbm] * 3,
        out_specs=vmem,
        scratch_shapes=[
            pltpu.VMEM((slab, slab), BF16),
            pltpu.VMEM((blocks, BLOCK, BLOCK), BF16),
            pltpu.VMEM((blocks, BLOCK, BLOCK), BF16),
            pltpu.VMEM((rows, slab), F32),
        ]
        + ([pltpu.VMEM((slab, slab), BF16)] if extra else [])
        + [pltpu.SemaphoreType.DMA((3, blocks))]
        + ([pltpu.SemaphoreType.DMA((blocks,))] if extra else []),
        compiler_params=pltpu.CompilerParams(vmem_limit_bytes=40 * MB),
        name=name,
    )(core, *dense, window, inv_high, inv_low)


def product_kernel(first, start, order, left, right, out, a, b, a_sems, b_sems):
    groups, rows, _ = a.shape
    width = b.shape[1]
    for g in range(groups):
        pltpu.make_async_copy(right.at[g, pl.ds(start, width)], b.at[g], b_sems.at[g]).start()
        for n in range(rows // ROWS):
            source = pl.ds(pl.multiple_of(order[first + n] * ROWS, ROWS), ROWS)
            pltpu.make_async_copy(
                left.at[g, source], a.at[g, pl.ds(n * ROWS, ROWS)], a_sems.at[g]
            ).start()
    for g in range(groups):
        pltpu.make_async_copy(a.at[g], a.at[g], a_sems.at[g]).wait()
        pltpu.make_async_copy(b.at[g], b.at[g], b_sems.at[g]).wait()
        for col in range(0, width, 256):
            cols = slice(col, col + 256)
            term = lax.dot_general(
                a[g], b[g, cols, :], (((1,), (1,)), ((), ())), preferred_element_type=F32
            )
            if g == 0:
                out[:, cols] = term
            else:
                out[:, cols] = out[:, cols] + term


def product(order, left, right, first, rows, start, width, name):
    groups, _, depth = left.shape
    return pl.pallas_call(
        functools.partial(product_kernel, first, start),
        out_shape=jax.ShapeDtypeStruct((rows, width), F32),
        in_specs=[
            pl.BlockSpec(memory_space=pltpu.SMEM),
            pl.BlockSpec(memory_space=pl.ANY),
            pl.BlockSpec(memory_space=pl.ANY),
        ],
        out_specs=pl.BlockSpec(memory_space=pltpu.VMEM),
        scratch_shapes=[
            pltpu.VMEM((groups, rows, depth), BF16),
            pltpu.VMEM((groups, width, depth), BF16),
            pltpu.SemaphoreType.DMA((groups,)),
            pltpu.SemaphoreType.DMA((groups,)),
        ],
        compiler_params=pltpu.CompilerParams(vmem_limit_bytes=24 * MB),
        cost_estimate=pl.CostEstimate(
            flops=2 * groups * rows * width * depth,
            bytes_accessed=2 * groups * (rows + width) * depth + 4 * rows * width,
            transcendentals=0,
        ),
        name=name,
    )(order, left, right)


def partner_pairs(axis, second):
    pairs = []
    for z, y, x, c in np.ndindex(SIDE, SIDE, SIDE, 2):
        place = {"z": z, "y": y, "x": x}
        flip = (3 if c else 1) ^ (2 if second else 0)
        other = dict(place)
        other[axis] ^= flip
        index = lambda at: ((at["z"] * SIDE + at["y"]) * SIDE + at["x"]) * 2 + c
        pairs.append((index(place), index(other)))
    return pairs


def block_order(axes, place, core):
    flip = jnp.where(core == 0, 1, 3)
    masks = jnp.stack([jnp.full_like(flip, 2), flip, flip ^ 2, jnp.zeros_like(flip)])
    lists = {name: place[name] ^ masks for name in AXES}
    shape = {name: [1, 1, 1] for name in AXES}
    for position, name in enumerate(axes):
        shape[name][position] = SIDE
    at = {name: lists[name].reshape(shape[name]) for name in AXES}
    return (((at["z"] * SIDE + at["y"]) * SIDE + at["x"]).reshape(-1)).astype(jnp.int32)


def per_device(hist_factor, hist_solution, diag_factor, samples):
    slab = hist_factor.shape[1]
    samples_all = hist_solution.shape[1]
    core = lax.axis_index("pcol")
    place = {name: lax.axis_index(name) for name in AXES}
    chip = (place["z"] * SIDE + place["y"]) * SIDE + place["x"]
    core_arg = core.astype(jnp.int32).reshape(1)

    per_core = slab // STRIP
    local = chip % per_core
    info = jnp.stack([local // 2, local % 2]).astype(jnp.int32)
    packed = pack(info, diag_factor.T)
    window = lax.all_gather(packed, AXES, axis=0, tiled=True)

    half = samples_all // 2
    sends, keeps = [], []
    for number, (start, width, axes) in enumerate(PARTS):
        order = block_order(axes, place, core)
        sends.append(product(order, hist_solution, hist_factor, 0, half, start, width, f"send{number}"))
        keeps.append(
            product(order, hist_solution, hist_factor, half // ROWS, half, start, width, f"keep{number}")
        )
    for stage in range(3):
        for second in (False, True):
            got = [
                lax.ppermute(sends[n], EVERY, partner_pairs(PARTS[n][2][stage], second))
                for n in range(len(PARTS))
            ]
            if stage == 2 and second:
                keeps = [keeps[n] + got[n] for n in range(len(PARTS))]
                break
            middle = keeps[0].shape[0] // 2
            sends = [keeps[n][:middle] + got[n][:middle] for n in range(len(PARTS))]
            keeps = [keeps[n][middle:] + got[n][middle:] for n in range(len(PARTS))]
    pending = samples.astype(F32) - jnp.concatenate(keeps, axis=1)

    inv_high, inv_low = grow(core_arg, window, slab)
    first = solve_call(first_kernel, core_arg, (pending,), window, inv_high, inv_low, False, "solve0")
    other = lax.ppermute(first, "pcol", [(0, 1), (1, 0)])
    return solve_call(
        second_kernel, core_arg, (pending, first, other), window, inv_high, inv_low, True, "solve1"
    )


def solution(mesh):
    cube = Mesh(mesh.devices.reshape(SIDE, SIDE, SIDE, 2), EVERY)
    return jax.shard_map(
        per_device,
        mesh=cube,
        in_specs=(
            P(None, "pcol", AXES),
            P(None, None, AXES),
            P("pcol", AXES),
            P(AXES, "pcol"),
        ),
        out_specs=P(AXES, "pcol"),
        check_vma=False,
    )
```

time: 1020 us -> 204 us (0.20)
  waiting for transfers between devices: 496 us -> 44.2 us
  other arithmetic: 336 us -> 4.13 us
  matrix products: 73.9 us -> 0 us
  Pallas kernels: 0 us -> 69.3 us
  local copies, waits for them, and re-layouts: 94.8 us -> 37.2 us
  starting transfers between devices: 0.52 us -> 34.5 us
    another operation x4 -> x1, other arithmetic: 332 us -> 0.07 us  [per_device(): info = jnp.stack([local // 2, local % 2]).astype(jnp.int32)]
    reduce_scatter x1 -> x0, waiting for transfers between devices: 322 us -> none  [per_device(): lax.psum_scatter(jnp.einsum('brc,bsc->rs', hist_solution, hist_factor, pr...]
    all_gather x1, waiting for transfers between devices: 150 us -> 0.02 us  [per_device(): window = lax.all_gather(packed, AXES, axis=0, tiled=True)]
    another operation x162 -> x0, local copies, waits for them, and re-layouts: 94.8 us -> none  [per_device(): lax.linalg.triangular_solve(jnp.tril(tile), pending, left_side=False, low...]
    pallas_call x0 -> x10, Pallas kernels: none -> 69.3 us  [the longest x6 53.4 us: product(): pl.pallas_call(functools.partial(product_kernel, first, start), out_shape...]
    another operation x62 -> x0, matrix products: 48.2 us -> none  [per_device(): lax.linalg.triangular_solve(jnp.tril(tile), pending, left_side=False, low...]
    ppermute x0 -> x19, waiting for transfers between devices: none -> 44.1 us  [the longest x18 43.1 us: per_device(): lax.ppermute(sends[n], EVERY, partner_pairs(PARTS[n][2][stage], second))]
    unnamed x4 -> x26, local copies, waits for them, and re-layouts: 0.01 us -> 36.9 us
  transfers between devices with their start and end apart: 4 -> 20, of which waited for: 3 -> 12; matrix products, arithmetic and copies ran while one was open for 20% -> 2% of each run, Pallas kernels for 0% -> 26%
where the time goes in v1:
time: 204 us; the launch traced here: 203 us
  Pallas kernels  69.3 us (34%)
  waiting for transfers between devices  44.2 us (22%)
  local copies, waits for them, and re-layouts  37.2 us (18%)
  starting transfers between devices  34.5 us (17%)
  between operations  13.7 us (7%)
  other arithmetic  4.13 us (2%)
    pallas_call x6, Pallas kernels, product(): pl.pallas_call(functools.partial(product_kernel, first, start), out_shape...  53.4 us
    ppermute x18, waiting for transfers between devices, per_device(): lax.ppermute(sends[n], EVERY, partner_pairs(PARTS[n][2][stage], second))  43.1 us
    unnamed x26, local copies, waits for them, and re-layouts  36.9 us
    ppermute x18, starting transfers between devices, per_device(): lax.ppermute(sends[n], EVERY, partner_pairs(PARTS[n][2][stage], second))  23.6 us
    ppermute x1, starting transfers between devices, per_device(): other = lax.ppermute(first, 'pcol', [(0, 1), (1, 0)])  10.9 us
    pallas_call x1, Pallas kernels, grow(): pl.pallas_call(grow_kernel, out_shape=(shape, shape), grid_spec=pltpu.Pre...  7.27 us
    pallas_call x2, Pallas kernels, solve_call(): pl.pallas_call(kernel, out_shape=jax.ShapeDtypeStruct((rows, slab), F32),...  6.68 us
  transfers between devices with their start and end apart: 20, of which 12 were waited for; matrix products, arithmetic and copies ran while one was open for 2% of the time, Pallas kernels for 26%

profile of v1, /device:TPU:1, one launch (start us, length us, event | category | flops | bytes accessed | tf_op | source)
XLA Modules:
  0.0 203.0 jit_solution(9677138105772919267)
XLA Ops:
  6.5 0.1 pad_add_fusion.1.info
  6.6 0.9 copy-done.9
  7.6 1.9 pack_inverse.1
  9.5 0.1 xor_multiply_fusion
  9.6 0.1 add_multiply_fusion.1
  9.6 0.1 broadcast_add_fusion.2
  9.7 0.1 add.251.order
  9.8 4.6 %copy-done = bf16[3,2048,1024]{2,1,0:T(8,128)(2,1)S(1)} copy-done((bf16[3,2048,1024]{2,1,0:T(8,128)(2,1)S(1)}, bf16[3,2048,1024]{2,1,0:T(8,128)(2,1)}, u32[]{:S(2)}) %copy-start) | copy-done | bytes 12582936
  14.4 2.8 %copy-done.5 = bf16[3,1024,1024]{2,1,0:T(8,128)(2,1)S(1)} copy-done((bf16[3,1024,1024]{2,1,0:T(8,128)(2,1)S(1)}, bf16[3,1024,1024]{2,1,0:T(8,128)(2,1)}, u32[]{:S(2)}) %copy-start.5) | copy-done | bytes 6291480
  17.2 7.3 %send2.1 = f32[512,512]{1,0:T(8,128)S(1)} custom-call(s32[64]{0:T(128)S(1)} %add.251.order, bf16[3,1024,1024]{2,1,0:T(8,128)(2,1)S(1)} %copy-done.5, bf16[3,2048,1024]{2,1,0:T(8,128)(2,1)S(1)} %copy-done), custom_call_target="tpu_custom_call" | custom-call | flops 1610612736 | bytes 7340032 | tf_op jit(solution)/shard_map/send2/pallas_call | solution.py:282
  24.5 4.7 %collective-permute-start.12 = (f32[512,512]{1,0:T(8,128)S(1)}, f32[512,512]{1,0:T(8,128)}, u32[]{:S(2)}, u32[]{:S(2)}) collective-permute-start(f32[512,512]{1,0:T(8,128)S(1)} %send2.1), channel_id=1, source_target_pairs={{0,32},{1,97},{2,34},{3,99},{4,36},{5,101},{6,38},{7,103},{8,40},{... | collective-permute-start | bytes 3145736 | tf_op jit(solution)/shard_map/ppermute | solution.py:355
  29.2 0.1 add.218.order
  29.3 4.6 %copy-done.1 = bf16[3,2048,1024]{2,1,0:T(8,128)(2,1)S(1)} copy-done((bf16[3,2048,1024]{2,1,0:T(8,128)(2,1)S(1)}, bf16[3,2048,1024]{2,1,0:T(8,128)(2,1)}, u32[]{:S(2)}) %copy-start.1) | copy-done | bytes 12582936
  33.9 2.8 %copy-done.6 = bf16[3,1024,1024]{2,1,0:T(8,128)(2,1)S(1)} copy-done((bf16[3,1024,1024]{2,1,0:T(8,128)(2,1)S(1)}, bf16[3,1024,1024]{2,1,0:T(8,128)(2,1)}, u32[]{:S(2)}) %copy-start.6) | copy-done | bytes 6291480
  36.7 10.5 %send0.1 = f32[512,768]{1,0:T(8,128)} custom-call(s32[64]{0:T(128)S(1)} %add.218.order, bf16[3,1024,1024]{2,1,0:T(8,128)(2,1)S(1)} %copy-done.6, bf16[3,2048,1024]{2,1,0:T(8,128)(2,1)S(1)} %copy-done.1), custom_call_target="tpu_custom_call" | custom-call | flops 2415919104 | bytes 9437184 | tf_op jit(solution)/shard_map/send0/pallas_call | solution.py:282
  47.3 2.6 %collective-permute-start = (f32[512,768]{1,0:T(8,128)}, f32[512,768]{1,0:T(8,128)}, u32[]{:S(2)}, u32[]{:S(2)}) collective-permute-start(f32[512,768]{1,0:T(8,128)} %send0.1), channel_id=1, source_target_pairs={{0,2},{1,7},{2,0},{3,5},{4,6},{5,3},{6,4},{7,1},{8,10},{9,15},{10,... | collective-permute-start | bytes 4718600 | tf_op jit(solution)/shard_map/ppermute | solution.py:355
  49.9 0.1 add.233.order
  50.0 5.0 %copy-done.2 = bf16[3,2048,1024]{2,1,0:T(8,128)(2,1)S(1)} copy-done((bf16[3,2048,1024]{2,1,0:T(8,128)(2,1)S(1)}, bf16[3,2048,1024]{2,1,0:T(8,128)(2,1)}, u32[]{:S(2)}) %copy-start.2) | copy-done | bytes 12582936
  54.9 2.9 %copy-done.7 = bf16[3,1024,1024]{2,1,0:T(8,128)(2,1)S(1)} copy-done((bf16[3,1024,1024]{2,1,0:T(8,128)(2,1)S(1)}, bf16[3,1024,1024]{2,1,0:T(8,128)(2,1)}, u32[]{:S(2)}) %copy-start.7) | copy-done | bytes 6291480
  57.8 9.4 %send1.1 = f32[512,768]{1,0:T(8,128)S(1)} custom-call(s32[64]{0:T(128)S(1)} %add.233.order, bf16[3,1024,1024]{2,1,0:T(8,128)(2,1)S(1)} %copy-done.7, bf16[3,2048,1024]{2,1,0:T(8,128)(2,1)S(1)} %copy-done.2), custom_call_target="tpu_custom_call" | custom-call | flops 2415919104 | bytes 9437184 | tf_op jit(solution)/shard_map/send1/pallas_call | solution.py:282
  67.2 3.0 %collective-permute-start.6 = (f32[512,768]{1,0:T(8,128)S(1)}, f32[512,768]{1,0:T(8,128)S(1)}, u32[]{:S(2)}, u32[]{:S(2)}) collective-permute-start(f32[512,768]{1,0:T(8,128)S(1)} %send1.1), channel_id=1, source_target_pairs={{0,8},{1,25},{2,10},{3,27},{4,12},{5,29},{6,14},{7,31},{8,0},{9,17... | collective-permute-start | bytes 4718600 | tf_op jit(solution)/shard_map/ppermute | solution.py:355
  70.3 4.6 %copy-done.3 = bf16[3,2048,1024]{2,1,0:T(8,128)(2,1)S(1)} copy-done((bf16[3,2048,1024]{2,1,0:T(8,128)(2,1)S(1)}, bf16[3,2048,1024]{2,1,0:T(8,128)(2,1)}, u32[]{:S(2)}) %copy-start.3) | copy-done | bytes 12582936
  74.8 4.0 %copy-done.8 = bf16[3,1024,1024]{2,1,0:T(8,128)(2,1)S(1)} copy-done((bf16[3,1024,1024]{2,1,0:T(8,128)(2,1)S(1)}, bf16[3,1024,1024]{2,1,0:T(8,128)(2,1)}, u32[]{:S(2)}) %copy-start.8) | copy-done | bytes 6291480
  78.8 7.3 %keep2.1 = f32[512,512]{1,0:T(8,128)S(1)} custom-call(s32[64]{0:T(128)S(1)} %add.251.order, bf16[3,1024,1024]{2,1,0:T(8,128)(2,1)S(1)} %copy-done.8, bf16[3,2048,1024]{2,1,0:T(8,128)(2,1)S(1)} %copy-done.3), custom_call_target="tpu_custom_call" | custom-call | flops 1610612736 | bytes 7340032 | tf_op jit(solution)/shard_map/keep2/pallas_call | solution.py:282
  86.2 1.4 slice_add_fusion.5
  87.6 0.1 collective-permute-start.13
  87.7 4.8 %copy-done.4 = bf16[3,2048,1024]{2,1,0:T(8,128)(2,1)S(1)} copy-done((bf16[3,2048,1024]{2,1,0:T(8,128)(2,1)S(1)}, bf16[3,2048,1024]{2,1,0:T(8,128)(2,1)}, u32[]{:S(2)}) %copy-start.4) | copy-done | bytes 12582936
  92.5 9.4 %keep0.1 = f32[512,768]{1,0:T(8,128)S(1)} custom-call(s32[64]{0:T(128)S(1)} %add.218.order, bf16[3,1024,1024]{2,1,0:T(8,128)(2,1)S(1)} %bitcast.7, bf16[3,2048,1024]{2,1,0:T(8,128)(2,1)S(1)} %copy-done.4), custom_call_target="tpu_custom_call" | custom-call | flops 2415919104 | bytes 9437184 | tf_op jit(solution)/shard_map/keep0/pallas_call | solution.py:282
  101.9 9.4 %keep1.1 = f32[512,768]{1,0:T(8,128)S(1)} custom-call(s32[64]{0:T(128)S(1)} %add.233.order, bf16[3,1024,1024]{2,1,0:T(8,128)(2,1)S(1)} %bitcast.7, bf16[3,2048,1024]{2,1,0:T(8,128)(2,1)S(1)} %copy-done.4), custom_call_target="tpu_custom_call" | custom-call | flops 2415919104 | bytes 9437184 | tf_op jit(solution)/shard_map/keep1/pallas_call | solution.py:282
  111.3 0.1 slice_add_fusion.11
  111.4 0.1 collective-permute-start.14
  111.5 1.6 slice_add_fusion.3
  113.1 0.1 collective-permute-start.1
  113.2 13.3 %collective-permute-done.14 = f32[128,512]{1,0:T(8,128)S(1)} collective-permute-done((f32[128,512]{1,0:T(8,128)S(1)}, f32[128,512]{1,0:T(8,128)S(1)}, u32[]{:S(2)}, u32[]{:S(2)}) %collective-permute-start.14) | collective-permute-done | bytes 262176 | tf_op jit(solution)/shard_map/ppermute | solution.py:355
  126.6 0.1 collective-permute-start.15
  126.7 0.2 slice_add_fusion.1
  126.9 0.1 collective-permute-start.7
  127.0 13.3 %collective-permute-done.15 = f32[64,512]{1,0:T(8,128)S(1)} collective-permute-done((f32[64,512]{1,0:T(8,128)S(1)}, f32[64,512]{1,0:T(8,128)S(1)}, u32[]{:S(2)}, u32[]{:S(2)}) %collective-permute-start.15) | collective-permute-done | bytes 131104 | tf_op jit(solution)/shard_map/ppermute | solution.py:355
  140.3 2.5 %collective-permute-start.16 = (f32[32,512]{1,0:T(8,128)S(1)}, f32[32,512]{1,0:T(8,128)S(1)}, u32[]{:S(2)}, u32[]{:S(2)}) collective-permute-start(f32[32,512]{1,0:T(8,128)S(1)} %get-tuple-element.34), channel_id=1, source_target_pairs={{0,8},{1,25},{2,10},{3,27},{4,12},{5,29},{6,14},{7,31},{8,0},{9,17... | collective-permute-start | bytes 196616 | tf_op jit(solution)/shard_map/ppermute | solution.py:355
  142.8 2.9 %collective-permute-done.16 = f32[32,512]{1,0:T(8,128)S(1)} collective-permute-done((f32[32,512]{1,0:T(8,128)S(1)}, f32[32,512]{1,0:T(8,128)S(1)}, u32[]{:S(2)}, u32[]{:S(2)}) %collective-permute-start.16) | collective-permute-done | bytes 65568 | tf_op jit(solution)/shard_map/ppermute | solution.py:355
  145.8 0.1 slice_add_fusion.9
  145.9 2.8 %collective-permute-start.2 = (f32[128,768]{1,0:T(8,128)S(1)}, f32[128,768]{1,0:T(8,128)S(1)}, u32[]{:S(2)}, u32[]{:S(2)}) collective-permute-start(f32[128,768]{1,0:T(8,128)S(1)} %get-tuple-element.18), channel_id=1, source_target_pairs={{0,8},{1,25},{2,10},{3,27},{4,12},{5,29},{6,14},{7,31},{8,0},{9,17... | collective-permute-start | bytes 1179656 | tf_op jit(solution)/shard_map/ppermute | solution.py:355
  148.6 0.1 slice_add_fusion.7
  148.7 2.1 %collective-permute-start.8 = (f32[128,768]{1,0:T(8,128)S(1)}, f32[128,768]{1,0:T(8,128)S(1)}, u32[]{:S(2)}, u32[]{:S(2)}) collective-permute-start(f32[128,768]{1,0:T(8,128)S(1)} %get-tuple-element.20), channel_id=1, source_target_pairs={{0,32},{1,97},{2,34},{3,99},{4,36},{5,101},{6,38},{7,103},{8,40},{... | collective-permute-start | bytes 1179656 | tf_op jit(solution)/shard_map/ppermute | solution.py:355
  150.8 3.5 %collective-permute-done.2 = f32[128,768]{1,0:T(8,128)S(1)} collective-permute-done((f32[128,768]{1,0:T(8,128)S(1)}, f32[128,768]{1,0:T(8,128)S(1)}, u32[]{:S(2)}, u32[]{:S(2)}) %collective-permute-start.2) | collective-permute-done | bytes 393248 | tf_op jit(solution)/shard_map/ppermute | solution.py:355
  154.3 0.1 slice_add_fusion.15
  154.4 0.8 collective-permute-start.3
  155.2 1.4 collective-permute-done.8
  156.7 0.4 collective-permute-start.9
  157.1 1.9 collective-permute-done.3
  159.0 2.2 %collective-permute-start.4 = (f32[32,768]{1,0:T(8,128)S(1)}, f32[32,768]{1,0:T(8,128)S(1)}, u32[]{:S(2)}, u32[]{:S(2)}) collective-permute-start(f32[32,768]{1,0:T(8,128)S(1)} %get-tuple-element.30), channel_id=1, source_target_pairs={{0,32},{1,97},{2,34},{3,99},{4,36},{5,101},{6,38},{7,103},{8,40},{... | collective-permute-start | bytes 294920 | tf_op jit(solution)/shard_map/ppermute | solution.py:355
  161.2 0.4 collective-permute-done.9
  161.6 1.9 collective-permute-start.10
  163.5 1.6 collective-permute-done.4
  165.1 0.1 collective-permute-start.5
  165.3 1.1 collective-permute-done.10
  166.4 0.1 collective-permute-start.11
  166.5 2.4 %collective-permute-done.5 = f32[16,768]{1,0:T(8,128)S(1)} collective-permute-done((f32[16,768]{1,0:T(8,128)S(1)}, f32[16,768]{1,0:T(8,128)S(1)}, u32[]{:S(2)}, u32[]{:S(2)}) %collective-permute-start.5) | collective-permute-done | bytes 49184 | tf_op jit(solution)/shard_map/ppermute | solution.py:355
  168.9 1.3 collective-permute-done.11
  170.3 7.3 %grow_inverse.1 = (bf16[4,512,512]{2,1,0:T(8,128)(2,1)S(1)}, bf16[4,512,512]{2,1,0:T(8,128)(2,1)S(1)}) custom-call(s32[1]{0:T(128)} %bitcast.core, bf16[4096,2304]{1,0:T(8,128)(2,1)} %all-gather.2.cloned.1.call-done.window), custom_call_target="tpu_custom_call" | custom-call | tf_op jit(solution)/shard_map/grow_inverse/pallas_call | solution.py:128
  177.6 0.1 solve0.1.own
  177.7 10.9 %collective-permute-start.18 = (f32[16,2048]{1,0:T(8,128)S(1)}, f32[16,2048]{1,0:T(8,128)S(1)}, u32[]{:S(2)}, u32[]{:S(2)}) collective-permute-start(f32[16,2048]{1,0:T(8,128)S(1)} %solve0.1.own), channel_id=1, source_target_pairs={{0,1},{1,0},{2,3},{3,2},{4,5},{5,4},{6,7},{7,6},{8,9},{9,8},{10,11... | collective-permute-start | bytes 393224 | tf_op jit(solution)/shard_map/ppermute | solution.py:368
  188.6 1.0 collective-permute-done.18.other
  189.6 6.5 %solve1.1 = f32[16,2048]{1,0:T(8,128)} custom-call(s32[1]{0:T(128)} %bitcast.core, f32[16,2048]{1,0:T(8,128)S(1)} %maximum_subtract_fusion.right, f32[16,2048]{1,0:T(8,128)S(1)} %solve0.1.own, f32[16,2048]{1,0:T(8,128)S(1)} %collective-permute-done.18.other, bf16[4096,2304]{1,0:T(8,128)(2,1)} %all-gather.2.cloned.1.call-done.window, ...), custom_call_target="tpu_custom_call" | custom-call | tf_op jit(solution)/shard_map/solve1/pallas_call | solution.py:237
  (41 shorter events, 0.3 us)
Async XLA Ops:
  6.5 163.7 %all-gather.2.cloned.1.call-start = ((), (), s32[]{:S(2)}) async-start(), calls=%async_computation | async-start | bytes 19169280 | tf_op jit(solution)/shard_map/all_gather | solution.py:342
  6.6 0.9 copy-start.9
  9.8 4.6 %copy-start = (bf16[3,2048,1024]{2,1,0:T(8,128)(2,1)S(1)}, bf16[3,2048,1024]{2,1,0:T(8,128)(2,1)}, u32[]{:S(2)}) copy-start(bf16[3,2048,1024]{2,1,0:T(8,128)(2,1)} %right.11) | copy-start | bytes 37748740
  14.4 2.8 %copy-start.5 = (bf16[3,1024,1024]{2,1,0:T(8,128)(2,1)S(1)}, bf16[3,1024,1024]{2,1,0:T(8,128)(2,1)}, u32[]{:S(2)}) copy-start(bf16[3,1024,1024]{2,1,0:T(8,128)(2,1)} %left.11) | copy-start | bytes 18874372
  24.5 61.6 %collective-permute-start.12 = (f32[512,512]{1,0:T(8,128)S(1)}, f32[512,512]{1,0:T(8,128)}, u32[]{:S(2)}, u32[]{:S(2)}) collective-permute-start(f32[512,512]{1,0:T(8,128)S(1)} %send2.1), channel_id=1, source_target_pairs={{0,32},{1,97},{2,34},{3,99},{4,36},{5,101},{6,38},{7,103},{8,40},{... | collective-permute-start | bytes 3145736 | tf_op jit(solution)/shard_map/ppermute | solution.py:355
  29.3 4.7 %copy-start.1 = (bf16[3,2048,1024]{2,1,0:T(8,128)(2,1)S(1)}, bf16[3,2048,1024]{2,1,0:T(8,128)(2,1)}, u32[]{:S(2)}) copy-start(bf16[3,2048,1024]{2,1,0:T(8,128)(2,1)} %right.11) | copy-start | bytes 37748740
  33.9 2.8 %copy-start.6 = (bf16[3,1024,1024]{2,1,0:T(8,128)(2,1)S(1)}, bf16[3,1024,1024]{2,1,0:T(8,128)(2,1)}, u32[]{:S(2)}) copy-start(bf16[3,1024,1024]{2,1,0:T(8,128)(2,1)} %left.11) | copy-start | bytes 18874372
  36.7 51.0 %slice-start = ((s8[6291456]{0:T(1024)(128)(4,1)}), s8[2097152]{0:T(1024)(128)(4,1)S(1)}, s32[]{:S(2)}) async-start(s8[6291456]{0:T(1024)(128)(4,1)} %bitcast.6), calls=%async_computation.1 | async-start | bytes 4194304
  47.3 64.2 %collective-permute-start = (f32[512,768]{1,0:T(8,128)}, f32[512,768]{1,0:T(8,128)}, u32[]{:S(2)}, u32[]{:S(2)}) collective-permute-start(f32[512,768]{1,0:T(8,128)} %send0.1), channel_id=1, source_target_pairs={{0,2},{1,7},{2,0},{3,5},{4,6},{5,3},{6,4},{7,1},{8,10},{9,15},{10,... | collective-permute-start | bytes 4718600 | tf_op jit(solution)/shard_map/ppermute | solution.py:355
  49.9 5.0 %copy-start.2 = (bf16[3,2048,1024]{2,1,0:T(8,128)(2,1)S(1)}, bf16[3,2048,1024]{2,1,0:T(8,128)(2,1)}, u32[]{:S(2)}) copy-start(bf16[3,2048,1024]{2,1,0:T(8,128)(2,1)} %right.11) | copy-start | bytes 37748740
  54.9 2.9 %copy-start.7 = (bf16[3,1024,1024]{2,1,0:T(8,128)(2,1)S(1)}, bf16[3,1024,1024]{2,1,0:T(8,128)(2,1)}, u32[]{:S(2)}) copy-start(bf16[3,1024,1024]{2,1,0:T(8,128)(2,1)} %left.11) | copy-start | bytes 18874372
  57.8 29.9 %slice-start.1 = ((s8[6291456]{0:T(1024)(128)(4,1)}), s8[4194304]{0:T(1024)(128)(4,1)S(1)}, s32[]{:S(2)}) async-start(s8[6291456]{0:T(1024)(128)(4,1)} %bitcast.6), calls=%async_computation.2 | async-start | bytes 8388608
  67.2 59.4 %collective-permute-start.6 = (f32[512,768]{1,0:T(8,128)S(1)}, f32[512,768]{1,0:T(8,128)S(1)}, u32[]{:S(2)}, u32[]{:S(2)}) collective-permute-start(f32[512,768]{1,0:T(8,128)S(1)} %send1.1), channel_id=1, source_target_pairs={{0,8},{1,25},{2,10},{3,27},{4,12},{5,29},{6,14},{7,31},{8,0},{9,17... | collective-permute-start | bytes 4718600 | tf_op jit(solution)/shard_map/ppermute | solution.py:355
  70.2 4.6 %copy-start.3 = (bf16[3,2048,1024]{2,1,0:T(8,128)(2,1)S(1)}, bf16[3,2048,1024]{2,1,0:T(8,128)(2,1)}, u32[]{:S(2)}) copy-start(bf16[3,2048,1024]{2,1,0:T(8,128)(2,1)} %right.11) | copy-start | bytes 37748740
  74.8 4.0 %copy-start.8 = (bf16[3,1024,1024]{2,1,0:T(8,128)(2,1)S(1)}, bf16[3,1024,1024]{2,1,0:T(8,128)(2,1)}, u32[]{:S(2)}) copy-start(bf16[3,1024,1024]{2,1,0:T(8,128)(2,1)} %left.11) | copy-start | bytes 18874372
  87.6 23.7 %collective-permute-start.13 = (f32[256,512]{1,0:T(8,128)S(1)}, f32[256,512]{1,0:T(8,128)S(1)}, u32[]{:S(2)}, u32[]{:S(2)}) collective-permute-start(f32[256,512]{1,0:T(8,128)S(1)} %get-tuple-element.16), channel_id=1, source_target_pairs={{0,96},{1,33},{2,98},{3,35},{4,100},{5,37},{6,102},{7,39},{8,104},... | collective-permute-start | bytes 1572872 | tf_op jit(solution)/shard_map/ppermute | solution.py:355
  87.7 4.8 %copy-start.4 = (bf16[3,2048,1024]{2,1,0:T(8,128)(2,1)S(1)}, bf16[3,2048,1024]{2,1,0:T(8,128)(2,1)}, u32[]{:S(2)}) copy-start(bf16[3,2048,1024]{2,1,0:T(8,128)(2,1)} %right.11) | copy-start | bytes 37748740
  111.4 15.1 %collective-permute-start.14 = (f32[128,512]{1,0:T(8,128)S(1)}, f32[128,512]{1,0:T(8,128)S(1)}, u32[]{:S(2)}, u32[]{:S(2)}) collective-permute-start(f32[128,512]{1,0:T(8,128)S(1)} %get-tuple-element.22), channel_id=1, source_target_pairs={{0,2},{1,7},{2,0},{3,5},{4,6},{5,3},{6,4},{7,1},{8,10},{9,15},{10,... | collective-permute-start | bytes 786440 | tf_op jit(solution)/shard_map/ppermute | solution.py:355
  113.1 32.6 %collective-permute-start.1 = (f32[256,768]{1,0:T(8,128)S(1)}, f32[256,768]{1,0:T(8,128)S(1)}, u32[]{:S(2)}, u32[]{:S(2)}) collective-permute-start(f32[256,768]{1,0:T(8,128)S(1)} %get-tuple-element.12), channel_id=1, source_target_pairs={{0,6},{1,3},{2,4},{3,1},{4,2},{5,7},{6,0},{7,5},{8,14},{9,11},{10,... | collective-permute-start | bytes 2359304 | tf_op jit(solution)/shard_map/ppermute | solution.py:355
  126.6 13.7 %collective-permute-start.15 = (f32[64,512]{1,0:T(8,128)S(1)}, f32[64,512]{1,0:T(8,128)S(1)}, u32[]{:S(2)}, u32[]{:S(2)}) collective-permute-start(f32[64,512]{1,0:T(8,128)S(1)} %get-tuple-element.28), channel_id=1, source_target_pairs={{0,6},{1,3},{2,4},{3,1},{4,2},{5,7},{6,0},{7,5},{8,14},{9,11},{10,... | collective-permute-start | bytes 393224 | tf_op jit(solution)/shard_map/ppermute | solution.py:355
  126.9 21.7 %collective-permute-start.7 = (f32[256,768]{1,0:T(8,128)S(1)}, f32[256,768]{1,0:T(8,128)S(1)}, u32[]{:S(2)}, u32[]{:S(2)}) collective-permute-start(f32[256,768]{1,0:T(8,128)S(1)} %get-tuple-element.14), channel_id=1, source_target_pairs={{0,24},{1,9},{2,26},{3,11},{4,28},{5,13},{6,30},{7,15},{8,16},{9,1... | collective-permute-start | bytes 2359304 | tf_op jit(solution)/shard_map/ppermute | solution.py:355
  140.3 5.5 %collective-permute-start.16 = (f32[32,512]{1,0:T(8,128)S(1)}, f32[32,512]{1,0:T(8,128)S(1)}, u32[]{:S(2)}, u32[]{:S(2)}) collective-permute-start(f32[32,512]{1,0:T(8,128)S(1)} %get-tuple-element.34), channel_id=1, source_target_pairs={{0,8},{1,25},{2,10},{3,27},{4,12},{5,29},{6,14},{7,31},{8,0},{9,17... | collective-permute-start | bytes 196616 | tf_op jit(solution)/shard_map/ppermute | solution.py:355
  145.7 5.1 %collective-permute-start.17 = (f32[16,512]{1,0:T(8,128)S(1)}, f32[16,512]{1,0:T(8,128)S(1)}, u32[]{:S(2)}, u32[]{:S(2)}) collective-permute-start(f32[16,512]{1,0:T(8,128)S(1)} %slice_add_fusion.28), channel_id=1, source_target_pairs={{0,24},{1,9},{2,26},{3,11},{4,28},{5,13},{6,30},{7,15},{8,16},{9,1... | collective-permute-start | bytes 98312 | tf_op jit(solution)/shard_map/ppermute | solution.py:355
  145.9 8.5 %collective-permute-start.2 = (f32[128,768]{1,0:T(8,128)S(1)}, f32[128,768]{1,0:T(8,128)S(1)}, u32[]{:S(2)}, u32[]{:S(2)}) collective-permute-start(f32[128,768]{1,0:T(8,128)S(1)} %get-tuple-element.18), channel_id=1, source_target_pairs={{0,8},{1,25},{2,10},{3,27},{4,12},{5,29},{6,14},{7,31},{8,0},{9,17... | collective-permute-start | bytes 1179656 | tf_op jit(solution)/shard_map/ppermute | solution.py:355
  148.7 7.9 %collective-permute-start.8 = (f32[128,768]{1,0:T(8,128)S(1)}, f32[128,768]{1,0:T(8,128)S(1)}, u32[]{:S(2)}, u32[]{:S(2)}) collective-permute-start(f32[128,768]{1,0:T(8,128)S(1)} %get-tuple-element.20), channel_id=1, source_target_pairs={{0,32},{1,97},{2,34},{3,99},{4,36},{5,101},{6,38},{7,103},{8,40},{... | collective-permute-start | bytes 1179656 | tf_op jit(solution)/shard_map/ppermute | solution.py:355
  154.4 15.8 %copy-start.10 = (bf16[16,2048]{1,0:T(8,128)(2,1)S(1)}, bf16[16,2048]{1,0:T(8,128)(2,1)}, u32[]{:S(2)}) copy-start(bf16[16,2048]{1,0:T(8,128)(2,1)} %param.7) | copy-start | bytes 196612
  154.4 4.6 %collective-permute-start.3 = (f32[64,768]{1,0:T(8,128)S(1)}, f32[64,768]{1,0:T(8,128)S(1)}, u32[]{:S(2)}, u32[]{:S(2)}) collective-permute-start(f32[64,768]{1,0:T(8,128)S(1)} %get-tuple-element.24), channel_id=1, source_target_pairs={{0,24},{1,9},{2,26},{3,11},{4,28},{5,13},{6,30},{7,15},{8,16},{9,1... | collective-permute-start | bytes 589832 | tf_op jit(solution)/shard_map/ppermute | solution.py:355
  156.7 4.9 %collective-permute-start.9 = (f32[64,768]{1,0:T(8,128)S(1)}, f32[64,768]{1,0:T(8,128)S(1)}, u32[]{:S(2)}, u32[]{:S(2)}) collective-permute-start(f32[64,768]{1,0:T(8,128)S(1)} %get-tuple-element.26), channel_id=1, source_target_pairs={{0,96},{1,33},{2,98},{3,35},{4,100},{5,37},{6,102},{7,39},{8,104},... | collective-permute-start | bytes 589832 | tf_op jit(solution)/shard_map/ppermute | solution.py:355
  159.0 6.1 %collective-permute-start.4 = (f32[32,768]{1,0:T(8,128)S(1)}, f32[32,768]{1,0:T(8,128)S(1)}, u32[]{:S(2)}, u32[]{:S(2)}) collective-permute-start(f32[32,768]{1,0:T(8,128)S(1)} %get-tuple-element.30), channel_id=1, source_target_pairs={{0,32},{1,97},{2,34},{3,99},{4,36},{5,101},{6,38},{7,103},{8,40},{... | collective-permute-start | bytes 294920 | tf_op jit(solution)/shard_map/ppermute | solution.py:355
  161.6 4.8 %collective-permute-start.10 = (f32[32,768]{1,0:T(8,128)S(1)}, f32[32,768]{1,0:T(8,128)S(1)}, u32[]{:S(2)}, u32[]{:S(2)}) collective-permute-start(f32[32,768]{1,0:T(8,128)S(1)} %get-tuple-element.32), channel_id=1, source_target_pairs={{0,2},{1,7},{2,0},{3,5},{4,6},{5,3},{6,4},{7,1},{8,10},{9,15},{10,... | collective-permute-start | bytes 294920 | tf_op jit(solution)/shard_map/ppermute | solution.py:355
  165.1 3.8 %collective-permute-start.5 = (f32[16,768]{1,0:T(8,128)S(1)}, f32[16,768]{1,0:T(8,128)S(1)}, u32[]{:S(2)}, u32[]{:S(2)}) collective-permute-start(f32[16,768]{1,0:T(8,128)S(1)} %slice_add_fusion.26), channel_id=1, source_target_pairs={{0,96},{1,33},{2,98},{3,35},{4,100},{5,37},{6,102},{7,39},{8,104},... | collective-permute-start | bytes 147464 | tf_op jit(solution)/shard_map/ppermute | solution.py:355
  166.4 3.8 %collective-permute-start.11 = (f32[16,768]{1,0:T(8,128)S(1)}, f32[16,768]{1,0:T(8,128)S(1)}, u32[]{:S(2)}, u32[]{:S(2)}) collective-permute-start(f32[16,768]{1,0:T(8,128)S(1)} %slice_add_fusion.24), channel_id=1, source_target_pairs={{0,6},{1,3},{2,4},{3,1},{4,2},{5,7},{6,0},{7,5},{8,14},{9,11},{10,... | collective-permute-start | bytes 147464 | tf_op jit(solution)/shard_map/ppermute | solution.py:355
  177.7 11.9 %collective-permute-start.18 = (f32[16,2048]{1,0:T(8,128)S(1)}, f32[16,2048]{1,0:T(8,128)S(1)}, u32[]{:S(2)}, u32[]{:S(2)}) collective-permute-start(f32[16,2048]{1,0:T(8,128)S(1)} %solve0.1.own), channel_id=1, source_target_pairs={{0,1},{1,0},{2,3},{3,2},{4,5},{5,4},{6,7},{7,6},{8,9},{9,8},{10,11... | collective-permute-start | bytes 393224 | tf_op jit(solution)/shard_map/ppermute | solution.py:368
Sparse Core Ops, SparseCore 0:
  10.1 133.9 all-gather.1

commit v2 on v1

--- a/solution.py
+++ b/solution.py
@@ -233,7 +233,7 @@
     rows, slab = dense[0].shape
     blocks = slab // BLOCK
     vmem = pl.BlockSpec(memory_space=pltpu.VMEM)
-    hbm = pl.BlockSpec(memory_space=pl.ANY)
+    hbm = pl.BlockSpec(memory_space=pltpu.HBM)
     return pl.pallas_call(
         kernel,
         out_shape=jax.ShapeDtypeStruct((rows, slab), F32),
@@ -253,51 +253,67 @@
     )(core, *dense, window, inv_high, inv_low)
 
 
-def product_kernel(first, start, order, left, right, out, a, b, a_sems, b_sems):
-    groups, rows, _ = a.shape
-    width = b.shape[1]
+def product_kernel(parts, half, order, left, right, *refs):
+    outs, (a, b, picked, a_sems, b_sems) = refs[: len(parts)], refs[len(parts) :]
+    groups, _, depth = left.shape
+    rows = picked.shape[0]
+    spans = [(n, col) for n in range(len(parts)) for col in range(0, parts[n][2], 256)]
+    loads = []
     for g in range(groups):
-        pltpu.make_async_copy(right.at[g, pl.ds(start, width)], b.at[g], b_sems.at[g]).start()
-        for n in range(rows // ROWS):
-            source = pl.ds(pl.multiple_of(order[first + n] * ROWS, ROWS), ROWS)
-            pltpu.make_async_copy(
-                left.at[g, source], a.at[g, pl.ds(n * ROWS, ROWS)], a_sems.at[g]
-            ).start()
-    for g in range(groups):
-        pltpu.make_async_copy(a.at[g], a.at[g], a_sems.at[g]).wait()
-        pltpu.make_async_copy(b.at[g], b.at[g], b_sems.at[g]).wait()
-        for col in range(0, width, 256):
-            cols = slice(col, col + 256)
-            term = lax.dot_general(
-                a[g], b[g, cols, :], (((1,), (1,)), ((), ())), preferred_element_type=F32
+        lanes = pl.ds(g * depth, depth)
+        copy = pltpu.make_async_copy(left.at[g], a.at[:, lanes], a_sems.at[g])
+        copy.start()
+        loads.append(copy)
+    tiles = []
+    for t, (n, col) in enumerate(spans):
+        tile = []
+        for g in range(groups):
+            lanes = pl.ds(g * depth, depth)
+            copy = pltpu.make_async_copy(
+                right.at[g, pl.ds(parts[n][1] + col, 256)], b.at[t, :, lanes], b_sems.at[t, g]
             )
-            if g == 0:
-                out[:, cols] = term
-            else:
-                out[:, cols] = out[:, cols] + term
-
-
-def product(order, left, right, first, rows, start, width, name):
-    groups, _, depth = left.shape
+            copy.start()
+            tile.append(copy)
+        tiles.append(tile)
+    for t, (n, col) in enumerate(spans):
+        if col == 0:
+            if t == 0:
+                for copy in loads:
+                    copy.wait()
+            base = parts[n][0] * 2 * (rows // ROWS) + half * (rows // ROWS)
+            for r in range(rows // ROWS):
+                source = pl.ds(pl.multiple_of(order[base + r] * ROWS, ROWS), ROWS)
+                picked[r * ROWS : (r + 1) * ROWS, :] = a[source, :]
+        for copy in tiles[t]:
+            copy.wait()
+        outs[n][:, col : col + 256] = lax.dot_general(
+            picked[...], b[t], (((1,), (1,)), ((), ())), preferred_element_type=F32
+        )
+
+
+def product(order, left, right, parts, half, name):
+    groups, rows, depth = left.shape
+    width = sum(part[2] for part in parts)
     return pl.pallas_call(
-        functools.partial(product_kernel, first, start),
-        out_shape=jax.ShapeDtypeStruct((rows, width), F32),
+        functools.partial(product_kernel, parts, half),
+        out_shape=[jax.ShapeDtypeStruct((rows // 2, part[2]), F32) for part in parts],
         in_specs=[
             pl.BlockSpec(memory_space=pltpu.SMEM),
-            pl.BlockSpec(memory_space=pl.ANY),
-            pl.BlockSpec(memory_space=pl.ANY),
+            pl.BlockSpec(memory_space=pltpu.HBM),
+            pl.BlockSpec(memory_space=pltpu.HBM),
         ],
-        out_specs=pl.BlockSpec(memory_space=pltpu.VMEM),
+        out_specs=[pl.BlockSpec(memory_space=pltpu.VMEM)] * len(parts),
         scratch_shapes=[
-            pltpu.VMEM((groups, rows, depth), BF16),
-            pltpu.VMEM((groups, width, depth), BF16),
+            pltpu.VMEM((rows, groups * depth), BF16),
+            pltpu.VMEM((width // 256, 256, groups * depth), BF16),
+            pltpu.VMEM((rows // 2, groups * depth), BF16),
             pltpu.SemaphoreType.DMA((groups,)),
-            pltpu.SemaphoreType.DMA((groups,)),
+            pltpu.SemaphoreType.DMA((width // 256, groups)),
         ],
-        compiler_params=pltpu.CompilerParams(vmem_limit_bytes=24 * MB),
+        compiler_params=pltpu.CompilerParams(vmem_limit_bytes=40 * MB),
         cost_estimate=pl.CostEstimate(
-            flops=2 * groups * rows * width * depth,
-            bytes_accessed=2 * groups * (rows + width) * depth + 4 * rows * width,
+            flops=groups * rows * width * depth,
+            bytes_accessed=2 * groups * (rows + width) * depth + 2 * rows * width,
             transcendentals=0,
         ),
         name=name,
@@ -329,7 +345,6 @@
 
 def per_device(hist_factor, hist_solution, diag_factor, samples):
     slab = hist_factor.shape[1]
-    samples_all = hist_solution.shape[1]
     core = lax.axis_index("pcol")
     place = {name: lax.axis_index(name) for name in AXES}
     chip = (place["z"] * SIDE + place["y"]) * SIDE + place["x"]
@@ -341,14 +356,13 @@
     packed = pack(info, diag_factor.T)
     window = lax.all_gather(packed, AXES, axis=0, tiled=True)
 
-    half = samples_all // 2
-    sends, keeps = [], []
-    for number, (start, width, axes) in enumerate(PARTS):
-        order = block_order(axes, place, core)
-        sends.append(product(order, hist_solution, hist_factor, 0, half, start, width, f"send{number}"))
-        keeps.append(
-            product(order, hist_solution, hist_factor, half // ROWS, half, start, width, f"keep{number}")
-        )
+    order = jnp.concatenate([block_order(axes, place, core) for _, _, axes in PARTS])
+    parts = [(n, start, width) for n, (start, width, _) in enumerate(PARTS)]
+    sends = [
+        *product(order, hist_solution, hist_factor, parts[:1], 0, "send_first"),
+        *product(order, hist_solution, hist_factor, parts[1:], 0, "send_rest"),
+    ]
+    keeps = list(product(order, hist_solution, hist_factor, parts, 1, "keep_all"))
     for stage in range(3):
         for second in (False, True):
             got = [

time: 204 us -> 176 us (0.86)
  waiting for transfers between devices: 44.2 us -> 82.2 us
  local copies, waits for them, and re-layouts: 37.2 us -> 4.03 us
  Pallas kernels: 69.3 us -> 52.6 us
  starting transfers between devices: 34.5 us -> 21.6 us
  other arithmetic: 4.13 us -> 1.6 us
    ppermute x18, waiting for transfers between devices: 43.1 us -> 81.2 us  [per_device(): lax.ppermute(sends[n], EVERY, partner_pairs(PARTS[n][2][stage], second))]
    unnamed x26 -> x6, local copies, waits for them, and re-layouts: 36.9 us -> 3.75 us
    pallas_call x6 -> x3, Pallas kernels: 53.4 us -> 36.8 us  [product(): pl.pallas_call(functools.partial(product_kernel, parts, half), out_shape=...]
    ppermute x18, starting transfers between devices: 23.6 us -> 13.6 us  [per_device(): lax.ppermute(sends[n], EVERY, partner_pairs(PARTS[n][2][stage], second))]
    ppermute x1, starting transfers between devices: 10.9 us -> 7.98 us  [per_device(): other = lax.ppermute(first, 'pcol', [(0, 1), (1, 0)])]
    add x12, other arithmetic: 3.76 us -> 1.15 us  [per_device(): keeps = [keeps[n][middle:] + got[n][middle:] for n in range(len(PARTS))]]
  transfers between devices with their start and end apart: 20 -> 20, of which waited for: 12 -> 12; matrix products, arithmetic and copies ran while one was open for 2% -> 1% of each run, Pallas kernels for 26% -> 21%
where the time goes in v2:
time: 176 us
  waiting for transfers between devices  82.2 us (47%)
  Pallas kernels  52.6 us (30%)
  starting transfers between devices  21.6 us (12%)
  between operations  13.7 us (8%)
  local copies, waits for them, and re-layouts  4.03 us (2%)
    ppermute x18, waiting for transfers between devices, per_device(): lax.ppermute(sends[n], EVERY, partner_pairs(PARTS[n][2][stage], second))  81.2 us
    pallas_call x3, Pallas kernels, product(): pl.pallas_call(functools.partial(product_kernel, parts, half), out_shape=...  36.8 us
    ppermute x18, starting transfers between devices, per_device(): lax.ppermute(sends[n], EVERY, partner_pairs(PARTS[n][2][stage], second))  13.6 us
    ppermute x1, starting transfers between devices, per_device(): other = lax.ppermute(first, 'pcol', [(0, 1), (1, 0)])  7.98 us
    pallas_call x1, Pallas kernels, grow(): pl.pallas_call(grow_kernel, out_shape=(shape, shape), grid_spec=pltpu.Pre...  7.28 us
    pallas_call x2, Pallas kernels, solve_call(): pl.pallas_call(kernel, out_shape=jax.ShapeDtypeStruct((rows, slab), F32),...  6.67 us
    unnamed x6, local copies, waits for them, and re-layouts  3.75 us
  transfers between devices with their start and end apart: 20, of which 12 were waited for; matrix products, arithmetic and copies ran while one was open for 1% of the time, Pallas kernels for 21%

profile of v2, /device:TPU:1, one launch (start us, length us, event | category | flops | bytes accessed | tf_op | source)
XLA Modules:
  0.0 175.8 jit_solution(2994217233237820381)
XLA Ops:
  6.5 0.1 pad_add_fusion.2.info
  6.6 0.9 copy-done.1
  7.6 1.9 %pack_inverse.1 = bf16[64,2304]{1,0:T(8,128)(2,1)} custom-call(s32[2]{0:T(128)S(1)} %pad_add_fusion.2.info, bf16[64,2048]{1,0:T(8,128)(2,1)S(1)} %bitcast.6), custom_call_target="tpu_custom_call" | custom-call | tf_op jit(solution)/shard_map/pack_inverse/pallas_call | solution.py:71
  9.4 0.0 all-gather.2.cloned.1.call-update
  9.5 0.1 xor_multiply_fusion
  9.6 0.1 add_multiply_fusion.1
  9.6 0.1 broadcast_add_fusion.2
  9.7 0.1 add.218
  9.8 0.1 add.222
  9.9 0.1 add.229
  10.0 0.1 pad_add_fusion.order
  10.1 2.8 %copy-done = bf16[3,1024,1024]{2,1,0:T(8,128)(2,1)S(1)} copy-done((bf16[3,1024,1024]{2,1,0:T(8,128)(2,1)S(1)}, bf16[3,1024,1024]{2,1,0:T(8,128)(2,1)}, u32[]{:S(2)}) %copy-start) | copy-done | bytes 6291480
  12.9 11.3 %send_rest.1 = (f32[512,768]{1,0:T(8,128)S(1)}, f32[512,512]{1,0:T(8,128)S(1)}) custom-call(s32[192]{0:T(256)S(1)} %pad_add_fusion.order, bf16[3,1024,1024]{2,1,0:T(8,128)(2,1)S(1)} %copy-done, bf16[3,2048,1024]{2,1,0:T(8,128)(2,1)} %right.5), custom_call_target="tpu_custom_call" | custom-call | flops 4026531840 | bytes 16777216 | tf_op jit(solution)/shard_map/send_rest/pallas_call | solution.py:297
  24.2 4.7 %collective-permute-start.12 = (f32[512,512]{1,0:T(8,128)S(1)}, f32[512,512]{1,0:T(8,128)S(1)}, u32[]{:S(2)}, u32[]{:S(2)}) collective-permute-start(f32[512,512]{1,0:T(8,128)S(1)} %get-tuple-element.16), channel_id=1, source_target_pairs={{0,32},{1,97},{2,34},{3,99},{4,36},{5,101},{6,38},{7,103},{8,40},{... | collective-permute-start | bytes 3145736 | tf_op jit(solution)/shard_map/ppermute | solution.py:369
  28.8 7.5 %send_first.1 = f32[512,768]{1,0:T(8,128)S(1)} custom-call(s32[192]{0:T(256)S(1)} %pad_add_fusion.order, bf16[3,1024,1024]{2,1,0:T(8,128)(2,1)S(1)} %copy-done, bf16[3,2048,1024]{2,1,0:T(8,128)(2,1)} %right.5), custom_call_target="tpu_custom_call" | custom-call | flops 2415919104 | bytes 12582912 | tf_op jit(solution)/shard_map/send_first/pallas_call | solution.py:297
  36.3 2.6 %collective-permute-start = (f32[512,768]{1,0:T(8,128)S(1)}, f32[512,768]{1,0:T(8,128)S(1)}, u32[]{:S(2)}, u32[]{:S(2)}) collective-permute-start(f32[512,768]{1,0:T(8,128)S(1)} %send_first.1), channel_id=1, source_target_pairs={{0,2},{1,7},{2,0},{3,5},{4,6},{5,3},{6,4},{7,1},{8,10},{9,15},{10,... | collective-permute-start | bytes 4718600 | tf_op jit(solution)/shard_map/ppermute | solution.py:369
  38.9 2.7 %collective-permute-start.6 = (f32[512,768]{1,0:T(8,128)S(1)}, f32[512,768]{1,0:T(8,128)S(1)}, u32[]{:S(2)}, u32[]{:S(2)}) collective-permute-start(f32[512,768]{1,0:T(8,128)S(1)} %get-tuple-element.14), channel_id=1, source_target_pairs={{0,8},{1,25},{2,10},{3,27},{4,12},{5,29},{6,14},{7,31},{8,0},{9,17... | collective-permute-start | bytes 4718600 | tf_op jit(solution)/shard_map/ppermute | solution.py:369
  41.6 18.0 %keep_all.1 = (f32[512,768]{1,0:T(8,128)S(1)}, f32[512,768]{1,0:T(8,128)S(1)}, f32[512,512]{1,0:T(8,128)S(1)}) custom-call(s32[192]{0:T(256)S(1)} %pad_add_fusion.order, bf16[3,1024,1024]{2,1,0:T(8,128)(2,1)S(1)} %copy-done, bf16[3,2048,1024]{2,1,0:T(8,128)(2,1)} %right.5), custom_call_target="tpu_custom_call" | custom-call | flops 6442450944 | bytes 23068672 | tf_op jit(solution)/shard_map/keep_all/pallas_call | solution.py:297
  59.6 0.0 collective-permute-done.12
  59.6 0.2 slice_add_fusion.5
  59.8 0.1 collective-permute-start.13
  59.9 10.4 %collective-permute-done.13 = f32[256,512]{1,0:T(8,128)S(1)} collective-permute-done((f32[256,512]{1,0:T(8,128)S(1)}, f32[256,512]{1,0:T(8,128)S(1)}, u32[]{:S(2)}, u32[]{:S(2)}) %collective-permute-start.13) | collective-permute-done | bytes 524320 | tf_op jit(solution)/shard_map/ppermute | solution.py:369
  70.3 0.1 slice_add_fusion.11
  70.4 1.5 collective-permute-start.14
  71.9 0.0 collective-permute-done
  71.9 0.2 slice_add_fusion.3
  72.1 0.1 collective-permute-start.1
  72.2 5.3 %collective-permute-done.14 = f32[128,512]{1,0:T(8,128)S(1)} collective-permute-done((f32[128,512]{1,0:T(8,128)S(1)}, f32[128,512]{1,0:T(8,128)S(1)}, u32[]{:S(2)}, u32[]{:S(2)}) %collective-permute-start.14) | collective-permute-done | bytes 262176 | tf_op jit(solution)/shard_map/ppermute | solution.py:369
  77.5 0.1 collective-permute-start.15
  77.6 0.0 collective-permute-done.6
  77.6 0.2 slice_add_fusion.1
  77.9 0.1 collective-permute-start.7
  77.9 25.8 %collective-permute-done.15 = f32[64,512]{1,0:T(8,128)S(1)} collective-permute-done((f32[64,512]{1,0:T(8,128)S(1)}, f32[64,512]{1,0:T(8,128)S(1)}, u32[]{:S(2)}, u32[]{:S(2)}) %collective-permute-start.15) | collective-permute-done | bytes 131104 | tf_op jit(solution)/shard_map/ppermute | solution.py:369
  103.7 0.1 collective-permute-start.16
  103.8 6.8 %collective-permute-done.16 = f32[32,512]{1,0:T(8,128)S(1)} collective-permute-done((f32[32,512]{1,0:T(8,128)S(1)}, f32[32,512]{1,0:T(8,128)S(1)}, u32[]{:S(2)}, u32[]{:S(2)}) %collective-permute-start.16) | collective-permute-done | bytes 65568 | tf_op jit(solution)/shard_map/ppermute | solution.py:369
  110.6 0.0 collective-permute-done.1
  110.6 0.1 slice_add_fusion.9
  110.7 0.1 collective-permute-start.2
  110.8 0.0 collective-permute-done.7
  110.8 0.1 slice_add_fusion.7
  111.0 0.1 collective-permute-start.8
  111.1 3.4 %collective-permute-done.17 = f32[16,512]{1,0:T(8,128)S(1)} collective-permute-done((f32[16,512]{1,0:T(8,128)S(1)}, f32[16,512]{1,0:T(8,128)S(1)}, u32[]{:S(2)}, u32[]{:S(2)}) %collective-permute-start.17) | collective-permute-done | bytes 32800 | tf_op jit(solution)/shard_map/ppermute | solution.py:369
  114.5 13.6 %collective-permute-done.2 = f32[128,768]{1,0:T(8,128)S(1)} collective-permute-done((f32[128,768]{1,0:T(8,128)S(1)}, f32[128,768]{1,0:T(8,128)S(1)}, u32[]{:S(2)}, u32[]{:S(2)}) %collective-permute-start.2) | collective-permute-done | bytes 393248 | tf_op jit(solution)/shard_map/ppermute | solution.py:369
  128.1 0.1 slice_add_fusion.15
  128.1 0.0 copy-start.2
  128.1 0.1 collective-permute-start.3
  128.2 0.0 collective-permute-done.8
  128.2 0.1 slice_add_fusion.13
  128.3 0.1 collective-permute-start.9
  128.4 8.9 %collective-permute-done.3 = f32[64,768]{1,0:T(8,128)S(1)} collective-permute-done((f32[64,768]{1,0:T(8,128)S(1)}, f32[64,768]{1,0:T(8,128)S(1)}, u32[]{:S(2)}, u32[]{:S(2)}) %collective-permute-start.3) | collective-permute-done | bytes 196640 | tf_op jit(solution)/shard_map/ppermute | solution.py:369
  137.4 0.1 collective-permute-start.4
  137.5 1.1 collective-permute-start.10
  138.6 3.9 %collective-permute-done.4 = f32[32,768]{1,0:T(8,128)S(1)} collective-permute-done((f32[32,768]{1,0:T(8,128)S(1)}, f32[32,768]{1,0:T(8,128)S(1)}, u32[]{:S(2)}, u32[]{:S(2)}) %collective-permute-start.4) | collective-permute-done | bytes 98336 | tf_op jit(solution)/shard_map/ppermute | solution.py:369
  142.5 0.1 collective-permute-start.5
  142.6 0.3 collective-permute-done.10
  142.9 0.1 collective-permute-start.11
  143.0 2.7 %collective-permute-done.5 = f32[16,768]{1,0:T(8,128)S(1)} collective-permute-done((f32[16,768]{1,0:T(8,128)S(1)}, f32[16,768]{1,0:T(8,128)S(1)}, u32[]{:S(2)}, u32[]{:S(2)}) %collective-permute-start.5) | collective-permute-done | bytes 49184 | tf_op jit(solution)/shard_map/ppermute | solution.py:369
  145.7 0.2 collective-permute-done.11
  145.9 0.0 all-gather.2.cloned.1.call-done.window
  146.0 7.3 %grow_inverse.1 = (bf16[4,512,512]{2,1,0:T(8,128)(2,1)S(1)}, bf16[4,512,512]{2,1,0:T(8,128)(2,1)S(1)}) custom-call(s32[1]{0:T(128)} %bitcast.core, bf16[4096,2304]{1,0:T(8,128)(2,1)} %all-gather.2.cloned.1.call-done.window), custom_call_target="tpu_custom_call" | custom-call | tf_op jit(solution)/shard_map/grow_inverse/pallas_call | solution.py:128
  153.3 0.1 solve0.1.own
  153.4 8.0 %collective-permute-start.18 = (f32[16,2048]{1,0:T(8,128)S(1)}, f32[16,2048]{1,0:T(8,128)S(1)}, u32[]{:S(2)}, u32[]{:S(2)}) collective-permute-start(f32[16,2048]{1,0:T(8,128)S(1)} %solve0.1.own), channel_id=1, source_target_pairs={{0,1},{1,0},{2,3},{3,2},{4,5},{5,4},{6,7},{7,6},{8,9},{9,8},{10,11... | collective-permute-start | bytes 393224 | tf_op jit(solution)/shard_map/ppermute | solution.py:382
  161.4 1.0 collective-permute-done.18.other
  162.4 6.5 %solve1.1 = f32[16,2048]{1,0:T(8,128)} custom-call(s32[1]{0:T(128)} %bitcast.core, f32[16,2048]{1,0:T(8,128)S(1)} %maximum_subtract_fusion.right, f32[16,2048]{1,0:T(8,128)S(1)} %solve0.1.own, f32[16,2048]{1,0:T(8,128)S(1)} %collective-permute-done.18.other, bf16[4096,2304]{1,0:T(8,128)(2,1)} %all-gather.2.cloned.1.call-done.window, ...), custom_call_target="tpu_custom_call" | custom-call | tf_op jit(solution)/shard_map/solve1/pallas_call | solution.py:237
  (18 shorter events, 0.2 us)
Async XLA Ops:
  6.5 139.4 %all-gather.2.cloned.1.call-start = ((), (), s32[]{:S(2)}) async-start(), calls=%async_computation | async-start | bytes 19169280 | tf_op jit(solution)/shard_map/all_gather | solution.py:357
  6.6 0.9 copy-start.1
  10.1 2.8 %copy-start = (bf16[3,1024,1024]{2,1,0:T(8,128)(2,1)S(1)}, bf16[3,1024,1024]{2,1,0:T(8,128)(2,1)}, u32[]{:S(2)}) copy-start(bf16[3,1024,1024]{2,1,0:T(8,128)(2,1)} %left.5) | copy-start | bytes 18874372
  24.2 35.4 %collective-permute-start.12 = (f32[512,512]{1,0:T(8,128)S(1)}, f32[512,512]{1,0:T(8,128)S(1)}, u32[]{:S(2)}, u32[]{:S(2)}) collective-permute-start(f32[512,512]{1,0:T(8,128)S(1)} %get-tuple-element.16), channel_id=1, source_target_pairs={{0,32},{1,97},{2,34},{3,99},{4,36},{5,101},{6,38},{7,103},{8,40},{... | collective-permute-start | bytes 3145736 | tf_op jit(solution)/shard_map/ppermute | solution.py:369
  36.3 35.6 %collective-permute-start = (f32[512,768]{1,0:T(8,128)S(1)}, f32[512,768]{1,0:T(8,128)S(1)}, u32[]{:S(2)}, u32[]{:S(2)}) collective-permute-start(f32[512,768]{1,0:T(8,128)S(1)} %send_first.1), channel_id=1, source_target_pairs={{0,2},{1,7},{2,0},{3,5},{4,6},{5,3},{6,4},{7,1},{8,10},{9,15},{10,... | collective-permute-start | bytes 4718600 | tf_op jit(solution)/shard_map/ppermute | solution.py:369
  38.9 38.8 %collective-permute-start.6 = (f32[512,768]{1,0:T(8,128)S(1)}, f32[512,768]{1,0:T(8,128)S(1)}, u32[]{:S(2)}, u32[]{:S(2)}) collective-permute-start(f32[512,768]{1,0:T(8,128)S(1)} %get-tuple-element.14), channel_id=1, source_target_pairs={{0,8},{1,25},{2,10},{3,27},{4,12},{5,29},{6,14},{7,31},{8,0},{9,17... | collective-permute-start | bytes 4718600 | tf_op jit(solution)/shard_map/ppermute | solution.py:369
  59.8 10.5 %collective-permute-start.13 = (f32[256,512]{1,0:T(8,128)S(1)}, f32[256,512]{1,0:T(8,128)S(1)}, u32[]{:S(2)}, u32[]{:S(2)}) collective-permute-start(f32[256,512]{1,0:T(8,128)S(1)} %get-tuple-element.26), channel_id=1, source_target_pairs={{0,96},{1,33},{2,98},{3,35},{4,100},{5,37},{6,102},{7,39},{8,104},... | collective-permute-start | bytes 1572872 | tf_op jit(solution)/shard_map/ppermute | solution.py:369
  70.4 7.1 %collective-permute-start.14 = (f32[128,512]{1,0:T(8,128)S(1)}, f32[128,512]{1,0:T(8,128)S(1)}, u32[]{:S(2)}, u32[]{:S(2)}) collective-permute-start(f32[128,512]{1,0:T(8,128)S(1)} %get-tuple-element.32), channel_id=1, source_target_pairs={{0,2},{1,7},{2,0},{3,5},{4,6},{5,3},{6,4},{7,1},{8,10},{9,15},{10,... | collective-permute-start | bytes 786440 | tf_op jit(solution)/shard_map/ppermute | solution.py:369
  72.1 38.5 %collective-permute-start.1 = (f32[256,768]{1,0:T(8,128)S(1)}, f32[256,768]{1,0:T(8,128)S(1)}, u32[]{:S(2)}, u32[]{:S(2)}) collective-permute-start(f32[256,768]{1,0:T(8,128)S(1)} %get-tuple-element.22), channel_id=1, source_target_pairs={{0,6},{1,3},{2,4},{3,1},{4,2},{5,7},{6,0},{7,5},{8,14},{9,11},{10,... | collective-permute-start | bytes 2359304 | tf_op jit(solution)/shard_map/ppermute | solution.py:369
  77.5 26.2 %collective-permute-start.15 = (f32[64,512]{1,0:T(8,128)S(1)}, f32[64,512]{1,0:T(8,128)S(1)}, u32[]{:S(2)}, u32[]{:S(2)}) collective-permute-start(f32[64,512]{1,0:T(8,128)S(1)} %get-tuple-element.38), channel_id=1, source_target_pairs={{0,6},{1,3},{2,4},{3,1},{4,2},{5,7},{6,0},{7,5},{8,14},{9,11},{10,... | collective-permute-start | bytes 393224 | tf_op jit(solution)/shard_map/ppermute | solution.py:369
  77.9 33.0 %collective-permute-start.7 = (f32[256,768]{1,0:T(8,128)S(1)}, f32[256,768]{1,0:T(8,128)S(1)}, u32[]{:S(2)}, u32[]{:S(2)}) collective-permute-start(f32[256,768]{1,0:T(8,128)S(1)} %get-tuple-element.24), channel_id=1, source_target_pairs={{0,24},{1,9},{2,26},{3,11},{4,28},{5,13},{6,30},{7,15},{8,16},{9,1... | collective-permute-start | bytes 2359304 | tf_op jit(solution)/shard_map/ppermute | solution.py:369
  103.7 6.9 %collective-permute-start.16 = (f32[32,512]{1,0:T(8,128)S(1)}, f32[32,512]{1,0:T(8,128)S(1)}, u32[]{:S(2)}, u32[]{:S(2)}) collective-permute-start(f32[32,512]{1,0:T(8,128)S(1)} %get-tuple-element.44), channel_id=1, source_target_pairs={{0,8},{1,25},{2,10},{3,27},{4,12},{5,29},{6,14},{7,31},{8,0},{9,17... | collective-permute-start | bytes 196616 | tf_op jit(solution)/shard_map/ppermute | solution.py:369
  110.6 3.8 %collective-permute-start.17 = (f32[16,512]{1,0:T(8,128)S(1)}, f32[16,512]{1,0:T(8,128)S(1)}, u32[]{:S(2)}, u32[]{:S(2)}) collective-permute-start(f32[16,512]{1,0:T(8,128)S(1)} %slice_add_fusion.28), channel_id=1, source_target_pairs={{0,24},{1,9},{2,26},{3,11},{4,28},{5,13},{6,30},{7,15},{8,16},{9,1... | collective-permute-start | bytes 98312 | tf_op jit(solution)/shard_map/ppermute | solution.py:369
  110.7 17.3 %collective-permute-start.2 = (f32[128,768]{1,0:T(8,128)S(1)}, f32[128,768]{1,0:T(8,128)S(1)}, u32[]{:S(2)}, u32[]{:S(2)}) collective-permute-start(f32[128,768]{1,0:T(8,128)S(1)} %get-tuple-element.28), channel_id=1, source_target_pairs={{0,8},{1,25},{2,10},{3,27},{4,12},{5,29},{6,14},{7,31},{8,0},{9,17... | collective-permute-start | bytes 1179656 | tf_op jit(solution)/shard_map/ppermute | solution.py:369
  111.0 17.3 %collective-permute-start.8 = (f32[128,768]{1,0:T(8,128)S(1)}, f32[128,768]{1,0:T(8,128)S(1)}, u32[]{:S(2)}, u32[]{:S(2)}) collective-permute-start(f32[128,768]{1,0:T(8,128)S(1)} %get-tuple-element.30), channel_id=1, source_target_pairs={{0,32},{1,97},{2,34},{3,99},{4,36},{5,101},{6,38},{7,103},{8,40},{... | collective-permute-start | bytes 1179656 | tf_op jit(solution)/shard_map/ppermute | solution.py:369
  128.1 17.8 %copy-start.2 = (bf16[16,2048]{1,0:T(8,128)(2,1)S(1)}, bf16[16,2048]{1,0:T(8,128)(2,1)}, u32[]{:S(2)}) copy-start(bf16[16,2048]{1,0:T(8,128)(2,1)} %param.7) | copy-start | bytes 196612
  128.1 9.2 %collective-permute-start.3 = (f32[64,768]{1,0:T(8,128)S(1)}, f32[64,768]{1,0:T(8,128)S(1)}, u32[]{:S(2)}, u32[]{:S(2)}) collective-permute-start(f32[64,768]{1,0:T(8,128)S(1)} %get-tuple-element.34), channel_id=1, source_target_pairs={{0,24},{1,9},{2,26},{3,11},{4,28},{5,13},{6,30},{7,15},{8,16},{9,1... | collective-permute-start | bytes 589832 | tf_op jit(solution)/shard_map/ppermute | solution.py:369
  128.3 9.2 %collective-permute-start.9 = (f32[64,768]{1,0:T(8,128)S(1)}, f32[64,768]{1,0:T(8,128)S(1)}, u32[]{:S(2)}, u32[]{:S(2)}) collective-permute-start(f32[64,768]{1,0:T(8,128)S(1)} %get-tuple-element.36), channel_id=1, source_target_pairs={{0,96},{1,33},{2,98},{3,35},{4,100},{5,37},{6,102},{7,39},{8,104},... | collective-permute-start | bytes 589832 | tf_op jit(solution)/shard_map/ppermute | solution.py:369
  137.4 5.2 %collective-permute-start.4 = (f32[32,768]{1,0:T(8,128)S(1)}, f32[32,768]{1,0:T(8,128)S(1)}, u32[]{:S(2)}, u32[]{:S(2)}) collective-permute-start(f32[32,768]{1,0:T(8,128)S(1)} %get-tuple-element.40), channel_id=1, source_target_pairs={{0,32},{1,97},{2,34},{3,99},{4,36},{5,101},{6,38},{7,103},{8,40},{... | collective-permute-start | bytes 294920 | tf_op jit(solution)/shard_map/ppermute | solution.py:369
  137.5 5.4 %collective-permute-start.10 = (f32[32,768]{1,0:T(8,128)S(1)}, f32[32,768]{1,0:T(8,128)S(1)}, u32[]{:S(2)}, u32[]{:S(2)}) collective-permute-start(f32[32,768]{1,0:T(8,128)S(1)} %get-tuple-element.42), channel_id=1, source_target_pairs={{0,2},{1,7},{2,0},{3,5},{4,6},{5,3},{6,4},{7,1},{8,10},{9,15},{10,... | collective-permute-start | bytes 294920 | tf_op jit(solution)/shard_map/ppermute | solution.py:369
  142.5 3.1 %collective-permute-start.5 = (f32[16,768]{1,0:T(8,128)S(1)}, f32[16,768]{1,0:T(8,128)S(1)}, u32[]{:S(2)}, u32[]{:S(2)}) collective-permute-start(f32[16,768]{1,0:T(8,128)S(1)} %slice_add_fusion.26), channel_id=1, source_target_pairs={{0,96},{1,33},{2,98},{3,35},{4,100},{5,37},{6,102},{7,39},{8,104},... | collective-permute-start | bytes 147464 | tf_op jit(solution)/shard_map/ppermute | solution.py:369
  142.9 3.0 %collective-permute-start.11 = (f32[16,768]{1,0:T(8,128)S(1)}, f32[16,768]{1,0:T(8,128)S(1)}, u32[]{:S(2)}, u32[]{:S(2)}) collective-permute-start(f32[16,768]{1,0:T(8,128)S(1)} %slice_add_fusion.24), channel_id=1, source_target_pairs={{0,6},{1,3},{2,4},{3,1},{4,2},{5,7},{6,0},{7,5},{8,14},{9,11},{10,... | collective-permute-start | bytes 147464 | tf_op jit(solution)/shard_map/ppermute | solution.py:369
  153.4 9.0 %collective-permute-start.18 = (f32[16,2048]{1,0:T(8,128)S(1)}, f32[16,2048]{1,0:T(8,128)S(1)}, u32[]{:S(2)}, u32[]{:S(2)}) collective-permute-start(f32[16,2048]{1,0:T(8,128)S(1)} %solve0.1.own), channel_id=1, source_target_pairs={{0,1},{1,0},{2,3},{3,2},{4,5},{5,4},{6,7},{7,6},{8,9},{9,8},{10,11... | collective-permute-start | bytes 393224 | tf_op jit(solution)/shard_map/ppermute | solution.py:382
Sparse Core Ops, SparseCore 0:
  10.1 135.6 all-gather.1

commit v3 on v2

v3 whole, which is shorter than its diff:
```python
import functools

import jax
import jax.numpy as jnp
import numpy as np
from jax import lax
from jax.experimental import pallas as pl
from jax.experimental.pallas import tpu as pltpu
from jax.sharding import Mesh
from jax.sharding import PartitionSpec as P

F32 = jnp.float32
BF16 = jnp.bfloat16
SIDE = 4
ROWS = 16
STRIP = 64
BLOCK = 512
AXES = ("z", "y", "x")
EVERY = ("z", "y", "x", "pcol")
PARTS = ((0, 1024, "zyx"), (1024, 1024, "zxy"))
GATHER = ("yx", "xy")
MB = 1 << 20


def split2(value):
    high = value.astype(BF16)
    return high, (value - high.astype(F32)).astype(BF16)


def dot(a, b):
    return jnp.dot(a, b, preferred_element_type=F32)


def dot_exact(a, b):
    high, low = split2(a)
    rows = a.shape[0]
    both = dot(jnp.concatenate([high, low], axis=0), b)
    return both[:rows] + both[rows:]


def dot_pair(a, b_high, b_low):
    high, low = split2(a)
    rows = a.shape[0]
    both = dot(jnp.concatenate([high, low], axis=0), b_high)
    return both[:rows] + both[rows:] + dot(high, b_low)


def grow_kernel(chips, own_a, got_a, own_b, got_b, lower, below, out_high, out_low, small, sems):
    slab = lower.shape[0]
    half = slab // 2
    for n, (own, got) in enumerate(((own_a, got_a), (own_b, got_b))):
        share = own.shape[0] // 8
        for position in range(16):
            source = own if position < 8 else got
            base = (position % 8) * share
            row = pl.multiple_of(chips[16 * n + position] * STRIP, STRIP)
            if n == 0:
                moves = (
                    (base, STRIP, lower, row, 0),
                    (base + STRIP, STRIP // 2, lower, half + row, 0),
                )
            else:
                moves = (
                    (base, STRIP // 2, lower, half + row + STRIP // 2, 0),
                    (base + STRIP // 2, STRIP, below, row, 1),
                )
            for start, count, target, to, sem in moves:
                pltpu.make_async_copy(
                    source.at[pl.ds(start, count)],
                    target.at[pl.ds(pl.multiple_of(to, STRIP // 2), count)],
                    sems.at[sem],
                ).start()
    pltpu.make_async_copy(lower, lower, sems.at[0]).wait()

    rows = lax.broadcasted_iota(jnp.int32, (STRIP, 128), 0)
    lanes = lax.broadcasted_iota(jnp.int32, (STRIP, 128), 1)
    left = lanes < STRIP
    inner = jnp.where(left, lanes, lanes - STRIP)
    together = 4

    def invert(group, carry):
        todo, upper, scale = [], [], []
        for n in range(together):
            start = pl.multiple_of((group * together + n) * 128, 128)
            cols = pl.ds(start, 128)
            first = lower[pl.ds(start, STRIP), cols].astype(F32)
            second = lower[pl.ds(start + STRIP, STRIP), cols].astype(F32)
            block = jnp.where(left, first, second)
            diagonal = jnp.where(inner == rows, block, 0.0)
            one = jnp.sum(jnp.where(left, diagonal, 0.0), axis=1, keepdims=True)
            two = jnp.sum(jnp.where(left, 0.0, diagonal), axis=1, keepdims=True)
            upper.append(jnp.where(inner > rows, block, 0.0))
            scale.append(jnp.where(left, 1.0 / one, 1.0 / two))
            todo.append(jnp.where(inner == rows, 1.0, 0.0))
        for k in range(STRIP - 1, 0, -1):
            top = min(STRIP, (k + 7) // 8 * 8)
            for n in range(together):
                row = todo[n][k : k + 1, :] * scale[n][k : k + 1, :]
                col = jnp.where(
                    left[:top], upper[n][:top, k : k + 1], upper[n][:top, STRIP + k : STRIP + k + 1]
                )
                changed = todo[n][:top] - col * row
                todo[n] = (
                    changed if top == STRIP else jnp.concatenate([changed, todo[n][top:]], axis=0)
                )
        for n in range(together):
            small[group * together + n] = todo[n] * scale[n]
        return carry

    lax.fori_loop(0, slab // 128 // together, invert, 0)

    rows = lax.broadcasted_iota(jnp.int32, (128, 128), 0)
    lanes = lax.broadcasted_iota(jnp.int32, (128, 128), 1)
    corner = (rows < STRIP) & (lanes >= STRIP)
    same = (rows < STRIP) == (lanes < STRIP)
    level = []
    for k in range(slab // 128):
        rng = slice(k * 128, k * 128 + 128)
        both = jnp.where(same, jnp.concatenate([small[k], small[k]], axis=0), 0.0)
        off = jnp.where(corner, lower[rng, rng].astype(F32), 0.0).astype(BF16)
        level.append(both - dot_pair(dot_exact(both, off), *split2(both)))
    size = 128
    while size < BLOCK:
        grown = []
        for n in range(0, len(level), 2):
            start = n * size
            off = lower[start : start + size, start + size : start + 2 * size]
            high, low = split2(level[n + 1])
            corner_block = -dot_pair(dot_exact(level[n], off), high, low)
            if 2 * size < BLOCK:
                top = jnp.concatenate([level[n], corner_block], axis=1)
                bottom = jnp.concatenate([jnp.zeros_like(corner_block), level[n + 1]], axis=1)
                grown.append(jnp.concatenate([top, bottom], axis=0))
            else:
                b = n // 2
                corner_high, corner_low = split2(corner_block)
                first_high, first_low = split2(level[n])
                zero = jnp.zeros((size, size), BF16)
                for ref, first, mixed, second in (
                    (out_high, first_high, corner_high, high),
                    (out_low, first_low, corner_low, low),
                ):
                    ref[b, :size, :size] = first
                    ref[b, :size, size:] = mixed
                    ref[b, size:, :size] = zero
                    ref[b, size:, size:] = second
        level = grown
        size *= 2
    pltpu.make_async_copy(below, below, sems.at[1]).wait()


def grow(chips, pieces, slab):
    inverse = jax.ShapeDtypeStruct((slab // BLOCK, BLOCK, BLOCK), BF16)
    vmem = pl.BlockSpec(memory_space=pltpu.VMEM)
    return pl.pallas_call(
        grow_kernel,
        out_shape=(
            jax.ShapeDtypeStruct((slab, slab), BF16),
            jax.ShapeDtypeStruct((slab // 2, slab), BF16),
            inverse,
            inverse,
        ),
        in_specs=[pl.BlockSpec(memory_space=pltpu.SMEM)] + [pl.BlockSpec(memory_space=pltpu.HBM)] * 4,
        out_specs=[vmem] * 4,
        scratch_shapes=[
            pltpu.VMEM((slab // 128, STRIP, 128), F32),
            pltpu.SemaphoreType.DMA((2,)),
        ],
        compiler_params=pltpu.CompilerParams(vmem_limit_bytes=36 * MB),
        cost_estimate=pl.CostEstimate(
            flops=4 * 10**9, bytes_accessed=4 * slab * slab, transcendentals=0
        ),
        name="grow_inverse",
    )(chips, *pieces)


def solve_block(blocks, pending, factor, high, low, out, wait, after):
    for b in range(blocks):
        cols = slice(b * BLOCK, (b + 1) * BLOCK)
        wait(b)
        y = dot_pair(pending[:, cols], high[b], low[b])
        out[: pending.shape[0], cols] = y
        if b + 1 < blocks:
            rest = slice((b + 1) * BLOCK, blocks * BLOCK)
            pending[:, rest] = pending[:, rest] - dot_exact(y, factor[cols, rest])
        after(b, y)


def solve_copies(lower, inv_high, inv_low, factor, high, low, sems):
    copies = []
    slab = lower.shape[1]
    for b in range(slab // BLOCK):
        group = [
            pltpu.make_async_copy(inv_high.at[b], high.at[b], sems.at[0, b]),
            pltpu.make_async_copy(inv_low.at[b], low.at[b], sems.at[1, b]),
        ]
        if (b + 1) * BLOCK < slab:
            rest = pl.ds((b + 1) * BLOCK, slab - (b + 1) * BLOCK)
            rows = pl.ds(b * BLOCK, BLOCK)
            group.append(
                pltpu.make_async_copy(
                    lower.at[rows, rest], factor.at[rows, rest], sems.at[2, b]
                )
            )
        copies.append(group)
    return copies


def below_copies(below, under, sems):
    copies = []
    for b in range(below.shape[0] // BLOCK):
        rows = pl.ds(b * BLOCK, BLOCK)
        copies.append(pltpu.make_async_copy(below.at[rows], under.at[rows], sems.at[3, b]))
    return copies


def first_kernel(
    core, right, lower, below, inv_high, inv_low, out, factor, under, high, low, pending, sems
):
    rows, slab = right.shape

    @pl.when(core[0] == 0)
    def _():
        copies = solve_copies(lower, inv_high, inv_low, factor, high, low, sems)
        belows = below_copies(below, under, sems)
        for b, group in enumerate(copies):
            for copy in group:
                copy.start()
            if b < len(belows):
                belows[b].start()
        pending[...] = right[...]

        def wait(b):
            for copy in copies[b]:
                copy.wait()

        def after(b, y):
            if b < len(belows):
                belows[b].wait()
                term = dot_exact(y, under[b * BLOCK : (b + 1) * BLOCK, :])
                out[rows:, :] = term if b == 0 else out[rows:, :] + term

        solve_block(slab // BLOCK, pending, factor, high, low, out, wait, after)

    @pl.when(core[0] != 0)
    def _():
        out[...] = jnp.zeros_like(out)


def second_kernel(
    core, right, own, other, lower, below, inv_high, inv_low, out, factor, under, high, low, pending, sems
):
    rows, slab = right.shape
    half = slab // 2

    @pl.when(core[0] != 0)
    def _():
        copies = solve_copies(lower, inv_high, inv_low, factor, high, low, sems)
        belows = below_copies(below, under, sems)
        for copy in belows:
            copy.start()
        for group in copies:
            for copy in group:
                copy.start()
        pending[...] = right[...] - other[rows:, :]
        for b, copy in enumerate(belows):
            copy.wait()
            cols = slice(half + b * BLOCK, half + (b + 1) * BLOCK)
            term = dot_exact(other[:rows, cols], under[b * BLOCK : (b + 1) * BLOCK, :])
            pending[...] = pending[...] - term

        def wait(b):
            for copy in copies[b]:
                copy.wait()

        solve_block(slab // BLOCK, pending, factor, high, low, out, wait, lambda b, y: None)

    @pl.when(core[0] == 0)
    def _():
        out[...] = own[:rows, :]


def solve_call(kernel, core, dense, factor, out_rows, name):
    rows, slab = dense[0].shape
    blocks = slab // BLOCK
    vmem = pl.BlockSpec(memory_space=pltpu.VMEM)
    return pl.pallas_call(
        kernel,
        out_shape=jax.ShapeDtypeStruct((out_rows, slab), F32),
        in_specs=[pl.BlockSpec(memory_space=pltpu.SMEM)]
        + [vmem] * len(dense)
        + [pl.BlockSpec(memory_space=pl.ANY)] * 4,
        out_specs=vmem,
        scratch_shapes=[
            pltpu.VMEM((slab, slab), BF16),
            pltpu.VMEM((slab // 2, slab), BF16),
            pltpu.VMEM((blocks, BLOCK, BLOCK), BF16),
            pltpu.VMEM((blocks, BLOCK, BLOCK), BF16),
            pltpu.VMEM((rows, slab), F32),
            pltpu.SemaphoreType.DMA((4, blocks)),
        ],
        compiler_params=pltpu.CompilerParams(vmem_limit_bytes=28 * MB),
        name=name,
    )(core, *dense, *factor)


def product_kernel(parts, half, order, left, right, *refs):
    outs, (a, b, picked, a_sems, b_sems) = refs[: len(parts)], refs[len(parts) :]
    groups, _, depth = left.shape
    rows = picked.shape[0]
    loads = []
    for g in range(groups):
        lanes = pl.ds(g * depth, depth)
        copy = pltpu.make_async_copy(left.at[g], a.at[:, lanes], a_sems.at[g])
        copy.start()
        loads.append(copy)
    tiles = []
    for n, (_, start, width) in enumerate(parts):
        tile = []
        for g in range(groups):
            lanes = pl.ds(g * depth, depth)
            copy = pltpu.make_async_copy(
                right.at[g, pl.ds(start, width)], b.at[n, :, lanes], b_sems.at[n, g]
            )
            copy.start()
            tile.append(copy)
        tiles.append(tile)
    for copy in loads:
        copy.wait()
    for n, (number, _, _) in enumerate(parts):
        base = (2 * number + half) * (rows // ROWS)
        for r in range(rows // ROWS):
            source = pl.ds(pl.multiple_of(order[base + r] * ROWS, ROWS), ROWS)
            picked[r * ROWS : (r + 1) * ROWS, :] = a[source, :]
        for copy in tiles[n]:
            copy.wait()
        outs[n][...] = lax.dot_general(
            picked[...], b[n], (((1,), (1,)), ((), ())), preferred_element_type=F32
        )


def product(order, left, right, parts, half, name):
    groups, rows, depth = left.shape
    width = sum(part[2] for part in parts)
    return pl.pallas_call(
        functools.partial(product_kernel, parts, half),
        out_shape=[jax.ShapeDtypeStruct((rows // 2, part[2]), F32) for part in parts],
        in_specs=[
            pl.BlockSpec(memory_space=pltpu.SMEM),
            pl.BlockSpec(memory_space=pltpu.HBM),
            pl.BlockSpec(memory_space=pltpu.HBM),
        ],
        out_specs=[pl.BlockSpec(memory_space=pltpu.VMEM)] * len(parts),
        scratch_shapes=[
            pltpu.VMEM((rows, groups * depth), BF16),
            pltpu.VMEM((len(parts), parts[0][2], groups * depth), BF16),
            pltpu.VMEM((rows // 2, groups * depth), BF16),
            pltpu.SemaphoreType.DMA((groups,)),
            pltpu.SemaphoreType.DMA((len(parts), groups)),
        ],
        compiler_params=pltpu.CompilerParams(vmem_limit_bytes=40 * MB),
        cost_estimate=pl.CostEstimate(
            flops=groups * rows * width * depth,
            bytes_accessed=2 * groups * (rows + width) * depth + 2 * rows * width,
            transcendentals=0,
        ),
        name=name,
    )(order, left, right)


def chip_index(z, y, x, c):
    return ((z * SIDE + y) * SIDE + x) * 2 + c


def flip_pairs(axis, masks):
    pairs = []
    for z, y, x, c in np.ndindex(SIDE, SIDE, SIDE, 2):
        place = {"z": z, "y": y, "x": x}
        place[axis] ^= masks[c]
        pairs.append((chip_index(z, y, x, c), chip_index(place["z"], place["y"], place["x"], c)))
    return pairs


def partner_pairs(axis, second):
    return flip_pairs(axis, (3, 1) if second else (1, 3))


def block_order(axes, place, core):
    flip = jnp.where(core == 0, 1, 3)
    masks = jnp.stack([jnp.full_like(flip, 2), flip, flip ^ 2, jnp.zeros_like(flip)])
    lists = {name: place[name] ^ masks for name in AXES}
    shape = {name: [1, 1, 1] for name in AXES}
    for position, name in enumerate(axes):
        shape[name][position] = SIDE
    at = {name: lists[name].reshape(shape[name]) for name in AXES}
    return (((at["z"] * SIDE + at["y"]) * SIDE + at["x"]).reshape(-1)).astype(jnp.int32)


def gather_factor(strip, place, core):
    z = place["z"]
    pairs = [
        (chip_index(0, y, x, 1), chip_index(0, y, x, 0)) for y in range(SIDE) for x in range(SIDE)
    ]
    got = lax.ppermute(strip, EVERY, pairs)
    under = jnp.where(core == 0, got, strip)
    got = lax.ppermute(jnp.concatenate([strip, under]), EVERY, flip_pairs("z", (2, 2)))
    home = (z < 2) == (core == 0)
    mine = jnp.where(home, strip, got[:STRIP])
    under = jnp.where(z < 2, under, got[STRIP:])
    got = lax.ppermute(jnp.concatenate([mine, under]), EVERY, flip_pairs("z", (1, 1)))
    even = z % 2 == 0
    first = jnp.where(even, mine, got[:STRIP])
    second = jnp.where(even, got[:STRIP], mine)
    under = jnp.where(z % 2 == core, under, got[STRIP:])
    cut = STRIP // 2
    held = [
        jnp.concatenate([first, second[:cut]]),
        jnp.concatenate([second[cut:], under]),
    ]
    pieces = [None, None]
    for step in range(4):
        got = [
            lax.ppermute(held[n], EVERY, partner_pairs(GATHER[n][step // 2], step % 2 == 1))
            for n in range(2)
        ]
        if step == 3:
            pieces = [held[0], got[0], held[1], got[1]]
        else:
            held = [jnp.concatenate([held[n], got[n]]) for n in range(2)]
    flip = jnp.where(core == 0, 1, 3)
    masks = jnp.stack([jnp.zeros_like(flip), flip, flip ^ 2, jnp.full_like(flip, 2)])
    ys, xs = place["y"] ^ masks, place["x"] ^ masks
    chips = [
        ys[None, :] * SIDE + xs[:, None],
        ys[:, None] * SIDE + xs[None, :],
    ]
    return pieces, jnp.concatenate([c.reshape(-1) for c in chips]).astype(jnp.int32)


def per_device(hist_factor, hist_solution, diag_factor, samples):
    slab = hist_factor.shape[1]
    core = lax.axis_index("pcol")
    place = {name: lax.axis_index(name) for name in AXES}
    core_arg = core.astype(jnp.int32).reshape(1)

    order = jnp.concatenate([block_order(axes, place, core) for _, _, axes in PARTS])
    parts = [(n, start, width) for n, (start, width, _) in enumerate(PARTS)]
    sends = [
        *product(order, hist_solution, hist_factor, parts[:1], 0, "send_first"),
        *product(order, hist_solution, hist_factor, parts[1:], 0, "send_rest"),
    ]
    keeps = list(product(order, hist_solution, hist_factor, parts, 1, "keep_all"))

    pieces, chips = gather_factor(diag_factor.T, place, core)
    factor = grow(chips, pieces, slab)

    for step in range(6):
        got = [
            lax.ppermute(sends[n], EVERY, partner_pairs(PARTS[n][2][step // 2], step % 2 == 1))
            for n in range(len(PARTS))
        ]
        if step == 5:
            keeps = [keeps[n] + got[n] for n in range(len(PARTS))]
        else:
            middle = keeps[0].shape[0] // 2
            sends = [keeps[n][:middle] + got[n][:middle] for n in range(len(PARTS))]
            keeps = [keeps[n][middle:] + got[n][middle:] for n in range(len(PARTS))]
    pending = samples.astype(F32) - jnp.concatenate(keeps, axis=1)

    first = solve_call(first_kernel, core_arg, (pending,), factor, 2 * ROWS, "solve0")
    other = lax.ppermute(first, "pcol", [(0, 1)])
    return solve_call(second_kernel, core_arg, (pending, first, other), factor, ROWS, "solve1")


def solution(mesh):
    cube = Mesh(mesh.devices.reshape(SIDE, SIDE, SIDE, 2), EVERY)
    return jax.shard_map(
        per_device,
        mesh=cube,
        in_specs=(
            P(None, "pcol", AXES),
            P(None, None, AXES),
            P("pcol", AXES),
            P(AXES, "pcol"),
        ),
        out_specs=P(AXES, "pcol"),
        check_vma=False,
    )
```

time: 176 us -> 205 us (1.16)
  local copies, waits for them, and re-layouts: 4.03 us -> 18.5 us
  other arithmetic: 1.6 us -> 15.6 us
  between operations: 13.7 us -> 0.47 us
  starting transfers between devices: 21.6 us -> 32.9 us
  waiting for transfers between devices: 82.2 us -> 84.3 us
    ppermute x19 -> x24, starting transfers between devices: 21.6 us -> 32.9 us  [the longest x12 18.5 us: per_device(): lax.ppermute(sends[n], EVERY, partner_pairs(PARTS[n][2][step // 2], step...]
    unnamed x6 -> x14, local copies, waits for them, and re-layouts: 3.75 us -> 14.6 us
    pallas_call x4 -> x3, Pallas kernels: 15.8 us -> 25.1 us  [the longest x1 20 us: grow(): pl.pallas_call(grow_kernel, out_shape=(jax.ShapeDtypeStruct((slab, slab),...]
    pallas_call x3, Pallas kernels: 36.8 us -> 28.1 us  [product(): pl.pallas_call(functools.partial(product_kernel, parts, half), out_shape=...]
    add x12 -> x8, other arithmetic: 1.15 us -> 9.09 us  [per_device(): keeps = [keeps[n][middle:] + got[n][middle:] for n in range(len(PARTS))]]
    concatenate x0 -> x2, local copies, waits for them, and re-layouts: none -> 2.71 us  [gather_factor(): held = [jnp.concatenate([held[n], got[n]]) for n in range(2)]]
    concatenate x0 -> x9, other arithmetic: none -> 2.42 us  [the longest x1 0.99 us: gather_factor(): jnp.concatenate([strip, under])]
    ppermute x19 -> x24, waiting for transfers between devices: 82.2 us -> 84.3 us  [the longest x12 48.5 us: per_device(): lax.ppermute(sends[n], EVERY, partner_pairs(PARTS[n][2][step // 2], step...]
  transfers between devices with their start and end apart: 20 -> 24, of which waited for: 12 -> 13; matrix products, arithmetic and copies ran while one was open for 1% -> 9% of each run, Pallas kernels for 21% -> 14%
where the time goes in v3:
time: 205 us
  waiting for transfers between devices  84.3 us (41%)
  Pallas kernels  53.2 us (26%)
  starting transfers between devices  32.9 us (16%)
  local copies, waits for them, and re-layouts  18.5 us (9%)
  other arithmetic  15.6 us (8%)
    ppermute x12, waiting for transfers between devices, per_device(): lax.ppermute(sends[n], EVERY, partner_pairs(PARTS[n][2][step // 2], step...  48.5 us
    pallas_call x3, Pallas kernels, product(): pl.pallas_call(functools.partial(product_kernel, parts, half), out_shape=...  28.1 us
    pallas_call x1, Pallas kernels, grow(): pl.pallas_call(grow_kernel, out_shape=(jax.ShapeDtypeStruct((slab, slab),...  20 us
    ppermute x12, starting transfers between devices, per_device(): lax.ppermute(sends[n], EVERY, partner_pairs(PARTS[n][2][step // 2], step...  18.5 us
    unnamed x14, local copies, waits for them, and re-layouts  14.6 us
    ppermute x1, waiting for transfers between devices, gather_factor(): lax.ppermute(jnp.concatenate([strip, under]), EVERY, flip_pairs('z', (2,...  13.7 us
    ppermute x1, waiting for transfers between devices, per_device(): other = lax.ppermute(first, 'pcol', [(0, 1)])  12.9 us
    ppermute x8, starting transfers between devices, gather_factor(): lax.ppermute(held[n], EVERY, partner_pairs(GATHER[n][step // 2], step % 2...  9.13 us
  transfers between devices with their start and end apart: 24, of which 13 were waited for; matrix products, arithmetic and copies ran while one was open for 9% of the time, Pallas kernels for 14%

profile of v3, /device:TPU:1, one launch (start us, length us, event | category | flops | bytes accessed | tf_op | source)
XLA Modules:
  0.0 204.9 jit_solution(7847147961809245782)
XLA Ops:
  0.0 3.3 %collective-permute-start.12 = (bf16[64,2048]{1,0:T(8,128)(2,1)}, bf16[64,2048]{1,0:T(8,128)(2,1)S(1)}, u32[]{:S(2)}, u32[]{:S(2)}) collective-permute-start(bf16[64,2048]{1,0:T(8,128)(2,1)} %bitcast.6), channel_id=1, source_target_pairs={{1,0},{3,2},{5,4},{7,6},{9,8},{11,10},{13,12},{15,14},{17,16},{19,... | collective-permute-start | bytes 786440 | tf_op jit(solution)/shard_map/ppermute | solution.py:404
  3.4 1.2 collective-permute-done.12
  4.7 1.0 broadcast_select_fusion
  5.7 1.0 pad_maximum_fusion.4
  6.7 0.6 collective-permute-start.13
  7.7 13.7 %collective-permute-done.13 = bf16[128,2048]{1,0:T(8,128)(2,1)S(1)} collective-permute-done((bf16[128,2048]{1,0:T(8,128)(2,1)S(1)}, bf16[128,2048]{1,0:T(8,128)(2,1)S(1)}, u32[]{:S(2)}, u32[]{:S(2)}) %collective-permute-start.13) | collective-permute-done | bytes 524320 | tf_op jit(solution)/shard_map/ppermute | solution.py:406
  21.4 1.0 slice_select_fusion.1
  22.4 0.8 pad_maximum_fusion.5
  23.2 2.8 %copy-done.1 = bf16[3,1024,1024]{2,1,0:T(8,128)(2,1)S(1)} copy-done((bf16[3,1024,1024]{2,1,0:T(8,128)(2,1)S(1)}, bf16[3,1024,1024]{2,1,0:T(8,128)(2,1)}, u32[]{:S(2)}) %copy-start.1) | copy-done | bytes 6291480
  26.0 9.0 %send_first.1 = f32[512,1024]{1,0:T(8,128)} custom-call(s32[128]{0:T(128)S(1)} %pad_add_fusion.1.order, bf16[3,1024,1024]{2,1,0:T(8,128)(2,1)S(1)} %copy-done.1, bf16[3,2048,1024]{2,1,0:T(8,128)(2,1)} %right.5), custom_call_target="tpu_custom_call" | custom-call | flops 3221225472 | bytes 14680064 | tf_op jit(solution)/shard_map/send_first/pallas_call | solution.py:345
  35.1 0.5 collective-permute-start
  35.6 7.7 %send_rest.1 = f32[512,1024]{1,0:T(8,128)S(1)} custom-call(s32[128]{0:T(128)S(1)} %pad_add_fusion.1.order, bf16[3,1024,1024]{2,1,0:T(8,128)(2,1)S(1)} %copy-done.1, bf16[3,2048,1024]{2,1,0:T(8,128)(2,1)} %right.5), custom_call_target="tpu_custom_call" | custom-call | flops 3221225472 | bytes 14680064 | tf_op jit(solution)/shard_map/send_rest/pallas_call | solution.py:345
  43.3 2.3 %collective-permute-start.6 = (f32[512,1024]{1,0:T(8,128)S(1)}, f32[512,1024]{1,0:T(8,128)}, u32[]{:S(2)}, u32[]{:S(2)}) collective-permute-start(f32[512,1024]{1,0:T(8,128)S(1)} %send_rest.1), channel_id=1, source_target_pairs={{0,32},{1,97},{2,34},{3,99},{4,36},{5,101},{6,38},{7,103},{8,40},{... | collective-permute-start | bytes 6291464 | tf_op jit(solution)/shard_map/ppermute | solution.py:459
  45.6 0.8 constant_dynamic-update-slice_fusion.4
  46.5 0.8 fusion.2
  47.2 0.8 constant_dynamic-update-slice_fusion.8
  48.1 2.6 %collective-permute-start.19 = (bf16[96,2048]{1,0:T(8,128)(2,1)S(1)}, bf16[96,2048]{1,0:T(8,128)(2,1)S(1)}, u32[]{:S(2)}, u32[]{:S(2)}) collective-permute-start(bf16[96,2048]{1,0:T(8,128)(2,1)S(1)} %pad_maximum_fusion.7), channel_id=1, source_target_pairs={{0,2},{1,7},{2,0},{3,5},{4,6},{5,3},{6,4},{7,1},{8,10},{9,15},{10,... | collective-permute-start | bytes 1179656 | tf_op jit(solution)/shard_map/ppermute | solution.py:423
  50.7 3.0 %collective-permute-start.15 = (bf16[96,2048]{1,0:T(8,128)(2,1)S(1)}, bf16[96,2048]{1,0:T(8,128)(2,1)S(1)}, u32[]{:S(2)}, u32[]{:S(2)}) collective-permute-start(bf16[96,2048]{1,0:T(8,128)(2,1)S(1)} %pad_maximum_fusion.6), channel_id=1, source_target_pairs={{0,8},{1,25},{2,10},{3,27},{4,12},{5,29},{6,14},{7,31},{8,0},{9,17... | collective-permute-start | bytes 1179656 | tf_op jit(solution)/shard_map/ppermute | solution.py:423
  53.7 2.8 %copy-done.2 = bf16[3,1024,1024]{2,1,0:T(8,128)(2,1)S(1)} copy-done((bf16[3,1024,1024]{2,1,0:T(8,128)(2,1)S(1)}, bf16[3,1024,1024]{2,1,0:T(8,128)(2,1)}, u32[]{:S(2)}) %copy-start.2) | copy-done | bytes 6291480
  56.5 11.4 %keep_all.1 = (f32[512,1024]{1,0:T(8,128)S(1)}, f32[512,1024]{1,0:T(8,128)S(1)}) custom-call(s32[128]{0:T(128)S(1)} %pad_add_fusion.1.order, bf16[3,1024,1024]{2,1,0:T(8,128)(2,1)S(1)} %copy-done.2, bf16[3,2048,1024]{2,1,0:T(8,128)(2,1)} %right.5), custom_call_target="tpu_custom_call" | custom-call | flops 6442450944 | bytes 23068672 | tf_op jit(solution)/shard_map/keep_all/pallas_call | solution.py:345
  68.3 0.8 constant_dynamic-update-slice_fusion.7
  69.1 2.1 %slice_add_fusion.3 = (f32[256,1024]{1,0:T(8,128)S(1)}, f32[256,1024]{1,0:T(8,128)S(1)}) fusion(f32[512,1024]{1,0:T(8,128)} %collective-permute-done, f32[512,1024]{1,0:T(8,128)S(1)} %get-tuple-element.11), kind=kLoop, calls=%fused_computation.5 | loop fusion | flops 524288 | bytes 6291456 | tf_op jit(solution)/shard_map/add | solution.py:467
  71.2 0.3 collective-permute-start.1
  71.5 7.8 %collective-permute-done.20 = bf16[192,2048]{1,0:T(8,128)(2,1)S(1)} collective-permute-done((bf16[192,2048]{1,0:T(8,128)(2,1)S(1)}, bf16[192,2048]{1,0:T(8,128)(2,1)S(1)}, u32[]{:S(2)}, u32[]{:S(2)}) %collective-permute-start.20) | collective-permute-done | bytes 786464 | tf_op jit(solution)/shard_map/ppermute | solution.py:423
  79.3 0.2 pad_maximum_fusion.1
  79.5 0.1 collective-permute-start.21
  79.6 0.2 pad_maximum_fusion
  79.8 0.8 collective-permute-start.17
  80.5 0.8 constant_dynamic-update-slice_fusion.2
  81.3 8.8 %collective-permute-done.6 = f32[512,1024]{1,0:T(8,128)} collective-permute-done((f32[512,1024]{1,0:T(8,128)S(1)}, f32[512,1024]{1,0:T(8,128)}, u32[]{:S(2)}, u32[]{:S(2)}) %collective-permute-start.6) | collective-permute-done | bytes 2097184 | tf_op jit(solution)/shard_map/ppermute | solution.py:459
  90.1 2.1 %slice_add_fusion.1 = (f32[256,1024]{1,0:T(8,128)S(1)}, f32[256,1024]{1,0:T(8,128)S(1)}) fusion(f32[512,1024]{1,0:T(8,128)} %collective-permute-done.6, f32[512,1024]{1,0:T(8,128)S(1)} %get-tuple-element.12), kind=kLoop, calls=%fused_computation.3 | loop fusion | flops 524288 | bytes 6291456 | tf_op jit(solution)/shard_map/add | solution.py:467
  92.2 0.2 collective-permute-start.7
  92.3 1.0 constant_dynamic-update-slice_fusion.6
  93.3 1.0 constant_dynamic-update-slice_fusion.1
  94.3 1.6 collective-permute-done.1
  95.9 1.2 slice_add_fusion.7
  97.1 3.3 %collective-permute-start.2 = (f32[128,1024]{1,0:T(8,128)}, f32[128,1024]{1,0:T(8,128)}, u32[]{:S(2)}, u32[]{:S(2)}) collective-permute-start(f32[128,1024]{1,0:T(8,128)} %get-tuple-element.30), channel_id=1, source_target_pairs={{0,8},{1,25},{2,10},{3,27},{4,12},{5,29},{6,14},{7,31},{8,0},{9,17... | collective-permute-start | bytes 1572872 | tf_op jit(solution)/shard_map/ppermute | solution.py:459
  100.4 1.3 constant_dynamic-update-slice_fusion.5.own_b
  101.7 0.4 collective-permute-start.22
  102.1 1.4 constant_dynamic-update-slice_fusion.own_a
  103.4 2.1 %collective-permute-start.18 = (bf16[768,2048]{1,0:T(8,128)(2,1)}, bf16[768,2048]{1,0:T(8,128)(2,1)}, u32[]{:S(2)}, u32[]{:S(2)}) collective-permute-start(bf16[768,2048]{1,0:T(8,128)(2,1)} %constant_dynamic-update-slice_fusion.own_a), channel_id=1, source_target_pairs={{0,6},{1,3},{2,4},{3,1},{4,2},{5,7},{6,0},{7,5},{8,14},{9,11},{10,... | collective-permute-start | bytes 9437192 | tf_op jit(solution)/shard_map/ppermute | solution.py:423
  105.5 1.7 collective-permute-done.7
  107.2 1.2 slice_add_fusion.5
  108.4 3.3 %collective-permute-start.8 = (f32[128,1024]{1,0:T(8,128)}, f32[128,1024]{1,0:T(8,128)}, u32[]{:S(2)}, u32[]{:S(2)}) collective-permute-start(f32[128,1024]{1,0:T(8,128)} %get-tuple-element.32), channel_id=1, source_target_pairs={{0,2},{1,7},{2,0},{3,5},{4,6},{5,3},{6,4},{7,1},{8,10},{9,15},{10,... | collective-permute-start | bytes 1572872 | tf_op jit(solution)/shard_map/ppermute | solution.py:459
  112.0 1.3 slice_add_fusion.11
  113.2 2.3 %collective-permute-start.3 = (f32[64,1024]{1,0:T(8,128)S(1)}, f32[64,1024]{1,0:T(8,128)S(1)}, u32[]{:S(2)}, u32[]{:S(2)}) collective-permute-start(f32[64,1024]{1,0:T(8,128)S(1)} %get-tuple-element.34), channel_id=1, source_target_pairs={{0,24},{1,9},{2,26},{3,11},{4,28},{5,13},{6,30},{7,15},{8,16},{9,1... | collective-permute-start | bytes 786440 | tf_op jit(solution)/shard_map/ppermute | solution.py:459
  115.5 8.0 %collective-permute-done.8 = f32[128,1024]{1,0:T(8,128)} collective-permute-done((f32[128,1024]{1,0:T(8,128)}, f32[128,1024]{1,0:T(8,128)}, u32[]{:S(2)}, u32[]{:S(2)}) %collective-permute-start.8) | collective-permute-done | bytes 524320 | tf_op jit(solution)/shard_map/ppermute | solution.py:459
  123.5 1.2 slice_add_fusion.9
  124.8 1.5 collective-permute-start.9
  126.3 20.6 %collective-permute-done.3 = f32[64,1024]{1,0:T(8,128)S(1)} collective-permute-done((f32[64,1024]{1,0:T(8,128)S(1)}, f32[64,1024]{1,0:T(8,128)S(1)}, u32[]{:S(2)}, u32[]{:S(2)}) %collective-permute-start.3) | collective-permute-done | bytes 262176 | tf_op jit(solution)/shard_map/ppermute | solution.py:459
  146.9 4.2 %collective-permute-start.4 = (f32[32,1024]{1,0:T(8,128)S(1)}, f32[32,1024]{1,0:T(8,128)S(1)}, u32[]{:S(2)}, u32[]{:S(2)}) collective-permute-start(f32[32,1024]{1,0:T(8,128)S(1)} %get-tuple-element.41), channel_id=1, source_target_pairs={{0,2},{1,7},{2,0},{3,5},{4,6},{5,3},{6,4},{7,1},{8,10},{9,15},{10,... | collective-permute-start | bytes 393224 | tf_op jit(solution)/shard_map/ppermute | solution.py:459
  151.2 4.0 %collective-permute-done.4 = f32[32,1024]{1,0:T(8,128)S(1)} collective-permute-done((f32[32,1024]{1,0:T(8,128)S(1)}, f32[32,1024]{1,0:T(8,128)S(1)}, u32[]{:S(2)}, u32[]{:S(2)}) %collective-permute-start.4) | collective-permute-done | bytes 131104 | tf_op jit(solution)/shard_map/ppermute | solution.py:459
  155.2 0.5 collective-permute-start.5
  155.7 0.8 collective-permute-done.10
  156.5 0.1 collective-permute-start.11
  156.7 2.0 collective-permute-done.5
  158.6 1.1 collective-permute-done.11
  159.8 20.0 %grow_inverse.1 = (bf16[2048,2048]{1,0:T(8,128)(2,1)}, bf16[1024,2048]{1,0:T(8,128)(2,1)}, bf16[4,512,512]{2,1,0:T(8,128)(2,1)S(1)}, bf16[4,512,512]{2,1,0:T(8,128)(2,1)S(1)}) custom-call(s32[32]{0:T(128)S(1)} %pad_add_fusion.3.chips, bf16[768,2048]{1,0:T(8,128)(2,1)} %constant_dynamic-update-slice_fusion.own_a, ...), custom_call_target="tpu_custom_call" | custom-call | flops 4000000000 | bytes 16777216 | tf_op jit(solution)/shard_map/grow_inverse/pallas_call | solution.py:155
  179.8 3.4 %copy-done = bf16[2048,2048]{1,0:T(8,128)(2,1)S(1)} copy-done((bf16[2048,2048]{1,0:T(8,128)(2,1)S(1)}, bf16[2048,2048]{1,0:T(8,128)(2,1)}, u32[]{:S(2)}) %copy-start) | copy-done | bytes 8388632
  183.2 2.2 %copy-done.3 = bf16[1024,2048]{1,0:T(8,128)(2,1)S(1)} copy-done((bf16[1024,2048]{1,0:T(8,128)(2,1)S(1)}, bf16[1024,2048]{1,0:T(8,128)(2,1)}, u32[]{:S(2)}) %copy-start.3) | copy-done | bytes 4194328
  185.4 0.2 solve0.1.own
  185.6 1.3 collective-permute-start.23
  186.9 12.9 %collective-permute-done.23.other = f32[32,2048]{1,0:T(8,128)S(1)} collective-permute-done((f32[32,2048]{1,0:T(8,128)S(1)}, f32[32,2048]{1,0:T(8,128)S(1)}, u32[]{:S(2)}, u32[]{:S(2)}) %collective-permute-start.23) | collective-permute-done | bytes 262176 | tf_op jit(solution)/shard_map/ppermute | solution.py:471
  199.8 4.9 %solve1.1 = f32[16,2048]{1,0:T(8,128)} custom-call(s32[1]{0:T(128)} %bitcast.core, f32[16,2048]{1,0:T(8,128)S(1)} %maximum_subtract_fusion.right, f32[32,2048]{1,0:T(8,128)S(1)} %solve0.1.own, f32[32,2048]{1,0:T(8,128)S(1)} %collective-permute-done.23.other, bf16[2048,2048]{1,0:T(8,128)(2,1)S(1)} %copy-done, bf16[1024,2048]{1,0:T(8,128)(2,1)S(1)} %copy-done.3, ...), custom_call_target="tpu_custom_call" | custom-call | tf_op jit(solution)/shard_map/solve1/pallas_call | solution.py:287
  (44 shorter events, 1.4 us)
Async XLA Ops:
  0.0 4.7 %collective-permute-start.12 = (bf16[64,2048]{1,0:T(8,128)(2,1)}, bf16[64,2048]{1,0:T(8,128)(2,1)S(1)}, u32[]{:S(2)}, u32[]{:S(2)}) collective-permute-start(bf16[64,2048]{1,0:T(8,128)(2,1)} %bitcast.6), channel_id=1, source_target_pairs={{1,0},{3,2},{5,4},{7,6},{9,8},{11,10},{13,12},{15,14},{17,16},{19,... | collective-permute-start | bytes 786440 | tf_op jit(solution)/shard_map/ppermute | solution.py:404
  6.7 14.7 %collective-permute-start.13 = (bf16[128,2048]{1,0:T(8,128)(2,1)S(1)}, bf16[128,2048]{1,0:T(8,128)(2,1)S(1)}, u32[]{:S(2)}, u32[]{:S(2)}) collective-permute-start(bf16[128,2048]{1,0:T(8,128)(2,1)S(1)} %pad_maximum_fusion.4), channel_id=1, source_target_pairs={{0,64},{1,65},{2,66},{3,67},{4,68},{5,69},{6,70},{7,71},{8,72},{9,... | collective-permute-start | bytes 1572872 | tf_op jit(solution)/shard_map/ppermute | solution.py:406
  23.2 22.4 %collective-permute-start.14 = (bf16[128,2048]{1,0:T(8,128)(2,1)}, bf16[128,2048]{1,0:T(8,128)(2,1)S(1)}, u32[]{:S(2)}, u32[]{:S(2)}) collective-permute-start(bf16[128,2048]{1,0:T(8,128)(2,1)} %pad_maximum_fusion.5), channel_id=1, source_target_pairs={{0,32},{1,33},{2,34},{3,35},{4,36},{5,37},{6,38},{7,39},{8,40},{9,... | collective-permute-start | bytes 1572872 | tf_op jit(solution)/shard_map/ppermute | solution.py:410
  23.2 2.8 %copy-start.1 = (bf16[3,1024,1024]{2,1,0:T(8,128)(2,1)S(1)}, bf16[3,1024,1024]{2,1,0:T(8,128)(2,1)}, u32[]{:S(2)}) copy-start(bf16[3,1024,1024]{2,1,0:T(8,128)(2,1)} %left.5) | copy-start | bytes 18874372
  35.1 34.0 %collective-permute-start = (f32[512,1024]{1,0:T(8,128)}, f32[512,1024]{1,0:T(8,128)}, u32[]{:S(2)}, u32[]{:S(2)}) collective-permute-start(f32[512,1024]{1,0:T(8,128)} %send_first.1), channel_id=1, source_target_pairs={{0,32},{1,97},{2,34},{3,99},{4,36},{5,101},{6,38},{7,103},{8,40},{... | collective-permute-start | bytes 6291464 | tf_op jit(solution)/shard_map/ppermute | solution.py:459
  43.3 46.7 %collective-permute-start.6 = (f32[512,1024]{1,0:T(8,128)S(1)}, f32[512,1024]{1,0:T(8,128)}, u32[]{:S(2)}, u32[]{:S(2)}) collective-permute-start(f32[512,1024]{1,0:T(8,128)S(1)} %send_rest.1), channel_id=1, source_target_pairs={{0,32},{1,97},{2,34},{3,99},{4,36},{5,101},{6,38},{7,103},{8,40},{... | collective-permute-start | bytes 6291464 | tf_op jit(solution)/shard_map/ppermute | solution.py:459
  48.1 19.8 %collective-permute-start.19 = (bf16[96,2048]{1,0:T(8,128)(2,1)S(1)}, bf16[96,2048]{1,0:T(8,128)(2,1)S(1)}, u32[]{:S(2)}, u32[]{:S(2)}) collective-permute-start(bf16[96,2048]{1,0:T(8,128)(2,1)S(1)} %pad_maximum_fusion.7), channel_id=1, source_target_pairs={{0,2},{1,7},{2,0},{3,5},{4,6},{5,3},{6,4},{7,1},{8,10},{9,15},{10,... | collective-permute-start | bytes 1179656 | tf_op jit(solution)/shard_map/ppermute | solution.py:423
  50.7 17.3 %collective-permute-start.15 = (bf16[96,2048]{1,0:T(8,128)(2,1)S(1)}, bf16[96,2048]{1,0:T(8,128)(2,1)S(1)}, u32[]{:S(2)}, u32[]{:S(2)}) collective-permute-start(bf16[96,2048]{1,0:T(8,128)(2,1)S(1)} %pad_maximum_fusion.6), channel_id=1, source_target_pairs={{0,8},{1,25},{2,10},{3,27},{4,12},{5,29},{6,14},{7,31},{8,0},{9,17... | collective-permute-start | bytes 1179656 | tf_op jit(solution)/shard_map/ppermute | solution.py:423
  53.7 2.8 %copy-start.2 = (bf16[3,1024,1024]{2,1,0:T(8,128)(2,1)S(1)}, bf16[3,1024,1024]{2,1,0:T(8,128)(2,1)}, u32[]{:S(2)}) copy-start(bf16[3,1024,1024]{2,1,0:T(8,128)(2,1)} %left.5) | copy-start | bytes 18874372
  68.0 11.3 %collective-permute-start.20 = (bf16[192,2048]{1,0:T(8,128)(2,1)S(1)}, bf16[192,2048]{1,0:T(8,128)(2,1)S(1)}, u32[]{:S(2)}, u32[]{:S(2)}) collective-permute-start(bf16[192,2048]{1,0:T(8,128)(2,1)S(1)} %pad_maximum_fusion.3), channel_id=1, source_target_pairs={{0,6},{1,3},{2,4},{3,1},{4,2},{5,7},{6,0},{7,5},{8,14},{9,11},{10,... | collective-permute-start | bytes 2359304 | tf_op jit(solution)/shard_map/ppermute | solution.py:423
  68.2 11.4 %collective-permute-start.16 = (bf16[192,2048]{1,0:T(8,128)(2,1)S(1)}, bf16[192,2048]{1,0:T(8,128)(2,1)S(1)}, u32[]{:S(2)}, u32[]{:S(2)}) collective-permute-start(bf16[192,2048]{1,0:T(8,128)(2,1)S(1)} %pad_maximum_fusion.2), channel_id=1, source_target_pairs={{0,24},{1,9},{2,26},{3,11},{4,28},{5,13},{6,30},{7,15},{8,16},{9,1... | collective-permute-start | bytes 2359304 | tf_op jit(solution)/shard_map/ppermute | solution.py:423
  71.2 24.7 %collective-permute-start.1 = (f32[256,1024]{1,0:T(8,128)S(1)}, f32[256,1024]{1,0:T(8,128)S(1)}, u32[]{:S(2)}, u32[]{:S(2)}) collective-permute-start(f32[256,1024]{1,0:T(8,128)S(1)} %get-tuple-element.26), channel_id=1, source_target_pairs={{0,96},{1,33},{2,98},{3,35},{4,100},{5,37},{6,102},{7,39},{8,104},... | collective-permute-start | bytes 3145736 | tf_op jit(solution)/shard_map/ppermute | solution.py:459
  79.5 20.9 %collective-permute-start.21 = (bf16[384,2048]{1,0:T(8,128)(2,1)S(1)}, bf16[384,2048]{1,0:T(8,128)(2,1)S(1)}, u32[]{:S(2)}, u32[]{:S(2)}) collective-permute-start(bf16[384,2048]{1,0:T(8,128)(2,1)S(1)} %pad_maximum_fusion.1), channel_id=1, source_target_pairs={{0,8},{1,25},{2,10},{3,27},{4,12},{5,29},{6,14},{7,31},{8,0},{9,17... | collective-permute-start | bytes 4718600 | tf_op jit(solution)/shard_map/ppermute | solution.py:423
  79.8 22.3 %collective-permute-start.17 = (bf16[384,2048]{1,0:T(8,128)(2,1)S(1)}, bf16[384,2048]{1,0:T(8,128)(2,1)S(1)}, u32[]{:S(2)}, u32[]{:S(2)}) collective-permute-start(bf16[384,2048]{1,0:T(8,128)(2,1)S(1)} %pad_maximum_fusion), channel_id=1, source_target_pairs={{0,2},{1,7},{2,0},{3,5},{4,6},{5,3},{6,4},{7,1},{8,10},{9,15},{10,... | collective-permute-start | bytes 4718600 | tf_op jit(solution)/shard_map/ppermute | solution.py:423
  92.2 15.1 %collective-permute-start.7 = (f32[256,1024]{1,0:T(8,128)S(1)}, f32[256,1024]{1,0:T(8,128)S(1)}, u32[]{:S(2)}, u32[]{:S(2)}) collective-permute-start(f32[256,1024]{1,0:T(8,128)S(1)} %get-tuple-element.28), channel_id=1, source_target_pairs={{0,96},{1,33},{2,98},{3,35},{4,100},{5,37},{6,102},{7,39},{8,104},... | collective-permute-start | bytes 3145736 | tf_op jit(solution)/shard_map/ppermute | solution.py:459
  97.1 14.9 %collective-permute-start.2 = (f32[128,1024]{1,0:T(8,128)}, f32[128,1024]{1,0:T(8,128)}, u32[]{:S(2)}, u32[]{:S(2)}) collective-permute-start(f32[128,1024]{1,0:T(8,128)} %get-tuple-element.30), channel_id=1, source_target_pairs={{0,8},{1,25},{2,10},{3,27},{4,12},{5,29},{6,14},{7,31},{8,0},{9,17... | collective-permute-start | bytes 1572872 | tf_op jit(solution)/shard_map/ppermute | solution.py:459
  101.7 58.1 %collective-permute-start.22 = (bf16[768,2048]{1,0:T(8,128)(2,1)}, bf16[768,2048]{1,0:T(8,128)(2,1)S(1)}, u32[]{:S(2)}, u32[]{:S(2)}) collective-permute-start(bf16[768,2048]{1,0:T(8,128)(2,1)} %constant_dynamic-update-slice_fusion.5.own_b), channel_id=1, source_target_pairs={{0,24},{1,9},{2,26},{3,11},{4,28},{5,13},{6,30},{7,15},{8,16},{9,1... | collective-permute-start | bytes 9437192 | tf_op jit(solution)/shard_map/ppermute | solution.py:423
  103.4 56.3 %collective-permute-start.18 = (bf16[768,2048]{1,0:T(8,128)(2,1)}, bf16[768,2048]{1,0:T(8,128)(2,1)}, u32[]{:S(2)}, u32[]{:S(2)}) collective-permute-start(bf16[768,2048]{1,0:T(8,128)(2,1)} %constant_dynamic-update-slice_fusion.own_a), channel_id=1, source_target_pairs={{0,6},{1,3},{2,4},{3,1},{4,2},{5,7},{6,0},{7,5},{8,14},{9,11},{10,... | collective-permute-start | bytes 9437192 | tf_op jit(solution)/shard_map/ppermute | solution.py:423
  108.4 51.3 %copy-start.4 = (bf16[16,2048]{1,0:T(8,128)(2,1)S(1)}, bf16[16,2048]{1,0:T(8,128)(2,1)}, u32[]{:S(2)}) copy-start(bf16[16,2048]{1,0:T(8,128)(2,1)} %param.7) | copy-start | bytes 196612
  108.4 15.1 %collective-permute-start.8 = (f32[128,1024]{1,0:T(8,128)}, f32[128,1024]{1,0:T(8,128)}, u32[]{:S(2)}, u32[]{:S(2)}) collective-permute-start(f32[128,1024]{1,0:T(8,128)} %get-tuple-element.32), channel_id=1, source_target_pairs={{0,2},{1,7},{2,0},{3,5},{4,6},{5,3},{6,4},{7,1},{8,10},{9,15},{10,... | collective-permute-start | bytes 1572872 | tf_op jit(solution)/shard_map/ppermute | solution.py:459
  113.2 33.6 %collective-permute-start.3 = (f32[64,1024]{1,0:T(8,128)S(1)}, f32[64,1024]{1,0:T(8,128)S(1)}, u32[]{:S(2)}, u32[]{:S(2)}) collective-permute-start(f32[64,1024]{1,0:T(8,128)S(1)} %get-tuple-element.34), channel_id=1, source_target_pairs={{0,24},{1,9},{2,26},{3,11},{4,28},{5,13},{6,30},{7,15},{8,16},{9,1... | collective-permute-start | bytes 786440 | tf_op jit(solution)/shard_map/ppermute | solution.py:459
  124.8 26.3 %collective-permute-start.9 = (f32[64,1024]{1,0:T(8,128)S(1)}, f32[64,1024]{1,0:T(8,128)S(1)}, u32[]{:S(2)}, u32[]{:S(2)}) collective-permute-start(f32[64,1024]{1,0:T(8,128)S(1)} %get-tuple-element.36), channel_id=1, source_target_pairs={{0,6},{1,3},{2,4},{3,1},{4,2},{5,7},{6,0},{7,5},{8,14},{9,11},{10,... | collective-permute-start | bytes 786440 | tf_op jit(solution)/shard_map/ppermute | solution.py:459
  146.9 8.3 %collective-permute-start.4 = (f32[32,1024]{1,0:T(8,128)S(1)}, f32[32,1024]{1,0:T(8,128)S(1)}, u32[]{:S(2)}, u32[]{:S(2)}) collective-permute-start(f32[32,1024]{1,0:T(8,128)S(1)} %get-tuple-element.41), channel_id=1, source_target_pairs={{0,2},{1,7},{2,0},{3,5},{4,6},{5,3},{6,4},{7,1},{8,10},{9,15},{10,... | collective-permute-start | bytes 393224 | tf_op jit(solution)/shard_map/ppermute | solution.py:459
  151.1 5.4 %collective-permute-start.10 = (f32[32,1024]{1,0:T(8,128)S(1)}, f32[32,1024]{1,0:T(8,128)S(1)}, u32[]{:S(2)}, u32[]{:S(2)}) collective-permute-start(f32[32,1024]{1,0:T(8,128)S(1)} %get-tuple-element.43), channel_id=1, source_target_pairs={{0,8},{1,25},{2,10},{3,27},{4,12},{5,29},{6,14},{7,31},{8,0},{9,17... | collective-permute-start | bytes 393224 | tf_op jit(solution)/shard_map/ppermute | solution.py:459
  155.2 3.4 %collective-permute-start.5 = (f32[16,1024]{1,0:T(8,128)S(1)}, f32[16,1024]{1,0:T(8,128)S(1)}, u32[]{:S(2)}, u32[]{:S(2)}) collective-permute-start(f32[16,1024]{1,0:T(8,128)S(1)} %slice_add_fusion.18), channel_id=1, source_target_pairs={{0,6},{1,3},{2,4},{3,1},{4,2},{5,7},{6,0},{7,5},{8,14},{9,11},{10,... | collective-permute-start | bytes 196616 | tf_op jit(solution)/shard_map/ppermute | solution.py:459
  156.5 3.2 %collective-permute-start.11 = (f32[16,1024]{1,0:T(8,128)S(1)}, f32[16,1024]{1,0:T(8,128)S(1)}, u32[]{:S(2)}, u32[]{:S(2)}) collective-permute-start(f32[16,1024]{1,0:T(8,128)S(1)} %slice_add_fusion.16), channel_id=1, source_target_pairs={{0,24},{1,9},{2,26},{3,11},{4,28},{5,13},{6,30},{7,15},{8,16},{9,1... | collective-permute-start | bytes 196616 | tf_op jit(solution)/shard_map/ppermute | solution.py:459
  179.8 3.4 %copy-start = (bf16[2048,2048]{1,0:T(8,128)(2,1)S(1)}, bf16[2048,2048]{1,0:T(8,128)(2,1)}, u32[]{:S(2)}) copy-start(bf16[2048,2048]{1,0:T(8,128)(2,1)} %get-tuple-element.13.lower) | copy-start | bytes 25165828
  183.2 2.2 %copy-start.3 = (bf16[1024,2048]{1,0:T(8,128)(2,1)S(1)}, bf16[1024,2048]{1,0:T(8,128)(2,1)}, u32[]{:S(2)}) copy-start(bf16[1024,2048]{1,0:T(8,128)(2,1)} %get-tuple-element.14.below) | copy-start | bytes 12582916
  185.6 14.2 %collective-permute-start.23 = (f32[32,2048]{1,0:T(8,128)S(1)}, f32[32,2048]{1,0:T(8,128)S(1)}, u32[]{:S(2)}, u32[]{:S(2)}) collective-permute-start(f32[32,2048]{1,0:T(8,128)S(1)} %solve0.1.own), channel_id=1, source_target_pairs={{0,1},{2,3},{4,5},{6,7},{8,9},{10,11},{12,13},{14,15},{16,17},{18,... | collective-permute-start | bytes 786440 | tf_op jit(solution)/shard_map/ppermute | solution.py:471

commit v4 on v3

--- a/solution.py
+++ b/solution.py
@@ -45,7 +45,7 @@
     return both[:rows] + both[rows:] + dot(high, b_low)
 
 
-def grow_kernel(chips, own_a, got_a, own_b, got_b, lower, below, out_high, out_low, small, sems):
+def grow_kernel(chips, own_a, got_a, own_b, got_b, lower, below, out_high, out_low, sems):
     slab = lower.shape[0]
     half = slab // 2
     for n, (own, got) in enumerate(((own_a, got_a), (own_b, got_b))):
@@ -72,51 +72,20 @@
                 ).start()
     pltpu.make_async_copy(lower, lower, sems.at[0]).wait()
 
-    rows = lax.broadcasted_iota(jnp.int32, (STRIP, 128), 0)
-    lanes = lax.broadcasted_iota(jnp.int32, (STRIP, 128), 1)
-    left = lanes < STRIP
-    inner = jnp.where(left, lanes, lanes - STRIP)
-    together = 4
-
-    def invert(group, carry):
-        todo, upper, scale = [], [], []
-        for n in range(together):
-            start = pl.multiple_of((group * together + n) * 128, 128)
-            cols = pl.ds(start, 128)
-            first = lower[pl.ds(start, STRIP), cols].astype(F32)
-            second = lower[pl.ds(start + STRIP, STRIP), cols].astype(F32)
-            block = jnp.where(left, first, second)
-            diagonal = jnp.where(inner == rows, block, 0.0)
-            one = jnp.sum(jnp.where(left, diagonal, 0.0), axis=1, keepdims=True)
-            two = jnp.sum(jnp.where(left, 0.0, diagonal), axis=1, keepdims=True)
-            upper.append(jnp.where(inner > rows, block, 0.0))
-            scale.append(jnp.where(left, 1.0 / one, 1.0 / two))
-            todo.append(jnp.where(inner == rows, 1.0, 0.0))
-        for k in range(STRIP - 1, 0, -1):
-            top = min(STRIP, (k + 7) // 8 * 8)
-            for n in range(together):
-                row = todo[n][k : k + 1, :] * scale[n][k : k + 1, :]
-                col = jnp.where(
-                    left[:top], upper[n][:top, k : k + 1], upper[n][:top, STRIP + k : STRIP + k + 1]
-                )
-                changed = todo[n][:top] - col * row
-                todo[n] = (
-                    changed if top == STRIP else jnp.concatenate([changed, todo[n][top:]], axis=0)
-                )
-        for n in range(together):
-            small[group * together + n] = todo[n] * scale[n]
-        return carry
-
-    lax.fori_loop(0, slab // 128 // together, invert, 0)
-
     rows = lax.broadcasted_iota(jnp.int32, (128, 128), 0)
     lanes = lax.broadcasted_iota(jnp.int32, (128, 128), 1)
     corner = (rows < STRIP) & (lanes >= STRIP)
     same = (rows < STRIP) == (lanes < STRIP)
+    upright, turned = [], []
+    for k in range(half // 128):
+        rng = slice(half + k * 128, half + k * 128 + 128)
+        pair = lower[rng, :128].astype(F32) + lower[rng, 128:256].astype(F32)
+        swapped = pltpu.roll(pair, STRIP, 1)
+        upright.append(jnp.where(same, jnp.where(rows < STRIP, pair, swapped), 0.0))
+        turned.append(jnp.where(same, jnp.where(rows < STRIP, swapped, pair), 0.0))
     level = []
-    for k in range(slab // 128):
+    for k, both in enumerate(upright + turned):
         rng = slice(k * 128, k * 128 + 128)
-        both = jnp.where(same, jnp.concatenate([small[k], small[k]], axis=0), 0.0)
         off = jnp.where(corner, lower[rng, rng].astype(F32), 0.0).astype(BF16)
         level.append(both - dot_pair(dot_exact(both, off), *split2(both)))
     size = 128
@@ -162,10 +131,7 @@
         ),
         in_specs=[pl.BlockSpec(memory_space=pltpu.SMEM)] + [pl.BlockSpec(memory_space=pltpu.HBM)] * 4,
         out_specs=[vmem] * 4,
-        scratch_shapes=[
-            pltpu.VMEM((slab // 128, STRIP, 128), F32),
-            pltpu.SemaphoreType.DMA((2,)),
-        ],
+        scratch_shapes=[pltpu.SemaphoreType.DMA((2,))],
         compiler_params=pltpu.CompilerParams(vmem_limit_bytes=36 * MB),
         cost_estimate=pl.CostEstimate(
             flops=4 * 10**9, bytes_accessed=4 * slab * slab, transcendentals=0
@@ -299,73 +265,87 @@
             pltpu.VMEM((rows, slab), F32),
             pltpu.SemaphoreType.DMA((4, blocks)),
         ],
-        compiler_params=pltpu.CompilerParams(vmem_limit_bytes=28 * MB),
+        compiler_params=pltpu.CompilerParams(vmem_limit_bytes=56 * MB),
         name=name,
     )(core, *dense, *factor)
 
 
-def product_kernel(parts, half, order, left, right, *refs):
+def product_kernel(parts, half, order, left, right, _, *refs):
     outs, (a, b, picked, a_sems, b_sems) = refs[: len(parts)], refs[len(parts) :]
     groups, _, depth = left.shape
     rows = picked.shape[0]
-    loads = []
-    for g in range(groups):
-        lanes = pl.ds(g * depth, depth)
-        copy = pltpu.make_async_copy(left.at[g], a.at[:, lanes], a_sems.at[g])
+    slab = rows // 2
+    step = b.shape[1]
+    spans = [(n, col) for n in range(len(parts)) for col in range(0, parts[n][2], step)]
+    lanes = [pl.ds(g * depth, depth) for g in range(groups)]
+
+    def slabs(n):
+        copies = []
+        for h in range(2):
+            block = order[(2 * parts[n][0] + half) * (rows // ROWS) + h * (slab // ROWS)]
+            source = pl.ds(pl.multiple_of(block // (slab // ROWS) * slab, slab), slab)
+            for g in range(groups):
+                copies.append(
+                    pltpu.make_async_copy(
+                        left.at[g, source], a.at[pl.ds(h * slab, slab), lanes[g]], a_sems.at[h, g]
+                    )
+                )
+        return copies
+
+    loads = slabs(0)
+    for copy in loads:
         copy.start()
-        loads.append(copy)
     tiles = []
-    for n, (_, start, width) in enumerate(parts):
-        tile = []
-        for g in range(groups):
-            lanes = pl.ds(g * depth, depth)
-            copy = pltpu.make_async_copy(
-                right.at[g, pl.ds(start, width)], b.at[n, :, lanes], b_sems.at[n, g]
+    for t, (n, col) in enumerate(spans):
+        tile = [
+            pltpu.make_async_copy(
+                right.at[g, pl.ds(parts[n][1] + col, step)], b.at[t, :, lanes[g]], b_sems.at[t, g]
             )
+            for g in range(groups)
+        ]
+        for copy in tile:
             copy.start()
-            tile.append(copy)
         tiles.append(tile)
     for copy in loads:
         copy.wait()
-    for n, (number, _, _) in enumerate(parts):
-        base = (2 * number + half) * (rows // ROWS)
-        for r in range(rows // ROWS):
-            source = pl.ds(pl.multiple_of(order[base + r] * ROWS, ROWS), ROWS)
-            picked[r * ROWS : (r + 1) * ROWS, :] = a[source, :]
-        for copy in tiles[n]:
+    for t, (n, col) in enumerate(spans):
+        if col == 0:
+            base = (2 * parts[n][0] + half) * (rows // ROWS)
+            for r in range(rows // ROWS):
+                inside = order[base + r] % (slab // ROWS) + r // (slab // ROWS) * (slab // ROWS)
+                source = pl.ds(pl.multiple_of(inside * ROWS, ROWS), ROWS)
+                picked[r * ROWS : (r + 1) * ROWS, :] = a[source, :]
+        for copy in tiles[t]:
             copy.wait()
-        outs[n][...] = lax.dot_general(
-            picked[...], b[n], (((1,), (1,)), ((), ())), preferred_element_type=F32
+        outs[n][:, col : col + step] = lax.dot_general(
+            picked[...], b[t], (((1,), (1,)), ((), ())), preferred_element_type=F32
         )
 
 
-def product(order, left, right, parts, half, name):
+def product(order, left, right, token, parts, half, name):
     groups, rows, depth = left.shape
     width = sum(part[2] for part in parts)
+    step = 512
     return pl.pallas_call(
         functools.partial(product_kernel, parts, half),
         out_shape=[jax.ShapeDtypeStruct((rows // 2, part[2]), F32) for part in parts],
-        in_specs=[
-            pl.BlockSpec(memory_space=pltpu.SMEM),
-            pl.BlockSpec(memory_space=pltpu.HBM),
-            pl.BlockSpec(memory_space=pltpu.HBM),
-        ],
+        in_specs=[pl.BlockSpec(memory_space=pltpu.SMEM)] + [pl.BlockSpec(memory_space=pltpu.HBM)] * 3,
         out_specs=[pl.BlockSpec(memory_space=pltpu.VMEM)] * len(parts),
         scratch_shapes=[
-            pltpu.VMEM((rows, groups * depth), BF16),
-            pltpu.VMEM((len(parts), parts[0][2], groups * depth), BF16),
             pltpu.VMEM((rows // 2, groups * depth), BF16),
-            pltpu.SemaphoreType.DMA((groups,)),
-            pltpu.SemaphoreType.DMA((len(parts), groups)),
+            pltpu.VMEM((width // step, step, groups * depth), BF16),
+            pltpu.VMEM((rows // 2, groups * depth), BF16),
+            pltpu.SemaphoreType.DMA((2, groups)),
+            pltpu.SemaphoreType.DMA((width // step, groups)),
         ],
-        compiler_params=pltpu.CompilerParams(vmem_limit_bytes=40 * MB),
+        compiler_params=pltpu.CompilerParams(vmem_limit_bytes=56 * MB),
         cost_estimate=pl.CostEstimate(
             flops=groups * rows * width * depth,
-            bytes_accessed=2 * groups * (rows + width) * depth + 2 * rows * width,
+            bytes_accessed=2 * groups * (rows // 2 + width) * depth + 2 * rows * width,
             transcendentals=0,
         ),
         name=name,
-    )(order, left, right)
+    )(order, left, right, token)
 
 
 def chip_index(z, y, x, c):
@@ -396,37 +376,72 @@
     return (((at["z"] * SIDE + at["y"]) * SIDE + at["x"]).reshape(-1)).astype(jnp.int32)
 
 
-def gather_factor(strip, place, core):
-    z = place["z"]
-    pairs = [
-        (chip_index(0, y, x, 1), chip_index(0, y, x, 0)) for y in range(SIDE) for x in range(SIDE)
-    ]
-    got = lax.ppermute(strip, EVERY, pairs)
-    under = jnp.where(core == 0, got, strip)
-    got = lax.ppermute(jnp.concatenate([strip, under]), EVERY, flip_pairs("z", (2, 2)))
-    home = (z < 2) == (core == 0)
-    mine = jnp.where(home, strip, got[:STRIP])
-    under = jnp.where(z < 2, under, got[STRIP:])
-    got = lax.ppermute(jnp.concatenate([mine, under]), EVERY, flip_pairs("z", (1, 1)))
-    even = z % 2 == 0
-    first = jnp.where(even, mine, got[:STRIP])
-    second = jnp.where(even, got[:STRIP], mine)
-    under = jnp.where(z % 2 == core, under, got[STRIP:])
+def pair_kernel(flags, strip, got, both):
+    both[:STRIP] = strip[...]
+    both[STRIP:] = jnp.where(flags[0] > 0, strip[...], got[...])
+
+
+def choose_kernel(flags, held, got, _, both):
+    both[:STRIP] = jnp.where(flags[1] > 0, held[:STRIP], got[:STRIP])
+    both[STRIP:] = jnp.where(flags[2] > 0, held[STRIP:], got[STRIP:])
+
+
+def pack_kernel(flags, held, got, _, out_a, out_b, odd):
+    mine = flags[3] > 0
+    width = held.shape[1]
     cut = STRIP // 2
-    held = [
-        jnp.concatenate([first, second[:cut]]),
-        jnp.concatenate([second[cut:], under]),
-    ]
-    pieces = [None, None]
-    for step in range(4):
-        got = [
-            lax.ppermute(held[n], EVERY, partner_pairs(GATHER[n][step // 2], step % 2 == 1))
-            for n in range(2)
-        ]
-        if step == 3:
-            pieces = [held[0], got[0], held[1], got[1]]
-        else:
-            held = [jnp.concatenate([held[n], got[n]]) for n in range(2)]
+    even = out_a.at[:STRIP]
+    even[...] = jnp.where(mine, held[:STRIP], got[:STRIP])
+    odd[...] = jnp.where(mine, got[:STRIP], held[:STRIP])
+    out_b[cut:] = jnp.where(mine, held[STRIP:], got[STRIP:])
+
+    at = pl.multiple_of(flags[4] * 128, 128)
+    turn = flags[5] > 0
+    one = even[:, pl.ds(at, 128)].astype(F32)
+    two = odd[:, pl.ds(pl.multiple_of(at + width // 2, 128), 128)].astype(F32)
+    one = jnp.where(turn, pltpu.roll(one, STRIP, 1), one)
+    two = jnp.where(turn, two, pltpu.roll(two, STRIP, 1))
+    rows = lax.broadcasted_iota(jnp.int32, (STRIP, 128), 0)
+    lanes = lax.broadcasted_iota(jnp.int32, (STRIP, 128), 1)
+    left = lanes < STRIP
+    inner = jnp.where(left, lanes, lanes - STRIP)
+    block = jnp.where(left, one, two)
+    diagonal = jnp.where(inner == rows, block, 0.0)
+    scale = jnp.where(
+        left,
+        1.0 / jnp.sum(jnp.where(left, diagonal, 0.0), axis=1, keepdims=True),
+        1.0 / jnp.sum(jnp.where(left, 0.0, diagonal), axis=1, keepdims=True),
+    )
+    upper = jnp.where(inner > rows, block, 0.0)
+    todo = jnp.where(inner == rows, 1.0, 0.0)
+    for k in range(STRIP - 1, 0, -1):
+        row = todo[k : k + 1, :] * scale[k : k + 1, :]
+        col = jnp.where(left, upper[:, k : k + 1], upper[:, STRIP + k : STRIP + k + 1])
+        todo = todo - col * row
+    high, low = split2(todo * scale)
+    odd[:, :128] = high
+    odd[:, 128:256] = low
+    out_a[STRIP:] = odd[:cut]
+    out_b[:cut] = odd[cut:]
+
+
+def small_call(kernel, name, shapes, scratch, flags, *operands, token=None):
+    vmem = pl.BlockSpec(memory_space=pltpu.VMEM)
+    tokens = () if token is None else (token,)
+    return pl.pallas_call(
+        kernel,
+        out_shape=[jax.ShapeDtypeStruct(shape, BF16) for shape in shapes],
+        in_specs=[pl.BlockSpec(memory_space=pltpu.SMEM)]
+        + [vmem] * len(operands)
+        + [pl.BlockSpec(memory_space=pl.ANY)] * len(tokens),
+        out_specs=[vmem] * len(shapes),
+        scratch_shapes=scratch,
+        compiler_params=pltpu.CompilerParams(vmem_limit_bytes=16 * MB),
+        name=name,
+    )(flags, *operands, *tokens)
+
+
+def gather_order(place, core):
     flip = jnp.where(core == 0, 1, 3)
     masks = jnp.stack([jnp.zeros_like(flip), flip, flip ^ 2, jnp.full_like(flip, 2)])
     ys, xs = place["y"] ^ masks, place["x"] ^ masks
@@ -434,7 +449,7 @@
         ys[None, :] * SIDE + xs[:, None],
         ys[:, None] * SIDE + xs[None, :],
     ]
-    return pieces, jnp.concatenate([c.reshape(-1) for c in chips]).astype(jnp.int32)
+    return jnp.concatenate([c.reshape(-1) for c in chips]).astype(jnp.int32)
 
 
 def per_device(hist_factor, hist_solution, diag_factor, samples):
@@ -445,14 +460,50 @@
 
     order = jnp.concatenate([block_order(axes, place, core) for _, _, axes in PARTS])
     parts = [(n, start, width) for n, (start, width, _) in enumerate(PARTS)]
-    sends = [
-        *product(order, hist_solution, hist_factor, parts[:1], 0, "send_first"),
-        *product(order, hist_solution, hist_factor, parts[1:], 0, "send_rest"),
+    z = place["z"]
+    at = place["y"] * SIDE + place["x"]
+    outer = (z == 0) | (z == 3)
+    flags = jnp.stack(
+        [core > 0, (z < 2) == (core == 0), z < 2, outer == (core == 0), at // 2, at % 2]
+    ).astype(jnp.int32)
+    chips = gather_order(place, core)
+    strip = diag_factor.T
+    width = strip.shape[1]
+
+    to_first = [
+        (chip_index(0, y, x, 1), chip_index(0, y, x, 0)) for y in range(SIDE) for x in range(SIDE)
     ]
-    keeps = list(product(order, hist_solution, hist_factor, parts, 1, "keep_all"))
-
-    pieces, chips = gather_factor(diag_factor.T, place, core)
-    factor = grow(chips, pieces, slab)
+    got = lax.ppermute(strip, EVERY, to_first)
+    (held,) = small_call(pair_kernel, "pair", [(2 * STRIP, width)], [], flags, strip, got)
+    got = lax.ppermute(held, EVERY, flip_pairs("z", (3, 3)))
+    (send0,) = product(order, hist_solution, hist_factor, held, parts[:1], 0, "send_first")
+    (held,) = small_call(
+        choose_kernel, "choose", [(2 * STRIP, width)], [], flags, held, got, token=send0
+    )
+    got = lax.ppermute(held, EVERY, flip_pairs("z", (1, 1)))
+    (send1,) = product(order, hist_solution, hist_factor, held, parts[1:], 0, "send_rest")
+    share = STRIP + STRIP // 2
+    held = small_call(
+        pack_kernel,
+        "pack",
+        [(share, width)] * 2,
+        [pltpu.VMEM((STRIP, width), BF16)],
+        flags,
+        held,
+        got,
+        token=send1,
+    )
+    sends = [send0, send1]
+    keeps = list(product(order, hist_solution, hist_factor, held[0], parts, 1, "keep_all"))
+
+    for step in range(4):
+        got = [
+            lax.ppermute(held[n], EVERY, partner_pairs(GATHER[n][step // 2], step % 2 == 1))
+            for n in range(2)
+        ]
+        if step < 3:
+            held = [jnp.concatenate([held[n], got[n]]) for n in range(2)]
+    factor = grow(chips, [held[0], got[0], held[1], got[1]], slab)
 
     for step in range(6):
         got = [

time: 205 us -> 196 us (0.956)
  starting transfers between devices: 32.9 us -> 24.8 us
  Pallas kernels: 53.2 us -> 58.6 us
  local copies, waits for them, and re-layouts: 18.5 us -> 13.5 us
  other arithmetic: 15.6 us -> 11.8 us
    ppermute x12, waiting for transfers between devices: 48.5 us -> 57.1 us  [per_device(): lax.ppermute(sends[n], EVERY, partner_pairs(PARTS[n][2][step // 2], step...]
    ppermute x11, waiting for transfers between devices: 22.8 us -> 14.4 us  [the longest x8 9.98 us: per_device(): lax.ppermute(held[n], EVERY, partner_pairs(GATHER[n][step // 2], step % 2...]
    pallas_call x1, Pallas kernels: 20 us -> 13.8 us  [grow(): pl.pallas_call(grow_kernel, out_shape=(jax.ShapeDtypeStruct((slab, slab),...]
    ppermute x12, starting transfers between devices: 18.5 us -> 12.3 us  [per_device(): lax.ppermute(sends[n], EVERY, partner_pairs(PARTS[n][2][step // 2], step...]
    pallas_call x3, Pallas kernels: 28.1 us -> 33.6 us  [product(): pl.pallas_call(functools.partial(product_kernel, parts, half), out_shape=...]
    pallas_call x2, Pallas kernels: 5.03 us -> 8.46 us  [solve_call(): pl.pallas_call(kernel, out_shape=jax.ShapeDtypeStruct((out_rows, slab), F...]
    unnamed x14 -> x34, local copies, waits for them, and re-layouts: 14.6 us -> 11.7 us
    pallas_call x0 -> x3, Pallas kernels: none -> 2.74 us  [small_call(): pl.pallas_call(kernel, out_shape=[jax.ShapeDtypeStruct(shape, BF16) for s...]
  transfers between devices with their start and end apart: 24 -> 24, of which waited for: 13 -> 14; matrix products, arithmetic and copies ran while one was open for 9% -> 9% of each run, Pallas kernels for 14% -> 18%
where the time goes in v4:
time: 196 us; the launch traced here: 195 us
  waiting for transfers between devices  86.3 us (44%)
  Pallas kernels  58.6 us (30%)
  starting transfers between devices  24.8 us (13%)
  local copies, waits for them, and re-layouts  13.5 us (7%)
  other arithmetic  11.8 us (6%)
    ppermute x12, waiting for transfers between devices, per_device(): lax.ppermute(sends[n], EVERY, partner_pairs(PARTS[n][2][step // 2], step...  57.1 us
    pallas_call x3, Pallas kernels, product(): pl.pallas_call(functools.partial(product_kernel, parts, half), out_shape=...  33.6 us
    ppermute x1, waiting for transfers between devices, per_device(): other = lax.ppermute(first, 'pcol', [(0, 1)])  14.8 us
    pallas_call x1, Pallas kernels, grow(): pl.pallas_call(grow_kernel, out_shape=(jax.ShapeDtypeStruct((slab, slab),...  13.8 us
    ppermute x12, starting transfers between devices, per_device(): lax.ppermute(sends[n], EVERY, partner_pairs(PARTS[n][2][step // 2], step...  12.3 us
    unnamed x34, local copies, waits for them, and re-layouts  11.7 us
    ppermute x8, waiting for transfers between devices, per_device(): lax.ppermute(held[n], EVERY, partner_pairs(GATHER[n][step // 2], step % 2...  9.98 us
    add x8, other arithmetic, per_device(): keeps = [keeps[n][middle:] + got[n][middle:] for n in range(len(PARTS))]  8.74 us
  transfers between devices with their start and end apart: 24, of which 14 were waited for; matrix products, arithmetic and copies ran while one was open for 9% of the time, Pallas kernels for 18%

profile of v4, /device:TPU:1, one launch (start us, length us, event | category | flops | bytes accessed | tf_op | source)
XLA Modules:
  0.0 195.4 jit_solution(1427169222808738292)
XLA Ops:
  0.0 3.3 %collective-permute-start = (bf16[64,2048]{1,0:T(8,128)(2,1)}, bf16[64,2048]{1,0:T(8,128)(2,1)S(1)}, u32[]{:S(2)}, u32[]{:S(2)}) collective-permute-start(bf16[64,2048]{1,0:T(8,128)(2,1)} %bitcast.10), channel_id=1, source_target_pairs={{1,0},{3,2},{5,4},{7,6},{9,8},{11,10},{13,12},{15,14},{17,16},{19,... | collective-permute-start | bytes 786440 | tf_op jit(solution)/shard_map/ppermute | solution.py:476
  3.6 1.1 collective-permute-done.got
  4.7 0.9 copy-done.9
  5.6 0.6 pair.1._.held
  6.2 0.9 collective-permute-start.1
  7.4 0.6 pad_add_fusion.1.order
  8.0 9.3 %send_first.1._ = f32[512,1024]{1,0:T(8,128)} custom-call(s32[128]{0:T(128)} %pad_add_fusion.1.order, bf16[3,1024,1024]{2,1,0:T(8,128)(2,1)} %left.5, bf16[3,2048,1024]{2,1,0:T(8,128)(2,1)} %right.5, bf16[128,2048]{1,0:T(8,128)(2,1)} %copy-done.3), custom_call_target="tpu_custom_call" | custom-call | flops 3221225472 | bytes 11534336 | tf_op jit(solution)/shard_map/send_first/pallas_call | solution.py:329
  17.4 3.3 %collective-permute-done.1.got = bf16[128,2048]{1,0:T(8,128)(2,1)S(1)} collective-permute-done((bf16[128,2048]{1,0:T(8,128)(2,1)S(1)}, bf16[128,2048]{1,0:T(8,128)(2,1)S(1)}, u32[]{:S(2)}, u32[]{:S(2)}) %collective-permute-start.1) | collective-permute-done | bytes 524320 | tf_op jit(solution)/shard_map/ppermute | solution.py:478
  20.7 1.0 copy-done.4
  21.7 0.6 choose.1._.held
  22.4 0.6 collective-permute-start.3
  23.1 9.3 %send_rest.1._ = f32[512,1024]{1,0:T(8,128)} custom-call(s32[128]{0:T(128)} %pad_add_fusion.1.order, bf16[3,1024,1024]{2,1,0:T(8,128)(2,1)} %left.5, bf16[3,2048,1024]{2,1,0:T(8,128)(2,1)} %right.5, bf16[128,2048]{1,0:T(8,128)(2,1)} %copy-done.5), custom_call_target="tpu_custom_call" | custom-call | flops 3221225472 | bytes 11534336 | tf_op jit(solution)/shard_map/send_rest/pallas_call | solution.py:329
  32.5 2.1 %collective-permute-start.9 = (f32[512,1024]{1,0:T(8,128)}, f32[512,1024]{1,0:T(8,128)}, u32[]{:S(2)}, u32[]{:S(2)}) collective-permute-start(f32[512,1024]{1,0:T(8,128)} %send_rest.1._), channel_id=1, source_target_pairs={{0,32},{1,97},{2,34},{3,99},{4,36},{5,101},{6,38},{7,103},{8,40},{... | collective-permute-start | bytes 6291464 | tf_op jit(solution)/shard_map/ppermute | solution.py:510
  34.6 1.6 copy-done.2
  36.2 1.0 copy-done.6
  37.3 1.5 pack.1
  38.8 2.7 %collective-permute-start.19 = (bf16[96,2048]{1,0:T(8,128)(2,1)S(1)}, bf16[96,2048]{1,0:T(8,128)(2,1)S(1)}, u32[]{:S(2)}, u32[]{:S(2)}) collective-permute-start(bf16[96,2048]{1,0:T(8,128)(2,1)S(1)} %get-tuple-element.16), channel_id=1, source_target_pairs={{0,2},{1,7},{2,0},{3,5},{4,6},{5,3},{6,4},{7,1},{8,10},{9,15},{10,... | collective-permute-start | bytes 1179656 | tf_op jit(solution)/shard_map/ppermute | solution.py:501
  41.5 2.7 %collective-permute-start.15 = (bf16[96,2048]{1,0:T(8,128)(2,1)S(1)}, bf16[96,2048]{1,0:T(8,128)(2,1)S(1)}, u32[]{:S(2)}, u32[]{:S(2)}) collective-permute-start(bf16[96,2048]{1,0:T(8,128)(2,1)S(1)} %get-tuple-element.13._), channel_id=1, source_target_pairs={{0,8},{1,25},{2,10},{3,27},{4,12},{5,29},{6,14},{7,31},{8,0},{9,17... | collective-permute-start | bytes 1179656 | tf_op jit(solution)/shard_map/ppermute | solution.py:501
  44.2 15.0 %keep_all.1 = (f32[512,1024]{1,0:T(8,128)}, f32[512,1024]{1,0:T(8,128)}) custom-call(s32[128]{0:T(128)} %pad_add_fusion.1.order, bf16[3,1024,1024]{2,1,0:T(8,128)(2,1)} %left.5, bf16[3,2048,1024]{2,1,0:T(8,128)(2,1)} %right.5, bf16[96,2048]{1,0:T(8,128)(2,1)} %copy-done.7), custom_call_target="tpu_custom_call" | custom-call | flops 6442450944 | bytes 19922944 | tf_op jit(solution)/shard_map/keep_all/pallas_call | solution.py:329
  59.2 0.8 constant_dynamic-update-slice_fusion.7
  60.0 1.0 constant_dynamic-update-slice_fusion.3
  61.0 1.0 pad_maximum_fusion.2
  62.3 0.8 constant_dynamic-update-slice_fusion.6
  63.1 2.0 %slice_add_fusion.3 = (f32[256,1024]{1,0:T(8,128)S(1)}, f32[256,1024]{1,0:T(8,128)S(1)}) fusion(f32[512,1024]{1,0:T(8,128)} %collective-permute-done.3, f32[512,1024]{1,0:T(8,128)S(1)} %copy-done.11), kind=kLoop, calls=%fused_computation.5 | loop fusion | flops 524288 | bytes 6291456 | tf_op jit(solution)/shard_map/add | solution.py:518
  65.1 0.4 collective-permute-start.4
  65.5 7.9 %collective-permute-done.16 = bf16[192,2048]{1,0:T(8,128)(2,1)S(1)} collective-permute-done((bf16[192,2048]{1,0:T(8,128)(2,1)S(1)}, bf16[192,2048]{1,0:T(8,128)(2,1)S(1)}, u32[]{:S(2)}, u32[]{:S(2)}) %collective-permute-start.16) | collective-permute-done | bytes 786464 | tf_op jit(solution)/shard_map/ppermute | solution.py:501
  73.5 0.4 collective-permute-start.17
  74.0 0.5 collective-permute-start.21
  74.5 0.9 constant_dynamic-update-slice_fusion.5
  75.4 1.9 slice_add_fusion.1
  77.4 0.4 collective-permute-start.10
  77.8 12.7 %collective-permute-done.4 = f32[256,1024]{1,0:T(8,128)S(1)} collective-permute-done((f32[256,1024]{1,0:T(8,128)S(1)}, f32[256,1024]{1,0:T(8,128)S(1)}, u32[]{:S(2)}, u32[]{:S(2)}) %collective-permute-start.4) | collective-permute-done | bytes 1048608 | tf_op jit(solution)/shard_map/ppermute | solution.py:510
  90.5 1.1 slice_add_fusion.7
  91.7 0.6 collective-permute-start.5
  92.3 1.8 collective-permute-done.17
  94.2 0.3 collective-permute-done.21
  94.5 1.3 constant_dynamic-update-slice_fusion.4.own_b
  95.8 0.3 collective-permute-start.22
  96.2 7.7 %collective-permute-done.10 = f32[256,1024]{1,0:T(8,128)S(1)} collective-permute-done((f32[256,1024]{1,0:T(8,128)S(1)}, f32[256,1024]{1,0:T(8,128)S(1)}, u32[]{:S(2)}, u32[]{:S(2)}) %collective-permute-start.10) | collective-permute-done | bytes 1048608 | tf_op jit(solution)/shard_map/ppermute | solution.py:510
  103.9 1.1 slice_add_fusion.5
  105.0 2.5 %collective-permute-start.11 = (f32[128,1024]{1,0:T(8,128)}, f32[128,1024]{1,0:T(8,128)}, u32[]{:S(2)}, u32[]{:S(2)}) collective-permute-start(f32[128,1024]{1,0:T(8,128)} %get-tuple-element.32), channel_id=1, source_target_pairs={{0,2},{1,7},{2,0},{3,5},{4,6},{5,3},{6,4},{7,1},{8,10},{9,15},{10,... | collective-permute-start | bytes 1572872 | tf_op jit(solution)/shard_map/ppermute | solution.py:510
  107.7 1.3 slice_add_fusion.11
  108.9 1.4 collective-permute-start.6
  110.3 10.2 %collective-permute-done.11 = f32[128,1024]{1,0:T(8,128)} collective-permute-done((f32[128,1024]{1,0:T(8,128)}, f32[128,1024]{1,0:T(8,128)}, u32[]{:S(2)}, u32[]{:S(2)}) %collective-permute-start.11) | collective-permute-done | bytes 524320 | tf_op jit(solution)/shard_map/ppermute | solution.py:510
  120.5 1.2 slice_add_fusion.9
  121.8 0.2 collective-permute-start.12
  122.0 19.0 %collective-permute-done.6 = f32[64,1024]{1,0:T(8,128)S(1)} collective-permute-done((f32[64,1024]{1,0:T(8,128)S(1)}, f32[64,1024]{1,0:T(8,128)S(1)}, u32[]{:S(2)}, u32[]{:S(2)}) %collective-permute-start.6) | collective-permute-done | bytes 262176 | tf_op jit(solution)/shard_map/ppermute | solution.py:510
  141.0 2.5 %collective-permute-start.7 = (f32[32,1024]{1,0:T(8,128)S(1)}, f32[32,1024]{1,0:T(8,128)S(1)}, u32[]{:S(2)}, u32[]{:S(2)}) collective-permute-start(f32[32,1024]{1,0:T(8,128)S(1)} %get-tuple-element.38), channel_id=1, source_target_pairs={{0,2},{1,7},{2,0},{3,5},{4,6},{5,3},{6,4},{7,1},{8,10},{9,15},{10,... | collective-permute-start | bytes 393224 | tf_op jit(solution)/shard_map/ppermute | solution.py:510
  143.6 1.0 collective-permute-start.13
  144.5 3.4 %collective-permute-done.7 = f32[32,1024]{1,0:T(8,128)S(1)} collective-permute-done((f32[32,1024]{1,0:T(8,128)S(1)}, f32[32,1024]{1,0:T(8,128)S(1)}, u32[]{:S(2)}, u32[]{:S(2)}) %collective-permute-start.7) | collective-permute-done | bytes 131104 | tf_op jit(solution)/shard_map/ppermute | solution.py:510
  147.9 0.3 collective-permute-start.8
  148.2 1.1 collective-permute-done.13
  149.3 0.5 collective-permute-start.14
  149.9 1.5 collective-permute-done.8
  151.3 1.5 collective-permute-done.14
  152.9 0.7 maximum_subtract_fusion.right
  153.6 13.8 %grow_inverse.1 = (bf16[2048,2048]{1,0:T(8,128)(2,1)}, bf16[1024,2048]{1,0:T(8,128)(2,1)}, bf16[4,512,512]{2,1,0:T(8,128)(2,1)S(1)}, bf16[4,512,512]{2,1,0:T(8,128)(2,1)S(1)}) custom-call(s32[32]{0:T(128)S(1)} %pad_add_fusion.3.chips, bf16[768,2048]{1,0:T(8,128)(2,1)S(1)} %constant_dynamic-update-slice_fusion.own_a, ...), custom_call_target="tpu_custom_call" | custom-call | flops 4000000000 | bytes 16777216 | tf_op jit(solution)/shard_map/grow_inverse/pallas_call | solution.py:124
  167.4 1.3 copy-done
  168.7 1.3 copy-done.1
  170.0 1.8 solve0.1.own
  171.8 1.3 collective-permute-start.23
  173.1 14.8 %collective-permute-done.23.other = f32[32,2048]{1,0:T(8,128)S(1)} collective-permute-done((f32[32,2048]{1,0:T(8,128)}, f32[32,2048]{1,0:T(8,128)S(1)}, u32[]{:S(2)}, u32[]{:S(2)}) %collective-permute-start.23) | collective-permute-done | bytes 262176 | tf_op jit(solution)/shard_map/ppermute | solution.py:522
  187.9 0.7 copy-done.12
  188.6 6.7 %solve1.1 = f32[16,2048]{1,0:T(8,128)} custom-call(s32[1]{0:T(128)} %bitcast.core, f32[16,2048]{1,0:T(8,128)} %maximum_subtract_fusion.right, f32[32,2048]{1,0:T(8,128)} %solve0.1.own, f32[32,2048]{1,0:T(8,128)} %copy-done.12, bf16[2048,2048]{1,0:T(8,128)(2,1)} %get-tuple-element.17.lower, bf16[1024,2048]{1,0:T(8,128)(2,1)} %get-tuple-element.18.below, ...), custom_call_target="tpu_custom_call" | custom-call | tf_op jit(solution)/shard_map/solve1/pallas_call | solution.py:253
  (59 shorter events, 2.0 us)
Async XLA Ops:
  0.0 4.7 %collective-permute-start = (bf16[64,2048]{1,0:T(8,128)(2,1)}, bf16[64,2048]{1,0:T(8,128)(2,1)S(1)}, u32[]{:S(2)}, u32[]{:S(2)}) collective-permute-start(bf16[64,2048]{1,0:T(8,128)(2,1)} %bitcast.10), channel_id=1, source_target_pairs={{1,0},{3,2},{5,4},{7,6},{9,8},{11,10},{13,12},{15,14},{17,16},{19,... | collective-permute-start | bytes 786440 | tf_op jit(solution)/shard_map/ppermute | solution.py:476
  4.7 0.9 copy-start.9
  6.2 1.8 copy-start.3
  6.2 14.4 %collective-permute-start.1 = (bf16[128,2048]{1,0:T(8,128)(2,1)S(1)}, bf16[128,2048]{1,0:T(8,128)(2,1)S(1)}, u32[]{:S(2)}, u32[]{:S(2)}) collective-permute-start(bf16[128,2048]{1,0:T(8,128)(2,1)S(1)} %pair.1._.held), channel_id=1, source_target_pairs={{0,96},{1,97},{2,98},{3,99},{4,100},{5,101},{6,102},{7,103},{8,104... | collective-permute-start | bytes 1572872 | tf_op jit(solution)/shard_map/ppermute | solution.py:478
  20.7 1.0 copy-start.4
  22.3 0.8 copy-start.5
  22.3 12.3 %collective-permute-start.2 = (bf16[128,2048]{1,0:T(8,128)(2,1)S(1)}, bf16[128,2048]{1,0:T(8,128)(2,1)S(1)}, u32[]{:S(2)}, u32[]{:S(2)}) collective-permute-start(bf16[128,2048]{1,0:T(8,128)(2,1)S(1)} %choose.1._.held), channel_id=1, source_target_pairs={{0,32},{1,33},{2,34},{3,35},{4,36},{5,37},{6,38},{7,39},{8,40},{9,... | collective-permute-start | bytes 1572872 | tf_op jit(solution)/shard_map/ppermute | solution.py:483
  22.4 40.7 %collective-permute-start.3 = (f32[512,1024]{1,0:T(8,128)}, f32[512,1024]{1,0:T(8,128)}, u32[]{:S(2)}, u32[]{:S(2)}) collective-permute-start(f32[512,1024]{1,0:T(8,128)} %send_first.1._), channel_id=1, source_target_pairs={{0,32},{1,97},{2,34},{3,99},{4,36},{5,101},{6,38},{7,103},{8,40},{... | collective-permute-start | bytes 6291464 | tf_op jit(solution)/shard_map/ppermute | solution.py:510
  32.5 43.0 %collective-permute-start.9 = (f32[512,1024]{1,0:T(8,128)}, f32[512,1024]{1,0:T(8,128)}, u32[]{:S(2)}, u32[]{:S(2)}) collective-permute-start(f32[512,1024]{1,0:T(8,128)} %send_rest.1._), channel_id=1, source_target_pairs={{0,32},{1,97},{2,34},{3,99},{4,36},{5,101},{6,38},{7,103},{8,40},{... | collective-permute-start | bytes 6291464 | tf_op jit(solution)/shard_map/ppermute | solution.py:510
  34.6 1.6 copy-start.2
  36.2 1.0 copy-start.6
  38.8 5.4 %copy-start.7 = (bf16[96,2048]{1,0:T(8,128)(2,1)}, bf16[96,2048]{1,0:T(8,128)(2,1)S(1)}, u32[]{:S(2)}) copy-start(bf16[96,2048]{1,0:T(8,128)(2,1)S(1)} %get-tuple-element.13._) | copy-start | bytes 1179652
  38.8 23.3 %collective-permute-start.19 = (bf16[96,2048]{1,0:T(8,128)(2,1)S(1)}, bf16[96,2048]{1,0:T(8,128)(2,1)S(1)}, u32[]{:S(2)}, u32[]{:S(2)}) collective-permute-start(bf16[96,2048]{1,0:T(8,128)(2,1)S(1)} %get-tuple-element.16), channel_id=1, source_target_pairs={{0,2},{1,7},{2,0},{3,5},{4,6},{5,3},{6,4},{7,1},{8,10},{9,15},{10,... | collective-permute-start | bytes 1179656 | tf_op jit(solution)/shard_map/ppermute | solution.py:501
  41.5 19.5 %collective-permute-start.15 = (bf16[96,2048]{1,0:T(8,128)(2,1)S(1)}, bf16[96,2048]{1,0:T(8,128)(2,1)S(1)}, u32[]{:S(2)}, u32[]{:S(2)}) collective-permute-start(bf16[96,2048]{1,0:T(8,128)(2,1)S(1)} %get-tuple-element.13._), channel_id=1, source_target_pairs={{0,8},{1,25},{2,10},{3,27},{4,12},{5,29},{6,14},{7,31},{8,0},{9,17... | collective-permute-start | bytes 1179656 | tf_op jit(solution)/shard_map/ppermute | solution.py:501
  59.2 3.9 %copy-start.11 = (f32[512,1024]{1,0:T(8,128)S(1)}, f32[512,1024]{1,0:T(8,128)}, u32[]{:S(2)}) copy-start(f32[512,1024]{1,0:T(8,128)} %get-tuple-element.14) | copy-start | bytes 6291460
  62.0 11.3 %collective-permute-start.16 = (bf16[192,2048]{1,0:T(8,128)(2,1)S(1)}, bf16[192,2048]{1,0:T(8,128)(2,1)S(1)}, u32[]{:S(2)}, u32[]{:S(2)}) collective-permute-start(bf16[192,2048]{1,0:T(8,128)(2,1)S(1)} %pad_maximum_fusion.2), channel_id=1, source_target_pairs={{0,24},{1,9},{2,26},{3,11},{4,28},{5,13},{6,30},{7,15},{8,16},{9,1... | collective-permute-start | bytes 2359304 | tf_op jit(solution)/shard_map/ppermute | solution.py:501
  62.2 11.6 %collective-permute-start.20 = (bf16[192,2048]{1,0:T(8,128)(2,1)S(1)}, bf16[192,2048]{1,0:T(8,128)(2,1)S(1)}, u32[]{:S(2)}, u32[]{:S(2)}) collective-permute-start(bf16[192,2048]{1,0:T(8,128)(2,1)S(1)} %pad_maximum_fusion.3), channel_id=1, source_target_pairs={{0,6},{1,3},{2,4},{3,1},{4,2},{5,7},{6,0},{7,5},{8,14},{9,11},{10,... | collective-permute-start | bytes 2359304 | tf_op jit(solution)/shard_map/ppermute | solution.py:501
  63.1 10.3 %copy-start.8 = (bf16[96,2048]{1,0:T(8,128)(2,1)S(1)}, bf16[96,2048]{1,0:T(8,128)(2,1)}, u32[]{:S(2)}) copy-start(bf16[96,2048]{1,0:T(8,128)(2,1)} %copy-done.7) | copy-start | bytes 1179652
  65.1 25.4 %collective-permute-start.4 = (f32[256,1024]{1,0:T(8,128)S(1)}, f32[256,1024]{1,0:T(8,128)S(1)}, u32[]{:S(2)}, u32[]{:S(2)}) collective-permute-start(f32[256,1024]{1,0:T(8,128)S(1)} %get-tuple-element.26), channel_id=1, source_target_pairs={{0,96},{1,33},{2,98},{3,35},{4,100},{5,37},{6,102},{7,39},{8,104},... | collective-permute-start | bytes 3145736 | tf_op jit(solution)/shard_map/ppermute | solution.py:510
  73.5 2.0 copy-start.10
  73.5 20.6 %collective-permute-start.17 = (bf16[384,2048]{1,0:T(8,128)(2,1)S(1)}, bf16[384,2048]{1,0:T(8,128)(2,1)S(1)}, u32[]{:S(2)}, u32[]{:S(2)}) collective-permute-start(bf16[384,2048]{1,0:T(8,128)(2,1)S(1)} %pad_maximum_fusion), channel_id=1, source_target_pairs={{0,2},{1,7},{2,0},{3,5},{4,6},{5,3},{6,4},{7,1},{8,10},{9,15},{10,... | collective-permute-start | bytes 4718600 | tf_op jit(solution)/shard_map/ppermute | solution.py:501
  74.0 20.6 %collective-permute-start.21 = (bf16[384,2048]{1,0:T(8,128)(2,1)S(1)}, bf16[384,2048]{1,0:T(8,128)(2,1)S(1)}, u32[]{:S(2)}, u32[]{:S(2)}) collective-permute-start(bf16[384,2048]{1,0:T(8,128)(2,1)S(1)} %pad_maximum_fusion.1), channel_id=1, source_target_pairs={{0,8},{1,25},{2,10},{3,27},{4,12},{5,29},{6,14},{7,31},{8,0},{9,17... | collective-permute-start | bytes 4718600 | tf_op jit(solution)/shard_map/ppermute | solution.py:501
  77.4 26.5 %collective-permute-start.10 = (f32[256,1024]{1,0:T(8,128)S(1)}, f32[256,1024]{1,0:T(8,128)S(1)}, u32[]{:S(2)}, u32[]{:S(2)}) collective-permute-start(f32[256,1024]{1,0:T(8,128)S(1)} %get-tuple-element.28), channel_id=1, source_target_pairs={{0,96},{1,33},{2,98},{3,35},{4,100},{5,37},{6,102},{7,39},{8,104},... | collective-permute-start | bytes 3145736 | tf_op jit(solution)/shard_map/ppermute | solution.py:510
  91.7 16.0 %collective-permute-start.5 = (f32[128,1024]{1,0:T(8,128)}, f32[128,1024]{1,0:T(8,128)}, u32[]{:S(2)}, u32[]{:S(2)}) collective-permute-start(f32[128,1024]{1,0:T(8,128)} %get-tuple-element.30), channel_id=1, source_target_pairs={{0,8},{1,25},{2,10},{3,27},{4,12},{5,29},{6,14},{7,31},{8,0},{9,17... | collective-permute-start | bytes 1572872 | tf_op jit(solution)/shard_map/ppermute | solution.py:510
  94.2 59.4 %collective-permute-start.18 = (bf16[768,2048]{1,0:T(8,128)(2,1)S(1)}, bf16[768,2048]{1,0:T(8,128)(2,1)}, u32[]{:S(2)}, u32[]{:S(2)}) collective-permute-start(bf16[768,2048]{1,0:T(8,128)(2,1)S(1)} %constant_dynamic-update-slice_fusion.own_a), channel_id=1, source_target_pairs={{0,6},{1,3},{2,4},{3,1},{4,2},{5,7},{6,0},{7,5},{8,14},{9,11},{10,... | collective-permute-start | bytes 9437192 | tf_op jit(solution)/shard_map/ppermute | solution.py:501
  95.8 57.7 %collective-permute-start.22 = (bf16[768,2048]{1,0:T(8,128)(2,1)}, bf16[768,2048]{1,0:T(8,128)(2,1)}, u32[]{:S(2)}, u32[]{:S(2)}) collective-permute-start(bf16[768,2048]{1,0:T(8,128)(2,1)} %constant_dynamic-update-slice_fusion.4.own_b), channel_id=1, source_target_pairs={{0,24},{1,9},{2,26},{3,11},{4,28},{5,13},{6,30},{7,15},{8,16},{9,1... | collective-permute-start | bytes 9437192 | tf_op jit(solution)/shard_map/ppermute | solution.py:501
  105.0 47.9 %copy-start.13 = (bf16[16,2048]{1,0:T(8,128)(2,1)S(1)}, bf16[16,2048]{1,0:T(8,128)(2,1)}, u32[]{:S(2)}) copy-start(bf16[16,2048]{1,0:T(8,128)(2,1)} %param.7) | copy-start | bytes 196612
  105.0 15.5 %collective-permute-start.11 = (f32[128,1024]{1,0:T(8,128)}, f32[128,1024]{1,0:T(8,128)}, u32[]{:S(2)}, u32[]{:S(2)}) collective-permute-start(f32[128,1024]{1,0:T(8,128)} %get-tuple-element.32), channel_id=1, source_target_pairs={{0,2},{1,7},{2,0},{3,5},{4,6},{5,3},{6,4},{7,1},{8,10},{9,15},{10,... | collective-permute-start | bytes 1572872 | tf_op jit(solution)/shard_map/ppermute | solution.py:510
  108.9 32.1 %collective-permute-start.6 = (f32[64,1024]{1,0:T(8,128)S(1)}, f32[64,1024]{1,0:T(8,128)S(1)}, u32[]{:S(2)}, u32[]{:S(2)}) collective-permute-start(f32[64,1024]{1,0:T(8,128)S(1)} %get-tuple-element.34), channel_id=1, source_target_pairs={{0,24},{1,9},{2,26},{3,11},{4,28},{5,13},{6,30},{7,15},{8,16},{9,1... | collective-permute-start | bytes 786440 | tf_op jit(solution)/shard_map/ppermute | solution.py:510
  121.8 21.8 %collective-permute-start.12 = (f32[64,1024]{1,0:T(8,128)S(1)}, f32[64,1024]{1,0:T(8,128)S(1)}, u32[]{:S(2)}, u32[]{:S(2)}) collective-permute-start(f32[64,1024]{1,0:T(8,128)S(1)} %get-tuple-element.36), channel_id=1, source_target_pairs={{0,6},{1,3},{2,4},{3,1},{4,2},{5,7},{6,0},{7,5},{8,14},{9,11},{10,... | collective-permute-start | bytes 786440 | tf_op jit(solution)/shard_map/ppermute | solution.py:510
  141.0 6.9 %collective-permute-start.7 = (f32[32,1024]{1,0:T(8,128)S(1)}, f32[32,1024]{1,0:T(8,128)S(1)}, u32[]{:S(2)}, u32[]{:S(2)}) collective-permute-start(f32[32,1024]{1,0:T(8,128)S(1)} %get-tuple-element.38), channel_id=1, source_target_pairs={{0,2},{1,7},{2,0},{3,5},{4,6},{5,3},{6,4},{7,1},{8,10},{9,15},{10,... | collective-permute-start | bytes 393224 | tf_op jit(solution)/shard_map/ppermute | solution.py:510
  143.6 5.8 %collective-permute-start.13 = (f32[32,1024]{1,0:T(8,128)S(1)}, f32[32,1024]{1,0:T(8,128)S(1)}, u32[]{:S(2)}, u32[]{:S(2)}) collective-permute-start(f32[32,1024]{1,0:T(8,128)S(1)} %get-tuple-element.40), channel_id=1, source_target_pairs={{0,8},{1,25},{2,10},{3,27},{4,12},{5,29},{6,14},{7,31},{8,0},{9,17... | collective-permute-start | bytes 393224 | tf_op jit(solution)/shard_map/ppermute | solution.py:510
  147.9 3.4 %collective-permute-start.8 = (f32[16,1024]{1,0:T(8,128)S(1)}, f32[16,1024]{1,0:T(8,128)S(1)}, u32[]{:S(2)}, u32[]{:S(2)}) collective-permute-start(f32[16,1024]{1,0:T(8,128)S(1)} %slice_add_fusion.18), channel_id=1, source_target_pairs={{0,6},{1,3},{2,4},{3,1},{4,2},{5,7},{6,0},{7,5},{8,14},{9,11},{10,... | collective-permute-start | bytes 196616 | tf_op jit(solution)/shard_map/ppermute | solution.py:510
  149.3 3.5 %collective-permute-start.14 = (f32[16,1024]{1,0:T(8,128)S(1)}, f32[16,1024]{1,0:T(8,128)S(1)}, u32[]{:S(2)}, u32[]{:S(2)}) collective-permute-start(f32[16,1024]{1,0:T(8,128)S(1)} %slice_add_fusion.16), channel_id=1, source_target_pairs={{0,24},{1,9},{2,26},{3,11},{4,28},{5,13},{6,30},{7,15},{8,16},{9,1... | collective-permute-start | bytes 196616 | tf_op jit(solution)/shard_map/ppermute | solution.py:510
  167.4 1.3 copy-start
  168.7 1.3 copy-start.1
  171.8 16.1 %collective-permute-start.23 = (f32[32,2048]{1,0:T(8,128)}, f32[32,2048]{1,0:T(8,128)S(1)}, u32[]{:S(2)}, u32[]{:S(2)}) collective-permute-start(f32[32,2048]{1,0:T(8,128)} %solve0.1.own), channel_id=1, source_target_pairs={{0,1},{2,3},{4,5},{6,7},{8,9},{10,11},{12,13},{14,15},{16,17},{18,... | collective-permute-start | bytes 786440 | tf_op jit(solution)/shard_map/ppermute | solution.py:522
  187.9 0.7 copy-start.12

commit v5 on v4

--- a/solution.py
+++ b/solution.py
@@ -20,6 +20,7 @@
 PARTS = ((0, 1024, "zyx"), (1024, 1024, "zxy"))
 GATHER = ("yx", "xy")
 MB = 1 << 20
+TOKEN = jax.ShapeDtypeStruct((8, 128), F32)
 
 
 def split2(value):
@@ -45,32 +46,53 @@
     return both[:rows] + both[rows:] + dot(high, b_low)
 
 
-def grow_kernel(chips, own_a, got_a, own_b, got_b, lower, below, out_high, out_low, sems):
+def strip_copies(chips, pieces, lower, below, sems):
+    own_a, got_a, own_b, got_b = pieces
+    half = lower.shape[0] // 2
+    cut = STRIP // 2
+    groups = ([], [], [])
+
+    def add(group, source, start, count, target, to):
+        groups[group].append(
+            pltpu.make_async_copy(
+                source.at[pl.ds(start, count)],
+                target.at[pl.ds(pl.multiple_of(to, cut), count)],
+                sems.at[group],
+            )
+        )
+
+    for position in range(16):
+        base = (position % 8) * (STRIP + cut)
+        row = pl.multiple_of(chips[position] * STRIP, STRIP)
+        source = own_a if position < 8 else got_a
+        add(0, source, base, STRIP, lower, row)
+        add(1, source, base + STRIP, cut, lower, half + row)
+        row = pl.multiple_of(chips[16 + position] * STRIP, STRIP)
+        source = own_b if position < 8 else got_b
+        add(1, source, base, cut, lower, half + row + cut)
+        if below is not None:
+            add(2, source, base + cut, STRIP, below, row)
+    return groups
+
+
+def start_all(copies):
+    for copy in copies:
+        copy.start()
+
+
+def wait_for(target, sem):
+    pltpu.make_async_copy(target, target, sem).wait()
+
+
+def grow_kernel(chips, own_a, got_a, own_b, got_b, out_high, out_low, token, lower, sems):
     slab = lower.shape[0]
     half = slab // 2
-    for n, (own, got) in enumerate(((own_a, got_a), (own_b, got_b))):
-        share = own.shape[0] // 8
-        for position in range(16):
-            source = own if position < 8 else got
-            base = (position % 8) * share
-            row = pl.multiple_of(chips[16 * n + position] * STRIP, STRIP)
-            if n == 0:
-                moves = (
-                    (base, STRIP, lower, row, 0),
-                    (base + STRIP, STRIP // 2, lower, half + row, 0),
-                )
-            else:
-                moves = (
-                    (base, STRIP // 2, lower, half + row + STRIP // 2, 0),
-                    (base + STRIP // 2, STRIP, below, row, 1),
-                )
-            for start, count, target, to, sem in moves:
-                pltpu.make_async_copy(
-                    source.at[pl.ds(start, count)],
-                    target.at[pl.ds(pl.multiple_of(to, STRIP // 2), count)],
-                    sems.at[sem],
-                ).start()
-    pltpu.make_async_copy(lower, lower, sems.at[0]).wait()
+    even, odd, _ = strip_copies(chips, (own_a, got_a, own_b, got_b), lower, None, sems)
+    start_all(even)
+    start_all(odd)
+    token[...] = jnp.zeros_like(token)
+    wait_for(lower.at[:half], sems.at[0])
+    wait_for(lower.at[half:], sems.at[1])
 
     rows = lax.broadcasted_iota(jnp.int32, (128, 128), 0)
     lanes = lax.broadcasted_iota(jnp.int32, (128, 128), 1)
@@ -115,7 +137,6 @@
                     ref[b, size:, size:] = second
         level = grown
         size *= 2
-    pltpu.make_async_copy(below, below, sems.at[1]).wait()
 
 
 def grow(chips, pieces, slab):
@@ -123,139 +144,94 @@
     vmem = pl.BlockSpec(memory_space=pltpu.VMEM)
     return pl.pallas_call(
         grow_kernel,
-        out_shape=(
-            jax.ShapeDtypeStruct((slab, slab), BF16),
-            jax.ShapeDtypeStruct((slab // 2, slab), BF16),
-            inverse,
-            inverse,
-        ),
-        in_specs=[pl.BlockSpec(memory_space=pltpu.SMEM)] + [pl.BlockSpec(memory_space=pltpu.HBM)] * 4,
-        out_specs=[vmem] * 4,
-        scratch_shapes=[pltpu.SemaphoreType.DMA((2,))],
-        compiler_params=pltpu.CompilerParams(vmem_limit_bytes=36 * MB),
-        cost_estimate=pl.CostEstimate(
-            flops=4 * 10**9, bytes_accessed=4 * slab * slab, transcendentals=0
-        ),
+        out_shape=(inverse, inverse, TOKEN),
+        in_specs=[pl.BlockSpec(memory_space=pltpu.SMEM)] + [pl.BlockSpec(memory_space=pl.ANY)] * 4,
+        out_specs=[vmem] * 3,
+        scratch_shapes=[pltpu.VMEM((slab, slab), BF16), pltpu.SemaphoreType.DMA((2,))],
+        compiler_params=pltpu.CompilerParams(vmem_limit_bytes=28 * MB),
+        cost_estimate=pl.CostEstimate(flops=4 * 10**9, bytes_accessed=2 * slab * slab, transcendentals=0),
         name="grow_inverse",
     )(chips, *pieces)
 
 
-def solve_block(blocks, pending, factor, high, low, out, wait, after):
+def solve_block(blocks, pending, factor, high, low, out, wait, before_update, after):
     for b in range(blocks):
         cols = slice(b * BLOCK, (b + 1) * BLOCK)
         wait(b)
         y = dot_pair(pending[:, cols], high[b], low[b])
         out[: pending.shape[0], cols] = y
+        before_update(b)
         if b + 1 < blocks:
             rest = slice((b + 1) * BLOCK, blocks * BLOCK)
             pending[:, rest] = pending[:, rest] - dot_exact(y, factor[cols, rest])
         after(b, y)
 
 
-def solve_copies(lower, inv_high, inv_low, factor, high, low, sems):
-    copies = []
-    slab = lower.shape[1]
-    for b in range(slab // BLOCK):
-        group = [
+def inverse_copies(inv_high, inv_low, high, low, sems):
+    return [
+        [
             pltpu.make_async_copy(inv_high.at[b], high.at[b], sems.at[0, b]),
             pltpu.make_async_copy(inv_low.at[b], low.at[b], sems.at[1, b]),
         ]
-        if (b + 1) * BLOCK < slab:
-            rest = pl.ds((b + 1) * BLOCK, slab - (b + 1) * BLOCK)
-            rows = pl.ds(b * BLOCK, BLOCK)
-            group.append(
-                pltpu.make_async_copy(
-                    lower.at[rows, rest], factor.at[rows, rest], sems.at[2, b]
-                )
-            )
-        copies.append(group)
-    return copies
-
-
-def below_copies(below, under, sems):
-    copies = []
-    for b in range(below.shape[0] // BLOCK):
-        rows = pl.ds(b * BLOCK, BLOCK)
-        copies.append(pltpu.make_async_copy(below.at[rows], under.at[rows], sems.at[3, b]))
-    return copies
-
-
-def first_kernel(
-    core, right, lower, below, inv_high, inv_low, out, factor, under, high, low, pending, sems
-):
-    rows, slab = right.shape
-
-    @pl.when(core[0] == 0)
-    def _():
-        copies = solve_copies(lower, inv_high, inv_low, factor, high, low, sems)
-        belows = below_copies(below, under, sems)
-        for b, group in enumerate(copies):
-            for copy in group:
-                copy.start()
-            if b < len(belows):
-                belows[b].start()
-        pending[...] = right[...]
-
-        def wait(b):
-            for copy in copies[b]:
-                copy.wait()
-
-        def after(b, y):
-            if b < len(belows):
-                belows[b].wait()
-                term = dot_exact(y, under[b * BLOCK : (b + 1) * BLOCK, :])
-                out[rows:, :] = term if b == 0 else out[rows:, :] + term
-
-        solve_block(slab // BLOCK, pending, factor, high, low, out, wait, after)
-
-    @pl.when(core[0] != 0)
-    def _():
-        out[...] = jnp.zeros_like(out)
-
-
-def second_kernel(
-    core, right, own, other, lower, below, inv_high, inv_low, out, factor, under, high, low, pending, sems
-):
+        for b in range(high.shape[0])
+    ]
+
+
+def solve_kernel(first, core, chips, right, *refs):
+    dense = refs[: 0 if first else 2]
+    pieces = refs[len(dense) : len(dense) + 4]
+    inv_high, inv_low, out, factor, under, high, low, pending, sems, strip_sems = refs[len(dense) + 4 :]
     rows, slab = right.shape
     half = slab // 2
-
-    @pl.when(core[0] != 0)
+    inner = half // BLOCK
+    active = (core[0] == 0) if first else (core[0] != 0)
+
+    @pl.when(active)
     def _():
-        copies = solve_copies(lower, inv_high, inv_low, factor, high, low, sems)
-        belows = below_copies(below, under, sems)
-        for copy in belows:
-            copy.start()
-        for group in copies:
-            for copy in group:
-                copy.start()
-        pending[...] = right[...] - other[rows:, :]
-        for b, copy in enumerate(belows):
-            copy.wait()
-            cols = slice(half + b * BLOCK, half + (b + 1) * BLOCK)
-            term = dot_exact(other[:rows, cols], under[b * BLOCK : (b + 1) * BLOCK, :])
-            pending[...] = pending[...] - term
+        even, odd, below = strip_copies(chips, pieces, factor, under, strip_sems)
+        inverse = inverse_copies(inv_high, inv_low, high, low, sems)
+        order = [inverse[0], even, *inverse[1:], odd, below] if first else [below, *inverse, even, odd]
+        for copies in order:
+            start_all(copies)
+        if first:
+            pending[...] = right[...]
+        else:
+            own, other = dense
+            pending[...] = right[...] - other[rows:, :]
+            wait_for(under, strip_sems.at[2])
+            pending[...] = pending[...] - dot_exact(other[:rows, half:], under[...])
 
         def wait(b):
-            for copy in copies[b]:
+            for copy in inverse[b]:
                 copy.wait()
 
-        solve_block(slab // BLOCK, pending, factor, high, low, out, wait, lambda b, y: None)
-
-    @pl.when(core[0] == 0)
+        def after(b, y):
+            if first and b + 1 == inner:
+                wait_for(under, strip_sems.at[2])
+                out[rows:, :] = dot_exact(out[:rows, :half], under[...])
+
+        def before_update(b):
+            if b == 0:
+                wait_for(factor.at[:half], strip_sems.at[0])
+            if b == inner:
+                wait_for(factor.at[half:], strip_sems.at[1])
+
+        solve_block(slab // BLOCK, pending, factor, high, low, out, wait, before_update, after)
+
+    @pl.when(jnp.logical_not(active))
     def _():
-        out[...] = own[:rows, :]
-
-
-def solve_call(kernel, core, dense, factor, out_rows, name):
+        out[...] = jnp.zeros_like(out) if first else dense[0][:rows, :]
+
+
+def solve_call(first, core, chips, dense, pieces, inverses, name):
     rows, slab = dense[0].shape
     blocks = slab // BLOCK
     vmem = pl.BlockSpec(memory_space=pltpu.VMEM)
+    smem = pl.BlockSpec(memory_space=pltpu.SMEM)
     return pl.pallas_call(
-        kernel,
-        out_shape=jax.ShapeDtypeStruct((out_rows, slab), F32),
-        in_specs=[pl.BlockSpec(memory_space=pltpu.SMEM)]
-        + [vmem] * len(dense)
-        + [pl.BlockSpec(memory_space=pl.ANY)] * 4,
+        functools.partial(solve_kernel, first),
+        out_shape=jax.ShapeDtypeStruct((2 * rows if first else rows, slab), F32),
+        in_specs=[smem, smem] + [vmem] * len(dense) + [pl.BlockSpec(memory_space=pl.ANY)] * 6,
         out_specs=vmem,
         scratch_shapes=[
             pltpu.VMEM((slab, slab), BF16),
@@ -263,15 +239,17 @@
             pltpu.VMEM((blocks, BLOCK, BLOCK), BF16),
             pltpu.VMEM((blocks, BLOCK, BLOCK), BF16),
             pltpu.VMEM((rows, slab), F32),
-            pltpu.SemaphoreType.DMA((4, blocks)),
+            pltpu.SemaphoreType.DMA((2, blocks)),
+            pltpu.SemaphoreType.DMA((3,)),
         ],
-        compiler_params=pltpu.CompilerParams(vmem_limit_bytes=56 * MB),
+        compiler_params=pltpu.CompilerParams(vmem_limit_bytes=36 * MB),
         name=name,
-    )(core, *dense, *factor)
+    )(core, chips, *dense, *pieces, *inverses)
 
 
 def product_kernel(parts, half, order, left, right, _, *refs):
-    outs, (a, b, picked, a_sems, b_sems) = refs[: len(parts)], refs[len(parts) :]
+    outs, token, (a, b, picked, a_sems, b_sems) = refs[: len(parts)], refs[len(parts)], refs[len(parts) + 1 :]
+    token[...] = jnp.zeros_like(token)
     groups, _, depth = left.shape
     rows = picked.shape[0]
     slab = rows // 2
@@ -325,12 +303,14 @@
 def product(order, left, right, token, parts, half, name):
     groups, rows, depth = left.shape
     width = sum(part[2] for part in parts)
-    step = 512
+    step = parts[0][2]
     return pl.pallas_call(
         functools.partial(product_kernel, parts, half),
-        out_shape=[jax.ShapeDtypeStruct((rows // 2, part[2]), F32) for part in parts],
-        in_specs=[pl.BlockSpec(memory_space=pltpu.SMEM)] + [pl.BlockSpec(memory_space=pltpu.HBM)] * 3,
-        out_specs=[pl.BlockSpec(memory_space=pltpu.VMEM)] * len(parts),
+        out_shape=[jax.ShapeDtypeStruct((rows // 2, part[2]), F32) for part in parts] + [TOKEN],
+        in_specs=[pl.BlockSpec(memory_space=pltpu.SMEM)]
+        + [pl.BlockSpec(memory_space=pltpu.HBM)] * 2
+        + [pl.BlockSpec(memory_space=pltpu.VMEM)],
+        out_specs=[pl.BlockSpec(memory_space=pltpu.VMEM)] * (len(parts) + 1),
         scratch_shapes=[
             pltpu.VMEM((rows // 2, groups * depth), BF16),
             pltpu.VMEM((width // step, step, groups * depth), BF16),
@@ -376,17 +356,20 @@
     return (((at["z"] * SIDE + at["y"]) * SIDE + at["x"]).reshape(-1)).astype(jnp.int32)
 
 
-def pair_kernel(flags, strip, got, both):
+def pair_kernel(flags, strip, got, both, token):
+    token[...] = jnp.zeros_like(token)
     both[:STRIP] = strip[...]
     both[STRIP:] = jnp.where(flags[0] > 0, strip[...], got[...])
 
 
-def choose_kernel(flags, held, got, _, both):
+def choose_kernel(flags, held, got, _, both, token):
+    token[...] = jnp.zeros_like(token)
     both[:STRIP] = jnp.where(flags[1] > 0, held[:STRIP], got[:STRIP])
     both[STRIP:] = jnp.where(flags[2] > 0, held[STRIP:], got[STRIP:])
 
 
-def pack_kernel(flags, held, got, _, out_a, out_b, odd):
+def pack_kernel(flags, held, got, _, out_a, out_b, token, odd):
+    token[...] = jnp.zeros_like(token)
     mine = flags[3] > 0
     width = held.shape[1]
     cut = STRIP // 2
@@ -430,15 +413,62 @@
     tokens = () if token is None else (token,)
     return pl.pallas_call(
         kernel,
-        out_shape=[jax.ShapeDtypeStruct(shape, BF16) for shape in shapes],
+        out_shape=[jax.ShapeDtypeStruct(shape, BF16) for shape in shapes] + [TOKEN],
         in_specs=[pl.BlockSpec(memory_space=pltpu.SMEM)]
-        + [vmem] * len(operands)
-        + [pl.BlockSpec(memory_space=pl.ANY)] * len(tokens),
-        out_specs=[vmem] * len(shapes),
+        + [vmem] * (len(operands) + len(tokens)),
+        out_specs=[vmem] * (len(shapes) + 1),
         scratch_shapes=scratch,
         compiler_params=pltpu.CompilerParams(vmem_limit_bytes=16 * MB),
         name=name,
     )(flags, *operands, *tokens)
+
+
+def join_kernel(held_a, got_a, held_b, got_b, _, out_a, out_b, token, sems):
+    copies = []
+    for n, (held, got, out) in enumerate(((held_a, got_a, out_a), (held_b, got_b, out_b))):
+        rows = held.shape[0]
+        copies.append(pltpu.make_async_copy(held, out.at[pl.ds(0, rows)], sems.at[n, 0]))
+        copies.append(pltpu.make_async_copy(got, out.at[pl.ds(rows, rows)], sems.at[n, 1]))
+    start_all(copies)
+    token[...] = jnp.zeros_like(token)
+    for copy in copies:
+        copy.wait()
+
+
+def join(held, got, token):
+    rows, width = held[0].shape
+    shape = jax.ShapeDtypeStruct((2 * rows, width), BF16)
+    anywhere = pl.BlockSpec(memory_space=pl.ANY)
+    *joined, token = pl.pallas_call(
+        join_kernel,
+        out_shape=[shape, shape, TOKEN],
+        in_specs=[anywhere] * 4 + [pl.BlockSpec(memory_space=pltpu.VMEM)],
+        out_specs=[anywhere] * 2 + [pl.BlockSpec(memory_space=pltpu.VMEM)],
+        scratch_shapes=[pltpu.SemaphoreType.DMA((2, 2))],
+        compiler_params=pltpu.CompilerParams(vmem_limit_bytes=4 * MB),
+        name="join",
+    )(held[0], got[0], held[1], got[1], token)
+    return joined, token
+
+
+def add_kernel(keep, got, _, send, kept, token):
+    token[...] = jnp.zeros_like(token)
+    middle = send.shape[0]
+    send[...] = keep[:middle] + got[:middle]
+    kept[...] = keep[middle:] + got[middle:]
+
+
+def add(keep, got, token):
+    vmem = pl.BlockSpec(memory_space=pltpu.VMEM)
+    shape = jax.ShapeDtypeStruct((keep.shape[0] // 2, keep.shape[1]), F32)
+    return pl.pallas_call(
+        add_kernel,
+        out_shape=[shape, shape, TOKEN],
+        in_specs=[vmem] * 3,
+        out_specs=[vmem] * 3,
+        compiler_params=pltpu.CompilerParams(vmem_limit_bytes=16 * MB),
+        name="add",
+    )(keep, got, token)
 
 
 def gather_order(place, core):
@@ -473,17 +503,30 @@
     to_first = [
         (chip_index(0, y, x, 1), chip_index(0, y, x, 0)) for y in range(SIDE) for x in range(SIDE)
     ]
+    def half_product(n, half, token, name):
+        return product(order, hist_solution, hist_factor, token, parts[n : n + 1], half, name)
+
+    def gather_step(held, step):
+        return [
+            lax.ppermute(held[n], EVERY, partner_pairs(GATHER[n][step // 2], step % 2 == 1))
+            for n in range(2)
+        ]
+
+    def sum_step(n, send, step):
+        return lax.ppermute(send, EVERY, partner_pairs(PARTS[n][2][step // 2], step % 2 == 1))
+
     got = lax.ppermute(strip, EVERY, to_first)
-    (held,) = small_call(pair_kernel, "pair", [(2 * STRIP, width)], [], flags, strip, got)
+    held, token = small_call(pair_kernel, "pair", [(2 * STRIP, width)], [], flags, strip, got)
     got = lax.ppermute(held, EVERY, flip_pairs("z", (3, 3)))
-    (send0,) = product(order, hist_solution, hist_factor, held, parts[:1], 0, "send_first")
-    (held,) = small_call(
-        choose_kernel, "choose", [(2 * STRIP, width)], [], flags, held, got, token=send0
+    send0, token = half_product(0, 0, token, "send0")
+    held, token = small_call(
+        choose_kernel, "choose", [(2 * STRIP, width)], [], flags, held, got, token=token
     )
     got = lax.ppermute(held, EVERY, flip_pairs("z", (1, 1)))
-    (send1,) = product(order, hist_solution, hist_factor, held, parts[1:], 0, "send_rest")
+    come = [sum_step(0, send0, 0), None]
+    send1, token = half_product(1, 0, token, "send1")
     share = STRIP + STRIP // 2
-    held = small_call(
+    *held, token = small_call(
         pack_kernel,
         "pack",
         [(share, width)] * 2,
@@ -491,36 +534,40 @@
         flags,
         held,
         got,
-        token=send1,
+        token=token,
     )
-    sends = [send0, send1]
-    keeps = list(product(order, hist_solution, hist_factor, held[0], parts, 1, "keep_all"))
-
-    for step in range(4):
-        got = [
-            lax.ppermute(held[n], EVERY, partner_pairs(GATHER[n][step // 2], step % 2 == 1))
-            for n in range(2)
-        ]
-        if step < 3:
-            held = [jnp.concatenate([held[n], got[n]]) for n in range(2)]
-    factor = grow(chips, [held[0], got[0], held[1], got[1]], slab)
-
-    for step in range(6):
-        got = [
-            lax.ppermute(sends[n], EVERY, partner_pairs(PARTS[n][2][step // 2], step % 2 == 1))
-            for n in range(len(PARTS))
-        ]
-        if step == 5:
-            keeps = [keeps[n] + got[n] for n in range(len(PARTS))]
-        else:
-            middle = keeps[0].shape[0] // 2
-            sends = [keeps[n][:middle] + got[n][:middle] for n in range(len(PARTS))]
-            keeps = [keeps[n][middle:] + got[n][middle:] for n in range(len(PARTS))]
-    pending = samples.astype(F32) - jnp.concatenate(keeps, axis=1)
-
-    first = solve_call(first_kernel, core_arg, (pending,), factor, 2 * ROWS, "solve0")
+    come[1] = sum_step(1, send1, 0)
+    got = gather_step(held, 0)
+    held, token = join(held, got, token)
+    got = gather_step(held, 1)
+    keep0, token = half_product(0, 1, token, "keep0")
+    held, token = join(held, got, token)
+    got = gather_step(held, 2)
+    keep1, token = half_product(1, 1, token, "keep1")
+    send0, keep0, token = add(keep0, come[0], token)
+    come[0] = sum_step(0, send0, 1)
+    held, token = join(held, got, token)
+    got = gather_step(held, 3)
+    send1, keep1, token = add(keep1, come[1], token)
+    come[1] = sum_step(1, send1, 1)
+    pieces = [held[0], got[0], held[1], got[1]]
+    *inverses, token = grow(chips, pieces, slab)
+    keeps = [keep0, keep1]
+    for step in range(1, 5):
+        for n in range(2):
+            if step == 4:
+                send, keeps[n], _ = add(keeps[n], come[n], token)
+            else:
+                middle = keeps[n].shape[0] // 2
+                send = keeps[n][:middle] + come[n][:middle]
+                keeps[n] = keeps[n][middle:] + come[n][middle:]
+            come[n] = sum_step(n, send, step + 1)
+    history = jnp.concatenate([keeps[n] + come[n] for n in range(2)], axis=1)
+    pending = samples.astype(F32) - history
+
+    first = solve_call(True, core_arg, chips, (pending,), pieces, inverses, "solve0")
     other = lax.ppermute(first, "pcol", [(0, 1)])
-    return solve_call(second_kernel, core_arg, (pending, first, other), factor, ROWS, "solve1")
+    return solve_call(False, core_arg, chips, (pending, first, other), pieces, inverses, "solve1")
 
 
 def solution(mesh):

time: 196 us -> 274 us (1.40)
  Pallas kernels: 58.6 us -> 155 us
  waiting for transfers between devices: 86.3 us -> 78.6 us
  other arithmetic: 11.8 us -> 5.98 us
  local copies, waits for them, and re-layouts: 13.5 us -> 9.95 us
    pallas_call x3 -> x10, Pallas kernels: 22.2 us -> 115 us  [the longest x3 98.7 us: join(): pl.pallas_call(join_kernel, out_shape=[shape, shape, TOKEN], in_specs=[an...]
    ppermute x20, waiting for transfers between devices: 67 us -> 57.7 us  [the longest x12 42.4 us: sum_step(): lax.ppermute(send, EVERY, partner_pairs(PARTS[n][2][step // 2], step % 2...]
    add x12 -> x8, other arithmetic: 8.79 us -> 4.85 us  [the longest x4 4.78 us: per_device(): keeps[n] = keeps[n][middle:] + come[n][middle:]]
    pallas_call x3 -> x4, Pallas kernels: 33.6 us -> 37.5 us  [product(): pl.pallas_call(functools.partial(product_kernel, parts, half), out_shape=...]
    ppermute x1, waiting for transfers between devices: 0.03 us -> 2.9 us  [per_device(): got = lax.ppermute(held, EVERY, flip_pairs('z', (1, 1)))]
    unnamed x34 -> x36, local copies, waits for them, and re-layouts: 11.7 us -> 9.51 us
  transfers between devices with their start and end apart: 24 -> 24, of which waited for: 14 -> 16; matrix products, arithmetic and copies ran while one was open for 9% -> 2% of each run, Pallas kernels for 18% -> 53%
where the time goes in v5:
time: 274 us; the launch traced here: 273 us
  Pallas kernels  155 us (57%)
  waiting for transfers between devices  78.6 us (29%)
  starting transfers between devices  23 us (8%)
  local copies, waits for them, and re-layouts  9.95 us (4%)
  other arithmetic  5.98 us (2%)
    pallas_call x3, Pallas kernels, join(): pl.pallas_call(join_kernel, out_shape=[shape, shape, TOKEN], in_specs=[an...  98.7 us
    ppermute x12, waiting for transfers between devices, sum_step(): lax.ppermute(send, EVERY, partner_pairs(PARTS[n][2][step // 2], step % 2...  42.4 us
    pallas_call x4, Pallas kernels, product(): pl.pallas_call(functools.partial(product_kernel, parts, half), out_shape=...  37.5 us
    ppermute x8, waiting for transfers between devices, gather_step(): lax.ppermute(held[n], EVERY, partner_pairs(GATHER[n][step // 2], step % 2...  15.3 us
    ppermute x1, waiting for transfers between devices, per_device(): other = lax.ppermute(first, 'pcol', [(0, 1)])  13.9 us
    ppermute x8, starting transfers between devices, gather_step(): lax.ppermute(held[n], EVERY, partner_pairs(GATHER[n][step // 2], step % 2...  9.87 us
    unnamed x36, local copies, waits for them, and re-layouts  9.51 us
    ppermute x12, starting transfers between devices, sum_step(): lax.ppermute(send, EVERY, partner_pairs(PARTS[n][2][step // 2], step % 2...  7.56 us
  transfers between devices with their start and end apart: 24, of which 16 were waited for; matrix products, arithmetic and copies ran while one was open for 2% of the time, Pallas kernels for 53%

profile of v5, /device:TPU:1, one launch (start us, length us, event | category | flops | bytes accessed | tf_op | source)
XLA Modules:
  0.0 273.3 jit_solution(4163498483703810328)
XLA Ops:
  0.0 3.3 %collective-permute-start = (bf16[64,2048]{1,0:T(8,128)(2,1)}, bf16[64,2048]{1,0:T(8,128)(2,1)S(1)}, u32[]{:S(2)}, u32[]{:S(2)}) collective-permute-start(bf16[64,2048]{1,0:T(8,128)(2,1)} %bitcast.10), channel_id=1, source_target_pairs={{1,0},{3,2},{5,4},{7,6},{9,8},{11,10},{13,12},{15,14},{17,16},{19,... | collective-permute-start | bytes 786440 | tf_op jit(solution)/shard_map/ppermute | solution.py:518
  3.7 1.0 collective-permute-done.got
  4.7 0.9 copy-done.8
  5.6 0.6 pair.1
  6.2 0.6 copy-done.10
  6.8 0.9 collective-permute-start.1
  8.0 0.7 pad_add_fusion.3.order
  8.7 9.4 %send0.1 = (f32[512,1024]{1,0:T(8,128)}, f32[8,128]{1,0:T(8,128)}) custom-call(s32[128]{0:T(128)} %pad_add_fusion.3.order, bf16[3,1024,1024]{2,1,0:T(8,128)(2,1)} %left.7, bf16[3,2048,1024]{2,1,0:T(8,128)(2,1)} %right.7, f32[8,128]{1,0:T(8,128)} %copy-done.10), custom_call_target="tpu_custom_call" | custom-call | flops 3221225472 | bytes 11534336 | tf_op jit(solution)/shard_map/send0/pallas_call | solution.py:307
  18.0 3.1 %collective-permute-done.1.got = bf16[128,2048]{1,0:T(8,128)(2,1)S(1)} collective-permute-done((bf16[128,2048]{1,0:T(8,128)(2,1)S(1)}, bf16[128,2048]{1,0:T(8,128)(2,1)S(1)}, u32[]{:S(2)}, u32[]{:S(2)}) %collective-permute-start.1) | collective-permute-done | bytes 524320 | tf_op jit(solution)/shard_map/ppermute | solution.py:520
  21.2 0.7 copy-done.16
  21.8 0.6 choose.1
  22.5 0.6 copy-done.15
  23.0 9.3 %send1.1 = (f32[512,1024]{1,0:T(8,128)}, f32[8,128]{1,0:T(8,128)}) custom-call(s32[128]{0:T(128)} %pad_add_fusion.3.order, bf16[3,1024,1024]{2,1,0:T(8,128)(2,1)} %left.7, bf16[3,2048,1024]{2,1,0:T(8,128)(2,1)} %right.7, f32[8,128]{1,0:T(8,128)} %copy-done.15), custom_call_target="tpu_custom_call" | custom-call | flops 3221225472 | bytes 11534336 | tf_op jit(solution)/shard_map/send1/pallas_call | solution.py:307
  32.4 2.9 %collective-permute-done.2.got = bf16[128,2048]{1,0:T(8,128)(2,1)S(1)} collective-permute-done((bf16[128,2048]{1,0:T(8,128)(2,1)S(1)}, bf16[128,2048]{1,0:T(8,128)(2,1)S(1)}, u32[]{:S(2)}, u32[]{:S(2)}) %collective-permute-start.2) | collective-permute-done | bytes 524320 | tf_op jit(solution)/shard_map/ppermute | solution.py:525
  35.3 0.7 copy-done.14
  35.9 1.5 pack.1
  37.5 2.9 %collective-permute-start.3 = (bf16[96,2048]{1,0:T(8,128)(2,1)S(1)}, bf16[96,2048]{1,0:T(8,128)(2,1)S(1)}, u32[]{:S(2)}, u32[]{:S(2)}) collective-permute-start(bf16[96,2048]{1,0:T(8,128)(2,1)S(1)} %get-tuple-element.47.held_a), channel_id=1, source_target_pairs={{0,8},{1,25},{2,10},{3,27},{4,12},{5,29},{6,14},{7,31},{8,0},{9,17... | collective-permute-start | bytes 1179656 | tf_op jit(solution)/shard_map/ppermute | solution.py:511
  40.4 2.5 collective-permute-start.4
  42.9 2.7 collective-permute-done.3.got_a
  45.5 2.7 collective-permute-done.4.got_b
  48.2 0.8 join.3
  49.6 2.5 collective-permute-start.17
  52.2 9.4 %keep0.1 = (f32[512,1024]{1,0:T(8,128)}, f32[8,128]{1,0:T(8,128)}) custom-call(s32[128]{0:T(128)} %pad_add_fusion.3.order, bf16[3,1024,1024]{2,1,0:T(8,128)(2,1)} %left.7, bf16[3,2048,1024]{2,1,0:T(8,128)(2,1)} %right.7, f32[8,128]{1,0:T(8,128)} %copy-done.9), custom_call_target="tpu_custom_call" | custom-call | flops 3221225472 | bytes 11534336 | tf_op jit(solution)/shard_map/keep0/pallas_call | solution.py:307
  61.6 0.9 copy-done.4
  62.5 0.9 copy-done.6
  63.4 1.1 copy-done.5
  64.5 1.1 copy-done.7
  65.7 0.7 copy-done.12
  66.3 1.4 join.4
  67.7 0.6 copy-done.11
  68.3 2.3 collective-permute-start.12
  70.6 0.5 collective-permute-start.13
  71.0 9.5 %keep1.1 = (f32[512,1024]{1,0:T(8,128)}, f32[8,128]{1,0:T(8,128)}) custom-call(s32[128]{0:T(128)} %pad_add_fusion.3.order, bf16[3,1024,1024]{2,1,0:T(8,128)(2,1)} %left.7, bf16[3,2048,1024]{2,1,0:T(8,128)(2,1)} %right.7, f32[8,128]{1,0:T(8,128)} %copy-done.11), custom_call_target="tpu_custom_call" | custom-call | flops 3221225472 | bytes 11534336 | tf_op jit(solution)/shard_map/keep1/pallas_call | solution.py:307
  80.6 0.7 copy-done.13
  81.4 7.4 %collective-permute-done.12.got_a = bf16[384,2048]{1,0:T(8,128)(2,1)} collective-permute-done((bf16[384,2048]{1,0:T(8,128)(2,1)S(1)}, bf16[384,2048]{1,0:T(8,128)(2,1)}, u32[]{:S(2)}, u32[]{:S(2)}) %collective-permute-start.12) | collective-permute-done | bytes 1572896 | tf_op jit(solution)/shard_map/ppermute | solution.py:511
  88.9 2.5 collective-permute-done.13.got_b
  91.4 96.5 %join.5 = (bf16[768,2048]{1,0:T(8,128)(2,1)S(1)}, bf16[768,2048]{1,0:T(8,128)(2,1)}, f32[8,128]{1,0:T(8,128)S(1)}) custom-call(bf16[384,2048]{1,0:T(8,128)(2,1)S(1)} %copy-done.3, bf16[384,2048]{1,0:T(8,128)(2,1)} %collective-permute-done.12.got_a, bf16[384,2048]{1,0:T(8,128)(2,1)} %get-tuple-element.61.held_b, ...), custom_call_target="tpu_custom_call" | custom-call | tf_op jit(solution)/shard_map/join/pallas_call | solution.py:442
  187.9 0.8 collective-permute-start.14
  188.8 0.5 collective-permute-start.15
  189.2 0.8 add.238
  190.0 1.5 collective-permute-start.18
  191.5 11.8 %collective-permute-done.8 = f32[256,1024]{1,0:T(8,128)S(1)} collective-permute-done((f32[256,1024]{1,0:T(8,128)S(1)}, f32[256,1024]{1,0:T(8,128)S(1)}, u32[]{:S(2)}, u32[]{:S(2)}) %collective-permute-start.8) | collective-permute-done | bytes 1048608 | tf_op jit(solution)/shard_map/ppermute | solution.py:516
  203.3 1.1 slice_add_fusion.3
  204.4 0.6 collective-permute-start.9
  205.0 9.5 %collective-permute-done.18 = f32[256,1024]{1,0:T(8,128)S(1)} collective-permute-done((f32[256,1024]{1,0:T(8,128)S(1)}, f32[256,1024]{1,0:T(8,128)S(1)}, u32[]{:S(2)}, u32[]{:S(2)}) %collective-permute-start.18) | collective-permute-done | bytes 1048608 | tf_op jit(solution)/shard_map/ppermute | solution.py:516
  214.5 1.1 slice_add_fusion.1
  215.6 0.6 collective-permute-start.19
  216.5 3.4 %collective-permute-done.9 = f32[128,1024]{1,0:T(8,128)} collective-permute-done((f32[128,1024]{1,0:T(8,128)}, f32[128,1024]{1,0:T(8,128)}, u32[]{:S(2)}, u32[]{:S(2)}) %collective-permute-start.9) | collective-permute-done | bytes 524320 | tf_op jit(solution)/shard_map/ppermute | solution.py:516
  219.9 1.3 slice_add_fusion.7
  221.3 9.9 %collective-permute-done.19 = f32[128,1024]{1,0:T(8,128)} collective-permute-done((f32[128,1024]{1,0:T(8,128)}, f32[128,1024]{1,0:T(8,128)}, u32[]{:S(2)}, u32[]{:S(2)}) %collective-permute-start.19) | collective-permute-done | bytes 524320 | tf_op jit(solution)/shard_map/ppermute | solution.py:516
  231.2 1.3 slice_add_fusion.5
  232.6 1.3 collective-permute-done.10
  233.9 0.7 collective-permute-start.11
  234.6 3.4 %collective-permute-done.20 = f32[64,1024]{1,0:T(8,128)S(1)} collective-permute-done((f32[64,1024]{1,0:T(8,128)S(1)}, f32[64,1024]{1,0:T(8,128)S(1)}, u32[]{:S(2)}, u32[]{:S(2)}) %collective-permute-start.20) | collective-permute-done | bytes 262176 | tf_op jit(solution)/shard_map/ppermute | solution.py:516
  238.1 0.9 collective-permute-start.21
  239.0 7.3 %grow_inverse.1 = (bf16[4,512,512]{2,1,0:T(8,128)(2,1)S(1)}, bf16[4,512,512]{2,1,0:T(8,128)(2,1)S(1)}, f32[8,128]{1,0:T(8,128)S(1)}) custom-call(s32[32]{0:T(128)S(1)} %pad_add_fusion.1.chips, bf16[768,2048]{1,0:T(8,128)(2,1)S(1)} %get-tuple-element.63.own_a.refs_0_.refs_2_, bf16[768,2048]{1,0:T(8,128)(2,1)} %collective-permute-done.14.got_a.refs_1_.refs_3_, ...), custom_call_target="tpu_custom_call" | custom-call | flops 4000000000 | bytes 8388608 | tf_op jit(solution)/shard_map/grow_inverse/pallas_call | solution.py:145
  246.3 0.6 add.239
  247.3 0.6 add.237
  248.0 2.1 collective-permute-done.22
  250.0 1.0 collective-permute-done.16
  251.1 0.7 solve0.1.refs_0_
  251.8 1.3 collective-permute-start.23
  253.1 13.9 %collective-permute-done.23.refs_1_ = f32[32,2048]{1,0:T(8,128)S(1)} collective-permute-done((f32[32,2048]{1,0:T(8,128)S(1)}, f32[32,2048]{1,0:T(8,128)S(1)}, u32[]{:S(2)}, u32[]{:S(2)}) %collective-permute-start.23) | collective-permute-done | bytes 262176 | tf_op jit(solution)/shard_map/ppermute | solution.py:569
  267.0 6.1 %solve1.1 = f32[16,2048]{1,0:T(8,128)} custom-call(s32[1]{0:T(128)} %bitcast.core, s32[32]{0:T(128)S(1)} %pad_add_fusion.1.chips, f32[16,2048]{1,0:T(8,128)S(1)} %maximum_subtract_fusion.right, f32[32,2048]{1,0:T(8,128)S(1)} %solve0.1.refs_0_, f32[32,2048]{1,0:T(8,128)S(1)} %collective-permute-done.23.refs_1_, ...), custom_call_target="tpu_custom_call" | custom-call | tf_op jit(solution)/shard_map/solve1/pallas_call | solution.py:231
  (59 shorter events, 2.5 us)
Async XLA Ops:
  0.0 4.7 %collective-permute-start = (bf16[64,2048]{1,0:T(8,128)(2,1)}, bf16[64,2048]{1,0:T(8,128)(2,1)S(1)}, u32[]{:S(2)}, u32[]{:S(2)}) collective-permute-start(bf16[64,2048]{1,0:T(8,128)(2,1)} %bitcast.10), channel_id=1, source_target_pairs={{1,0},{3,2},{5,4},{7,6},{9,8},{11,10},{13,12},{15,14},{17,16},{19,... | collective-permute-start | bytes 786440 | tf_op jit(solution)/shard_map/ppermute | solution.py:518
  4.7 0.9 copy-start.8
  6.2 0.6 copy-start.10
  6.8 14.3 %collective-permute-start.1 = (bf16[128,2048]{1,0:T(8,128)(2,1)S(1)}, bf16[128,2048]{1,0:T(8,128)(2,1)S(1)}, u32[]{:S(2)}, u32[]{:S(2)}) collective-permute-start(bf16[128,2048]{1,0:T(8,128)(2,1)S(1)} %get-tuple-element.41.held), channel_id=1, source_target_pairs={{0,96},{1,97},{2,98},{3,99},{4,100},{5,101},{6,102},{7,103},{8,104... | collective-permute-start | bytes 1572872 | tf_op jit(solution)/shard_map/ppermute | solution.py:520
  21.2 0.7 copy-start.16
  22.4 0.6 copy-start.15
  23.0 12.2 %collective-permute-start.2 = (bf16[128,2048]{1,0:T(8,128)(2,1)S(1)}, bf16[128,2048]{1,0:T(8,128)(2,1)S(1)}, u32[]{:S(2)}, u32[]{:S(2)}) collective-permute-start(bf16[128,2048]{1,0:T(8,128)(2,1)S(1)} %get-tuple-element.44.held), channel_id=1, source_target_pairs={{0,32},{1,33},{2,34},{3,35},{4,36},{5,37},{6,38},{7,39},{8,40},{9,... | collective-permute-start | bytes 1572872 | tf_op jit(solution)/shard_map/ppermute | solution.py:525
  35.3 0.7 copy-start.14
  37.5 8.1 %collective-permute-start.3 = (bf16[96,2048]{1,0:T(8,128)(2,1)S(1)}, bf16[96,2048]{1,0:T(8,128)(2,1)S(1)}, u32[]{:S(2)}, u32[]{:S(2)}) collective-permute-start(bf16[96,2048]{1,0:T(8,128)(2,1)S(1)} %get-tuple-element.47.held_a), channel_id=1, source_target_pairs={{0,8},{1,25},{2,10},{3,27},{4,12},{5,29},{6,14},{7,31},{8,0},{9,17... | collective-permute-start | bytes 1179656 | tf_op jit(solution)/shard_map/ppermute | solution.py:511
  40.4 7.8 %collective-permute-start.4 = (bf16[96,2048]{1,0:T(8,128)(2,1)S(1)}, bf16[96,2048]{1,0:T(8,128)(2,1)S(1)}, u32[]{:S(2)}, u32[]{:S(2)}) collective-permute-start(bf16[96,2048]{1,0:T(8,128)(2,1)S(1)} %get-tuple-element.48.held_b), channel_id=1, source_target_pairs={{0,2},{1,7},{2,0},{3,5},{4,6},{5,3},{6,4},{7,1},{8,10},{9,15},{10,... | collective-permute-start | bytes 1179656 | tf_op jit(solution)/shard_map/ppermute | solution.py:511
  49.0 0.6 copy-start.9
  49.0 12.5 %collective-permute-start.6 = (bf16[192,2048]{1,0:T(8,128)(2,1)S(1)}, bf16[192,2048]{1,0:T(8,128)(2,1)S(1)}, u32[]{:S(2)}, u32[]{:S(2)}) collective-permute-start(bf16[192,2048]{1,0:T(8,128)(2,1)S(1)} %get-tuple-element.53.held_a), channel_id=1, source_target_pairs={{0,24},{1,9},{2,26},{3,11},{4,28},{5,13},{6,30},{7,15},{8,16},{9,1... | collective-permute-start | bytes 2359304 | tf_op jit(solution)/shard_map/ppermute | solution.py:511
  49.1 13.4 %collective-permute-start.7 = (bf16[192,2048]{1,0:T(8,128)(2,1)S(1)}, bf16[192,2048]{1,0:T(8,128)(2,1)S(1)}, u32[]{:S(2)}, u32[]{:S(2)}) collective-permute-start(bf16[192,2048]{1,0:T(8,128)(2,1)S(1)} %get-tuple-element.54.held_b), channel_id=1, source_target_pairs={{0,6},{1,3},{2,4},{3,1},{4,2},{5,7},{6,0},{7,5},{8,14},{9,11},{10,... | collective-permute-start | bytes 2359304 | tf_op jit(solution)/shard_map/ppermute | solution.py:511
  49.5 31.0 %collective-permute-start.5 = (f32[512,1024]{1,0:T(8,128)}, f32[512,1024]{1,0:T(8,128)S(1)}, u32[]{:S(2)}, u32[]{:S(2)}) collective-permute-start(f32[512,1024]{1,0:T(8,128)} %get-tuple-element.52), channel_id=1, source_target_pairs={{0,32},{1,97},{2,34},{3,99},{4,36},{5,101},{6,38},{7,103},{8,40},{... | collective-permute-start | bytes 6291464 | tf_op jit(solution)/shard_map/ppermute | solution.py:516
  49.6 139.6 %collective-permute-start.17 = (f32[512,1024]{1,0:T(8,128)}, f32[512,1024]{1,0:T(8,128)S(1)}, u32[]{:S(2)}, u32[]{:S(2)}) collective-permute-start(f32[512,1024]{1,0:T(8,128)} %get-tuple-element.69), channel_id=1, source_target_pairs={{0,32},{1,97},{2,34},{3,99},{4,36},{5,101},{6,38},{7,103},{8,40},{... | collective-permute-start | bytes 6291464 | tf_op jit(solution)/shard_map/ppermute | solution.py:516
  61.6 0.9 copy-start.4
  62.5 0.9 copy-start.6
  63.4 1.1 copy-start.5
  64.5 1.1 copy-start.7
  65.6 0.7 copy-start.12
  67.7 0.6 copy-start.11
  68.3 12.2 %copy-start.2 = (bf16[384,2048]{1,0:T(8,128)(2,1)}, bf16[384,2048]{1,0:T(8,128)(2,1)S(1)}, u32[]{:S(2)}) copy-start(bf16[384,2048]{1,0:T(8,128)(2,1)S(1)} %get-tuple-element.60.held_a) | copy-start | bytes 4718596
  68.3 20.6 %collective-permute-start.12 = (bf16[384,2048]{1,0:T(8,128)(2,1)S(1)}, bf16[384,2048]{1,0:T(8,128)(2,1)}, u32[]{:S(2)}, u32[]{:S(2)}) collective-permute-start(bf16[384,2048]{1,0:T(8,128)(2,1)S(1)} %get-tuple-element.60.held_a), channel_id=1, source_target_pairs={{0,2},{1,7},{2,0},{3,5},{4,6},{5,3},{6,4},{7,1},{8,10},{9,15},{10,... | collective-permute-start | bytes 4718600 | tf_op jit(solution)/shard_map/ppermute | solution.py:511
  70.6 20.8 %collective-permute-start.13 = (bf16[384,2048]{1,0:T(8,128)(2,1)}, bf16[384,2048]{1,0:T(8,128)(2,1)}, u32[]{:S(2)}, u32[]{:S(2)}) collective-permute-start(bf16[384,2048]{1,0:T(8,128)(2,1)} %get-tuple-element.61.held_b), channel_id=1, source_target_pairs={{0,8},{1,25},{2,10},{3,27},{4,12},{5,29},{6,14},{7,31},{8,0},{9,17... | collective-permute-start | bytes 4718600 | tf_op jit(solution)/shard_map/ppermute | solution.py:511
  71.0 9.5 %copy-start.1 = (f32[512,1024]{1,0:T(8,128)S(1)}, f32[512,1024]{1,0:T(8,128)}, u32[]{:S(2)}) copy-start(f32[512,1024]{1,0:T(8,128)} %get-tuple-element.51.keep) | copy-start | bytes 6291460
  80.6 0.7 copy-start.13
  81.2 10.1 %copy-start.3 = (bf16[384,2048]{1,0:T(8,128)(2,1)S(1)}, bf16[384,2048]{1,0:T(8,128)(2,1)}, u32[]{:S(2)}) copy-start(bf16[384,2048]{1,0:T(8,128)(2,1)} %copy-done.2) | copy-start | bytes 4718596
  91.4 97.9 %copy-start = (f32[512,1024]{1,0:T(8,128)S(1)}, f32[512,1024]{1,0:T(8,128)}, u32[]{:S(2)}) copy-start(f32[512,1024]{1,0:T(8,128)} %get-tuple-element.68.keep) | copy-start | bytes 6291460
  187.9 51.1 %collective-permute-start.14 = (bf16[768,2048]{1,0:T(8,128)(2,1)S(1)}, bf16[768,2048]{1,0:T(8,128)(2,1)}, u32[]{:S(2)}, u32[]{:S(2)}) collective-permute-start(bf16[768,2048]{1,0:T(8,128)(2,1)S(1)} %get-tuple-element.63.own_a.refs_0_.refs_2_), channel_id=1, source_target_pairs={{0,6},{1,3},{2,4},{3,1},{4,2},{5,7},{6,0},{7,5},{8,14},{9,11},{10,... | collective-permute-start | bytes 9437192 | tf_op jit(solution)/shard_map/ppermute | solution.py:511
  188.8 50.2 %collective-permute-start.15 = (bf16[768,2048]{1,0:T(8,128)(2,1)}, bf16[768,2048]{1,0:T(8,128)(2,1)}, u32[]{:S(2)}, u32[]{:S(2)}) collective-permute-start(bf16[768,2048]{1,0:T(8,128)(2,1)} %get-tuple-element.64.own_b.refs_2_.refs_4_), channel_id=1, source_target_pairs={{0,24},{1,9},{2,26},{3,11},{4,28},{5,13},{6,30},{7,15},{8,16},{9,1... | collective-permute-start | bytes 9437192 | tf_op jit(solution)/shard_map/ppermute | solution.py:511
  189.2 14.0 %collective-permute-start.8 = (f32[256,1024]{1,0:T(8,128)S(1)}, f32[256,1024]{1,0:T(8,128)S(1)}, u32[]{:S(2)}, u32[]{:S(2)}) collective-permute-start(f32[256,1024]{1,0:T(8,128)S(1)} %get-tuple-element.59), channel_id=1, source_target_pairs={{0,96},{1,33},{2,98},{3,35},{4,100},{5,37},{6,102},{7,39},{8,104},... | collective-permute-start | bytes 3145736 | tf_op jit(solution)/shard_map/ppermute | solution.py:516
  190.0 24.5 %collective-permute-start.18 = (f32[256,1024]{1,0:T(8,128)S(1)}, f32[256,1024]{1,0:T(8,128)S(1)}, u32[]{:S(2)}, u32[]{:S(2)}) collective-permute-start(f32[256,1024]{1,0:T(8,128)S(1)} %get-tuple-element.72), channel_id=1, source_target_pairs={{0,96},{1,33},{2,98},{3,35},{4,100},{5,37},{6,102},{7,39},{8,104},... | collective-permute-start | bytes 3145736 | tf_op jit(solution)/shard_map/ppermute | solution.py:516
  204.4 15.5 %collective-permute-start.9 = (f32[128,1024]{1,0:T(8,128)}, f32[128,1024]{1,0:T(8,128)}, u32[]{:S(2)}, u32[]{:S(2)}) collective-permute-start(f32[128,1024]{1,0:T(8,128)} %get-tuple-element.82), channel_id=1, source_target_pairs={{0,8},{1,25},{2,10},{3,27},{4,12},{5,29},{6,14},{7,31},{8,0},{9,17... | collective-permute-start | bytes 1572872 | tf_op jit(solution)/shard_map/ppermute | solution.py:516
  215.6 15.5 %collective-permute-start.19 = (f32[128,1024]{1,0:T(8,128)}, f32[128,1024]{1,0:T(8,128)}, u32[]{:S(2)}, u32[]{:S(2)}) collective-permute-start(f32[128,1024]{1,0:T(8,128)} %get-tuple-element.84), channel_id=1, source_target_pairs={{0,2},{1,7},{2,0},{3,5},{4,6},{5,3},{6,4},{7,1},{8,10},{9,15},{10,... | collective-permute-start | bytes 1572872 | tf_op jit(solution)/shard_map/ppermute | solution.py:516
  221.2 12.7 %collective-permute-start.10 = (f32[64,1024]{1,0:T(8,128)S(1)}, f32[64,1024]{1,0:T(8,128)S(1)}, u32[]{:S(2)}, u32[]{:S(2)}) collective-permute-start(f32[64,1024]{1,0:T(8,128)S(1)} %get-tuple-element.86), channel_id=1, source_target_pairs={{0,24},{1,9},{2,26},{3,11},{4,28},{5,13},{6,30},{7,15},{8,16},{9,1... | collective-permute-start | bytes 786440 | tf_op jit(solution)/shard_map/ppermute | solution.py:516
  232.4 5.6 %collective-permute-start.20 = (f32[64,1024]{1,0:T(8,128)S(1)}, f32[64,1024]{1,0:T(8,128)S(1)}, u32[]{:S(2)}, u32[]{:S(2)}) collective-permute-start(f32[64,1024]{1,0:T(8,128)S(1)} %get-tuple-element.88), channel_id=1, source_target_pairs={{0,6},{1,3},{2,4},{3,1},{4,2},{5,7},{6,0},{7,5},{8,14},{9,11},{10,... | collective-permute-start | bytes 786440 | tf_op jit(solution)/shard_map/ppermute | solution.py:516
  233.9 13.4 %collective-permute-start.11 = (f32[32,1024]{1,0:T(8,128)S(1)}, f32[32,1024]{1,0:T(8,128)S(1)}, u32[]{:S(2)}, u32[]{:S(2)}) collective-permute-start(f32[32,1024]{1,0:T(8,128)S(1)} %get-tuple-element.89), channel_id=1, source_target_pairs={{0,2},{1,7},{2,0},{3,5},{4,6},{5,3},{6,4},{7,1},{8,10},{9,15},{10,... | collective-permute-start | bytes 393224 | tf_op jit(solution)/shard_map/ppermute | solution.py:516
  238.1 13.0 %copy-start.17 = (bf16[16,2048]{1,0:T(8,128)(2,1)S(1)}, bf16[16,2048]{1,0:T(8,128)(2,1)}, u32[]{:S(2)}) copy-start(bf16[16,2048]{1,0:T(8,128)(2,1)} %param.7) | copy-start | bytes 196612
  238.1 8.2 %collective-permute-start.21 = (f32[32,1024]{1,0:T(8,128)S(1)}, f32[32,1024]{1,0:T(8,128)S(1)}, u32[]{:S(2)}, u32[]{:S(2)}) collective-permute-start(f32[32,1024]{1,0:T(8,128)S(1)} %get-tuple-element.91), channel_id=1, source_target_pairs={{0,8},{1,25},{2,10},{3,27},{4,12},{5,29},{6,14},{7,31},{8,0},{9,17... | collective-permute-start | bytes 393224 | tf_op jit(solution)/shard_map/ppermute | solution.py:516
  246.9 3.1 %collective-permute-start.22 = (f32[16,1024]{1,0:T(8,128)S(1)}, f32[16,1024]{1,0:T(8,128)S(1)}, u32[]{:S(2)}, u32[]{:S(2)}) collective-permute-start(f32[16,1024]{1,0:T(8,128)S(1)} %get-tuple-element.74), channel_id=1, source_target_pairs={{0,24},{1,9},{2,26},{3,11},{4,28},{5,13},{6,30},{7,15},{8,16},{9,1... | collective-permute-start | bytes 196616 | tf_op jit(solution)/shard_map/ppermute | solution.py:516
  248.0 3.1 %collective-permute-start.16 = (f32[16,1024]{1,0:T(8,128)S(1)}, f32[16,1024]{1,0:T(8,128)S(1)}, u32[]{:S(2)}, u32[]{:S(2)}) collective-permute-start(f32[16,1024]{1,0:T(8,128)S(1)} %get-tuple-element.67), channel_id=1, source_target_pairs={{0,6},{1,3},{2,4},{3,1},{4,2},{5,7},{6,0},{7,5},{8,14},{9,11},{10,... | collective-permute-start | bytes 196616 | tf_op jit(solution)/shard_map/ppermute | solution.py:516
  251.8 15.2 %collective-permute-start.23 = (f32[32,2048]{1,0:T(8,128)S(1)}, f32[32,2048]{1,0:T(8,128)S(1)}, u32[]{:S(2)}, u32[]{:S(2)}) collective-permute-start(f32[32,2048]{1,0:T(8,128)S(1)} %solve0.1.refs_0_), channel_id=1, source_target_pairs={{0,1},{2,3},{4,5},{6,7},{8,9},{10,11},{12,13},{14,15},{16,17},{18,... | collective-permute-start | bytes 786440 | tf_op jit(solution)/shard_map/ppermute | solution.py:569

commit v6 on v5

--- a/solution.py
+++ b/solution.py
@@ -90,7 +90,7 @@
     even, odd, _ = strip_copies(chips, (own_a, got_a, own_b, got_b), lower, None, sems)
     start_all(even)
     start_all(odd)
-    token[...] = jnp.zeros_like(token)
+    del token
     wait_for(lower.at[:half], sems.at[0])
     wait_for(lower.at[half:], sems.at[1])
 
@@ -146,7 +146,7 @@
         grow_kernel,
         out_shape=(inverse, inverse, TOKEN),
         in_specs=[pl.BlockSpec(memory_space=pltpu.SMEM)] + [pl.BlockSpec(memory_space=pl.ANY)] * 4,
-        out_specs=[vmem] * 3,
+        out_specs=[vmem] * 2 + [pl.BlockSpec(memory_space=pltpu.HBM)],
         scratch_shapes=[pltpu.VMEM((slab, slab), BF16), pltpu.SemaphoreType.DMA((2,))],
         compiler_params=pltpu.CompilerParams(vmem_limit_bytes=28 * MB),
         cost_estimate=pl.CostEstimate(flops=4 * 10**9, bytes_accessed=2 * slab * slab, transcendentals=0),
@@ -249,7 +249,7 @@
 
 def product_kernel(parts, half, order, left, right, _, *refs):
     outs, token, (a, b, picked, a_sems, b_sems) = refs[: len(parts)], refs[len(parts)], refs[len(parts) + 1 :]
-    token[...] = jnp.zeros_like(token)
+    del token
     groups, _, depth = left.shape
     rows = picked.shape[0]
     slab = rows // 2
@@ -308,9 +308,9 @@
         functools.partial(product_kernel, parts, half),
         out_shape=[jax.ShapeDtypeStruct((rows // 2, part[2]), F32) for part in parts] + [TOKEN],
         in_specs=[pl.BlockSpec(memory_space=pltpu.SMEM)]
-        + [pl.BlockSpec(memory_space=pltpu.HBM)] * 2
-        + [pl.BlockSpec(memory_space=pltpu.VMEM)],
-        out_specs=[pl.BlockSpec(memory_space=pltpu.VMEM)] * (len(parts) + 1),
+        + [pl.BlockSpec(memory_space=pltpu.HBM)] * 3,
+        out_specs=[pl.BlockSpec(memory_space=pltpu.VMEM)] * len(parts)
+        + [pl.BlockSpec(memory_space=pltpu.HBM)],
         scratch_shapes=[
             pltpu.VMEM((rows // 2, groups * depth), BF16),
             pltpu.VMEM((width // step, step, groups * depth), BF16),
@@ -318,7 +318,7 @@
             pltpu.SemaphoreType.DMA((2, groups)),
             pltpu.SemaphoreType.DMA((width // step, groups)),
         ],
-        compiler_params=pltpu.CompilerParams(vmem_limit_bytes=56 * MB),
+        compiler_params=pltpu.CompilerParams(vmem_limit_bytes=48 * MB),
         cost_estimate=pl.CostEstimate(
             flops=groups * rows * width * depth,
             bytes_accessed=2 * groups * (rows // 2 + width) * depth + 2 * rows * width,
@@ -357,19 +357,19 @@
 
 
 def pair_kernel(flags, strip, got, both, token):
-    token[...] = jnp.zeros_like(token)
+    del token
     both[:STRIP] = strip[...]
     both[STRIP:] = jnp.where(flags[0] > 0, strip[...], got[...])
 
 
 def choose_kernel(flags, held, got, _, both, token):
-    token[...] = jnp.zeros_like(token)
+    del token
     both[:STRIP] = jnp.where(flags[1] > 0, held[:STRIP], got[:STRIP])
     both[STRIP:] = jnp.where(flags[2] > 0, held[STRIP:], got[STRIP:])
 
 
 def pack_kernel(flags, held, got, _, out_a, out_b, token, odd):
-    token[...] = jnp.zeros_like(token)
+    del token
     mine = flags[3] > 0
     width = held.shape[1]
     cut = STRIP // 2
@@ -410,49 +410,60 @@
 
 def small_call(kernel, name, shapes, scratch, flags, *operands, token=None):
     vmem = pl.BlockSpec(memory_space=pltpu.VMEM)
+    hbm = pl.BlockSpec(memory_space=pltpu.HBM)
     tokens = () if token is None else (token,)
     return pl.pallas_call(
         kernel,
         out_shape=[jax.ShapeDtypeStruct(shape, BF16) for shape in shapes] + [TOKEN],
         in_specs=[pl.BlockSpec(memory_space=pltpu.SMEM)]
-        + [vmem] * (len(operands) + len(tokens)),
-        out_specs=[vmem] * (len(shapes) + 1),
+        + [vmem] * len(operands)
+        + [hbm] * len(tokens),
+        out_specs=[vmem] * len(shapes) + [hbm],
         scratch_shapes=scratch,
         compiler_params=pltpu.CompilerParams(vmem_limit_bytes=16 * MB),
         name=name,
     )(flags, *operands, *tokens)
 
 
-def join_kernel(held_a, got_a, held_b, got_b, _, out_a, out_b, token, sems):
-    copies = []
+def join_kernel(held_a, got_a, held_b, got_b, _, out_a, out_b, token, stage, in_sems, out_sems):
+    del token
+    loads, stores = [], []
     for n, (held, got, out) in enumerate(((held_a, got_a, out_a), (held_b, got_b, out_b))):
         rows = held.shape[0]
-        copies.append(pltpu.make_async_copy(held, out.at[pl.ds(0, rows)], sems.at[n, 0]))
-        copies.append(pltpu.make_async_copy(got, out.at[pl.ds(rows, rows)], sems.at[n, 1]))
-    start_all(copies)
-    token[...] = jnp.zeros_like(token)
-    for copy in copies:
-        copy.wait()
+        for h, source in enumerate((held, got)):
+            place = pl.ds(h * rows, rows)
+            loads.append(pltpu.make_async_copy(source, stage.at[n, place], in_sems.at[n, h]))
+            stores.append(pltpu.make_async_copy(stage.at[n, place], out.at[place], out_sems.at[n, h]))
+    start_all(loads)
+    for load, store in zip(loads, stores):
+        load.wait()
+        store.start()
+    for store in stores:
+        store.wait()
 
 
 def join(held, got, token):
     rows, width = held[0].shape
     shape = jax.ShapeDtypeStruct((2 * rows, width), BF16)
-    anywhere = pl.BlockSpec(memory_space=pl.ANY)
+    hbm = pl.BlockSpec(memory_space=pltpu.HBM)
     *joined, token = pl.pallas_call(
         join_kernel,
         out_shape=[shape, shape, TOKEN],
-        in_specs=[anywhere] * 4 + [pl.BlockSpec(memory_space=pltpu.VMEM)],
-        out_specs=[anywhere] * 2 + [pl.BlockSpec(memory_space=pltpu.VMEM)],
-        scratch_shapes=[pltpu.SemaphoreType.DMA((2, 2))],
-        compiler_params=pltpu.CompilerParams(vmem_limit_bytes=4 * MB),
+        in_specs=[pl.BlockSpec(memory_space=pl.ANY)] * 4 + [hbm],
+        out_specs=[hbm] * 3,
+        scratch_shapes=[
+            pltpu.VMEM((2, 2 * rows, width), BF16),
+            pltpu.SemaphoreType.DMA((2, 2)),
+            pltpu.SemaphoreType.DMA((2, 2)),
+        ],
+        compiler_params=pltpu.CompilerParams(vmem_limit_bytes=12 * MB),
         name="join",
     )(held[0], got[0], held[1], got[1], token)
     return joined, token
 
 
 def add_kernel(keep, got, _, send, kept, token):
-    token[...] = jnp.zeros_like(token)
+    del token
     middle = send.shape[0]
     send[...] = keep[:middle] + got[:middle]
     kept[...] = keep[middle:] + got[middle:]
@@ -460,12 +471,13 @@
 
 def add(keep, got, token):
     vmem = pl.BlockSpec(memory_space=pltpu.VMEM)
+    hbm = pl.BlockSpec(memory_space=pltpu.HBM)
     shape = jax.ShapeDtypeStruct((keep.shape[0] // 2, keep.shape[1]), F32)
     return pl.pallas_call(
         add_kernel,
         out_shape=[shape, shape, TOKEN],
-        in_specs=[vmem] * 3,
-        out_specs=[vmem] * 3,
+        in_specs=[vmem, vmem, hbm],
+        out_specs=[vmem, vmem, hbm],
         compiler_params=pltpu.CompilerParams(vmem_limit_bytes=16 * MB),
         name="add",
     )(keep, got, token)
@@ -524,7 +536,6 @@
     )
     got = lax.ppermute(held, EVERY, flip_pairs("z", (1, 1)))
     come = [sum_step(0, send0, 0), None]
-    send1, token = half_product(1, 0, token, "send1")
     share = STRIP + STRIP // 2
     *held, token = small_call(
         pack_kernel,
@@ -536,20 +547,21 @@
         got,
         token=token,
     )
+    got = gather_step(held, 0)
+    send1, token = half_product(1, 0, token, "send1")
     come[1] = sum_step(1, send1, 0)
-    got = gather_step(held, 0)
     held, token = join(held, got, token)
     got = gather_step(held, 1)
     keep0, token = half_product(0, 1, token, "keep0")
     held, token = join(held, got, token)
     got = gather_step(held, 2)
-    keep1, token = half_product(1, 1, token, "keep1")
     send0, keep0, token = add(keep0, come[0], token)
     come[0] = sum_step(0, send0, 1)
+    keep1, token = half_product(1, 1, token, "keep1")
+    send1, keep1, token = add(keep1, come[1], token)
+    come[1] = sum_step(1, send1, 1)
     held, token = join(held, got, token)
     got = gather_step(held, 3)
-    send1, keep1, token = add(keep1, come[1], token)
-    come[1] = sum_step(1, send1, 1)
     pieces = [held[0], got[0], held[1], got[1]]
     *inverses, token = grow(chips, pieces, slab)
     keeps = [keep0, keep1]

time: 274 us -> 175 us (0.64)
  Pallas kernels: 155 us -> 54.7 us
  waiting for transfers between devices: 78.6 us -> 90 us
  local copies, waits for them, and re-layouts: 9.95 us -> 3.32 us
    pallas_call x3, Pallas kernels: 98.7 us -> 4.43 us  [join(): pl.pallas_call(join_kernel, out_shape=[shape, shape, TOKEN], in_specs=[pl...]
    ppermute x12, waiting for transfers between devices: 42.4 us -> 57.9 us  [sum_step(): lax.ppermute(send, EVERY, partner_pairs(PARTS[n][2][step // 2], step % 2...]
    ppermute x8, waiting for transfers between devices: 15.3 us -> 0.49 us  [gather_step(): lax.ppermute(held[n], EVERY, partner_pairs(GATHER[n][step // 2], step % 2...]
    ppermute x1, waiting for transfers between devices: 2.9 us -> 12.2 us  [per_device(): got = lax.ppermute(held, EVERY, flip_pairs('z', (1, 1)))]
    unnamed x36 -> x12, local copies, waits for them, and re-layouts: 9.51 us -> 2.88 us
    pallas_call x4, Pallas kernels: 37.5 us -> 32.8 us  [product(): pl.pallas_call(functools.partial(product_kernel, parts, half), out_shape=...]
    ppermute x8, starting transfers between devices: 9.87 us -> 6.53 us  [gather_step(): lax.ppermute(held[n], EVERY, partner_pairs(GATHER[n][step // 2], step % 2...]
  transfers between devices with their start and end apart: 24 -> 24, of which waited for: 16 -> 16; matrix products, arithmetic and copies ran while one was open for 2% -> 3% of each run, Pallas kernels for 53% -> 24%
where the time goes in v6:
time: 175 us
  waiting for transfers between devices  90 us (51%)
  Pallas kernels  54.7 us (31%)
  starting transfers between devices  20.9 us (12%)
  other arithmetic  5.39 us (3%)
  local copies, waits for them, and re-layouts  3.32 us (2%)
    ppermute x12, waiting for transfers between devices, sum_step(): lax.ppermute(send, EVERY, partner_pairs(PARTS[n][2][step // 2], step % 2...  57.9 us
    pallas_call x4, Pallas kernels, product(): pl.pallas_call(functools.partial(product_kernel, parts, half), out_shape=...  32.8 us
    ppermute x1, waiting for transfers between devices, per_device(): other = lax.ppermute(first, 'pcol', [(0, 1)])  13.2 us
    ppermute x1, waiting for transfers between devices, per_device(): got = lax.ppermute(held, EVERY, flip_pairs('z', (1, 1)))  12.2 us
    ppermute x12, starting transfers between devices, sum_step(): lax.ppermute(send, EVERY, partner_pairs(PARTS[n][2][step // 2], step % 2...  8.64 us
    pallas_call x1, Pallas kernels, grow(): pl.pallas_call(grow_kernel, out_shape=(inverse, inverse, TOKEN), in_specs...  7.29 us
    pallas_call x2, Pallas kernels, solve_call(): pl.pallas_call(functools.partial(solve_kernel, first), out_shape=jax.Shap...  6.81 us
    ppermute x8, starting transfers between devices, gather_step(): lax.ppermute(held[n], EVERY, partner_pairs(GATHER[n][step // 2], step % 2...  6.53 us
  transfers between devices with their start and end apart: 24, of which 16 were waited for; matrix products, arithmetic and copies ran while one was open for 3% of the time, Pallas kernels for 24%

profile of v6, /device:TPU:1, one launch (start us, length us, event | category | flops | bytes accessed | tf_op | source)
XLA Modules:
  0.0 174.8 jit_solution(12082350366973419968)
XLA Ops:
  0.0 3.3 %collective-permute-start = (bf16[64,2048]{1,0:T(8,128)(2,1)}, bf16[64,2048]{1,0:T(8,128)(2,1)S(1)}, u32[]{:S(2)}, u32[]{:S(2)}) collective-permute-start(bf16[64,2048]{1,0:T(8,128)(2,1)} %bitcast.10), channel_id=1, source_target_pairs={{1,0},{3,2},{5,4},{7,6},{9,8},{11,10},{13,12},{15,14},{17,16},{19,... | collective-permute-start | bytes 786440 | tf_op jit(solution)/shard_map/ppermute | solution.py:530
  3.7 1.0 collective-permute-done.got
  4.7 0.9 copy-done.2
  5.6 0.6 pair.1
  6.2 1.0 collective-permute-start.1
  7.3 0.1 add.166
  7.4 0.1 add.170
  7.6 7.9 %send0.1 = (f32[512,1024]{1,0:T(8,128)S(1)}, f32[8,128]{1,0:T(8,128)S(1)}) custom-call(s32[128]{0:T(128)S(1)} %pad_add_fusion.3.order, bf16[3,1024,1024]{2,1,0:T(8,128)(2,1)} %left.7, bf16[3,2048,1024]{2,1,0:T(8,128)(2,1)} %right.7, f32[8,128]{1,0:T(8,128)S(1)} %get-tuple-element.42._), custom_call_target="tpu_custom_call" | custom-call | flops 3221225472 | bytes 11534336 | tf_op jit(solution)/shard_map/send0/pallas_call | solution.py:307
  15.4 5.2 %collective-permute-done.1.got = bf16[128,2048]{1,0:T(8,128)(2,1)S(1)} collective-permute-done((bf16[128,2048]{1,0:T(8,128)(2,1)S(1)}, bf16[128,2048]{1,0:T(8,128)(2,1)S(1)}, u32[]{:S(2)}, u32[]{:S(2)}) %collective-permute-start.1) | collective-permute-done | bytes 524320 | tf_op jit(solution)/shard_map/ppermute | solution.py:532
  20.6 0.6 choose.1
  21.2 0.1 collective-permute-start.2
  21.3 12.2 %collective-permute-done.2.got = bf16[128,2048]{1,0:T(8,128)(2,1)S(1)} collective-permute-done((bf16[128,2048]{1,0:T(8,128)(2,1)S(1)}, bf16[128,2048]{1,0:T(8,128)(2,1)S(1)}, u32[]{:S(2)}, u32[]{:S(2)}) %collective-permute-start.2) | collective-permute-done | bytes 524320 | tf_op jit(solution)/shard_map/ppermute | solution.py:537
  33.5 1.6 pack.1
  35.1 2.9 %collective-permute-start.3 = (bf16[96,2048]{1,0:T(8,128)(2,1)S(1)}, bf16[96,2048]{1,0:T(8,128)(2,1)S(1)}, u32[]{:S(2)}, u32[]{:S(2)}) collective-permute-start(bf16[96,2048]{1,0:T(8,128)(2,1)S(1)} %get-tuple-element.46.held_a), channel_id=1, source_target_pairs={{0,8},{1,25},{2,10},{3,27},{4,12},{5,29},{6,14},{7,31},{8,0},{9,17... | collective-permute-start | bytes 1179656 | tf_op jit(solution)/shard_map/ppermute | solution.py:523
  38.0 2.5 %collective-permute-start.4 = (bf16[96,2048]{1,0:T(8,128)(2,1)S(1)}, bf16[96,2048]{1,0:T(8,128)(2,1)S(1)}, u32[]{:S(2)}, u32[]{:S(2)}) collective-permute-start(bf16[96,2048]{1,0:T(8,128)(2,1)S(1)} %get-tuple-element.47.held_b), channel_id=1, source_target_pairs={{0,2},{1,7},{2,0},{3,5},{4,6},{5,3},{6,4},{7,1},{8,10},{9,15},{10,... | collective-permute-start | bytes 1179656 | tf_op jit(solution)/shard_map/ppermute | solution.py:523
  40.5 0.1 collective-permute-start.5
  40.6 9.2 %send1.1 = (f32[512,1024]{1,0:T(8,128)}, f32[8,128]{1,0:T(8,128)S(1)}) custom-call(s32[128]{0:T(128)S(1)} %pad_add_fusion.3.order, bf16[3,1024,1024]{2,1,0:T(8,128)(2,1)} %left.7, bf16[3,2048,1024]{2,1,0:T(8,128)(2,1)} %right.7, f32[8,128]{1,0:T(8,128)S(1)} %get-tuple-element.48._), custom_call_target="tpu_custom_call" | custom-call | flops 3221225472 | bytes 11534336 | tf_op jit(solution)/shard_map/send1/pallas_call | solution.py:307
  49.9 1.6 join.3
  51.4 0.1 collective-permute-start.6
  51.5 0.1 collective-permute-start.7
  51.6 2.8 %collective-permute-start.14 = (f32[512,1024]{1,0:T(8,128)}, f32[512,1024]{1,0:T(8,128)S(1)}, u32[]{:S(2)}, u32[]{:S(2)}) collective-permute-start(f32[512,1024]{1,0:T(8,128)} %get-tuple-element.63), channel_id=1, source_target_pairs={{0,32},{1,97},{2,34},{3,99},{4,36},{5,101},{6,38},{7,103},{8,40},{... | collective-permute-start | bytes 6291464 | tf_op jit(solution)/shard_map/ppermute | solution.py:528
  54.4 7.9 %keep0.1 = (f32[512,1024]{1,0:T(8,128)S(1)}, f32[8,128]{1,0:T(8,128)S(1)}) custom-call(s32[128]{0:T(128)S(1)} %pad_add_fusion.3.order, bf16[3,1024,1024]{2,1,0:T(8,128)(2,1)} %left.7, bf16[3,2048,1024]{2,1,0:T(8,128)(2,1)} %right.7, f32[8,128]{1,0:T(8,128)S(1)} %get-tuple-element.50._), custom_call_target="tpu_custom_call" | custom-call | flops 3221225472 | bytes 11534336 | tf_op jit(solution)/shard_map/keep0/pallas_call | solution.py:307
  62.3 0.4 collective-permute-done.6.got_a
  62.7 0.1 collective-permute-done.7.got_b
  62.8 0.5 join.4
  63.3 0.3 collective-permute-start.12
  63.5 0.5 collective-permute-start.13
  64.1 2.5 %collective-permute-done.5.got = f32[512,1024]{1,0:T(8,128)S(1)} collective-permute-done((f32[512,1024]{1,0:T(8,128)S(1)}, f32[512,1024]{1,0:T(8,128)S(1)}, u32[]{:S(2)}, u32[]{:S(2)}) %collective-permute-start.5) | collective-permute-done | bytes 2097184 | tf_op jit(solution)/shard_map/ppermute | solution.py:528
  66.6 0.3 add.236
  66.9 1.0 copy-done
  67.9 1.0 copy-done.3
  68.9 7.9 %keep1.1 = (f32[512,1024]{1,0:T(8,128)S(1)}, f32[8,128]{1,0:T(8,128)S(1)}) custom-call(s32[128]{0:T(128)S(1)} %pad_add_fusion.3.order, bf16[3,1024,1024]{2,1,0:T(8,128)(2,1)} %left.7, bf16[3,2048,1024]{2,1,0:T(8,128)(2,1)} %right.7, f32[8,128]{1,0:T(8,128)S(1)} %get-tuple-element.61._), custom_call_target="tpu_custom_call" | custom-call | flops 3221225472 | bytes 11534336 | tf_op jit(solution)/shard_map/keep1/pallas_call | solution.py:307
  76.7 12.3 %collective-permute-done.14.got = f32[512,1024]{1,0:T(8,128)S(1)} collective-permute-done((f32[512,1024]{1,0:T(8,128)}, f32[512,1024]{1,0:T(8,128)S(1)}, u32[]{:S(2)}, u32[]{:S(2)}) %collective-permute-start.14) | collective-permute-done | bytes 2097184 | tf_op jit(solution)/shard_map/ppermute | solution.py:528
  89.1 0.3 add.237
  89.4 2.4 %join.5 = (bf16[768,2048]{1,0:T(8,128)(2,1)S(1)}, bf16[768,2048]{1,0:T(8,128)(2,1)}, f32[8,128]{1,0:T(8,128)}) custom-call(bf16[384,2048]{1,0:T(8,128)(2,1)S(1)} %get-tuple-element.59.held_a, bf16[384,2048]{1,0:T(8,128)(2,1)S(1)} %collective-permute-done.12.got_a, bf16[384,2048]{1,0:T(8,128)(2,1)S(1)} %get-tuple-element.60.held_b, ...), custom_call_target="tpu_custom_call" | custom-call | tf_op jit(solution)/shard_map/join/pallas_call | solution.py:449
  91.8 0.1 collective-permute-start.15
  91.8 0.1 collective-permute-start.16
  92.0 0.1 collective-permute-start.8
  92.0 1.5 collective-permute-start.18
  93.5 12.6 %collective-permute-done.8 = f32[256,1024]{1,0:T(8,128)S(1)} collective-permute-done((f32[256,1024]{1,0:T(8,128)S(1)}, f32[256,1024]{1,0:T(8,128)S(1)}, u32[]{:S(2)}, u32[]{:S(2)}) %collective-permute-start.8) | collective-permute-done | bytes 1048608 | tf_op jit(solution)/shard_map/ppermute | solution.py:528
  106.1 1.1 slice_add_fusion.3
  107.2 0.5 collective-permute-start.9
  107.8 9.6 %collective-permute-done.18 = f32[256,1024]{1,0:T(8,128)S(1)} collective-permute-done((f32[256,1024]{1,0:T(8,128)S(1)}, f32[256,1024]{1,0:T(8,128)S(1)}, u32[]{:S(2)}, u32[]{:S(2)}) %collective-permute-start.18) | collective-permute-done | bytes 1048608 | tf_op jit(solution)/shard_map/ppermute | solution.py:528
  117.3 1.1 slice_add_fusion.1
  118.4 0.6 collective-permute-start.19
  119.3 3.5 %collective-permute-done.9 = f32[128,1024]{1,0:T(8,128)} collective-permute-done((f32[128,1024]{1,0:T(8,128)}, f32[128,1024]{1,0:T(8,128)}, u32[]{:S(2)}, u32[]{:S(2)}) %collective-permute-start.9) | collective-permute-done | bytes 524320 | tf_op jit(solution)/shard_map/ppermute | solution.py:528
  122.8 1.3 slice_add_fusion.7
  124.0 0.2 collective-permute-start.10
  124.3 9.7 %collective-permute-done.19 = f32[128,1024]{1,0:T(8,128)} collective-permute-done((f32[128,1024]{1,0:T(8,128)}, f32[128,1024]{1,0:T(8,128)}, u32[]{:S(2)}, u32[]{:S(2)}) %collective-permute-start.19) | collective-permute-done | bytes 524320 | tf_op jit(solution)/shard_map/ppermute | solution.py:528
  134.0 1.3 slice_add_fusion.5
  135.2 0.1 collective-permute-start.20
  135.4 1.6 collective-permute-done.10
  137.1 0.8 collective-permute-start.11
  137.9 2.9 %collective-permute-done.20 = f32[64,1024]{1,0:T(8,128)S(1)} collective-permute-done((f32[64,1024]{1,0:T(8,128)S(1)}, f32[64,1024]{1,0:T(8,128)S(1)}, u32[]{:S(2)}, u32[]{:S(2)}) %collective-permute-start.20) | collective-permute-done | bytes 262176 | tf_op jit(solution)/shard_map/ppermute | solution.py:528
  140.9 0.8 collective-permute-start.21
  141.7 7.3 %grow_inverse.1 = (bf16[4,512,512]{2,1,0:T(8,128)(2,1)S(1)}, bf16[4,512,512]{2,1,0:T(8,128)(2,1)S(1)}, f32[8,128]{1,0:T(8,128)S(1)}) custom-call(s32[32]{0:T(128)S(1)} %pad_add_fusion.1.chips, bf16[768,2048]{1,0:T(8,128)(2,1)S(1)} %get-tuple-element.66.own_a.refs_0_.refs_2_, bf16[768,2048]{1,0:T(8,128)(2,1)} %collective-permute-done.15.got_a.refs_1_.refs_3_, ...), custom_call_target="tpu_custom_call" | custom-call | flops 4000000000 | bytes 8388608 | tf_op jit(solution)/shard_map/grow_inverse/pallas_call | solution.py:145
  149.0 0.9 collective-permute-start.22
  150.0 0.1 collective-permute-start.17
  150.1 2.1 %collective-permute-done.22 = f32[16,1024]{1,0:T(8,128)S(1)} collective-permute-done((f32[16,1024]{1,0:T(8,128)S(1)}, f32[16,1024]{1,0:T(8,128)S(1)}, u32[]{:S(2)}, u32[]{:S(2)}) %collective-permute-start.22) | collective-permute-done | bytes 65568 | tf_op jit(solution)/shard_map/ppermute | solution.py:528
  152.2 1.0 collective-permute-done.17
  153.3 0.7 solve0.1.refs_0_
  153.9 1.3 collective-permute-start.23
  155.2 13.2 %collective-permute-done.23.refs_1_ = f32[32,2048]{1,0:T(8,128)S(1)} collective-permute-done((f32[32,2048]{1,0:T(8,128)S(1)}, f32[32,2048]{1,0:T(8,128)S(1)}, u32[]{:S(2)}, u32[]{:S(2)}) %collective-permute-start.23) | collective-permute-done | bytes 262176 | tf_op jit(solution)/shard_map/ppermute | solution.py:581
  168.5 6.1 %solve1.1 = f32[16,2048]{1,0:T(8,128)} custom-call(s32[1]{0:T(128)} %bitcast.core, s32[32]{0:T(128)S(1)} %pad_add_fusion.1.chips, f32[16,2048]{1,0:T(8,128)S(1)} %maximum_subtract_fusion.right, f32[32,2048]{1,0:T(8,128)S(1)} %solve0.1.refs_0_, f32[32,2048]{1,0:T(8,128)S(1)} %collective-permute-done.23.refs_1_, ...), custom_call_target="tpu_custom_call" | custom-call | tf_op jit(solution)/shard_map/solve1/pallas_call | solution.py:231
  (35 shorter events, 0.9 us)
Async XLA Ops:
  0.0 4.7 %collective-permute-start = (bf16[64,2048]{1,0:T(8,128)(2,1)}, bf16[64,2048]{1,0:T(8,128)(2,1)S(1)}, u32[]{:S(2)}, u32[]{:S(2)}) collective-permute-start(bf16[64,2048]{1,0:T(8,128)(2,1)} %bitcast.10), channel_id=1, source_target_pairs={{1,0},{3,2},{5,4},{7,6},{9,8},{11,10},{13,12},{15,14},{17,16},{19,... | collective-permute-start | bytes 786440 | tf_op jit(solution)/shard_map/ppermute | solution.py:530
  4.7 0.9 copy-start.2
  6.2 14.4 %collective-permute-start.1 = (bf16[128,2048]{1,0:T(8,128)(2,1)S(1)}, bf16[128,2048]{1,0:T(8,128)(2,1)S(1)}, u32[]{:S(2)}, u32[]{:S(2)}) collective-permute-start(bf16[128,2048]{1,0:T(8,128)(2,1)S(1)} %get-tuple-element.41.held), channel_id=1, source_target_pairs={{0,96},{1,97},{2,98},{3,99},{4,100},{5,101},{6,102},{7,103},{8,104... | collective-permute-start | bytes 1572872 | tf_op jit(solution)/shard_map/ppermute | solution.py:532
  21.2 12.3 %collective-permute-start.2 = (bf16[128,2048]{1,0:T(8,128)(2,1)S(1)}, bf16[128,2048]{1,0:T(8,128)(2,1)S(1)}, u32[]{:S(2)}, u32[]{:S(2)}) collective-permute-start(bf16[128,2048]{1,0:T(8,128)(2,1)S(1)} %get-tuple-element.44.held), channel_id=1, source_target_pairs={{0,32},{1,33},{2,34},{3,35},{4,36},{5,37},{6,38},{7,39},{8,40},{9,... | collective-permute-start | bytes 1572872 | tf_op jit(solution)/shard_map/ppermute | solution.py:537
  35.1 14.7 %collective-permute-start.3 = (bf16[96,2048]{1,0:T(8,128)(2,1)S(1)}, bf16[96,2048]{1,0:T(8,128)(2,1)S(1)}, u32[]{:S(2)}, u32[]{:S(2)}) collective-permute-start(bf16[96,2048]{1,0:T(8,128)(2,1)S(1)} %get-tuple-element.46.held_a), channel_id=1, source_target_pairs={{0,8},{1,25},{2,10},{3,27},{4,12},{5,29},{6,14},{7,31},{8,0},{9,17... | collective-permute-start | bytes 1179656 | tf_op jit(solution)/shard_map/ppermute | solution.py:523
  38.0 11.8 %collective-permute-start.4 = (bf16[96,2048]{1,0:T(8,128)(2,1)S(1)}, bf16[96,2048]{1,0:T(8,128)(2,1)S(1)}, u32[]{:S(2)}, u32[]{:S(2)}) collective-permute-start(bf16[96,2048]{1,0:T(8,128)(2,1)S(1)} %get-tuple-element.47.held_b), channel_id=1, source_target_pairs={{0,2},{1,7},{2,0},{3,5},{4,6},{5,3},{6,4},{7,1},{8,10},{9,15},{10,... | collective-permute-start | bytes 1179656 | tf_op jit(solution)/shard_map/ppermute | solution.py:523
  40.5 26.1 %collective-permute-start.5 = (f32[512,1024]{1,0:T(8,128)S(1)}, f32[512,1024]{1,0:T(8,128)S(1)}, u32[]{:S(2)}, u32[]{:S(2)}) collective-permute-start(f32[512,1024]{1,0:T(8,128)S(1)} %get-tuple-element.52), channel_id=1, source_target_pairs={{0,32},{1,97},{2,34},{3,99},{4,36},{5,101},{6,38},{7,103},{8,40},{... | collective-permute-start | bytes 6291464 | tf_op jit(solution)/shard_map/ppermute | solution.py:528
  51.4 11.2 %collective-permute-start.6 = (bf16[192,2048]{1,0:T(8,128)(2,1)S(1)}, bf16[192,2048]{1,0:T(8,128)(2,1)S(1)}, u32[]{:S(2)}, u32[]{:S(2)}) collective-permute-start(bf16[192,2048]{1,0:T(8,128)(2,1)S(1)} %get-tuple-element.53.held_a), channel_id=1, source_target_pairs={{0,24},{1,9},{2,26},{3,11},{4,28},{5,13},{6,30},{7,15},{8,16},{9,1... | collective-permute-start | bytes 2359304 | tf_op jit(solution)/shard_map/ppermute | solution.py:523
  51.5 11.2 %collective-permute-start.7 = (bf16[192,2048]{1,0:T(8,128)(2,1)S(1)}, bf16[192,2048]{1,0:T(8,128)(2,1)S(1)}, u32[]{:S(2)}, u32[]{:S(2)}) collective-permute-start(bf16[192,2048]{1,0:T(8,128)(2,1)S(1)} %get-tuple-element.54.held_b), channel_id=1, source_target_pairs={{0,6},{1,3},{2,4},{3,1},{4,2},{5,7},{6,0},{7,5},{8,14},{9,11},{10,... | collective-permute-start | bytes 2359304 | tf_op jit(solution)/shard_map/ppermute | solution.py:523
  51.6 37.4 %collective-permute-start.14 = (f32[512,1024]{1,0:T(8,128)}, f32[512,1024]{1,0:T(8,128)S(1)}, u32[]{:S(2)}, u32[]{:S(2)}) collective-permute-start(f32[512,1024]{1,0:T(8,128)} %get-tuple-element.63), channel_id=1, source_target_pairs={{0,32},{1,97},{2,34},{3,99},{4,36},{5,101},{6,38},{7,103},{8,40},{... | collective-permute-start | bytes 6291464 | tf_op jit(solution)/shard_map/ppermute | solution.py:528
  63.3 26.1 %collective-permute-start.12 = (bf16[384,2048]{1,0:T(8,128)(2,1)S(1)}, bf16[384,2048]{1,0:T(8,128)(2,1)S(1)}, u32[]{:S(2)}, u32[]{:S(2)}) collective-permute-start(bf16[384,2048]{1,0:T(8,128)(2,1)S(1)} %get-tuple-element.59.held_a), channel_id=1, source_target_pairs={{0,2},{1,7},{2,0},{3,5},{4,6},{5,3},{6,4},{7,1},{8,10},{9,15},{10,... | collective-permute-start | bytes 4718600 | tf_op jit(solution)/shard_map/ppermute | solution.py:523
  63.5 25.8 %collective-permute-start.13 = (bf16[384,2048]{1,0:T(8,128)(2,1)S(1)}, bf16[384,2048]{1,0:T(8,128)(2,1)S(1)}, u32[]{:S(2)}, u32[]{:S(2)}) collective-permute-start(bf16[384,2048]{1,0:T(8,128)(2,1)S(1)} %get-tuple-element.60.held_b), channel_id=1, source_target_pairs={{0,8},{1,25},{2,10},{3,27},{4,12},{5,29},{6,14},{7,31},{8,0},{9,17... | collective-permute-start | bytes 4718600 | tf_op jit(solution)/shard_map/ppermute | solution.py:523
  66.9 1.0 copy-start
  67.9 1.0 copy-start.3
  89.4 2.6 %copy-start.4 = (f32[256,1024]{1,0:T(8,128)S(1)}, f32[256,1024]{1,0:T(8,128)}, u32[]{:S(2)}) copy-start(f32[256,1024]{1,0:T(8,128)} %copy-done.3) | copy-start | bytes 3145732
  89.4 16.7 %copy-start.1 = (f32[256,1024]{1,0:T(8,128)S(1)}, f32[256,1024]{1,0:T(8,128)}, u32[]{:S(2)}) copy-start(f32[256,1024]{1,0:T(8,128)} %copy-done) | copy-start | bytes 3145732
  91.8 49.9 %collective-permute-start.15 = (bf16[768,2048]{1,0:T(8,128)(2,1)S(1)}, bf16[768,2048]{1,0:T(8,128)(2,1)}, u32[]{:S(2)}, u32[]{:S(2)}) collective-permute-start(bf16[768,2048]{1,0:T(8,128)(2,1)S(1)} %get-tuple-element.66.own_a.refs_0_.refs_2_), channel_id=1, source_target_pairs={{0,6},{1,3},{2,4},{3,1},{4,2},{5,7},{6,0},{7,5},{8,14},{9,11},{10,... | collective-permute-start | bytes 9437192 | tf_op jit(solution)/shard_map/ppermute | solution.py:523
  91.8 49.9 %collective-permute-start.16 = (bf16[768,2048]{1,0:T(8,128)(2,1)}, bf16[768,2048]{1,0:T(8,128)(2,1)}, u32[]{:S(2)}, u32[]{:S(2)}) collective-permute-start(bf16[768,2048]{1,0:T(8,128)(2,1)} %get-tuple-element.67.own_b.refs_2_.refs_4_), channel_id=1, source_target_pairs={{0,24},{1,9},{2,26},{3,11},{4,28},{5,13},{6,30},{7,15},{8,16},{9,1... | collective-permute-start | bytes 9437192 | tf_op jit(solution)/shard_map/ppermute | solution.py:523
  92.0 14.1 %collective-permute-start.8 = (f32[256,1024]{1,0:T(8,128)S(1)}, f32[256,1024]{1,0:T(8,128)S(1)}, u32[]{:S(2)}, u32[]{:S(2)}) collective-permute-start(f32[256,1024]{1,0:T(8,128)S(1)} %copy-done.4), channel_id=1, source_target_pairs={{0,96},{1,33},{2,98},{3,35},{4,100},{5,37},{6,102},{7,39},{8,104},... | collective-permute-start | bytes 3145736 | tf_op jit(solution)/shard_map/ppermute | solution.py:528
  92.0 25.3 %collective-permute-start.18 = (f32[256,1024]{1,0:T(8,128)S(1)}, f32[256,1024]{1,0:T(8,128)S(1)}, u32[]{:S(2)}, u32[]{:S(2)}) collective-permute-start(f32[256,1024]{1,0:T(8,128)S(1)} %get-tuple-element.72), channel_id=1, source_target_pairs={{0,96},{1,33},{2,98},{3,35},{4,100},{5,37},{6,102},{7,39},{8,104},... | collective-permute-start | bytes 3145736 | tf_op jit(solution)/shard_map/ppermute | solution.py:528
  107.2 15.5 %collective-permute-start.9 = (f32[128,1024]{1,0:T(8,128)}, f32[128,1024]{1,0:T(8,128)}, u32[]{:S(2)}, u32[]{:S(2)}) collective-permute-start(f32[128,1024]{1,0:T(8,128)} %get-tuple-element.82), channel_id=1, source_target_pairs={{0,8},{1,25},{2,10},{3,27},{4,12},{5,29},{6,14},{7,31},{8,0},{9,17... | collective-permute-start | bytes 1572872 | tf_op jit(solution)/shard_map/ppermute | solution.py:528
  118.4 15.5 %collective-permute-start.19 = (f32[128,1024]{1,0:T(8,128)}, f32[128,1024]{1,0:T(8,128)}, u32[]{:S(2)}, u32[]{:S(2)}) collective-permute-start(f32[128,1024]{1,0:T(8,128)} %get-tuple-element.84), channel_id=1, source_target_pairs={{0,2},{1,7},{2,0},{3,5},{4,6},{5,3},{6,4},{7,1},{8,10},{9,15},{10,... | collective-permute-start | bytes 1572872 | tf_op jit(solution)/shard_map/ppermute | solution.py:528
  124.0 13.1 %collective-permute-start.10 = (f32[64,1024]{1,0:T(8,128)S(1)}, f32[64,1024]{1,0:T(8,128)S(1)}, u32[]{:S(2)}, u32[]{:S(2)}) collective-permute-start(f32[64,1024]{1,0:T(8,128)S(1)} %get-tuple-element.86), channel_id=1, source_target_pairs={{0,24},{1,9},{2,26},{3,11},{4,28},{5,13},{6,30},{7,15},{8,16},{9,1... | collective-permute-start | bytes 786440 | tf_op jit(solution)/shard_map/ppermute | solution.py:528
  135.2 5.6 %collective-permute-start.20 = (f32[64,1024]{1,0:T(8,128)S(1)}, f32[64,1024]{1,0:T(8,128)S(1)}, u32[]{:S(2)}, u32[]{:S(2)}) collective-permute-start(f32[64,1024]{1,0:T(8,128)S(1)} %get-tuple-element.88), channel_id=1, source_target_pairs={{0,6},{1,3},{2,4},{3,1},{4,2},{5,7},{6,0},{7,5},{8,14},{9,11},{10,... | collective-permute-start | bytes 786440 | tf_op jit(solution)/shard_map/ppermute | solution.py:528
  137.1 12.9 %collective-permute-start.11 = (f32[32,1024]{1,0:T(8,128)S(1)}, f32[32,1024]{1,0:T(8,128)S(1)}, u32[]{:S(2)}, u32[]{:S(2)}) collective-permute-start(f32[32,1024]{1,0:T(8,128)S(1)} %get-tuple-element.89), channel_id=1, source_target_pairs={{0,2},{1,7},{2,0},{3,5},{4,6},{5,3},{6,4},{7,1},{8,10},{9,15},{10,... | collective-permute-start | bytes 393224 | tf_op jit(solution)/shard_map/ppermute | solution.py:528
  140.9 12.4 %copy-start.5 = (bf16[16,2048]{1,0:T(8,128)(2,1)S(1)}, bf16[16,2048]{1,0:T(8,128)(2,1)}, u32[]{:S(2)}) copy-start(bf16[16,2048]{1,0:T(8,128)(2,1)} %param.7) | copy-start | bytes 196612
  140.9 8.1 %collective-permute-start.21 = (f32[32,1024]{1,0:T(8,128)S(1)}, f32[32,1024]{1,0:T(8,128)S(1)}, u32[]{:S(2)}, u32[]{:S(2)}) collective-permute-start(f32[32,1024]{1,0:T(8,128)S(1)} %get-tuple-element.91), channel_id=1, source_target_pairs={{0,8},{1,25},{2,10},{3,27},{4,12},{5,29},{6,14},{7,31},{8,0},{9,17... | collective-permute-start | bytes 393224 | tf_op jit(solution)/shard_map/ppermute | solution.py:528
  149.0 3.2 %collective-permute-start.22 = (f32[16,1024]{1,0:T(8,128)S(1)}, f32[16,1024]{1,0:T(8,128)S(1)}, u32[]{:S(2)}, u32[]{:S(2)}) collective-permute-start(f32[16,1024]{1,0:T(8,128)S(1)} %get-tuple-element.74), channel_id=1, source_target_pairs={{0,24},{1,9},{2,26},{3,11},{4,28},{5,13},{6,30},{7,15},{8,16},{9,1... | collective-permute-start | bytes 196616 | tf_op jit(solution)/shard_map/ppermute | solution.py:528
  150.0 3.2 %collective-permute-start.17 = (f32[16,1024]{1,0:T(8,128)S(1)}, f32[16,1024]{1,0:T(8,128)S(1)}, u32[]{:S(2)}, u32[]{:S(2)}) collective-permute-start(f32[16,1024]{1,0:T(8,128)S(1)} %get-tuple-element.70), channel_id=1, source_target_pairs={{0,6},{1,3},{2,4},{3,1},{4,2},{5,7},{6,0},{7,5},{8,14},{9,11},{10,... | collective-permute-start | bytes 196616 | tf_op jit(solution)/shard_map/ppermute | solution.py:528
  153.9 14.5 %collective-permute-start.23 = (f32[32,2048]{1,0:T(8,128)S(1)}, f32[32,2048]{1,0:T(8,128)S(1)}, u32[]{:S(2)}, u32[]{:S(2)}) collective-permute-start(f32[32,2048]{1,0:T(8,128)S(1)} %solve0.1.refs_0_), channel_id=1, source_target_pairs={{0,1},{2,3},{4,5},{6,7},{8,9},{10,11},{12,13},{14,15},{16,17},{18,... | collective-permute-start | bytes 786440 | tf_op jit(solution)/shard_map/ppermute | solution.py:581

commit v7 on v6

--- a/solution.py
+++ b/solution.py
@@ -46,17 +46,18 @@
     return both[:rows] + both[rows:] + dot(high, b_low)
 
 
-def strip_copies(chips, pieces, lower, below, sems):
+def strip_copies(chips, pieces, lower, below, sems, spans):
     own_a, got_a, own_b, got_b = pieces
     half = lower.shape[0] // 2
     cut = STRIP // 2
     groups = ([], [], [])
 
     def add(group, source, start, count, target, to):
+        cols = pl.ds(*spans[group])
         groups[group].append(
             pltpu.make_async_copy(
-                source.at[pl.ds(start, count)],
-                target.at[pl.ds(pl.multiple_of(to, cut), count)],
+                source.at[pl.ds(start, count), cols],
+                target.at[pl.ds(pl.multiple_of(to, cut), count), cols],
                 sems.at[group],
             )
         )
@@ -87,7 +88,8 @@
 def grow_kernel(chips, own_a, got_a, own_b, got_b, out_high, out_low, token, lower, sems):
     slab = lower.shape[0]
     half = slab // 2
-    even, odd, _ = strip_copies(chips, (own_a, got_a, own_b, got_b), lower, None, sems)
+    spans = ((0, slab), (0, slab), (0, slab))
+    even, odd, _ = strip_copies(chips, (own_a, got_a, own_b, got_b), lower, None, sems, spans)
     start_all(even)
     start_all(odd)
     del token
@@ -188,7 +190,8 @@
 
     @pl.when(active)
     def _():
-        even, odd, below = strip_copies(chips, pieces, factor, under, strip_sems)
+        spans = ((BLOCK, slab - BLOCK), (half + BLOCK, half - BLOCK), (0, slab))
+        even, odd, below = strip_copies(chips, pieces, factor, under, strip_sems, spans)
         inverse = inverse_copies(inv_high, inv_low, high, low, sems)
         order = [inverse[0], even, *inverse[1:], odd, below] if first else [below, *inverse, even, odd]
         for copies in order:
@@ -212,9 +215,9 @@
 
         def before_update(b):
             if b == 0:
-                wait_for(factor.at[:half], strip_sems.at[0])
+                wait_for(factor.at[:half, BLOCK:], strip_sems.at[0])
             if b == inner:
-                wait_for(factor.at[half:], strip_sems.at[1])
+                wait_for(factor.at[half:, half + BLOCK :], strip_sems.at[1])
 
         solve_block(slab // BLOCK, pending, factor, high, low, out, wait, before_update, after)
 
@@ -356,27 +359,20 @@
     return (((at["z"] * SIDE + at["y"]) * SIDE + at["x"]).reshape(-1)).astype(jnp.int32)
 
 
-def pair_kernel(flags, strip, got, both, token):
-    del token
-    both[:STRIP] = strip[...]
-    both[STRIP:] = jnp.where(flags[0] > 0, strip[...], got[...])
-
-
-def choose_kernel(flags, held, got, _, both, token):
-    del token
-    both[:STRIP] = jnp.where(flags[1] > 0, held[:STRIP], got[:STRIP])
-    both[STRIP:] = jnp.where(flags[2] > 0, held[STRIP:], got[STRIP:])
-
-
-def pack_kernel(flags, held, got, _, out_a, out_b, token, odd):
+def choose_kernel(which, flags, held, got, *rest):
+    out = rest[-2]
+    out[...] = jnp.where(flags[which] > 0, held[...], got[...])
+
+
+def pack_kernel(flags, held, got, under, got_under, out_a, out_b, token, odd):
     del token
     mine = flags[3] > 0
     width = held.shape[1]
     cut = STRIP // 2
     even = out_a.at[:STRIP]
-    even[...] = jnp.where(mine, held[:STRIP], got[:STRIP])
-    odd[...] = jnp.where(mine, got[:STRIP], held[:STRIP])
-    out_b[cut:] = jnp.where(mine, held[STRIP:], got[STRIP:])
+    even[...] = jnp.where(mine, held[...], got[...])
+    odd[...] = jnp.where(mine, got[...], held[...])
+    out_b[cut:] = jnp.where(mine, under[...], got_under[...])
 
     at = pl.multiple_of(flags[4] * 128, 128)
     turn = flags[5] > 0
@@ -512,9 +508,18 @@
     strip = diag_factor.T
     width = strip.shape[1]
 
-    to_first = [
-        (chip_index(0, y, x, 1), chip_index(0, y, x, 0)) for y in range(SIDE) for x in range(SIDE)
-    ]
+    def along_z(*moves):
+        return [
+            (chip_index(start, y, x, c), chip_index(stop, y, x, d))
+            for start, c, stop, d in moves
+            for y in range(SIDE)
+            for x in range(SIDE)
+        ]
+
+    def choose(which, own, got, name, token=None):
+        kernel = functools.partial(choose_kernel, which)
+        return small_call(kernel, name, [(STRIP, width)], [], flags, own, got, token=token)
+
     def half_product(n, half, token, name):
         return product(order, hist_solution, hist_factor, token, parts[n : n + 1], half, name)
 
@@ -527,14 +532,17 @@
     def sum_step(n, send, step):
         return lax.ppermute(send, EVERY, partner_pairs(PARTS[n][2][step // 2], step % 2 == 1))
 
-    got = lax.ppermute(strip, EVERY, to_first)
-    held, token = small_call(pair_kernel, "pair", [(2 * STRIP, width)], [], flags, strip, got)
-    got = lax.ppermute(held, EVERY, flip_pairs("z", (3, 3)))
+    got = lax.ppermute(strip, EVERY, along_z((0, 0, 3, 0), (1, 0, 2, 0), (2, 1, 1, 1), (3, 1, 0, 1)))
+    got_under = lax.ppermute(strip, EVERY, along_z((0, 1, 0, 0)))
+    under, token = choose(0, strip, got_under, "below0")
+    got_under = lax.ppermute(under, EVERY, along_z((0, 0, 3, 0), (1, 1, 2, 1)))
+    mine, token = choose(1, strip, got, "strip1", token=token)
+    got = lax.ppermute(mine, EVERY, flip_pairs("z", (1, 1)))
     send0, token = half_product(0, 0, token, "send0")
-    held, token = small_call(
-        choose_kernel, "choose", [(2 * STRIP, width)], [], flags, held, got, token=token
+    under, token = choose(2, under, got_under, "below1", token=token)
+    got_under = lax.ppermute(
+        under, EVERY, along_z((0, 0, 1, 0), (3, 0, 2, 0), (1, 1, 0, 1), (2, 1, 3, 1))
     )
-    got = lax.ppermute(held, EVERY, flip_pairs("z", (1, 1)))
     come = [sum_step(0, send0, 0), None]
     share = STRIP + STRIP // 2
     *held, token = small_call(
@@ -543,9 +551,10 @@
         [(share, width)] * 2,
         [pltpu.VMEM((STRIP, width), BF16)],
         flags,
-        held,
+        mine,
         got,
-        token=token,
+        under,
+        got_under,
     )
     got = gather_step(held, 0)
     send1, token = half_product(1, 0, token, "send1")
@@ -555,13 +564,13 @@
     keep0, token = half_product(0, 1, token, "keep0")
     held, token = join(held, got, token)
     got = gather_step(held, 2)
+    keep1, token = half_product(1, 1, token, "keep1")
     send0, keep0, token = add(keep0, come[0], token)
     come[0] = sum_step(0, send0, 1)
-    keep1, token = half_product(1, 1, token, "keep1")
+    held, token = join(held, got, token)
+    got = gather_step(held, 3)
     send1, keep1, token = add(keep1, come[1], token)
     come[1] = sum_step(1, send1, 1)
-    held, token = join(held, got, token)
-    got = gather_step(held, 3)
     pieces = [held[0], got[0], held[1], got[1]]
     *inverses, token = grow(chips, pieces, slab)
     keeps = [keep0, keep1]

time: 175 us -> 180 us (1.029)
  starting transfers between devices: 20.9 us -> 22.9 us
    ppermute x3 -> x5, waiting for transfers between devices: 18.4 us -> 10.1 us  [the longest x1 5.81 us: per_device(): lax.ppermute(under, EVERY, along_z((0, 0, 1, 0), (3, 0, 2, 0), (1, 1, 0,...]
    ppermute x8, waiting for transfers between devices: 0.49 us -> 6.33 us  [gather_step(): lax.ppermute(held[n], EVERY, partner_pairs(GATHER[n][step // 2], step % 2...]
    ppermute x1, waiting for transfers between devices: 13.2 us -> 17.9 us  [per_device(): other = lax.ppermute(first, 'pcol', [(0, 1)])]
    ppermute x3 -> x5, starting transfers between devices: 4.42 us -> 6.68 us  [the longest x1 3.33 us: per_device(): got_under = lax.ppermute(strip, EVERY, along_z((0, 1, 0, 0)))]
  transfers between devices with their start and end apart: 24 -> 26, of which waited for: 16 -> 16; matrix products, arithmetic and copies ran while one was open for 3% -> 3% of each run, Pallas kernels for 24% -> 26%
where the time goes in v7:
time: 180 us
  waiting for transfers between devices  90.5 us (50%)
  Pallas kernels  56.4 us (31%)
  starting transfers between devices  22.9 us (13%)
  other arithmetic  5.45 us (3%)
  local copies, waits for them, and re-layouts  3.98 us (2%)
    ppermute x12, waiting for transfers between devices, sum_step(): lax.ppermute(send, EVERY, partner_pairs(PARTS[n][2][step // 2], step % 2...  56.2 us
    pallas_call x4, Pallas kernels, product(): pl.pallas_call(functools.partial(product_kernel, parts, half), out_shape=...  34.1 us
    ppermute x1, waiting for transfers between devices, per_device(): other = lax.ppermute(first, 'pcol', [(0, 1)])  17.9 us
    ppermute x8, starting transfers between devices, gather_step(): lax.ppermute(held[n], EVERY, partner_pairs(GATHER[n][step // 2], step % 2...  7.72 us
    pallas_call x1, Pallas kernels, grow(): pl.pallas_call(grow_kernel, out_shape=(inverse, inverse, TOKEN), in_specs...  7.29 us
    ppermute x12, starting transfers between devices, sum_step(): lax.ppermute(send, EVERY, partner_pairs(PARTS[n][2][step // 2], step % 2...  7.17 us
    pallas_call x2, Pallas kernels, solve_call(): pl.pallas_call(functools.partial(solve_kernel, first), out_shape=jax.Shap...  6.81 us
    ppermute x8, waiting for transfers between devices, gather_step(): lax.ppermute(held[n], EVERY, partner_pairs(GATHER[n][step // 2], step % 2...  6.33 us
  transfers between devices with their start and end apart: 26, of which 16 were waited for; matrix products, arithmetic and copies ran while one was open for 3% of the time, Pallas kernels for 26%

profile of v7, /device:TPU:1, one launch (start us, length us, event | category | flops | bytes accessed | tf_op | source)
XLA Modules:
  0.0 179.8 jit_solution(8459150502953815414)
XLA Ops:
  0.0 3.3 %collective-permute-start.1 = (bf16[64,2048]{1,0:T(8,128)(2,1)}, bf16[64,2048]{1,0:T(8,128)(2,1)S(1)}, u32[]{:S(2)}, u32[]{:S(2)}) collective-permute-start(bf16[64,2048]{1,0:T(8,128)(2,1)} %bitcast.10), channel_id=1, source_target_pairs={{1,0},{3,2},{5,4},{7,6},{9,8},{11,10},{13,12},{15,14},{17,16},{19,... | collective-permute-start | bytes 786440 | tf_op jit(solution)/shard_map/ppermute | solution.py:536
  3.3 1.3 collective-permute-start
  5.0 0.1 add.166
  5.1 0.1 add.170
  5.2 0.1 stack.64.flags
  5.4 1.0 copy-done.2
  6.3 0.6 below0.1
  6.9 0.7 collective-permute-start.3
  7.6 4.3 %collective-permute-done.got = bf16[64,2048]{1,0:T(8,128)(2,1)S(1)} collective-permute-done((bf16[64,2048]{1,0:T(8,128)(2,1)}, bf16[64,2048]{1,0:T(8,128)(2,1)S(1)}, u32[]{:S(2)}, u32[]{:S(2)}) %collective-permute-start) | collective-permute-done | bytes 262176 | tf_op jit(solution)/shard_map/ppermute | solution.py:535
  11.9 0.6 strip1.1
  12.5 0.1 collective-permute-start.2
  12.6 9.2 %send0.1 = (f32[512,1024]{1,0:T(8,128)}, f32[8,128]{1,0:T(8,128)S(1)}) custom-call(s32[128]{0:T(128)S(1)} %pad_add_fusion.3.order, bf16[3,1024,1024]{2,1,0:T(8,128)(2,1)} %left.7, bf16[3,2048,1024]{2,1,0:T(8,128)(2,1)} %right.7, f32[8,128]{1,0:T(8,128)S(1)} %get-tuple-element.45._), custom_call_target="tpu_custom_call" | custom-call | flops 3221225472 | bytes 11534336 | tf_op jit(solution)/shard_map/send0/pallas_call | solution.py:310
  21.8 0.6 below1.1
  22.3 1.3 collective-permute-start.4
  23.7 5.8 %collective-permute-done.4.got_under = bf16[64,2048]{1,0:T(8,128)(2,1)S(1)} collective-permute-done((bf16[64,2048]{1,0:T(8,128)(2,1)S(1)}, bf16[64,2048]{1,0:T(8,128)(2,1)S(1)}, u32[]{:S(2)}, u32[]{:S(2)}) %collective-permute-start.4) | collective-permute-done | bytes 262176 | tf_op jit(solution)/shard_map/ppermute | solution.py:543
  29.5 1.5 pack.1
  31.0 2.9 %collective-permute-start.5 = (bf16[96,2048]{1,0:T(8,128)(2,1)S(1)}, bf16[96,2048]{1,0:T(8,128)(2,1)S(1)}, u32[]{:S(2)}, u32[]{:S(2)}) collective-permute-start(bf16[96,2048]{1,0:T(8,128)(2,1)S(1)} %get-tuple-element.48.held_a), channel_id=1, source_target_pairs={{0,8},{1,25},{2,10},{3,27},{4,12},{5,29},{6,14},{7,31},{8,0},{9,17... | collective-permute-start | bytes 1179656 | tf_op jit(solution)/shard_map/ppermute | solution.py:528
  33.9 2.5 %collective-permute-start.6 = (bf16[96,2048]{1,0:T(8,128)(2,1)S(1)}, bf16[96,2048]{1,0:T(8,128)(2,1)S(1)}, u32[]{:S(2)}, u32[]{:S(2)}) collective-permute-start(bf16[96,2048]{1,0:T(8,128)(2,1)S(1)} %get-tuple-element.49.held_b), channel_id=1, source_target_pairs={{0,2},{1,7},{2,0},{3,5},{4,6},{5,3},{6,4},{7,1},{8,10},{9,15},{10,... | collective-permute-start | bytes 1179656 | tf_op jit(solution)/shard_map/ppermute | solution.py:528
  36.4 9.2 %send1.1 = (f32[512,1024]{1,0:T(8,128)}, f32[8,128]{1,0:T(8,128)S(1)}) custom-call(s32[128]{0:T(128)S(1)} %pad_add_fusion.3.order, bf16[3,1024,1024]{2,1,0:T(8,128)(2,1)} %left.7, bf16[3,2048,1024]{2,1,0:T(8,128)(2,1)} %right.7, f32[8,128]{1,0:T(8,128)S(1)} %get-tuple-element.50._), custom_call_target="tpu_custom_call" | custom-call | flops 3221225472 | bytes 11534336 | tf_op jit(solution)/shard_map/send1/pallas_call | solution.py:310
  45.6 1.6 join.3
  47.1 0.1 collective-permute-start.8
  47.2 0.1 collective-permute-start.9
  47.3 0.1 collective-permute-start.7
  47.4 2.7 %collective-permute-start.19 = (f32[512,1024]{1,0:T(8,128)}, f32[512,1024]{1,0:T(8,128)S(1)}, u32[]{:S(2)}, u32[]{:S(2)}) collective-permute-start(f32[512,1024]{1,0:T(8,128)} %get-tuple-element.71), channel_id=1, source_target_pairs={{0,32},{1,97},{2,34},{3,99},{4,36},{5,101},{6,38},{7,103},{8,40},{... | collective-permute-start | bytes 6291464 | tf_op jit(solution)/shard_map/ppermute | solution.py:533
  50.1 7.9 %keep0.1 = (f32[512,1024]{1,0:T(8,128)S(1)}, f32[8,128]{1,0:T(8,128)S(1)}) custom-call(s32[128]{0:T(128)S(1)} %pad_add_fusion.3.order, bf16[3,1024,1024]{2,1,0:T(8,128)(2,1)} %left.7, bf16[3,2048,1024]{2,1,0:T(8,128)(2,1)} %right.7, f32[8,128]{1,0:T(8,128)S(1)} %get-tuple-element.52._), custom_call_target="tpu_custom_call" | custom-call | flops 3221225472 | bytes 11534336 | tf_op jit(solution)/shard_map/keep0/pallas_call | solution.py:310
  58.0 0.4 collective-permute-done.8.got_a
  58.4 0.1 collective-permute-done.9.got_b
  58.5 0.5 join.4
  59.0 0.3 collective-permute-start.14
  59.3 0.5 collective-permute-start.15
  59.8 7.9 %keep1.1 = (f32[512,1024]{1,0:T(8,128)S(1)}, f32[8,128]{1,0:T(8,128)S(1)}) custom-call(s32[128]{0:T(128)S(1)} %pad_add_fusion.3.order, bf16[3,1024,1024]{2,1,0:T(8,128)(2,1)} %left.7, bf16[3,2048,1024]{2,1,0:T(8,128)(2,1)} %right.7, f32[8,128]{1,0:T(8,128)S(1)} %get-tuple-element.58._), custom_call_target="tpu_custom_call" | custom-call | flops 3221225472 | bytes 11534336 | tf_op jit(solution)/shard_map/keep1/pallas_call | solution.py:310
  67.7 6.0 %collective-permute-done.7.got = f32[512,1024]{1,0:T(8,128)S(1)} collective-permute-done((f32[512,1024]{1,0:T(8,128)}, f32[512,1024]{1,0:T(8,128)S(1)}, u32[]{:S(2)}, u32[]{:S(2)}) %collective-permute-start.7) | collective-permute-done | bytes 2097184 | tf_op jit(solution)/shard_map/ppermute | solution.py:533
  73.7 0.2 add.236
  73.9 5.6 %collective-permute-done.14.got_a = bf16[384,2048]{1,0:T(8,128)(2,1)S(1)} collective-permute-done((bf16[384,2048]{1,0:T(8,128)(2,1)S(1)}, bf16[384,2048]{1,0:T(8,128)(2,1)S(1)}, u32[]{:S(2)}, u32[]{:S(2)}) %collective-permute-start.14) | collective-permute-done | bytes 1572896 | tf_op jit(solution)/shard_map/ppermute | solution.py:528
  79.5 0.2 collective-permute-done.15.got_b
  79.8 1.2 copy-done
  80.9 1.4 copy-done.1
  82.3 2.3 %join.5 = (bf16[768,2048]{1,0:T(8,128)(2,1)S(1)}, bf16[768,2048]{1,0:T(8,128)(2,1)}, f32[8,128]{1,0:T(8,128)S(1)}) custom-call(bf16[384,2048]{1,0:T(8,128)(2,1)S(1)} %get-tuple-element.62.held_a, bf16[384,2048]{1,0:T(8,128)(2,1)S(1)} %collective-permute-done.14.got_a, bf16[384,2048]{1,0:T(8,128)(2,1)S(1)} %get-tuple-element.63.held_b, ...), custom_call_target="tpu_custom_call" | custom-call | tf_op jit(solution)/shard_map/join/pallas_call | solution.py:445
  84.7 0.8 collective-permute-start.16
  85.5 0.5 collective-permute-start.17
  86.0 10.6 %collective-permute-done.19.got = f32[512,1024]{1,0:T(8,128)S(1)} collective-permute-done((f32[512,1024]{1,0:T(8,128)}, f32[512,1024]{1,0:T(8,128)S(1)}, u32[]{:S(2)}, u32[]{:S(2)}) %collective-permute-start.19) | collective-permute-done | bytes 2097184 | tf_op jit(solution)/shard_map/ppermute | solution.py:533
  96.6 0.3 add.238
  96.9 0.1 collective-permute-start.20
  97.0 13.5 %collective-permute-done.10 = f32[256,1024]{1,0:T(8,128)S(1)} collective-permute-done((f32[256,1024]{1,0:T(8,128)S(1)}, f32[256,1024]{1,0:T(8,128)S(1)}, u32[]{:S(2)}, u32[]{:S(2)}) %collective-permute-start.10) | collective-permute-done | bytes 1048608 | tf_op jit(solution)/shard_map/ppermute | solution.py:533
  110.5 1.2 slice_add_fusion.3
  111.7 0.8 collective-permute-start.11
  112.5 9.3 %collective-permute-done.20 = f32[256,1024]{1,0:T(8,128)S(1)} collective-permute-done((f32[256,1024]{1,0:T(8,128)S(1)}, f32[256,1024]{1,0:T(8,128)S(1)}, u32[]{:S(2)}, u32[]{:S(2)}) %collective-permute-start.20) | collective-permute-done | bytes 1048608 | tf_op jit(solution)/shard_map/ppermute | solution.py:533
  121.8 1.1 slice_add_fusion.1
  122.9 0.9 collective-permute-start.21
  124.0 3.2 %collective-permute-done.11 = f32[128,1024]{1,0:T(8,128)} collective-permute-done((f32[128,1024]{1,0:T(8,128)}, f32[128,1024]{1,0:T(8,128)}, u32[]{:S(2)}, u32[]{:S(2)}) %collective-permute-start.11) | collective-permute-done | bytes 524320 | tf_op jit(solution)/shard_map/ppermute | solution.py:533
  127.2 1.3 slice_add_fusion.7
  128.5 0.1 collective-permute-start.12
  128.6 4.2 %collective-permute-done.21 = f32[128,1024]{1,0:T(8,128)} collective-permute-done((f32[128,1024]{1,0:T(8,128)}, f32[128,1024]{1,0:T(8,128)}, u32[]{:S(2)}, u32[]{:S(2)}) %collective-permute-start.21) | collective-permute-done | bytes 524320 | tf_op jit(solution)/shard_map/ppermute | solution.py:533
  132.7 1.3 slice_add_fusion.5
  134.2 1.0 collective-permute-start.13
  135.2 6.3 %collective-permute-done.22 = f32[64,1024]{1,0:T(8,128)S(1)} collective-permute-done((f32[64,1024]{1,0:T(8,128)S(1)}, f32[64,1024]{1,0:T(8,128)S(1)}, u32[]{:S(2)}, u32[]{:S(2)}) %collective-permute-start.22) | collective-permute-done | bytes 262176 | tf_op jit(solution)/shard_map/ppermute | solution.py:533
  141.5 1.4 collective-permute-start.23
  142.9 7.3 %grow_inverse.1 = (bf16[4,512,512]{2,1,0:T(8,128)(2,1)S(1)}, bf16[4,512,512]{2,1,0:T(8,128)(2,1)S(1)}, f32[8,128]{1,0:T(8,128)S(1)}) custom-call(s32[32]{0:T(128)S(1)} %pad_add_fusion.1.chips, bf16[768,2048]{1,0:T(8,128)(2,1)S(1)} %get-tuple-element.65.own_a.refs_0_.refs_2_, bf16[768,2048]{1,0:T(8,128)(2,1)} %collective-permute-done.16.got_a.refs_1_.refs_3_, ...), custom_call_target="tpu_custom_call" | custom-call | flops 4000000000 | bytes 8388608 | tf_op jit(solution)/shard_map/grow_inverse/pallas_call | solution.py:147
  150.4 3.0 %collective-permute-done.24 = f32[16,1024]{1,0:T(8,128)S(1)} collective-permute-done((f32[16,1024]{1,0:T(8,128)S(1)}, f32[16,1024]{1,0:T(8,128)S(1)}, u32[]{:S(2)}, u32[]{:S(2)}) %collective-permute-start.24) | collective-permute-done | bytes 65568 | tf_op jit(solution)/shard_map/ppermute | solution.py:533
  153.4 0.1 collective-permute-done.18
  153.6 0.7 solve0.1.refs_0_
  154.3 1.3 collective-permute-start.25
  155.6 17.9 %collective-permute-done.25.refs_1_ = f32[32,2048]{1,0:T(8,128)S(1)} collective-permute-done((f32[32,2048]{1,0:T(8,128)S(1)}, f32[32,2048]{1,0:T(8,128)S(1)}, u32[]{:S(2)}, u32[]{:S(2)}) %collective-permute-start.25) | collective-permute-done | bytes 262176 | tf_op jit(solution)/shard_map/ppermute | solution.py:590
  173.4 6.1 %solve1.1 = f32[16,2048]{1,0:T(8,128)} custom-call(s32[1]{0:T(128)} %bitcast.core, s32[32]{0:T(128)S(1)} %pad_add_fusion.1.chips, f32[16,2048]{1,0:T(8,128)S(1)} %maximum_subtract_fusion.right, f32[32,2048]{1,0:T(8,128)S(1)} %solve0.1.refs_0_, f32[32,2048]{1,0:T(8,128)S(1)} %collective-permute-done.25.refs_1_, ...), custom_call_target="tpu_custom_call" | custom-call | tf_op jit(solution)/shard_map/solve1/pallas_call | solution.py:234
  (36 shorter events, 1.1 us)
Async XLA Ops:
  0.0 5.4 %collective-permute-start.1 = (bf16[64,2048]{1,0:T(8,128)(2,1)}, bf16[64,2048]{1,0:T(8,128)(2,1)S(1)}, u32[]{:S(2)}, u32[]{:S(2)}) collective-permute-start(bf16[64,2048]{1,0:T(8,128)(2,1)} %bitcast.10), channel_id=1, source_target_pairs={{1,0},{3,2},{5,4},{7,6},{9,8},{11,10},{13,12},{15,14},{17,16},{19,... | collective-permute-start | bytes 786440 | tf_op jit(solution)/shard_map/ppermute | solution.py:536
  3.3 8.5 %collective-permute-start = (bf16[64,2048]{1,0:T(8,128)(2,1)}, bf16[64,2048]{1,0:T(8,128)(2,1)S(1)}, u32[]{:S(2)}, u32[]{:S(2)}) collective-permute-start(bf16[64,2048]{1,0:T(8,128)(2,1)} %bitcast.11), channel_id=1, source_target_pairs={{0,96},{2,98},{4,100},{6,102},{8,104},{10,106},{12,108},{14,110},{... | collective-permute-start | bytes 786440 | tf_op jit(solution)/shard_map/ppermute | solution.py:535
  5.4 1.0 copy-start.2
  6.9 14.9 %collective-permute-start.3 = (bf16[64,2048]{1,0:T(8,128)(2,1)S(1)}, bf16[64,2048]{1,0:T(8,128)(2,1)S(1)}, u32[]{:S(2)}, u32[]{:S(2)}) collective-permute-start(bf16[64,2048]{1,0:T(8,128)(2,1)S(1)} %get-tuple-element.44.held), channel_id=1, source_target_pairs={{0,96},{2,98},{4,100},{6,102},{8,104},{10,106},{12,108},{14,110},{... | collective-permute-start | bytes 786440 | tf_op jit(solution)/shard_map/ppermute | solution.py:538
  12.5 11.2 %collective-permute-start.2 = (bf16[64,2048]{1,0:T(8,128)(2,1)S(1)}, bf16[64,2048]{1,0:T(8,128)(2,1)S(1)}, u32[]{:S(2)}, u32[]{:S(2)}) collective-permute-start(bf16[64,2048]{1,0:T(8,128)(2,1)S(1)} %get-tuple-element.43.held), channel_id=1, source_target_pairs={{0,32},{1,33},{2,34},{3,35},{4,36},{5,37},{6,38},{7,39},{8,40},{9,... | collective-permute-start | bytes 786440 | tf_op jit(solution)/shard_map/ppermute | solution.py:540
  22.3 7.1 %collective-permute-start.4 = (bf16[64,2048]{1,0:T(8,128)(2,1)S(1)}, bf16[64,2048]{1,0:T(8,128)(2,1)S(1)}, u32[]{:S(2)}, u32[]{:S(2)}) collective-permute-start(bf16[64,2048]{1,0:T(8,128)(2,1)S(1)} %get-tuple-element.47.under), channel_id=1, source_target_pairs={{0,32},{2,34},{4,36},{6,38},{8,40},{10,42},{12,44},{14,46},{16,48}... | collective-permute-start | bytes 786440 | tf_op jit(solution)/shard_map/ppermute | solution.py:543
  31.0 14.5 %collective-permute-start.5 = (bf16[96,2048]{1,0:T(8,128)(2,1)S(1)}, bf16[96,2048]{1,0:T(8,128)(2,1)S(1)}, u32[]{:S(2)}, u32[]{:S(2)}) collective-permute-start(bf16[96,2048]{1,0:T(8,128)(2,1)S(1)} %get-tuple-element.48.held_a), channel_id=1, source_target_pairs={{0,8},{1,25},{2,10},{3,27},{4,12},{5,29},{6,14},{7,31},{8,0},{9,17... | collective-permute-start | bytes 1179656 | tf_op jit(solution)/shard_map/ppermute | solution.py:528
  33.9 11.7 %collective-permute-start.6 = (bf16[96,2048]{1,0:T(8,128)(2,1)S(1)}, bf16[96,2048]{1,0:T(8,128)(2,1)S(1)}, u32[]{:S(2)}, u32[]{:S(2)}) collective-permute-start(bf16[96,2048]{1,0:T(8,128)(2,1)S(1)} %get-tuple-element.49.held_b), channel_id=1, source_target_pairs={{0,2},{1,7},{2,0},{3,5},{4,6},{5,3},{6,4},{7,1},{8,10},{9,15},{10,... | collective-permute-start | bytes 1179656 | tf_op jit(solution)/shard_map/ppermute | solution.py:528
  47.1 11.2 %collective-permute-start.8 = (bf16[192,2048]{1,0:T(8,128)(2,1)S(1)}, bf16[192,2048]{1,0:T(8,128)(2,1)S(1)}, u32[]{:S(2)}, u32[]{:S(2)}) collective-permute-start(bf16[192,2048]{1,0:T(8,128)(2,1)S(1)} %get-tuple-element.55.held_a), channel_id=1, source_target_pairs={{0,24},{1,9},{2,26},{3,11},{4,28},{5,13},{6,30},{7,15},{8,16},{9,1... | collective-permute-start | bytes 2359304 | tf_op jit(solution)/shard_map/ppermute | solution.py:528
  47.2 11.2 %collective-permute-start.9 = (bf16[192,2048]{1,0:T(8,128)(2,1)S(1)}, bf16[192,2048]{1,0:T(8,128)(2,1)S(1)}, u32[]{:S(2)}, u32[]{:S(2)}) collective-permute-start(bf16[192,2048]{1,0:T(8,128)(2,1)S(1)} %get-tuple-element.56.held_b), channel_id=1, source_target_pairs={{0,6},{1,3},{2,4},{3,1},{4,2},{5,7},{6,0},{7,5},{8,14},{9,11},{10,... | collective-permute-start | bytes 2359304 | tf_op jit(solution)/shard_map/ppermute | solution.py:528
  47.3 26.4 %collective-permute-start.7 = (f32[512,1024]{1,0:T(8,128)}, f32[512,1024]{1,0:T(8,128)S(1)}, u32[]{:S(2)}, u32[]{:S(2)}) collective-permute-start(f32[512,1024]{1,0:T(8,128)} %get-tuple-element.54), channel_id=1, source_target_pairs={{0,32},{1,97},{2,34},{3,99},{4,36},{5,101},{6,38},{7,103},{8,40},{... | collective-permute-start | bytes 6291464 | tf_op jit(solution)/shard_map/ppermute | solution.py:533
  47.4 49.2 %collective-permute-start.19 = (f32[512,1024]{1,0:T(8,128)}, f32[512,1024]{1,0:T(8,128)S(1)}, u32[]{:S(2)}, u32[]{:S(2)}) collective-permute-start(f32[512,1024]{1,0:T(8,128)} %get-tuple-element.71), channel_id=1, source_target_pairs={{0,32},{1,97},{2,34},{3,99},{4,36},{5,101},{6,38},{7,103},{8,40},{... | collective-permute-start | bytes 6291464 | tf_op jit(solution)/shard_map/ppermute | solution.py:533
  59.0 20.6 %collective-permute-start.14 = (bf16[384,2048]{1,0:T(8,128)(2,1)S(1)}, bf16[384,2048]{1,0:T(8,128)(2,1)S(1)}, u32[]{:S(2)}, u32[]{:S(2)}) collective-permute-start(bf16[384,2048]{1,0:T(8,128)(2,1)S(1)} %get-tuple-element.62.held_a), channel_id=1, source_target_pairs={{0,2},{1,7},{2,0},{3,5},{4,6},{5,3},{6,4},{7,1},{8,10},{9,15},{10,... | collective-permute-start | bytes 4718600 | tf_op jit(solution)/shard_map/ppermute | solution.py:528
  59.3 20.5 %collective-permute-start.15 = (bf16[384,2048]{1,0:T(8,128)(2,1)S(1)}, bf16[384,2048]{1,0:T(8,128)(2,1)S(1)}, u32[]{:S(2)}, u32[]{:S(2)}) collective-permute-start(bf16[384,2048]{1,0:T(8,128)(2,1)S(1)} %get-tuple-element.63.held_b), channel_id=1, source_target_pairs={{0,8},{1,25},{2,10},{3,27},{4,12},{5,29},{6,14},{7,31},{8,0},{9,17... | collective-permute-start | bytes 4718600 | tf_op jit(solution)/shard_map/ppermute | solution.py:528
  79.8 1.2 copy-start
  80.9 1.4 copy-start.1
  84.7 58.2 %collective-permute-start.16 = (bf16[768,2048]{1,0:T(8,128)(2,1)S(1)}, bf16[768,2048]{1,0:T(8,128)(2,1)}, u32[]{:S(2)}, u32[]{:S(2)}) collective-permute-start(bf16[768,2048]{1,0:T(8,128)(2,1)S(1)} %get-tuple-element.65.own_a.refs_0_.refs_2_), channel_id=1, source_target_pairs={{0,6},{1,3},{2,4},{3,1},{4,2},{5,7},{6,0},{7,5},{8,14},{9,11},{10,... | collective-permute-start | bytes 9437192 | tf_op jit(solution)/shard_map/ppermute | solution.py:528
  85.5 57.4 %collective-permute-start.17 = (bf16[768,2048]{1,0:T(8,128)(2,1)}, bf16[768,2048]{1,0:T(8,128)(2,1)}, u32[]{:S(2)}, u32[]{:S(2)}) collective-permute-start(bf16[768,2048]{1,0:T(8,128)(2,1)} %get-tuple-element.66.own_b.refs_2_.refs_4_), channel_id=1, source_target_pairs={{0,24},{1,9},{2,26},{3,11},{4,28},{5,13},{6,30},{7,15},{8,16},{9,1... | collective-permute-start | bytes 9437192 | tf_op jit(solution)/shard_map/ppermute | solution.py:528
  86.0 24.5 %collective-permute-start.10 = (f32[256,1024]{1,0:T(8,128)S(1)}, f32[256,1024]{1,0:T(8,128)S(1)}, u32[]{:S(2)}, u32[]{:S(2)}) collective-permute-start(f32[256,1024]{1,0:T(8,128)S(1)} %get-tuple-element.61), channel_id=1, source_target_pairs={{0,96},{1,33},{2,98},{3,35},{4,100},{5,37},{6,102},{7,39},{8,104},... | collective-permute-start | bytes 3145736 | tf_op jit(solution)/shard_map/ppermute | solution.py:533
  96.9 24.9 %collective-permute-start.20 = (f32[256,1024]{1,0:T(8,128)S(1)}, f32[256,1024]{1,0:T(8,128)S(1)}, u32[]{:S(2)}, u32[]{:S(2)}) collective-permute-start(f32[256,1024]{1,0:T(8,128)S(1)} %get-tuple-element.74), channel_id=1, source_target_pairs={{0,96},{1,33},{2,98},{3,35},{4,100},{5,37},{6,102},{7,39},{8,104},... | collective-permute-start | bytes 3145736 | tf_op jit(solution)/shard_map/ppermute | solution.py:533
  111.7 15.5 %collective-permute-start.11 = (f32[128,1024]{1,0:T(8,128)}, f32[128,1024]{1,0:T(8,128)}, u32[]{:S(2)}, u32[]{:S(2)}) collective-permute-start(f32[128,1024]{1,0:T(8,128)} %get-tuple-element.84), channel_id=1, source_target_pairs={{0,8},{1,25},{2,10},{3,27},{4,12},{5,29},{6,14},{7,31},{8,0},{9,17... | collective-permute-start | bytes 1572872 | tf_op jit(solution)/shard_map/ppermute | solution.py:533
  122.9 9.9 %collective-permute-start.21 = (f32[128,1024]{1,0:T(8,128)}, f32[128,1024]{1,0:T(8,128)}, u32[]{:S(2)}, u32[]{:S(2)}) collective-permute-start(f32[128,1024]{1,0:T(8,128)} %get-tuple-element.86), channel_id=1, source_target_pairs={{0,2},{1,7},{2,0},{3,5},{4,6},{5,3},{6,4},{7,1},{8,10},{9,15},{10,... | collective-permute-start | bytes 1572872 | tf_op jit(solution)/shard_map/ppermute | solution.py:533
  128.5 5.7 %collective-permute-start.12 = (f32[64,1024]{1,0:T(8,128)S(1)}, f32[64,1024]{1,0:T(8,128)S(1)}, u32[]{:S(2)}, u32[]{:S(2)}) collective-permute-start(f32[64,1024]{1,0:T(8,128)S(1)} %get-tuple-element.88), channel_id=1, source_target_pairs={{0,24},{1,9},{2,26},{3,11},{4,28},{5,13},{6,30},{7,15},{8,16},{9,1... | collective-permute-start | bytes 786440 | tf_op jit(solution)/shard_map/ppermute | solution.py:533
  134.0 7.5 %collective-permute-start.22 = (f32[64,1024]{1,0:T(8,128)S(1)}, f32[64,1024]{1,0:T(8,128)S(1)}, u32[]{:S(2)}, u32[]{:S(2)}) collective-permute-start(f32[64,1024]{1,0:T(8,128)S(1)} %get-tuple-element.90), channel_id=1, source_target_pairs={{0,6},{1,3},{2,4},{3,1},{4,2},{5,7},{6,0},{7,5},{8,14},{9,11},{10,... | collective-permute-start | bytes 786440 | tf_op jit(solution)/shard_map/ppermute | solution.py:533
  134.2 16.1 %collective-permute-start.13 = (f32[32,1024]{1,0:T(8,128)S(1)}, f32[32,1024]{1,0:T(8,128)S(1)}, u32[]{:S(2)}, u32[]{:S(2)}) collective-permute-start(f32[32,1024]{1,0:T(8,128)S(1)} %get-tuple-element.91), channel_id=1, source_target_pairs={{0,2},{1,7},{2,0},{3,5},{4,6},{5,3},{6,4},{7,1},{8,10},{9,15},{10,... | collective-permute-start | bytes 393224 | tf_op jit(solution)/shard_map/ppermute | solution.py:533
  141.5 12.1 %copy-start.3 = (bf16[16,2048]{1,0:T(8,128)(2,1)S(1)}, bf16[16,2048]{1,0:T(8,128)(2,1)}, u32[]{:S(2)}) copy-start(bf16[16,2048]{1,0:T(8,128)(2,1)} %param.7) | copy-start | bytes 196612
  141.5 8.7 %collective-permute-start.23 = (f32[32,1024]{1,0:T(8,128)S(1)}, f32[32,1024]{1,0:T(8,128)S(1)}, u32[]{:S(2)}, u32[]{:S(2)}) collective-permute-start(f32[32,1024]{1,0:T(8,128)S(1)} %get-tuple-element.93), channel_id=1, source_target_pairs={{0,8},{1,25},{2,10},{3,27},{4,12},{5,29},{6,14},{7,31},{8,0},{9,17... | collective-permute-start | bytes 393224 | tf_op jit(solution)/shard_map/ppermute | solution.py:533
  150.2 3.2 %collective-permute-start.24 = (f32[16,1024]{1,0:T(8,128)S(1)}, f32[16,1024]{1,0:T(8,128)S(1)}, u32[]{:S(2)}, u32[]{:S(2)}) collective-permute-start(f32[16,1024]{1,0:T(8,128)S(1)} %get-tuple-element.76), channel_id=1, source_target_pairs={{0,24},{1,9},{2,26},{3,11},{4,28},{5,13},{6,30},{7,15},{8,16},{9,1... | collective-permute-start | bytes 196616 | tf_op jit(solution)/shard_map/ppermute | solution.py:533
  150.3 3.2 %collective-permute-start.18 = (f32[16,1024]{1,0:T(8,128)S(1)}, f32[16,1024]{1,0:T(8,128)S(1)}, u32[]{:S(2)}, u32[]{:S(2)}) collective-permute-start(f32[16,1024]{1,0:T(8,128)S(1)} %get-tuple-element.69), channel_id=1, source_target_pairs={{0,6},{1,3},{2,4},{3,1},{4,2},{5,7},{6,0},{7,5},{8,14},{9,11},{10,... | collective-permute-start | bytes 196616 | tf_op jit(solution)/shard_map/ppermute | solution.py:533
  154.3 19.2 %collective-permute-start.25 = (f32[32,2048]{1,0:T(8,128)S(1)}, f32[32,2048]{1,0:T(8,128)S(1)}, u32[]{:S(2)}, u32[]{:S(2)}) collective-permute-start(f32[32,2048]{1,0:T(8,128)S(1)} %solve0.1.refs_0_), channel_id=1, source_target_pairs={{0,1},{2,3},{4,5},{6,7},{8,9},{10,11},{12,13},{14,15},{16,17},{18,... | collective-permute-start | bytes 786440 | tf_op jit(solution)/shard_map/ppermute | solution.py:590

commit v8 on v7

--- a/solution.py
+++ b/solution.py
@@ -20,6 +20,7 @@
 PARTS = ((0, 1024, "zyx"), (1024, 1024, "zxy"))
 GATHER = ("yx", "xy")
 MB = 1 << 20
+SMALL = pl.CostEstimate(flops=1000, bytes_accessed=1000, transcendentals=0)
 TOKEN = jax.ShapeDtypeStruct((8, 128), F32)
 
 
@@ -151,7 +152,7 @@
         out_specs=[vmem] * 2 + [pl.BlockSpec(memory_space=pltpu.HBM)],
         scratch_shapes=[pltpu.VMEM((slab, slab), BF16), pltpu.SemaphoreType.DMA((2,))],
         compiler_params=pltpu.CompilerParams(vmem_limit_bytes=28 * MB),
-        cost_estimate=pl.CostEstimate(flops=4 * 10**9, bytes_accessed=2 * slab * slab, transcendentals=0),
+        cost_estimate=SMALL,
         name="grow_inverse",
     )(chips, *pieces)
 
@@ -246,6 +247,7 @@
             pltpu.SemaphoreType.DMA((3,)),
         ],
         compiler_params=pltpu.CompilerParams(vmem_limit_bytes=36 * MB),
+        cost_estimate=SMALL,
         name=name,
     )(core, chips, *dense, *pieces, *inverses)
 
@@ -322,11 +324,7 @@
             pltpu.SemaphoreType.DMA((width // step, groups)),
         ],
         compiler_params=pltpu.CompilerParams(vmem_limit_bytes=48 * MB),
-        cost_estimate=pl.CostEstimate(
-            flops=groups * rows * width * depth,
-            bytes_accessed=2 * groups * (rows // 2 + width) * depth + 2 * rows * width,
-            transcendentals=0,
-        ),
+        cost_estimate=SMALL,
         name=name,
     )(order, left, right, token)
 
@@ -417,6 +415,7 @@
         out_specs=[vmem] * len(shapes) + [hbm],
         scratch_shapes=scratch,
         compiler_params=pltpu.CompilerParams(vmem_limit_bytes=16 * MB),
+        cost_estimate=SMALL,
         name=name,
     )(flags, *operands, *tokens)
 
@@ -453,6 +452,7 @@
             pltpu.SemaphoreType.DMA((2, 2)),
         ],
         compiler_params=pltpu.CompilerParams(vmem_limit_bytes=12 * MB),
+        cost_estimate=SMALL,
         name="join",
     )(held[0], got[0], held[1], got[1], token)
     return joined, token
@@ -475,6 +475,7 @@
         in_specs=[vmem, vmem, hbm],
         out_specs=[vmem, vmem, hbm],
         compiler_params=pltpu.CompilerParams(vmem_limit_bytes=16 * MB),
+        cost_estimate=SMALL,
         name="add",
     )(keep, got, token)
 

time: 180 us -> 176 us (0.978)
  waiting for transfers between devices: 90.5 us -> 85 us
  other arithmetic: 5.45 us -> 2.39 us
  starting transfers between devices: 22.9 us -> 25.5 us
    ppermute x12, waiting for transfers between devices: 56.2 us -> 43.1 us  [sum_step(): lax.ppermute(send, EVERY, partner_pairs(PARTS[n][2][step // 2], step % 2...]
    ppermute x8, waiting for transfers between devices: 6.33 us -> 12.8 us  [gather_step(): lax.ppermute(held[n], EVERY, partner_pairs(GATHER[n][step // 2], step % 2...]
    add x4, other arithmetic: 4.82 us -> 0.45 us  [per_device(): keeps[n] = keeps[n][middle:] + come[n][middle:]]
    ppermute x12, starting transfers between devices: 7.17 us -> 10.5 us  [sum_step(): lax.ppermute(send, EVERY, partner_pairs(PARTS[n][2][step // 2], step % 2...]
    unnamed x8 -> x10, local copies, waits for them, and re-layouts: 3.54 us -> 4.5 us
  transfers between devices with their start and end apart: 26 -> 26, of which waited for: 16 -> 13; matrix products, arithmetic and copies ran while one was open for 3% -> 2% of each run, Pallas kernels for 26% -> 28%
where the time goes in v8:
time: 176 us
  waiting for transfers between devices  85 us (48%)
  Pallas kernels  57.3 us (33%)
  starting transfers between devices  25.5 us (14%)
  local copies, waits for them, and re-layouts  4.94 us (3%)
  other arithmetic  2.39 us (1%)
    ppermute x12, waiting for transfers between devices, sum_step(): lax.ppermute(send, EVERY, partner_pairs(PARTS[n][2][step // 2], step % 2...  43.1 us
    pallas_call x4, Pallas kernels, product(): pl.pallas_call(functools.partial(product_kernel, parts, half), out_shape=...  34.1 us
    ppermute x1, waiting for transfers between devices, per_device(): other = lax.ppermute(first, 'pcol', [(0, 1)])  19 us
    ppermute x8, waiting for transfers between devices, gather_step(): lax.ppermute(held[n], EVERY, partner_pairs(GATHER[n][step // 2], step % 2...  12.8 us
    ppermute x12, starting transfers between devices, sum_step(): lax.ppermute(send, EVERY, partner_pairs(PARTS[n][2][step // 2], step % 2...  10.5 us
    pallas_call x1, Pallas kernels, grow(): pl.pallas_call(grow_kernel, out_shape=(inverse, inverse, TOKEN), in_specs...  7.3 us
    ppermute x8, starting transfers between devices, gather_step(): lax.ppermute(held[n], EVERY, partner_pairs(GATHER[n][step // 2], step % 2...  7.03 us
    pallas_call x2, Pallas kernels, solve_call(): pl.pallas_call(functools.partial(solve_kernel, first), out_shape=jax.Shap...  6.81 us
  transfers between devices with their start and end apart: 26, of which 13 were waited for; matrix products, arithmetic and copies ran while one was open for 2% of the time, Pallas kernels for 28%

profile of v8, /device:TPU:1, one launch (start us, length us, event | category | flops | bytes accessed | tf_op | source)
XLA Modules:
  0.0 175.7 jit_solution(2466888906094652067)
XLA Ops:
  0.0 3.3 %collective-permute-start.1 = (bf16[64,2048]{1,0:T(8,128)(2,1)}, bf16[64,2048]{1,0:T(8,128)(2,1)S(1)}, u32[]{:S(2)}, u32[]{:S(2)}) collective-permute-start(bf16[64,2048]{1,0:T(8,128)(2,1)} %bitcast.10), channel_id=1, source_target_pairs={{1,0},{3,2},{5,4},{7,6},{9,8},{11,10},{13,12},{15,14},{17,16},{19,... | collective-permute-start | bytes 786440 | tf_op jit(solution)/shard_map/ppermute | solution.py:537
  3.3 1.3 collective-permute-start
  5.0 1.0 copy-done.2
  5.9 0.6 below0.1
  6.5 0.7 collective-permute-start.3
  7.3 0.1 add.166
  7.4 0.1 add.170
  7.5 4.3 %collective-permute-done.got = bf16[64,2048]{1,0:T(8,128)(2,1)S(1)} collective-permute-done((bf16[64,2048]{1,0:T(8,128)(2,1)}, bf16[64,2048]{1,0:T(8,128)(2,1)S(1)}, u32[]{:S(2)}, u32[]{:S(2)}) %collective-permute-start) | collective-permute-done | bytes 262176 | tf_op jit(solution)/shard_map/ppermute | solution.py:536
  11.9 0.9 copy-done.3
  12.8 0.6 strip1.1
  13.4 0.1 collective-permute-start.2
  13.5 9.2 %send0.1 = (f32[512,1024]{1,0:T(8,128)}, f32[8,128]{1,0:T(8,128)S(1)}) custom-call(s32[128]{0:T(128)S(1)} %pad_add_fusion.3.order, bf16[3,1024,1024]{2,1,0:T(8,128)(2,1)} %left.7, bf16[3,2048,1024]{2,1,0:T(8,128)(2,1)} %right.7, f32[8,128]{1,0:T(8,128)S(1)} %get-tuple-element.45._), custom_call_target="tpu_custom_call" | custom-call | flops 1000 | bytes 1000 | tf_op jit(solution)/shard_map/send0/pallas_call | solution.py:312
  22.7 0.6 below1.1
  23.3 1.3 collective-permute-start.4
  24.6 5.8 %collective-permute-done.4.got_under = bf16[64,2048]{1,0:T(8,128)(2,1)S(1)} collective-permute-done((bf16[64,2048]{1,0:T(8,128)(2,1)S(1)}, bf16[64,2048]{1,0:T(8,128)(2,1)S(1)}, u32[]{:S(2)}, u32[]{:S(2)}) %collective-permute-start.4) | collective-permute-done | bytes 262176 | tf_op jit(solution)/shard_map/ppermute | solution.py:544
  30.4 1.5 pack.1
  32.0 2.9 %collective-permute-start.5 = (bf16[96,2048]{1,0:T(8,128)(2,1)S(1)}, bf16[96,2048]{1,0:T(8,128)(2,1)S(1)}, u32[]{:S(2)}, u32[]{:S(2)}) collective-permute-start(bf16[96,2048]{1,0:T(8,128)(2,1)S(1)} %get-tuple-element.48.held_a), channel_id=1, source_target_pairs={{0,8},{1,25},{2,10},{3,27},{4,12},{5,29},{6,14},{7,31},{8,0},{9,17... | collective-permute-start | bytes 1179656 | tf_op jit(solution)/shard_map/ppermute | solution.py:529
  34.9 2.5 %collective-permute-start.6 = (bf16[96,2048]{1,0:T(8,128)(2,1)S(1)}, bf16[96,2048]{1,0:T(8,128)(2,1)S(1)}, u32[]{:S(2)}, u32[]{:S(2)}) collective-permute-start(bf16[96,2048]{1,0:T(8,128)(2,1)S(1)} %get-tuple-element.49.held_b), channel_id=1, source_target_pairs={{0,2},{1,7},{2,0},{3,5},{4,6},{5,3},{6,4},{7,1},{8,10},{9,15},{10,... | collective-permute-start | bytes 1179656 | tf_op jit(solution)/shard_map/ppermute | solution.py:529
  37.4 9.1 %send1.1 = (f32[512,1024]{1,0:T(8,128)}, f32[8,128]{1,0:T(8,128)S(1)}) custom-call(s32[128]{0:T(128)S(1)} %pad_add_fusion.3.order, bf16[3,1024,1024]{2,1,0:T(8,128)(2,1)} %left.7, bf16[3,2048,1024]{2,1,0:T(8,128)(2,1)} %right.7, f32[8,128]{1,0:T(8,128)S(1)} %get-tuple-element.50._), custom_call_target="tpu_custom_call" | custom-call | flops 1000 | bytes 1000 | tf_op jit(solution)/shard_map/send1/pallas_call | solution.py:312
  46.5 1.6 join.3
  48.1 0.1 collective-permute-start.8
  48.2 0.1 collective-permute-start.9
  48.3 2.9 %collective-permute-start.19 = (f32[512,1024]{1,0:T(8,128)}, f32[512,1024]{1,0:T(8,128)S(1)}, u32[]{:S(2)}, u32[]{:S(2)}) collective-permute-start(f32[512,1024]{1,0:T(8,128)} %get-tuple-element.71), channel_id=1, source_target_pairs={{0,32},{1,97},{2,34},{3,99},{4,36},{5,101},{6,38},{7,103},{8,40},{... | collective-permute-start | bytes 6291464 | tf_op jit(solution)/shard_map/ppermute | solution.py:534
  51.2 7.9 %keep0.1 = (f32[512,1024]{1,0:T(8,128)S(1)}, f32[8,128]{1,0:T(8,128)S(1)}) custom-call(s32[128]{0:T(128)S(1)} %pad_add_fusion.3.order, bf16[3,1024,1024]{2,1,0:T(8,128)(2,1)} %left.7, bf16[3,2048,1024]{2,1,0:T(8,128)(2,1)} %right.7, f32[8,128]{1,0:T(8,128)S(1)} %get-tuple-element.52._), custom_call_target="tpu_custom_call" | custom-call | flops 1000 | bytes 1000 | tf_op jit(solution)/shard_map/keep0/pallas_call | solution.py:312
  59.1 0.2 collective-permute-done.8.got_a
  59.3 0.1 collective-permute-done.9.got_b
  59.4 0.5 join.4
  59.9 0.3 collective-permute-start.14
  60.2 0.5 collective-permute-start.15
  60.8 7.9 %keep1.1 = (f32[512,1024]{1,0:T(8,128)S(1)}, f32[8,128]{1,0:T(8,128)S(1)}) custom-call(s32[128]{0:T(128)S(1)} %pad_add_fusion.3.order, bf16[3,1024,1024]{2,1,0:T(8,128)(2,1)} %left.7, bf16[3,2048,1024]{2,1,0:T(8,128)(2,1)} %right.7, f32[8,128]{1,0:T(8,128)S(1)} %get-tuple-element.58._), custom_call_target="tpu_custom_call" | custom-call | flops 1000 | bytes 1000 | tf_op jit(solution)/shard_map/keep1/pallas_call | solution.py:312
  68.7 0.2 add.236
  68.9 0.1 collective-permute-start.10
  69.0 12.4 %collective-permute-done.14.got_a = bf16[384,2048]{1,0:T(8,128)(2,1)S(1)} collective-permute-done((bf16[384,2048]{1,0:T(8,128)(2,1)S(1)}, bf16[384,2048]{1,0:T(8,128)(2,1)S(1)}, u32[]{:S(2)}, u32[]{:S(2)}) %collective-permute-start.14) | collective-permute-done | bytes 1572896 | tf_op jit(solution)/shard_map/ppermute | solution.py:529
  81.4 1.2 copy-done
  82.6 1.4 copy-done.1
  84.0 2.3 %join.5 = (bf16[768,2048]{1,0:T(8,128)(2,1)S(1)}, bf16[768,2048]{1,0:T(8,128)(2,1)}, f32[8,128]{1,0:T(8,128)S(1)}) custom-call(bf16[384,2048]{1,0:T(8,128)(2,1)S(1)} %get-tuple-element.62.held_a, bf16[384,2048]{1,0:T(8,128)(2,1)S(1)} %collective-permute-done.14.got_a, bf16[384,2048]{1,0:T(8,128)(2,1)S(1)} %get-tuple-element.63.held_b, ...), custom_call_target="tpu_custom_call" | custom-call | flops 1000 | bytes 1000 | tf_op jit(solution)/shard_map/join/pallas_call | solution.py:444
  86.3 0.5 collective-permute-start.16
  86.8 0.2 collective-permute-start.17
  87.0 5.2 %collective-permute-done.19.got = f32[512,1024]{1,0:T(8,128)S(1)} collective-permute-done((f32[512,1024]{1,0:T(8,128)}, f32[512,1024]{1,0:T(8,128)S(1)}, u32[]{:S(2)}, u32[]{:S(2)}) %collective-permute-start.19) | collective-permute-done | bytes 2097184 | tf_op jit(solution)/shard_map/ppermute | solution.py:534
  92.2 0.3 add.238
  92.5 0.1 collective-permute-start.20
  92.6 1.6 collective-permute-done.10
  94.2 0.2 slice_add_fusion.3
  94.4 2.2 %collective-permute-start.11 = (f32[128,1024]{1,0:T(8,128)S(1)}, f32[128,1024]{1,0:T(8,128)S(1)}, u32[]{:S(2)}, u32[]{:S(2)}) collective-permute-start(f32[128,1024]{1,0:T(8,128)S(1)} %get-tuple-element.84), channel_id=1, source_target_pairs={{0,8},{1,25},{2,10},{3,27},{4,12},{5,29},{6,14},{7,31},{8,0},{9,17... | collective-permute-start | bytes 1572872 | tf_op jit(solution)/shard_map/ppermute | solution.py:534
  96.6 11.0 %collective-permute-done.20 = f32[256,1024]{1,0:T(8,128)S(1)} collective-permute-done((f32[256,1024]{1,0:T(8,128)S(1)}, f32[256,1024]{1,0:T(8,128)S(1)}, u32[]{:S(2)}, u32[]{:S(2)}) %collective-permute-start.20) | collective-permute-done | bytes 1048608 | tf_op jit(solution)/shard_map/ppermute | solution.py:534
  107.6 0.2 slice_add_fusion.1
  107.8 1.9 %collective-permute-start.21 = (f32[128,1024]{1,0:T(8,128)S(1)}, f32[128,1024]{1,0:T(8,128)S(1)}, u32[]{:S(2)}, u32[]{:S(2)}) collective-permute-start(f32[128,1024]{1,0:T(8,128)S(1)} %get-tuple-element.86), channel_id=1, source_target_pairs={{0,2},{1,7},{2,0},{3,5},{4,6},{5,3},{6,4},{7,1},{8,10},{9,15},{10,... | collective-permute-start | bytes 1572872 | tf_op jit(solution)/shard_map/ppermute | solution.py:534
  109.7 0.2 collective-permute-start.12
  110.0 13.2 %collective-permute-done.21 = f32[128,1024]{1,0:T(8,128)S(1)} collective-permute-done((f32[128,1024]{1,0:T(8,128)S(1)}, f32[128,1024]{1,0:T(8,128)S(1)}, u32[]{:S(2)}, u32[]{:S(2)}) %collective-permute-start.21) | collective-permute-done | bytes 524320 | tf_op jit(solution)/shard_map/ppermute | solution.py:534
  123.2 0.1 collective-permute-start.22
  123.3 8.6 %collective-permute-done.12 = f32[64,1024]{1,0:T(8,128)S(1)} collective-permute-done((f32[64,1024]{1,0:T(8,128)S(1)}, f32[64,1024]{1,0:T(8,128)S(1)}, u32[]{:S(2)}, u32[]{:S(2)}) %collective-permute-start.12) | collective-permute-done | bytes 262176 | tf_op jit(solution)/shard_map/ppermute | solution.py:534
  132.0 0.7 slice_add_fusion.10
  132.7 1.8 %collective-permute-start.13 = (f32[32,1024]{1,0:T(8,128)}, f32[32,1024]{1,0:T(8,128)S(1)}, u32[]{:S(2)}, u32[]{:S(2)}) collective-permute-start(f32[32,1024]{1,0:T(8,128)} %get-tuple-element.91), channel_id=1, source_target_pairs={{0,2},{1,7},{2,0},{3,5},{4,6},{5,3},{6,4},{7,1},{8,10},{9,15},{10,... | collective-permute-start | bytes 393224 | tf_op jit(solution)/shard_map/ppermute | solution.py:534
  134.4 0.7 slice_add_fusion.8
  135.1 0.4 collective-permute-start.23
  135.9 7.3 %grow_inverse.1 = (bf16[4,512,512]{2,1,0:T(8,128)(2,1)S(1)}, bf16[4,512,512]{2,1,0:T(8,128)(2,1)S(1)}, f32[8,128]{1,0:T(8,128)S(1)}) custom-call(s32[32]{0:T(128)S(1)} %pad_add_fusion.1.chips, bf16[768,2048]{1,0:T(8,128)(2,1)S(1)} %get-tuple-element.65.own_a.refs_0_.refs_2_, bf16[768,2048]{1,0:T(8,128)(2,1)} %collective-permute-done.16.got_a.refs_1_.refs_3_, ...), custom_call_target="tpu_custom_call" | custom-call | flops 1000 | bytes 1000 | tf_op jit(solution)/shard_map/grow_inverse/pallas_call | solution.py:148
  143.2 0.9 add.239
  144.3 0.6 collective-permute-start.18
  144.9 2.7 %collective-permute-done.24 = f32[16,1024]{1,0:T(8,128)S(1)} collective-permute-done((f32[16,1024]{1,0:T(8,128)S(1)}, f32[16,1024]{1,0:T(8,128)S(1)}, u32[]{:S(2)}, u32[]{:S(2)}) %collective-permute-start.24) | collective-permute-done | bytes 65568 | tf_op jit(solution)/shard_map/ppermute | solution.py:534
  147.6 0.7 collective-permute-done.18
  148.4 0.7 solve0.1.refs_0_
  149.1 1.3 collective-permute-start.25
  150.4 19.0 %collective-permute-done.25.refs_1_ = f32[32,2048]{1,0:T(8,128)S(1)} collective-permute-done((f32[32,2048]{1,0:T(8,128)S(1)}, f32[32,2048]{1,0:T(8,128)S(1)}, u32[]{:S(2)}, u32[]{:S(2)}) %collective-permute-start.25) | collective-permute-done | bytes 262176 | tf_op jit(solution)/shard_map/ppermute | solution.py:591
  169.3 6.1 %solve1.1 = f32[16,2048]{1,0:T(8,128)} custom-call(s32[1]{0:T(128)} %bitcast.core, s32[32]{0:T(128)S(1)} %pad_add_fusion.1.chips, f32[16,2048]{1,0:T(8,128)S(1)} %maximum_subtract_fusion.right, f32[32,2048]{1,0:T(8,128)S(1)} %solve0.1.refs_0_, f32[32,2048]{1,0:T(8,128)S(1)} %collective-permute-done.25.refs_1_, ...), custom_call_target="tpu_custom_call" | custom-call | flops 1000 | bytes 1000 | tf_op jit(solution)/shard_map/solve1/pallas_call | solution.py:235
  (38 shorter events, 1.1 us)
Async XLA Ops:
  0.0 5.0 %collective-permute-start.1 = (bf16[64,2048]{1,0:T(8,128)(2,1)}, bf16[64,2048]{1,0:T(8,128)(2,1)S(1)}, u32[]{:S(2)}, u32[]{:S(2)}) collective-permute-start(bf16[64,2048]{1,0:T(8,128)(2,1)} %bitcast.10), channel_id=1, source_target_pairs={{1,0},{3,2},{5,4},{7,6},{9,8},{11,10},{13,12},{15,14},{17,16},{19,... | collective-permute-start | bytes 786440 | tf_op jit(solution)/shard_map/ppermute | solution.py:537
  3.3 8.5 %collective-permute-start = (bf16[64,2048]{1,0:T(8,128)(2,1)}, bf16[64,2048]{1,0:T(8,128)(2,1)S(1)}, u32[]{:S(2)}, u32[]{:S(2)}) collective-permute-start(bf16[64,2048]{1,0:T(8,128)(2,1)} %bitcast.11), channel_id=1, source_target_pairs={{0,96},{2,98},{4,100},{6,102},{8,104},{10,106},{12,108},{14,110},{... | collective-permute-start | bytes 786440 | tf_op jit(solution)/shard_map/ppermute | solution.py:536
  5.0 1.0 copy-start.2
  6.5 16.2 %collective-permute-start.3 = (bf16[64,2048]{1,0:T(8,128)(2,1)S(1)}, bf16[64,2048]{1,0:T(8,128)(2,1)S(1)}, u32[]{:S(2)}, u32[]{:S(2)}) collective-permute-start(bf16[64,2048]{1,0:T(8,128)(2,1)S(1)} %get-tuple-element.44.held), channel_id=1, source_target_pairs={{0,96},{2,98},{4,100},{6,102},{8,104},{10,106},{12,108},{14,110},{... | collective-permute-start | bytes 786440 | tf_op jit(solution)/shard_map/ppermute | solution.py:539
  11.9 1.0 copy-start.3
  13.4 11.2 %collective-permute-start.2 = (bf16[64,2048]{1,0:T(8,128)(2,1)S(1)}, bf16[64,2048]{1,0:T(8,128)(2,1)S(1)}, u32[]{:S(2)}, u32[]{:S(2)}) collective-permute-start(bf16[64,2048]{1,0:T(8,128)(2,1)S(1)} %get-tuple-element.43.held), channel_id=1, source_target_pairs={{0,32},{1,33},{2,34},{3,35},{4,36},{5,37},{6,38},{7,39},{8,40},{9,... | collective-permute-start | bytes 786440 | tf_op jit(solution)/shard_map/ppermute | solution.py:541
  23.3 7.1 %collective-permute-start.4 = (bf16[64,2048]{1,0:T(8,128)(2,1)S(1)}, bf16[64,2048]{1,0:T(8,128)(2,1)S(1)}, u32[]{:S(2)}, u32[]{:S(2)}) collective-permute-start(bf16[64,2048]{1,0:T(8,128)(2,1)S(1)} %get-tuple-element.47.under), channel_id=1, source_target_pairs={{0,32},{2,34},{4,36},{6,38},{8,40},{10,42},{12,44},{14,46},{16,48}... | collective-permute-start | bytes 786440 | tf_op jit(solution)/shard_map/ppermute | solution.py:544
  32.0 14.5 %collective-permute-start.5 = (bf16[96,2048]{1,0:T(8,128)(2,1)S(1)}, bf16[96,2048]{1,0:T(8,128)(2,1)S(1)}, u32[]{:S(2)}, u32[]{:S(2)}) collective-permute-start(bf16[96,2048]{1,0:T(8,128)(2,1)S(1)} %get-tuple-element.48.held_a), channel_id=1, source_target_pairs={{0,8},{1,25},{2,10},{3,27},{4,12},{5,29},{6,14},{7,31},{8,0},{9,17... | collective-permute-start | bytes 1179656 | tf_op jit(solution)/shard_map/ppermute | solution.py:529
  34.9 11.7 %collective-permute-start.6 = (bf16[96,2048]{1,0:T(8,128)(2,1)S(1)}, bf16[96,2048]{1,0:T(8,128)(2,1)S(1)}, u32[]{:S(2)}, u32[]{:S(2)}) collective-permute-start(bf16[96,2048]{1,0:T(8,128)(2,1)S(1)} %get-tuple-element.49.held_b), channel_id=1, source_target_pairs={{0,2},{1,7},{2,0},{3,5},{4,6},{5,3},{6,4},{7,1},{8,10},{9,15},{10,... | collective-permute-start | bytes 1179656 | tf_op jit(solution)/shard_map/ppermute | solution.py:529
  37.4 31.3 %collective-permute-start.7 = (f32[512,1024]{1,0:T(8,128)}, f32[512,1024]{1,0:T(8,128)S(1)}, u32[]{:S(2)}, u32[]{:S(2)}) collective-permute-start(f32[512,1024]{1,0:T(8,128)} %get-tuple-element.54), channel_id=1, source_target_pairs={{0,32},{1,97},{2,34},{3,99},{4,36},{5,101},{6,38},{7,103},{8,40},{... | collective-permute-start | bytes 6291464 | tf_op jit(solution)/shard_map/ppermute | solution.py:534
  48.1 11.2 %collective-permute-start.8 = (bf16[192,2048]{1,0:T(8,128)(2,1)S(1)}, bf16[192,2048]{1,0:T(8,128)(2,1)S(1)}, u32[]{:S(2)}, u32[]{:S(2)}) collective-permute-start(bf16[192,2048]{1,0:T(8,128)(2,1)S(1)} %get-tuple-element.55.held_a), channel_id=1, source_target_pairs={{0,24},{1,9},{2,26},{3,11},{4,28},{5,13},{6,30},{7,15},{8,16},{9,1... | collective-permute-start | bytes 2359304 | tf_op jit(solution)/shard_map/ppermute | solution.py:529
  48.2 11.2 %collective-permute-start.9 = (bf16[192,2048]{1,0:T(8,128)(2,1)S(1)}, bf16[192,2048]{1,0:T(8,128)(2,1)S(1)}, u32[]{:S(2)}, u32[]{:S(2)}) collective-permute-start(bf16[192,2048]{1,0:T(8,128)(2,1)S(1)} %get-tuple-element.56.held_b), channel_id=1, source_target_pairs={{0,6},{1,3},{2,4},{3,1},{4,2},{5,7},{6,0},{7,5},{8,14},{9,11},{10,... | collective-permute-start | bytes 2359304 | tf_op jit(solution)/shard_map/ppermute | solution.py:529
  48.3 43.9 %collective-permute-start.19 = (f32[512,1024]{1,0:T(8,128)}, f32[512,1024]{1,0:T(8,128)S(1)}, u32[]{:S(2)}, u32[]{:S(2)}) collective-permute-start(f32[512,1024]{1,0:T(8,128)} %get-tuple-element.71), channel_id=1, source_target_pairs={{0,32},{1,97},{2,34},{3,99},{4,36},{5,101},{6,38},{7,103},{8,40},{... | collective-permute-start | bytes 6291464 | tf_op jit(solution)/shard_map/ppermute | solution.py:534
  59.9 21.5 %collective-permute-start.14 = (bf16[384,2048]{1,0:T(8,128)(2,1)S(1)}, bf16[384,2048]{1,0:T(8,128)(2,1)S(1)}, u32[]{:S(2)}, u32[]{:S(2)}) collective-permute-start(bf16[384,2048]{1,0:T(8,128)(2,1)S(1)} %get-tuple-element.62.held_a), channel_id=1, source_target_pairs={{0,2},{1,7},{2,0},{3,5},{4,6},{5,3},{6,4},{7,1},{8,10},{9,15},{10,... | collective-permute-start | bytes 4718600 | tf_op jit(solution)/shard_map/ppermute | solution.py:529
  60.2 21.2 %collective-permute-start.15 = (bf16[384,2048]{1,0:T(8,128)(2,1)S(1)}, bf16[384,2048]{1,0:T(8,128)(2,1)S(1)}, u32[]{:S(2)}, u32[]{:S(2)}) collective-permute-start(bf16[384,2048]{1,0:T(8,128)(2,1)S(1)} %get-tuple-element.63.held_b), channel_id=1, source_target_pairs={{0,8},{1,25},{2,10},{3,27},{4,12},{5,29},{6,14},{7,31},{8,0},{9,17... | collective-permute-start | bytes 4718600 | tf_op jit(solution)/shard_map/ppermute | solution.py:529
  68.9 25.3 %collective-permute-start.10 = (f32[256,1024]{1,0:T(8,128)S(1)}, f32[256,1024]{1,0:T(8,128)S(1)}, u32[]{:S(2)}, u32[]{:S(2)}) collective-permute-start(f32[256,1024]{1,0:T(8,128)S(1)} %get-tuple-element.61), channel_id=1, source_target_pairs={{0,96},{1,33},{2,98},{3,35},{4,100},{5,37},{6,102},{7,39},{8,104},... | collective-permute-start | bytes 3145736 | tf_op jit(solution)/shard_map/ppermute | solution.py:534
  81.4 1.2 copy-start
  82.6 1.4 copy-start.1
  86.3 49.5 %collective-permute-start.16 = (bf16[768,2048]{1,0:T(8,128)(2,1)S(1)}, bf16[768,2048]{1,0:T(8,128)(2,1)}, u32[]{:S(2)}, u32[]{:S(2)}) collective-permute-start(bf16[768,2048]{1,0:T(8,128)(2,1)S(1)} %get-tuple-element.65.own_a.refs_0_.refs_2_), channel_id=1, source_target_pairs={{0,6},{1,3},{2,4},{3,1},{4,2},{5,7},{6,0},{7,5},{8,14},{9,11},{10,... | collective-permute-start | bytes 9437192 | tf_op jit(solution)/shard_map/ppermute | solution.py:529
  86.8 49.1 %collective-permute-start.17 = (bf16[768,2048]{1,0:T(8,128)(2,1)}, bf16[768,2048]{1,0:T(8,128)(2,1)}, u32[]{:S(2)}, u32[]{:S(2)}) collective-permute-start(bf16[768,2048]{1,0:T(8,128)(2,1)} %get-tuple-element.66.own_b.refs_2_.refs_4_), channel_id=1, source_target_pairs={{0,24},{1,9},{2,26},{3,11},{4,28},{5,13},{6,30},{7,15},{8,16},{9,1... | collective-permute-start | bytes 9437192 | tf_op jit(solution)/shard_map/ppermute | solution.py:529
  92.5 15.1 %collective-permute-start.20 = (f32[256,1024]{1,0:T(8,128)S(1)}, f32[256,1024]{1,0:T(8,128)S(1)}, u32[]{:S(2)}, u32[]{:S(2)}) collective-permute-start(f32[256,1024]{1,0:T(8,128)S(1)} %get-tuple-element.74), channel_id=1, source_target_pairs={{0,96},{1,33},{2,98},{3,35},{4,100},{5,37},{6,102},{7,39},{8,104},... | collective-permute-start | bytes 3145736 | tf_op jit(solution)/shard_map/ppermute | solution.py:534
  94.4 15.3 %collective-permute-start.11 = (f32[128,1024]{1,0:T(8,128)S(1)}, f32[128,1024]{1,0:T(8,128)S(1)}, u32[]{:S(2)}, u32[]{:S(2)}) collective-permute-start(f32[128,1024]{1,0:T(8,128)S(1)} %get-tuple-element.84), channel_id=1, source_target_pairs={{0,8},{1,25},{2,10},{3,27},{4,12},{5,29},{6,14},{7,31},{8,0},{9,17... | collective-permute-start | bytes 1572872 | tf_op jit(solution)/shard_map/ppermute | solution.py:534
  107.8 15.4 %collective-permute-start.21 = (f32[128,1024]{1,0:T(8,128)S(1)}, f32[128,1024]{1,0:T(8,128)S(1)}, u32[]{:S(2)}, u32[]{:S(2)}) collective-permute-start(f32[128,1024]{1,0:T(8,128)S(1)} %get-tuple-element.86), channel_id=1, source_target_pairs={{0,2},{1,7},{2,0},{3,5},{4,6},{5,3},{6,4},{7,1},{8,10},{9,15},{10,... | collective-permute-start | bytes 1572872 | tf_op jit(solution)/shard_map/ppermute | solution.py:534
  109.7 22.2 %collective-permute-start.12 = (f32[64,1024]{1,0:T(8,128)S(1)}, f32[64,1024]{1,0:T(8,128)S(1)}, u32[]{:S(2)}, u32[]{:S(2)}) collective-permute-start(f32[64,1024]{1,0:T(8,128)S(1)} %get-tuple-element.88), channel_id=1, source_target_pairs={{0,24},{1,9},{2,26},{3,11},{4,28},{5,13},{6,30},{7,15},{8,16},{9,1... | collective-permute-start | bytes 786440 | tf_op jit(solution)/shard_map/ppermute | solution.py:534
  123.2 11.2 %collective-permute-start.22 = (f32[64,1024]{1,0:T(8,128)S(1)}, f32[64,1024]{1,0:T(8,128)S(1)}, u32[]{:S(2)}, u32[]{:S(2)}) collective-permute-start(f32[64,1024]{1,0:T(8,128)S(1)} %get-tuple-element.90), channel_id=1, source_target_pairs={{0,6},{1,3},{2,4},{3,1},{4,2},{5,7},{6,0},{7,5},{8,14},{9,11},{10,... | collective-permute-start | bytes 786440 | tf_op jit(solution)/shard_map/ppermute | solution.py:534
  132.7 11.6 %collective-permute-start.13 = (f32[32,1024]{1,0:T(8,128)}, f32[32,1024]{1,0:T(8,128)S(1)}, u32[]{:S(2)}, u32[]{:S(2)}) collective-permute-start(f32[32,1024]{1,0:T(8,128)} %get-tuple-element.91), channel_id=1, source_target_pairs={{0,2},{1,7},{2,0},{3,5},{4,6},{5,3},{6,4},{7,1},{8,10},{9,15},{10,... | collective-permute-start | bytes 393224 | tf_op jit(solution)/shard_map/ppermute | solution.py:534
  135.1 8.1 %collective-permute-start.23 = (f32[32,1024]{1,0:T(8,128)}, f32[32,1024]{1,0:T(8,128)}, u32[]{:S(2)}, u32[]{:S(2)}) collective-permute-start(f32[32,1024]{1,0:T(8,128)} %get-tuple-element.93), channel_id=1, source_target_pairs={{0,8},{1,25},{2,10},{3,27},{4,12},{5,29},{6,14},{7,31},{8,0},{9,17... | collective-permute-start | bytes 393224 | tf_op jit(solution)/shard_map/ppermute | solution.py:534
  135.9 12.5 %copy-start.4 = (bf16[16,2048]{1,0:T(8,128)(2,1)S(1)}, bf16[16,2048]{1,0:T(8,128)(2,1)}, u32[]{:S(2)}) copy-start(bf16[16,2048]{1,0:T(8,128)(2,1)} %param.7) | copy-start | bytes 196612
  144.1 3.5 %collective-permute-start.24 = (f32[16,1024]{1,0:T(8,128)S(1)}, f32[16,1024]{1,0:T(8,128)S(1)}, u32[]{:S(2)}, u32[]{:S(2)}) collective-permute-start(f32[16,1024]{1,0:T(8,128)S(1)} %get-tuple-element.76), channel_id=1, source_target_pairs={{0,24},{1,9},{2,26},{3,11},{4,28},{5,13},{6,30},{7,15},{8,16},{9,1... | collective-permute-start | bytes 196616 | tf_op jit(solution)/shard_map/ppermute | solution.py:534
  144.3 4.1 %collective-permute-start.18 = (f32[16,1024]{1,0:T(8,128)S(1)}, f32[16,1024]{1,0:T(8,128)S(1)}, u32[]{:S(2)}, u32[]{:S(2)}) collective-permute-start(f32[16,1024]{1,0:T(8,128)S(1)} %get-tuple-element.69), channel_id=1, source_target_pairs={{0,6},{1,3},{2,4},{3,1},{4,2},{5,7},{6,0},{7,5},{8,14},{9,11},{10,... | collective-permute-start | bytes 196616 | tf_op jit(solution)/shard_map/ppermute | solution.py:534
  149.1 20.3 %collective-permute-start.25 = (f32[32,2048]{1,0:T(8,128)S(1)}, f32[32,2048]{1,0:T(8,128)S(1)}, u32[]{:S(2)}, u32[]{:S(2)}) collective-permute-start(f32[32,2048]{1,0:T(8,128)S(1)} %solve0.1.refs_0_), channel_id=1, source_target_pairs={{0,1},{2,3},{4,5},{6,7},{8,9},{10,11},{12,13},{14,15},{16,17},{18,... | collective-permute-start | bytes 786440 | tf_op jit(solution)/shard_map/ppermute | solution.py:591

commit v9 on v8

--- a/solution.py
+++ b/solution.py
@@ -558,16 +558,16 @@
         got_under,
     )
     got = gather_step(held, 0)
+    held, token = join(held, got, token)
+    got = gather_step(held, 1)
     send1, token = half_product(1, 0, token, "send1")
     come[1] = sum_step(1, send1, 0)
     held, token = join(held, got, token)
-    got = gather_step(held, 1)
+    got = gather_step(held, 2)
     keep0, token = half_product(0, 1, token, "keep0")
-    held, token = join(held, got, token)
-    got = gather_step(held, 2)
-    keep1, token = half_product(1, 1, token, "keep1")
     send0, keep0, token = add(keep0, come[0], token)
     come[0] = sum_step(0, send0, 1)
+    keep1, token = half_product(1, 1, token, "keep1")
     held, token = join(held, got, token)
     got = gather_step(held, 3)
     send1, keep1, token = add(keep1, come[1], token)

time: 176 us -> 178 us (1.011)
  the two profiles are of different devices: /device:TPU:1 before, /device:TPU:81 now
where the time goes in v9:
time: 178 us
  waiting for transfers between devices  73 us (41%)
  Pallas kernels  57.1 us (32%)
  starting transfers between devices  41.4 us (23%)
  local copies, waits for them, and re-layouts  3.32 us (2%)
  other arithmetic  2.41 us (1%)
    ppermute x12, waiting for transfers between devices, sum_step(): lax.ppermute(send, EVERY, partner_pairs(PARTS[n][2][step // 2], step % 2...  42.3 us
    pallas_call x4, Pallas kernels, product(): pl.pallas_call(functools.partial(product_kernel, parts, half), out_shape=...  32.7 us
    ppermute x12, starting transfers between devices, sum_step(): lax.ppermute(send, EVERY, partner_pairs(PARTS[n][2][step // 2], step % 2...  22.4 us
    ppermute x1, waiting for transfers between devices, per_device(): other = lax.ppermute(first, 'pcol', [(0, 1)])  21.1 us
    ppermute x8, starting transfers between devices, gather_step(): lax.ppermute(held[n], EVERY, partner_pairs(GATHER[n][step // 2], step % 2...  9.6 us
    pallas_call x1, Pallas kernels, grow(): pl.pallas_call(grow_kernel, out_shape=(inverse, inverse, TOKEN), in_specs...  7.3 us
    pallas_call x2, Pallas kernels, solve_call(): pl.pallas_call(functools.partial(solve_kernel, first), out_shape=jax.Shap...  6.81 us
    ppermute x8, waiting for transfers between devices, gather_step(): lax.ppermute(held[n], EVERY, partner_pairs(GATHER[n][step // 2], step % 2...  6.25 us
  transfers between devices with their start and end apart: 26, of which 13 were waited for; matrix products, arithmetic and copies ran while one was open for 2% of the time, Pallas kernels for 27%

profile of v9, /device:TPU:81, one launch (start us, length us, event | category | flops | bytes accessed | tf_op | source)
XLA Modules:
  0.0 177.7 jit_solution(5691778178212738555)
XLA Ops:
  0.0 0.7 collective-permute-start.1
  0.7 1.8 collective-permute-start
  2.8 1.0 copy-done.2
  3.7 0.6 below0.1
  4.3 1.3 collective-permute-start.3
  5.7 0.1 add.166
  5.8 0.1 add.170
  5.9 0.1 collective-permute-done.got
  6.0 0.9 copy-done.3
  7.0 0.6 strip1.1
  7.6 2.4 %collective-permute-start.2 = (bf16[64,2048]{1,0:T(8,128)(2,1)S(1)}, bf16[64,2048]{1,0:T(8,128)(2,1)S(1)}, u32[]{:S(2)}, u32[]{:S(2)}) collective-permute-start(bf16[64,2048]{1,0:T(8,128)(2,1)S(1)} %get-tuple-element.43.held), channel_id=1, source_target_pairs={{0,32},{1,33},{2,34},{3,35},{4,36},{5,37},{6,38},{7,39},{8,40},{9,... | collective-permute-start | bytes 786440 | tf_op jit(solution)/shard_map/ppermute | solution.py:541
  10.0 7.9 %send0.1 = (f32[512,1024]{1,0:T(8,128)S(1)}, f32[8,128]{1,0:T(8,128)S(1)}) custom-call(s32[128]{0:T(128)S(1)} %pad_add_fusion.3.order, bf16[3,1024,1024]{2,1,0:T(8,128)(2,1)} %left.7, bf16[3,2048,1024]{2,1,0:T(8,128)(2,1)} %right.7, f32[8,128]{1,0:T(8,128)S(1)} %get-tuple-element.45._), custom_call_target="tpu_custom_call" | custom-call | flops 1000 | bytes 1000 | tf_op jit(solution)/shard_map/send0/pallas_call | solution.py:312
  17.9 0.6 below1.1
  18.4 1.9 %collective-permute-start.4 = (bf16[64,2048]{1,0:T(8,128)(2,1)S(1)}, bf16[64,2048]{1,0:T(8,128)(2,1)S(1)}, u32[]{:S(2)}, u32[]{:S(2)}) collective-permute-start(bf16[64,2048]{1,0:T(8,128)(2,1)S(1)} %get-tuple-element.47.under), channel_id=1, source_target_pairs={{0,32},{2,34},{4,36},{6,38},{8,40},{10,42},{12,44},{14,46},{16,48}... | collective-permute-start | bytes 786440 | tf_op jit(solution)/shard_map/ppermute | solution.py:544
  20.4 3.3 %collective-permute-done.4.got_under = bf16[64,2048]{1,0:T(8,128)(2,1)S(1)} collective-permute-done((bf16[64,2048]{1,0:T(8,128)(2,1)S(1)}, bf16[64,2048]{1,0:T(8,128)(2,1)S(1)}, u32[]{:S(2)}, u32[]{:S(2)}) %collective-permute-start.4) | collective-permute-done | bytes 262176 | tf_op jit(solution)/shard_map/ppermute | solution.py:544
  23.7 1.5 pack.1
  25.2 0.3 collective-permute-start.5
  25.5 2.5 %collective-permute-start.6 = (bf16[96,2048]{1,0:T(8,128)(2,1)S(1)}, bf16[96,2048]{1,0:T(8,128)(2,1)S(1)}, u32[]{:S(2)}, u32[]{:S(2)}) collective-permute-start(bf16[96,2048]{1,0:T(8,128)(2,1)S(1)} %get-tuple-element.49.held_b), channel_id=1, source_target_pairs={{0,2},{1,7},{2,0},{3,5},{4,6},{5,3},{6,4},{7,1},{8,10},{9,15},{10,... | collective-permute-start | bytes 1179656 | tf_op jit(solution)/shard_map/ppermute | solution.py:529
  27.9 2.4 %collective-permute-start.9 = (f32[512,1024]{1,0:T(8,128)S(1)}, f32[512,1024]{1,0:T(8,128)S(1)}, u32[]{:S(2)}, u32[]{:S(2)}) collective-permute-start(f32[512,1024]{1,0:T(8,128)S(1)} %get-tuple-element.57), channel_id=1, source_target_pairs={{0,32},{1,97},{2,34},{3,99},{4,36},{5,101},{6,38},{7,103},{8,40},{... | collective-permute-start | bytes 6291464 | tf_op jit(solution)/shard_map/ppermute | solution.py:534
  30.4 1.6 collective-permute-done.5.got_a
  31.9 1.4 collective-permute-done.6.got_b
  33.3 1.6 join.3
  34.9 1.0 collective-permute-start.7
  35.9 1.1 collective-permute-start.8
  37.0 9.2 %send1.1 = (f32[512,1024]{1,0:T(8,128)}, f32[8,128]{1,0:T(8,128)S(1)}) custom-call(s32[128]{0:T(128)S(1)} %pad_add_fusion.3.order, bf16[3,1024,1024]{2,1,0:T(8,128)(2,1)} %left.7, bf16[3,2048,1024]{2,1,0:T(8,128)(2,1)} %right.7, f32[8,128]{1,0:T(8,128)S(1)} %get-tuple-element.53._), custom_call_target="tpu_custom_call" | custom-call | flops 1000 | bytes 1000 | tf_op jit(solution)/shard_map/send1/pallas_call | solution.py:312
  46.2 2.5 %collective-permute-start.19 = (f32[512,1024]{1,0:T(8,128)}, f32[512,1024]{1,0:T(8,128)S(1)}, u32[]{:S(2)}, u32[]{:S(2)}) collective-permute-start(f32[512,1024]{1,0:T(8,128)} %get-tuple-element.71), channel_id=1, source_target_pairs={{0,32},{1,97},{2,34},{3,99},{4,36},{5,101},{6,38},{7,103},{8,40},{... | collective-permute-start | bytes 6291464 | tf_op jit(solution)/shard_map/ppermute | solution.py:534
  48.7 1.0 collective-permute-done.8.got_b
  49.7 0.5 join.4
  50.2 2.6 %collective-permute-start.14 = (bf16[384,2048]{1,0:T(8,128)(2,1)S(1)}, bf16[384,2048]{1,0:T(8,128)(2,1)S(1)}, u32[]{:S(2)}, u32[]{:S(2)}) collective-permute-start(bf16[384,2048]{1,0:T(8,128)(2,1)S(1)} %get-tuple-element.61.held_a), channel_id=1, source_target_pairs={{0,2},{1,7},{2,0},{3,5},{4,6},{5,3},{6,4},{7,1},{8,10},{9,15},{10,... | collective-permute-start | bytes 4718600 | tf_op jit(solution)/shard_map/ppermute | solution.py:529
  52.8 7.9 %keep0.1 = (f32[512,1024]{1,0:T(8,128)S(1)}, f32[8,128]{1,0:T(8,128)S(1)}) custom-call(s32[128]{0:T(128)S(1)} %pad_add_fusion.3.order, bf16[3,1024,1024]{2,1,0:T(8,128)(2,1)} %left.7, bf16[3,2048,1024]{2,1,0:T(8,128)(2,1)} %right.7, f32[8,128]{1,0:T(8,128)S(1)} %get-tuple-element.55._), custom_call_target="tpu_custom_call" | custom-call | flops 1000 | bytes 1000 | tf_op jit(solution)/shard_map/keep0/pallas_call | solution.py:312
  60.7 1.3 add.236
  62.0 1.0 copy-done
  63.0 2.3 %collective-permute-start.10 = (f32[256,1024]{1,0:T(8,128)}, f32[256,1024]{1,0:T(8,128)S(1)}, u32[]{:S(2)}, u32[]{:S(2)}) collective-permute-start(f32[256,1024]{1,0:T(8,128)} %get-tuple-element.60), channel_id=1, source_target_pairs={{0,96},{1,33},{2,98},{3,35},{4,100},{5,37},{6,102},{7,39},{8,104},... | collective-permute-start | bytes 3145736 | tf_op jit(solution)/shard_map/ppermute | solution.py:534
  65.3 7.9 %keep1.1 = (f32[512,1024]{1,0:T(8,128)S(1)}, f32[8,128]{1,0:T(8,128)S(1)}) custom-call(s32[128]{0:T(128)S(1)} %pad_add_fusion.3.order, bf16[3,1024,1024]{2,1,0:T(8,128)(2,1)} %left.7, bf16[3,2048,1024]{2,1,0:T(8,128)(2,1)} %right.7, f32[8,128]{1,0:T(8,128)S(1)} %get-tuple-element.63._), custom_call_target="tpu_custom_call" | custom-call | flops 1000 | bytes 1000 | tf_op jit(solution)/shard_map/keep1/pallas_call | solution.py:312
  73.2 2.2 %collective-permute-done.14.got_a = bf16[384,2048]{1,0:T(8,128)(2,1)S(1)} collective-permute-done((bf16[384,2048]{1,0:T(8,128)(2,1)S(1)}, bf16[384,2048]{1,0:T(8,128)(2,1)S(1)}, u32[]{:S(2)}, u32[]{:S(2)}) %collective-permute-start.14) | collective-permute-done | bytes 1572896 | tf_op jit(solution)/shard_map/ppermute | solution.py:529
  75.4 2.3 %join.5 = (bf16[768,2048]{1,0:T(8,128)(2,1)S(1)}, bf16[768,2048]{1,0:T(8,128)(2,1)}, f32[8,128]{1,0:T(8,128)S(1)}) custom-call(bf16[384,2048]{1,0:T(8,128)(2,1)S(1)} %get-tuple-element.61.held_a, bf16[384,2048]{1,0:T(8,128)(2,1)S(1)} %collective-permute-done.14.got_a, bf16[384,2048]{1,0:T(8,128)(2,1)S(1)} %get-tuple-element.62.held_b, ...), custom_call_target="tpu_custom_call" | custom-call | flops 1000 | bytes 1000 | tf_op jit(solution)/shard_map/join/pallas_call | solution.py:444
  77.8 0.5 collective-permute-start.16
  78.2 1.7 collective-permute-start.17
  79.9 0.3 add.238
  80.2 3.8 %collective-permute-start.20 = (f32[256,1024]{1,0:T(8,128)S(1)}, f32[256,1024]{1,0:T(8,128)S(1)}, u32[]{:S(2)}, u32[]{:S(2)}) collective-permute-start(f32[256,1024]{1,0:T(8,128)S(1)} %get-tuple-element.74), channel_id=1, source_target_pairs={{0,96},{1,33},{2,98},{3,35},{4,100},{5,37},{6,102},{7,39},{8,104},... | collective-permute-start | bytes 3145736 | tf_op jit(solution)/shard_map/ppermute | solution.py:534
  84.1 5.2 %collective-permute-done.10 = f32[256,1024]{1,0:T(8,128)S(1)} collective-permute-done((f32[256,1024]{1,0:T(8,128)}, f32[256,1024]{1,0:T(8,128)S(1)}, u32[]{:S(2)}, u32[]{:S(2)}) %collective-permute-start.10) | collective-permute-done | bytes 1048608 | tf_op jit(solution)/shard_map/ppermute | solution.py:534
  89.3 0.2 slice_add_fusion.3
  89.5 0.7 collective-permute-start.11
  90.1 16.3 %collective-permute-done.20 = f32[256,1024]{1,0:T(8,128)S(1)} collective-permute-done((f32[256,1024]{1,0:T(8,128)S(1)}, f32[256,1024]{1,0:T(8,128)S(1)}, u32[]{:S(2)}, u32[]{:S(2)}) %collective-permute-start.20) | collective-permute-done | bytes 1048608 | tf_op jit(solution)/shard_map/ppermute | solution.py:534
  106.5 0.2 slice_add_fusion.1
  106.6 1.5 collective-permute-start.21
  108.2 0.5 collective-permute-start.12
  108.8 13.3 %collective-permute-done.21 = f32[128,1024]{1,0:T(8,128)S(1)} collective-permute-done((f32[128,1024]{1,0:T(8,128)S(1)}, f32[128,1024]{1,0:T(8,128)S(1)}, u32[]{:S(2)}, u32[]{:S(2)}) %collective-permute-start.21) | collective-permute-done | bytes 524320 | tf_op jit(solution)/shard_map/ppermute | solution.py:534
  122.1 0.1 collective-permute-start.22
  122.2 4.9 %collective-permute-done.12 = f32[64,1024]{1,0:T(8,128)S(1)} collective-permute-done((f32[64,1024]{1,0:T(8,128)S(1)}, f32[64,1024]{1,0:T(8,128)S(1)}, u32[]{:S(2)}, u32[]{:S(2)}) %collective-permute-start.12) | collective-permute-done | bytes 262176 | tf_op jit(solution)/shard_map/ppermute | solution.py:534
  127.1 0.7 slice_add_fusion.10
  127.8 2.3 %collective-permute-start.13 = (f32[32,1024]{1,0:T(8,128)}, f32[32,1024]{1,0:T(8,128)S(1)}, u32[]{:S(2)}, u32[]{:S(2)}) collective-permute-start(f32[32,1024]{1,0:T(8,128)} %get-tuple-element.91), channel_id=1, source_target_pairs={{0,2},{1,7},{2,0},{3,5},{4,6},{5,3},{6,4},{7,1},{8,10},{9,15},{10,... | collective-permute-start | bytes 393224 | tf_op jit(solution)/shard_map/ppermute | solution.py:534
  130.1 0.7 slice_add_fusion.8
  130.8 3.5 %collective-permute-start.23 = (f32[32,1024]{1,0:T(8,128)}, f32[32,1024]{1,0:T(8,128)}, u32[]{:S(2)}, u32[]{:S(2)}) collective-permute-start(f32[32,1024]{1,0:T(8,128)} %get-tuple-element.93), channel_id=1, source_target_pairs={{0,8},{1,25},{2,10},{3,27},{4,12},{5,29},{6,14},{7,31},{8,0},{9,17... | collective-permute-start | bytes 393224 | tf_op jit(solution)/shard_map/ppermute | solution.py:534
  134.6 7.3 %grow_inverse.1 = (bf16[4,512,512]{2,1,0:T(8,128)(2,1)S(1)}, bf16[4,512,512]{2,1,0:T(8,128)(2,1)S(1)}, f32[8,128]{1,0:T(8,128)S(1)}) custom-call(s32[32]{0:T(128)S(1)} %pad_add_fusion.1.chips, bf16[768,2048]{1,0:T(8,128)(2,1)S(1)} %get-tuple-element.65.own_a.refs_0_.refs_2_, bf16[768,2048]{1,0:T(8,128)(2,1)} %collective-permute-done.16.got_a.refs_1_.refs_3_, ...), custom_call_target="tpu_custom_call" | custom-call | flops 1000 | bytes 1000 | tf_op jit(solution)/shard_map/grow_inverse/pallas_call | solution.py:148
  141.9 0.9 add.239
  142.8 2.2 %collective-permute-start.24 = (f32[16,1024]{1,0:T(8,128)S(1)}, f32[16,1024]{1,0:T(8,128)S(1)}, u32[]{:S(2)}, u32[]{:S(2)}) collective-permute-start(f32[16,1024]{1,0:T(8,128)S(1)} %get-tuple-element.76), channel_id=1, source_target_pairs={{0,24},{1,9},{2,26},{3,11},{4,28},{5,13},{6,30},{7,15},{8,16},{9,1... | collective-permute-start | bytes 196616 | tf_op jit(solution)/shard_map/ppermute | solution.py:534
  145.1 0.6 collective-permute-start.18
  145.6 2.0 %collective-permute-done.24 = f32[16,1024]{1,0:T(8,128)S(1)} collective-permute-done((f32[16,1024]{1,0:T(8,128)S(1)}, f32[16,1024]{1,0:T(8,128)S(1)}, u32[]{:S(2)}, u32[]{:S(2)}) %collective-permute-start.24) | collective-permute-done | bytes 65568 | tf_op jit(solution)/shard_map/ppermute | solution.py:534
  147.7 0.6 collective-permute-done.18
  148.3 0.7 solve0.1.refs_0_
  149.0 1.3 collective-permute-start.25
  150.3 21.1 %collective-permute-done.25.refs_1_ = f32[32,2048]{1,0:T(8,128)S(1)} collective-permute-done((f32[32,2048]{1,0:T(8,128)S(1)}, f32[32,2048]{1,0:T(8,128)S(1)}, u32[]{:S(2)}, u32[]{:S(2)}) %collective-permute-start.25) | collective-permute-done | bytes 262176 | tf_op jit(solution)/shard_map/ppermute | solution.py:591
  171.4 6.1 %solve1.1 = f32[16,2048]{1,0:T(8,128)} custom-call(s32[1]{0:T(128)} %bitcast.core, s32[32]{0:T(128)S(1)} %pad_add_fusion.1.chips, f32[16,2048]{1,0:T(8,128)S(1)} %maximum_subtract_fusion.right, f32[32,2048]{1,0:T(8,128)S(1)} %solve0.1.refs_0_, f32[32,2048]{1,0:T(8,128)S(1)} %collective-permute-done.25.refs_1_, ...), custom_call_target="tpu_custom_call" | custom-call | flops 1000 | bytes 1000 | tf_op jit(solution)/shard_map/solve1/pallas_call | solution.py:235
  (38 shorter events, 1.0 us)
Async XLA Ops:
  0.0 2.8 %collective-permute-start.1 = (bf16[64,2048]{1,0:T(8,128)(2,1)}, bf16[64,2048]{1,0:T(8,128)(2,1)S(1)}, u32[]{:S(2)}, u32[]{:S(2)}) collective-permute-start(bf16[64,2048]{1,0:T(8,128)(2,1)} %bitcast.10), channel_id=1, source_target_pairs={{1,0},{3,2},{5,4},{7,6},{9,8},{11,10},{13,12},{15,14},{17,16},{19,... | collective-permute-start | bytes 786440 | tf_op jit(solution)/shard_map/ppermute | solution.py:537
  0.7 5.4 %collective-permute-start = (bf16[64,2048]{1,0:T(8,128)(2,1)}, bf16[64,2048]{1,0:T(8,128)(2,1)S(1)}, u32[]{:S(2)}, u32[]{:S(2)}) collective-permute-start(bf16[64,2048]{1,0:T(8,128)(2,1)} %bitcast.11), channel_id=1, source_target_pairs={{0,96},{2,98},{4,100},{6,102},{8,104},{10,106},{12,108},{14,110},{... | collective-permute-start | bytes 786440 | tf_op jit(solution)/shard_map/ppermute | solution.py:536
  2.8 1.0 copy-start.2
  4.3 13.6 %collective-permute-start.3 = (bf16[64,2048]{1,0:T(8,128)(2,1)S(1)}, bf16[64,2048]{1,0:T(8,128)(2,1)S(1)}, u32[]{:S(2)}, u32[]{:S(2)}) collective-permute-start(bf16[64,2048]{1,0:T(8,128)(2,1)S(1)} %get-tuple-element.44.held), channel_id=1, source_target_pairs={{0,96},{2,98},{4,100},{6,102},{8,104},{10,106},{12,108},{14,110},{... | collective-permute-start | bytes 786440 | tf_op jit(solution)/shard_map/ppermute | solution.py:539
  6.0 0.9 copy-start.3
  7.6 12.8 %collective-permute-start.2 = (bf16[64,2048]{1,0:T(8,128)(2,1)S(1)}, bf16[64,2048]{1,0:T(8,128)(2,1)S(1)}, u32[]{:S(2)}, u32[]{:S(2)}) collective-permute-start(bf16[64,2048]{1,0:T(8,128)(2,1)S(1)} %get-tuple-element.43.held), channel_id=1, source_target_pairs={{0,32},{1,33},{2,34},{3,35},{4,36},{5,37},{6,38},{7,39},{8,40},{9,... | collective-permute-start | bytes 786440 | tf_op jit(solution)/shard_map/ppermute | solution.py:541
  18.4 5.2 %collective-permute-start.4 = (bf16[64,2048]{1,0:T(8,128)(2,1)S(1)}, bf16[64,2048]{1,0:T(8,128)(2,1)S(1)}, u32[]{:S(2)}, u32[]{:S(2)}) collective-permute-start(bf16[64,2048]{1,0:T(8,128)(2,1)S(1)} %get-tuple-element.47.under), channel_id=1, source_target_pairs={{0,32},{2,34},{4,36},{6,38},{8,40},{10,42},{12,44},{14,46},{16,48}... | collective-permute-start | bytes 786440 | tf_op jit(solution)/shard_map/ppermute | solution.py:544
  25.2 6.7 %collective-permute-start.5 = (bf16[96,2048]{1,0:T(8,128)(2,1)S(1)}, bf16[96,2048]{1,0:T(8,128)(2,1)S(1)}, u32[]{:S(2)}, u32[]{:S(2)}) collective-permute-start(bf16[96,2048]{1,0:T(8,128)(2,1)S(1)} %get-tuple-element.48.held_a), channel_id=1, source_target_pairs={{0,8},{1,25},{2,10},{3,27},{4,12},{5,29},{6,14},{7,31},{8,0},{9,17... | collective-permute-start | bytes 1179656 | tf_op jit(solution)/shard_map/ppermute | solution.py:529
  25.5 7.8 %collective-permute-start.6 = (bf16[96,2048]{1,0:T(8,128)(2,1)S(1)}, bf16[96,2048]{1,0:T(8,128)(2,1)S(1)}, u32[]{:S(2)}, u32[]{:S(2)}) collective-permute-start(bf16[96,2048]{1,0:T(8,128)(2,1)S(1)} %get-tuple-element.49.held_b), channel_id=1, source_target_pairs={{0,2},{1,7},{2,0},{3,5},{4,6},{5,3},{6,4},{7,1},{8,10},{9,15},{10,... | collective-permute-start | bytes 1179656 | tf_op jit(solution)/shard_map/ppermute | solution.py:529
  27.9 32.7 %collective-permute-start.9 = (f32[512,1024]{1,0:T(8,128)S(1)}, f32[512,1024]{1,0:T(8,128)S(1)}, u32[]{:S(2)}, u32[]{:S(2)}) collective-permute-start(f32[512,1024]{1,0:T(8,128)S(1)} %get-tuple-element.57), channel_id=1, source_target_pairs={{0,32},{1,97},{2,34},{3,99},{4,36},{5,101},{6,38},{7,103},{8,40},{... | collective-permute-start | bytes 6291464 | tf_op jit(solution)/shard_map/ppermute | solution.py:534
  34.9 13.8 %collective-permute-start.7 = (bf16[192,2048]{1,0:T(8,128)(2,1)S(1)}, bf16[192,2048]{1,0:T(8,128)(2,1)S(1)}, u32[]{:S(2)}, u32[]{:S(2)}) collective-permute-start(bf16[192,2048]{1,0:T(8,128)(2,1)S(1)} %get-tuple-element.51.held_a), channel_id=1, source_target_pairs={{0,24},{1,9},{2,26},{3,11},{4,28},{5,13},{6,30},{7,15},{8,16},{9,1... | collective-permute-start | bytes 2359304 | tf_op jit(solution)/shard_map/ppermute | solution.py:529
  35.9 13.8 %collective-permute-start.8 = (bf16[192,2048]{1,0:T(8,128)(2,1)S(1)}, bf16[192,2048]{1,0:T(8,128)(2,1)S(1)}, u32[]{:S(2)}, u32[]{:S(2)}) collective-permute-start(bf16[192,2048]{1,0:T(8,128)(2,1)S(1)} %get-tuple-element.52.held_b), channel_id=1, source_target_pairs={{0,6},{1,3},{2,4},{3,1},{4,2},{5,7},{6,0},{7,5},{8,14},{9,11},{10,... | collective-permute-start | bytes 2359304 | tf_op jit(solution)/shard_map/ppermute | solution.py:529
  46.2 33.8 %collective-permute-start.19 = (f32[512,1024]{1,0:T(8,128)}, f32[512,1024]{1,0:T(8,128)S(1)}, u32[]{:S(2)}, u32[]{:S(2)}) collective-permute-start(f32[512,1024]{1,0:T(8,128)} %get-tuple-element.71), channel_id=1, source_target_pairs={{0,32},{1,97},{2,34},{3,99},{4,36},{5,101},{6,38},{7,103},{8,40},{... | collective-permute-start | bytes 6291464 | tf_op jit(solution)/shard_map/ppermute | solution.py:534
  50.2 25.2 %collective-permute-start.14 = (bf16[384,2048]{1,0:T(8,128)(2,1)S(1)}, bf16[384,2048]{1,0:T(8,128)(2,1)S(1)}, u32[]{:S(2)}, u32[]{:S(2)}) collective-permute-start(bf16[384,2048]{1,0:T(8,128)(2,1)S(1)} %get-tuple-element.61.held_a), channel_id=1, source_target_pairs={{0,2},{1,7},{2,0},{3,5},{4,6},{5,3},{6,4},{7,1},{8,10},{9,15},{10,... | collective-permute-start | bytes 4718600 | tf_op jit(solution)/shard_map/ppermute | solution.py:529
  52.8 22.6 %collective-permute-start.15 = (bf16[384,2048]{1,0:T(8,128)(2,1)S(1)}, bf16[384,2048]{1,0:T(8,128)(2,1)S(1)}, u32[]{:S(2)}, u32[]{:S(2)}) collective-permute-start(bf16[384,2048]{1,0:T(8,128)(2,1)S(1)} %get-tuple-element.62.held_b), channel_id=1, source_target_pairs={{0,8},{1,25},{2,10},{3,27},{4,12},{5,29},{6,14},{7,31},{8,0},{9,17... | collective-permute-start | bytes 4718600 | tf_op jit(solution)/shard_map/ppermute | solution.py:529
  62.0 1.0 copy-start
  63.0 26.3 %collective-permute-start.10 = (f32[256,1024]{1,0:T(8,128)}, f32[256,1024]{1,0:T(8,128)S(1)}, u32[]{:S(2)}, u32[]{:S(2)}) collective-permute-start(f32[256,1024]{1,0:T(8,128)} %get-tuple-element.60), channel_id=1, source_target_pairs={{0,96},{1,33},{2,98},{3,35},{4,100},{5,37},{6,102},{7,39},{8,104},... | collective-permute-start | bytes 3145736 | tf_op jit(solution)/shard_map/ppermute | solution.py:534
  77.8 56.8 %collective-permute-start.16 = (bf16[768,2048]{1,0:T(8,128)(2,1)S(1)}, bf16[768,2048]{1,0:T(8,128)(2,1)}, u32[]{:S(2)}, u32[]{:S(2)}) collective-permute-start(bf16[768,2048]{1,0:T(8,128)(2,1)S(1)} %get-tuple-element.65.own_a.refs_0_.refs_2_), channel_id=1, source_target_pairs={{0,6},{1,3},{2,4},{3,1},{4,2},{5,7},{6,0},{7,5},{8,14},{9,11},{10,... | collective-permute-start | bytes 9437192 | tf_op jit(solution)/shard_map/ppermute | solution.py:529
  78.2 56.4 %collective-permute-start.17 = (bf16[768,2048]{1,0:T(8,128)(2,1)}, bf16[768,2048]{1,0:T(8,128)(2,1)}, u32[]{:S(2)}, u32[]{:S(2)}) collective-permute-start(bf16[768,2048]{1,0:T(8,128)(2,1)} %get-tuple-element.66.own_b.refs_2_.refs_4_), channel_id=1, source_target_pairs={{0,24},{1,9},{2,26},{3,11},{4,28},{5,13},{6,30},{7,15},{8,16},{9,1... | collective-permute-start | bytes 9437192 | tf_op jit(solution)/shard_map/ppermute | solution.py:529
  79.9 9.3 %copy-start.1 = (f32[256,1024]{1,0:T(8,128)S(1)}, f32[256,1024]{1,0:T(8,128)}, u32[]{:S(2)}) copy-start(f32[256,1024]{1,0:T(8,128)} %copy-done) | copy-start | bytes 3145732
  80.2 26.2 %collective-permute-start.20 = (f32[256,1024]{1,0:T(8,128)S(1)}, f32[256,1024]{1,0:T(8,128)S(1)}, u32[]{:S(2)}, u32[]{:S(2)}) collective-permute-start(f32[256,1024]{1,0:T(8,128)S(1)} %get-tuple-element.74), channel_id=1, source_target_pairs={{0,96},{1,33},{2,98},{3,35},{4,100},{5,37},{6,102},{7,39},{8,104},... | collective-permute-start | bytes 3145736 | tf_op jit(solution)/shard_map/ppermute | solution.py:534
  89.5 18.7 %collective-permute-start.11 = (f32[128,1024]{1,0:T(8,128)S(1)}, f32[128,1024]{1,0:T(8,128)S(1)}, u32[]{:S(2)}, u32[]{:S(2)}) collective-permute-start(f32[128,1024]{1,0:T(8,128)S(1)} %get-tuple-element.84), channel_id=1, source_target_pairs={{0,8},{1,25},{2,10},{3,27},{4,12},{5,29},{6,14},{7,31},{8,0},{9,17... | collective-permute-start | bytes 1572872 | tf_op jit(solution)/shard_map/ppermute | solution.py:534
  106.6 15.4 %collective-permute-start.21 = (f32[128,1024]{1,0:T(8,128)S(1)}, f32[128,1024]{1,0:T(8,128)S(1)}, u32[]{:S(2)}, u32[]{:S(2)}) collective-permute-start(f32[128,1024]{1,0:T(8,128)S(1)} %get-tuple-element.86), channel_id=1, source_target_pairs={{0,2},{1,7},{2,0},{3,5},{4,6},{5,3},{6,4},{7,1},{8,10},{9,15},{10,... | collective-permute-start | bytes 1572872 | tf_op jit(solution)/shard_map/ppermute | solution.py:534
  108.2 18.9 %collective-permute-start.12 = (f32[64,1024]{1,0:T(8,128)S(1)}, f32[64,1024]{1,0:T(8,128)S(1)}, u32[]{:S(2)}, u32[]{:S(2)}) collective-permute-start(f32[64,1024]{1,0:T(8,128)S(1)} %get-tuple-element.88), channel_id=1, source_target_pairs={{0,24},{1,9},{2,26},{3,11},{4,28},{5,13},{6,30},{7,15},{8,16},{9,1... | collective-permute-start | bytes 786440 | tf_op jit(solution)/shard_map/ppermute | solution.py:534
  122.1 8.0 %collective-permute-start.22 = (f32[64,1024]{1,0:T(8,128)S(1)}, f32[64,1024]{1,0:T(8,128)S(1)}, u32[]{:S(2)}, u32[]{:S(2)}) collective-permute-start(f32[64,1024]{1,0:T(8,128)S(1)} %get-tuple-element.90), channel_id=1, source_target_pairs={{0,6},{1,3},{2,4},{3,1},{4,2},{5,7},{6,0},{7,5},{8,14},{9,11},{10,... | collective-permute-start | bytes 786440 | tf_op jit(solution)/shard_map/ppermute | solution.py:534
  127.8 17.3 %collective-permute-start.13 = (f32[32,1024]{1,0:T(8,128)}, f32[32,1024]{1,0:T(8,128)S(1)}, u32[]{:S(2)}, u32[]{:S(2)}) collective-permute-start(f32[32,1024]{1,0:T(8,128)} %get-tuple-element.91), channel_id=1, source_target_pairs={{0,2},{1,7},{2,0},{3,5},{4,6},{5,3},{6,4},{7,1},{8,10},{9,15},{10,... | collective-permute-start | bytes 393224 | tf_op jit(solution)/shard_map/ppermute | solution.py:534
  130.8 11.1 %collective-permute-start.23 = (f32[32,1024]{1,0:T(8,128)}, f32[32,1024]{1,0:T(8,128)}, u32[]{:S(2)}, u32[]{:S(2)}) collective-permute-start(f32[32,1024]{1,0:T(8,128)} %get-tuple-element.93), channel_id=1, source_target_pairs={{0,8},{1,25},{2,10},{3,27},{4,12},{5,29},{6,14},{7,31},{8,0},{9,17... | collective-permute-start | bytes 393224 | tf_op jit(solution)/shard_map/ppermute | solution.py:534
  134.6 13.7 %copy-start.4 = (bf16[16,2048]{1,0:T(8,128)(2,1)S(1)}, bf16[16,2048]{1,0:T(8,128)(2,1)}, u32[]{:S(2)}) copy-start(bf16[16,2048]{1,0:T(8,128)(2,1)} %param.7) | copy-start | bytes 196612
  142.8 4.8 %collective-permute-start.24 = (f32[16,1024]{1,0:T(8,128)S(1)}, f32[16,1024]{1,0:T(8,128)S(1)}, u32[]{:S(2)}, u32[]{:S(2)}) collective-permute-start(f32[16,1024]{1,0:T(8,128)S(1)} %get-tuple-element.76), channel_id=1, source_target_pairs={{0,24},{1,9},{2,26},{3,11},{4,28},{5,13},{6,30},{7,15},{8,16},{9,1... | collective-permute-start | bytes 196616 | tf_op jit(solution)/shard_map/ppermute | solution.py:534
  145.1 3.2 %collective-permute-start.18 = (f32[16,1024]{1,0:T(8,128)S(1)}, f32[16,1024]{1,0:T(8,128)S(1)}, u32[]{:S(2)}, u32[]{:S(2)}) collective-permute-start(f32[16,1024]{1,0:T(8,128)S(1)} %get-tuple-element.69), channel_id=1, source_target_pairs={{0,6},{1,3},{2,4},{3,1},{4,2},{5,7},{6,0},{7,5},{8,14},{9,11},{10,... | collective-permute-start | bytes 196616 | tf_op jit(solution)/shard_map/ppermute | solution.py:534
  149.0 22.4 %collective-permute-start.25 = (f32[32,2048]{1,0:T(8,128)S(1)}, f32[32,2048]{1,0:T(8,128)S(1)}, u32[]{:S(2)}, u32[]{:S(2)}) collective-permute-start(f32[32,2048]{1,0:T(8,128)S(1)} %solve0.1.refs_0_), channel_id=1, source_target_pairs={{0,1},{2,3},{4,5},{6,7},{8,9},{10,11},{12,13},{14,15},{16,17},{18,... | collective-permute-start | bytes 786440 | tf_op jit(solution)/shard_map/ppermute | solution.py:591

commit v10 on v9

--- a/solution.py
+++ b/solution.py
@@ -577,7 +577,7 @@
     keeps = [keep0, keep1]
     for step in range(1, 5):
         for n in range(2):
-            if step == 4:
+            if step == 3:
                 send, keeps[n], _ = add(keeps[n], come[n], token)
             else:
                 middle = keeps[n].shape[0] // 2

time: 178 us -> 181 us (1.017)
  the two profiles are of different devices: /device:TPU:81 before, /device:TPU:1 now
where the time goes in v10:
time: 181 us; the launch traced here: 179 us
  waiting for transfers between devices  91.9 us (51%)
  Pallas kernels  57 us (31%)
  starting transfers between devices  22.9 us (13%)
  local copies, waits for them, and re-layouts  4.37 us (2%)
  other arithmetic  2.55 us (1%)
    ppermute x12, waiting for transfers between devices, sum_step(): lax.ppermute(send, EVERY, partner_pairs(PARTS[n][2][step // 2], step % 2...  55.4 us
    pallas_call x4, Pallas kernels, product(): pl.pallas_call(functools.partial(product_kernel, parts, half), out_shape=...  32.7 us
    ppermute x1, waiting for transfers between devices, per_device(): other = lax.ppermute(first, 'pcol', [(0, 1)])  19.2 us
    ppermute x8, starting transfers between devices, gather_step(): lax.ppermute(held[n], EVERY, partner_pairs(GATHER[n][step // 2], step % 2...  11.6 us
    pallas_call x1, Pallas kernels, grow(): pl.pallas_call(grow_kernel, out_shape=(inverse, inverse, TOKEN), in_specs...  7.3 us
    ppermute x8, waiting for transfers between devices, gather_step(): lax.ppermute(held[n], EVERY, partner_pairs(GATHER[n][step // 2], step % 2...  7.05 us
    pallas_call x2, Pallas kernels, solve_call(): pl.pallas_call(functools.partial(solve_kernel, first), out_shape=jax.Shap...  6.81 us
    ppermute x1, waiting for transfers between devices, per_device(): lax.ppermute(under, EVERY, along_z((0, 0, 1, 0), (3, 0, 2, 0), (1, 1, 0,...  5.81 us
  transfers between devices with their start and end apart: 26, of which 18 were waited for; matrix products, arithmetic and copies ran while one was open for 2% of the time, Pallas kernels for 26%

profile of v10, /device:TPU:1, one launch (start us, length us, event | category | flops | bytes accessed | tf_op | source)
XLA Modules:
  0.0 179.3 jit_solution(1581302312332934575)
XLA Ops:
  0.0 3.3 %collective-permute-start.1 = (bf16[64,2048]{1,0:T(8,128)(2,1)}, bf16[64,2048]{1,0:T(8,128)(2,1)S(1)}, u32[]{:S(2)}, u32[]{:S(2)}) collective-permute-start(bf16[64,2048]{1,0:T(8,128)(2,1)} %bitcast.10), channel_id=1, source_target_pairs={{1,0},{3,2},{5,4},{7,6},{9,8},{11,10},{13,12},{15,14},{17,16},{19,... | collective-permute-start | bytes 786440 | tf_op jit(solution)/shard_map/ppermute | solution.py:537
  3.3 1.3 collective-permute-start
  5.0 1.0 copy-done.2
  5.9 0.6 below0.1
  6.5 0.7 collective-permute-start.3
  7.3 0.1 add.166
  7.4 0.1 add.170
  7.5 4.3 %collective-permute-done.got = bf16[64,2048]{1,0:T(8,128)(2,1)S(1)} collective-permute-done((bf16[64,2048]{1,0:T(8,128)(2,1)}, bf16[64,2048]{1,0:T(8,128)(2,1)S(1)}, u32[]{:S(2)}, u32[]{:S(2)}) %collective-permute-start) | collective-permute-done | bytes 262176 | tf_op jit(solution)/shard_map/ppermute | solution.py:536
  11.9 0.9 copy-done.3
  12.8 0.6 strip1.1
  13.5 7.9 %send0.1 = (f32[512,1024]{1,0:T(8,128)S(1)}, f32[8,128]{1,0:T(8,128)S(1)}) custom-call(s32[128]{0:T(128)S(1)} %pad_add_fusion.3.order, bf16[3,1024,1024]{2,1,0:T(8,128)(2,1)} %left.7, bf16[3,2048,1024]{2,1,0:T(8,128)(2,1)} %right.7, f32[8,128]{1,0:T(8,128)S(1)} %get-tuple-element.45._), custom_call_target="tpu_custom_call" | custom-call | flops 1000 | bytes 1000 | tf_op jit(solution)/shard_map/send0/pallas_call | solution.py:312
  21.4 0.6 below1.1
  22.0 1.3 collective-permute-start.4
  23.3 5.8 %collective-permute-done.4.got_under = bf16[64,2048]{1,0:T(8,128)(2,1)S(1)} collective-permute-done((bf16[64,2048]{1,0:T(8,128)(2,1)S(1)}, bf16[64,2048]{1,0:T(8,128)(2,1)S(1)}, u32[]{:S(2)}, u32[]{:S(2)}) %collective-permute-start.4) | collective-permute-done | bytes 262176 | tf_op jit(solution)/shard_map/ppermute | solution.py:544
  29.1 1.5 pack.1
  30.6 2.9 %collective-permute-start.5 = (bf16[96,2048]{1,0:T(8,128)(2,1)S(1)}, bf16[96,2048]{1,0:T(8,128)(2,1)S(1)}, u32[]{:S(2)}, u32[]{:S(2)}) collective-permute-start(bf16[96,2048]{1,0:T(8,128)(2,1)S(1)} %get-tuple-element.48.held_a), channel_id=1, source_target_pairs={{0,8},{1,25},{2,10},{3,27},{4,12},{5,29},{6,14},{7,31},{8,0},{9,17... | collective-permute-start | bytes 1179656 | tf_op jit(solution)/shard_map/ppermute | solution.py:529
  33.5 2.5 %collective-permute-start.6 = (bf16[96,2048]{1,0:T(8,128)(2,1)S(1)}, bf16[96,2048]{1,0:T(8,128)(2,1)S(1)}, u32[]{:S(2)}, u32[]{:S(2)}) collective-permute-start(bf16[96,2048]{1,0:T(8,128)(2,1)S(1)} %get-tuple-element.49.held_b), channel_id=1, source_target_pairs={{0,2},{1,7},{2,0},{3,5},{4,6},{5,3},{6,4},{7,1},{8,10},{9,15},{10,... | collective-permute-start | bytes 1179656 | tf_op jit(solution)/shard_map/ppermute | solution.py:529
  36.0 2.7 %collective-permute-done.5.got_a = bf16[96,2048]{1,0:T(8,128)(2,1)S(1)} collective-permute-done((bf16[96,2048]{1,0:T(8,128)(2,1)S(1)}, bf16[96,2048]{1,0:T(8,128)(2,1)S(1)}, u32[]{:S(2)}, u32[]{:S(2)}) %collective-permute-start.5) | collective-permute-done | bytes 393248 | tf_op jit(solution)/shard_map/ppermute | solution.py:529
  38.7 2.7 %collective-permute-done.6.got_b = bf16[96,2048]{1,0:T(8,128)(2,1)S(1)} collective-permute-done((bf16[96,2048]{1,0:T(8,128)(2,1)S(1)}, bf16[96,2048]{1,0:T(8,128)(2,1)S(1)}, u32[]{:S(2)}, u32[]{:S(2)}) %collective-permute-start.6) | collective-permute-done | bytes 393248 | tf_op jit(solution)/shard_map/ppermute | solution.py:529
  41.4 1.6 join.3
  43.0 0.4 collective-permute-start.8
  43.4 9.1 %send1.1 = (f32[512,1024]{1,0:T(8,128)}, f32[8,128]{1,0:T(8,128)S(1)}) custom-call(s32[128]{0:T(128)S(1)} %pad_add_fusion.3.order, bf16[3,1024,1024]{2,1,0:T(8,128)(2,1)} %left.7, bf16[3,2048,1024]{2,1,0:T(8,128)(2,1)} %right.7, f32[8,128]{1,0:T(8,128)S(1)} %get-tuple-element.53._), custom_call_target="tpu_custom_call" | custom-call | flops 1000 | bytes 1000 | tf_op jit(solution)/shard_map/send1/pallas_call | solution.py:312
  52.6 1.6 collective-permute-done.7.got_a
  54.1 0.1 collective-permute-done.8.got_b
  54.2 0.5 join.4
  54.8 2.6 %collective-permute-start.13 = (bf16[384,2048]{1,0:T(8,128)(2,1)S(1)}, bf16[384,2048]{1,0:T(8,128)(2,1)S(1)}, u32[]{:S(2)}, u32[]{:S(2)}) collective-permute-start(bf16[384,2048]{1,0:T(8,128)(2,1)S(1)} %get-tuple-element.61.held_a), channel_id=1, source_target_pairs={{0,2},{1,7},{2,0},{3,5},{4,6},{5,3},{6,4},{7,1},{8,10},{9,15},{10,... | collective-permute-start | bytes 4718600 | tf_op jit(solution)/shard_map/ppermute | solution.py:529
  57.3 0.5 collective-permute-start.14
  57.9 0.7 collective-permute-start.19
  58.6 7.9 %keep0.1 = (f32[512,1024]{1,0:T(8,128)S(1)}, f32[8,128]{1,0:T(8,128)S(1)}) custom-call(s32[128]{0:T(128)S(1)} %pad_add_fusion.3.order, bf16[3,1024,1024]{2,1,0:T(8,128)(2,1)} %left.7, bf16[3,2048,1024]{2,1,0:T(8,128)(2,1)} %right.7, f32[8,128]{1,0:T(8,128)S(1)} %get-tuple-element.55._), custom_call_target="tpu_custom_call" | custom-call | flops 1000 | bytes 1000 | tf_op jit(solution)/shard_map/keep0/pallas_call | solution.py:312
  66.5 3.0 %collective-permute-done.9.got = f32[512,1024]{1,0:T(8,128)S(1)} collective-permute-done((f32[512,1024]{1,0:T(8,128)S(1)}, f32[512,1024]{1,0:T(8,128)S(1)}, u32[]{:S(2)}, u32[]{:S(2)}) %collective-permute-start.9) | collective-permute-done | bytes 2097184 | tf_op jit(solution)/shard_map/ppermute | solution.py:534
  69.5 0.3 add.242
  69.8 1.0 copy-done
  70.8 1.0 copy-done.5
  71.8 7.9 %keep1.1 = (f32[512,1024]{1,0:T(8,128)S(1)}, f32[8,128]{1,0:T(8,128)S(1)}) custom-call(s32[128]{0:T(128)S(1)} %pad_add_fusion.3.order, bf16[3,1024,1024]{2,1,0:T(8,128)(2,1)} %left.7, bf16[3,2048,1024]{2,1,0:T(8,128)(2,1)} %right.7, f32[8,128]{1,0:T(8,128)S(1)} %get-tuple-element.63._), custom_call_target="tpu_custom_call" | custom-call | flops 1000 | bytes 1000 | tf_op jit(solution)/shard_map/keep1/pallas_call | solution.py:312
  79.7 2.3 %join.5 = (bf16[768,2048]{1,0:T(8,128)(2,1)S(1)}, bf16[768,2048]{1,0:T(8,128)(2,1)}, f32[8,128]{1,0:T(8,128)S(1)}) custom-call(bf16[384,2048]{1,0:T(8,128)(2,1)S(1)} %get-tuple-element.61.held_a, bf16[384,2048]{1,0:T(8,128)(2,1)S(1)} %collective-permute-done.13.got_a, bf16[384,2048]{1,0:T(8,128)(2,1)S(1)} %get-tuple-element.62.held_b, ...), custom_call_target="tpu_custom_call" | custom-call | flops 1000 | bytes 1000 | tf_op jit(solution)/shard_map/join/pallas_call | solution.py:444
  82.1 1.2 collective-permute-start.15
  83.3 1.4 collective-permute-start.16
  84.7 7.7 %collective-permute-done.19.got = f32[512,1024]{1,0:T(8,128)S(1)} collective-permute-done((f32[512,1024]{1,0:T(8,128)}, f32[512,1024]{1,0:T(8,128)S(1)}, u32[]{:S(2)}, u32[]{:S(2)}) %collective-permute-start.19) | collective-permute-done | bytes 2097184 | tf_op jit(solution)/shard_map/ppermute | solution.py:534
  92.4 0.3 add.244
  92.7 0.1 collective-permute-start.20
  92.8 14.9 %collective-permute-done.10 = f32[256,1024]{1,0:T(8,128)S(1)} collective-permute-done((f32[256,1024]{1,0:T(8,128)S(1)}, f32[256,1024]{1,0:T(8,128)S(1)}, u32[]{:S(2)}, u32[]{:S(2)}) %collective-permute-start.10) | collective-permute-done | bytes 1048608 | tf_op jit(solution)/shard_map/ppermute | solution.py:534
  107.7 0.1 slice_add_fusion.3
  107.8 0.9 collective-permute-start.11
  108.7 10.2 %collective-permute-done.20 = f32[256,1024]{1,0:T(8,128)S(1)} collective-permute-done((f32[256,1024]{1,0:T(8,128)S(1)}, f32[256,1024]{1,0:T(8,128)S(1)}, u32[]{:S(2)}, u32[]{:S(2)}) %collective-permute-start.20) | collective-permute-done | bytes 1048608 | tf_op jit(solution)/shard_map/ppermute | solution.py:534
  118.9 0.2 slice_add_fusion.1
  119.1 0.3 collective-permute-start.21
  119.4 3.9 %collective-permute-done.11 = f32[128,1024]{1,0:T(8,128)S(1)} collective-permute-done((f32[128,1024]{1,0:T(8,128)S(1)}, f32[128,1024]{1,0:T(8,128)S(1)}, u32[]{:S(2)}, u32[]{:S(2)}) %collective-permute-start.11) | collective-permute-done | bytes 524320 | tf_op jit(solution)/shard_map/ppermute | solution.py:534
  123.2 0.8 slice_add_fusion.6
  124.0 6.7 %collective-permute-done.21 = f32[128,1024]{1,0:T(8,128)S(1)} collective-permute-done((f32[128,1024]{1,0:T(8,128)S(1)}, f32[128,1024]{1,0:T(8,128)S(1)}, u32[]{:S(2)}, u32[]{:S(2)}) %collective-permute-start.21) | collective-permute-done | bytes 524320 | tf_op jit(solution)/shard_map/ppermute | solution.py:534
  130.7 0.9 slice_add_fusion.4
  131.9 7.3 %grow_inverse.1 = (bf16[4,512,512]{2,1,0:T(8,128)(2,1)S(1)}, bf16[4,512,512]{2,1,0:T(8,128)(2,1)S(1)}, f32[8,128]{1,0:T(8,128)S(1)}) custom-call(s32[32]{0:T(128)S(1)} %pad_add_fusion.1.chips, bf16[768,2048]{1,0:T(8,128)(2,1)S(1)} %get-tuple-element.65.own_a.refs_0_.refs_2_, bf16[768,2048]{1,0:T(8,128)(2,1)} %collective-permute-done.15.got_a.refs_1_.refs_3_, ...), custom_call_target="tpu_custom_call" | custom-call | flops 1000 | bytes 1000 | tf_op jit(solution)/shard_map/grow_inverse/pallas_call | solution.py:148
  139.2 0.9 collective-permute-done.22.got
  140.1 1.0 add.245
  141.1 1.1 collective-permute-start.23
  142.3 1.0 add.243
  143.3 3.1 %collective-permute-done.23 = f32[32,1024]{1,0:T(8,128)S(1)} collective-permute-done((f32[32,1024]{1,0:T(8,128)S(1)}, f32[32,1024]{1,0:T(8,128)S(1)}, u32[]{:S(2)}, u32[]{:S(2)}) %collective-permute-start.23) | collective-permute-done | bytes 131104 | tf_op jit(solution)/shard_map/ppermute | solution.py:534
  146.5 1.8 %collective-permute-done.17 = f32[32,1024]{1,0:T(8,128)S(1)} collective-permute-done((f32[32,1024]{1,0:T(8,128)S(1)}, f32[32,1024]{1,0:T(8,128)S(1)}, u32[]{:S(2)}, u32[]{:S(2)}) %collective-permute-start.17) | collective-permute-done | bytes 131104 | tf_op jit(solution)/shard_map/ppermute | solution.py:534
  148.4 0.1 collective-permute-start.18
  148.5 1.6 collective-permute-done.24
  150.1 1.6 collective-permute-done.18
  151.7 0.7 solve0.1.refs_0_
  152.4 1.3 collective-permute-start.25
  153.7 19.2 %collective-permute-done.25.refs_1_ = f32[32,2048]{1,0:T(8,128)S(1)} collective-permute-done((f32[32,2048]{1,0:T(8,128)S(1)}, f32[32,2048]{1,0:T(8,128)S(1)}, u32[]{:S(2)}, u32[]{:S(2)}) %collective-permute-start.25) | collective-permute-done | bytes 262176 | tf_op jit(solution)/shard_map/ppermute | solution.py:591
  173.0 6.1 %solve1.1 = f32[16,2048]{1,0:T(8,128)} custom-call(s32[1]{0:T(128)} %bitcast.core, s32[32]{0:T(128)S(1)} %pad_add_fusion.1.chips, f32[16,2048]{1,0:T(8,128)S(1)} %maximum_subtract_fusion.right, f32[32,2048]{1,0:T(8,128)S(1)} %solve0.1.refs_0_, f32[32,2048]{1,0:T(8,128)S(1)} %collective-permute-done.25.refs_1_, ...), custom_call_target="tpu_custom_call" | custom-call | flops 1000 | bytes 1000 | tf_op jit(solution)/shard_map/solve1/pallas_call | solution.py:235
  (44 shorter events, 1.2 us)
Async XLA Ops:
  0.0 5.0 %collective-permute-start.1 = (bf16[64,2048]{1,0:T(8,128)(2,1)}, bf16[64,2048]{1,0:T(8,128)(2,1)S(1)}, u32[]{:S(2)}, u32[]{:S(2)}) collective-permute-start(bf16[64,2048]{1,0:T(8,128)(2,1)} %bitcast.10), channel_id=1, source_target_pairs={{1,0},{3,2},{5,4},{7,6},{9,8},{11,10},{13,12},{15,14},{17,16},{19,... | collective-permute-start | bytes 786440 | tf_op jit(solution)/shard_map/ppermute | solution.py:537
  3.3 8.5 %collective-permute-start = (bf16[64,2048]{1,0:T(8,128)(2,1)}, bf16[64,2048]{1,0:T(8,128)(2,1)S(1)}, u32[]{:S(2)}, u32[]{:S(2)}) collective-permute-start(bf16[64,2048]{1,0:T(8,128)(2,1)} %bitcast.11), channel_id=1, source_target_pairs={{0,96},{2,98},{4,100},{6,102},{8,104},{10,106},{12,108},{14,110},{... | collective-permute-start | bytes 786440 | tf_op jit(solution)/shard_map/ppermute | solution.py:536
  5.0 1.0 copy-start.2
  6.5 14.9 %collective-permute-start.3 = (bf16[64,2048]{1,0:T(8,128)(2,1)S(1)}, bf16[64,2048]{1,0:T(8,128)(2,1)S(1)}, u32[]{:S(2)}, u32[]{:S(2)}) collective-permute-start(bf16[64,2048]{1,0:T(8,128)(2,1)S(1)} %get-tuple-element.44.held), channel_id=1, source_target_pairs={{0,96},{2,98},{4,100},{6,102},{8,104},{10,106},{12,108},{14,110},{... | collective-permute-start | bytes 786440 | tf_op jit(solution)/shard_map/ppermute | solution.py:539
  11.9 1.0 copy-start.3
  13.4 9.9 %collective-permute-start.2 = (bf16[64,2048]{1,0:T(8,128)(2,1)S(1)}, bf16[64,2048]{1,0:T(8,128)(2,1)S(1)}, u32[]{:S(2)}, u32[]{:S(2)}) collective-permute-start(bf16[64,2048]{1,0:T(8,128)(2,1)S(1)} %get-tuple-element.43.held), channel_id=1, source_target_pairs={{0,32},{1,33},{2,34},{3,35},{4,36},{5,37},{6,38},{7,39},{8,40},{9,... | collective-permute-start | bytes 786440 | tf_op jit(solution)/shard_map/ppermute | solution.py:541
  22.0 7.1 %collective-permute-start.4 = (bf16[64,2048]{1,0:T(8,128)(2,1)S(1)}, bf16[64,2048]{1,0:T(8,128)(2,1)S(1)}, u32[]{:S(2)}, u32[]{:S(2)}) collective-permute-start(bf16[64,2048]{1,0:T(8,128)(2,1)S(1)} %get-tuple-element.47.under), channel_id=1, source_target_pairs={{0,32},{2,34},{4,36},{6,38},{8,40},{10,42},{12,44},{14,46},{16,48}... | collective-permute-start | bytes 786440 | tf_op jit(solution)/shard_map/ppermute | solution.py:544
  30.6 8.1 %collective-permute-start.5 = (bf16[96,2048]{1,0:T(8,128)(2,1)S(1)}, bf16[96,2048]{1,0:T(8,128)(2,1)S(1)}, u32[]{:S(2)}, u32[]{:S(2)}) collective-permute-start(bf16[96,2048]{1,0:T(8,128)(2,1)S(1)} %get-tuple-element.48.held_a), channel_id=1, source_target_pairs={{0,8},{1,25},{2,10},{3,27},{4,12},{5,29},{6,14},{7,31},{8,0},{9,17... | collective-permute-start | bytes 1179656 | tf_op jit(solution)/shard_map/ppermute | solution.py:529
  33.5 7.8 %collective-permute-start.6 = (bf16[96,2048]{1,0:T(8,128)(2,1)S(1)}, bf16[96,2048]{1,0:T(8,128)(2,1)S(1)}, u32[]{:S(2)}, u32[]{:S(2)}) collective-permute-start(bf16[96,2048]{1,0:T(8,128)(2,1)S(1)} %get-tuple-element.49.held_b), channel_id=1, source_target_pairs={{0,2},{1,7},{2,0},{3,5},{4,6},{5,3},{6,4},{7,1},{8,10},{9,15},{10,... | collective-permute-start | bytes 1179656 | tf_op jit(solution)/shard_map/ppermute | solution.py:529
  42.9 11.2 %collective-permute-start.7 = (bf16[192,2048]{1,0:T(8,128)(2,1)S(1)}, bf16[192,2048]{1,0:T(8,128)(2,1)S(1)}, u32[]{:S(2)}, u32[]{:S(2)}) collective-permute-start(bf16[192,2048]{1,0:T(8,128)(2,1)S(1)} %get-tuple-element.51.held_a), channel_id=1, source_target_pairs={{0,24},{1,9},{2,26},{3,11},{4,28},{5,13},{6,30},{7,15},{8,16},{9,1... | collective-permute-start | bytes 2359304 | tf_op jit(solution)/shard_map/ppermute | solution.py:529
  43.0 11.2 %collective-permute-start.8 = (bf16[192,2048]{1,0:T(8,128)(2,1)S(1)}, bf16[192,2048]{1,0:T(8,128)(2,1)S(1)}, u32[]{:S(2)}, u32[]{:S(2)}) collective-permute-start(bf16[192,2048]{1,0:T(8,128)(2,1)S(1)} %get-tuple-element.52.held_b), channel_id=1, source_target_pairs={{0,6},{1,3},{2,4},{3,1},{4,2},{5,7},{6,0},{7,5},{8,14},{9,11},{10,... | collective-permute-start | bytes 2359304 | tf_op jit(solution)/shard_map/ppermute | solution.py:529
  43.4 26.1 %collective-permute-start.9 = (f32[512,1024]{1,0:T(8,128)S(1)}, f32[512,1024]{1,0:T(8,128)S(1)}, u32[]{:S(2)}, u32[]{:S(2)}) collective-permute-start(f32[512,1024]{1,0:T(8,128)S(1)} %get-tuple-element.57), channel_id=1, source_target_pairs={{0,32},{1,97},{2,34},{3,99},{4,36},{5,101},{6,38},{7,103},{8,40},{... | collective-permute-start | bytes 6291464 | tf_op jit(solution)/shard_map/ppermute | solution.py:534
  54.8 24.9 %collective-permute-start.13 = (bf16[384,2048]{1,0:T(8,128)(2,1)S(1)}, bf16[384,2048]{1,0:T(8,128)(2,1)S(1)}, u32[]{:S(2)}, u32[]{:S(2)}) collective-permute-start(bf16[384,2048]{1,0:T(8,128)(2,1)S(1)} %get-tuple-element.61.held_a), channel_id=1, source_target_pairs={{0,2},{1,7},{2,0},{3,5},{4,6},{5,3},{6,4},{7,1},{8,10},{9,15},{10,... | collective-permute-start | bytes 4718600 | tf_op jit(solution)/shard_map/ppermute | solution.py:529
  57.3 22.4 %collective-permute-start.14 = (bf16[384,2048]{1,0:T(8,128)(2,1)S(1)}, bf16[384,2048]{1,0:T(8,128)(2,1)S(1)}, u32[]{:S(2)}, u32[]{:S(2)}) collective-permute-start(bf16[384,2048]{1,0:T(8,128)(2,1)S(1)} %get-tuple-element.62.held_b), channel_id=1, source_target_pairs={{0,8},{1,25},{2,10},{3,27},{4,12},{5,29},{6,14},{7,31},{8,0},{9,17... | collective-permute-start | bytes 4718600 | tf_op jit(solution)/shard_map/ppermute | solution.py:529
  57.9 34.5 %collective-permute-start.19 = (f32[512,1024]{1,0:T(8,128)}, f32[512,1024]{1,0:T(8,128)S(1)}, u32[]{:S(2)}, u32[]{:S(2)}) collective-permute-start(f32[512,1024]{1,0:T(8,128)} %get-tuple-element.71), channel_id=1, source_target_pairs={{0,32},{1,97},{2,34},{3,99},{4,36},{5,101},{6,38},{7,103},{8,40},{... | collective-permute-start | bytes 6291464 | tf_op jit(solution)/shard_map/ppermute | solution.py:534
  69.8 1.0 copy-start
  70.8 1.0 copy-start.5
  79.7 5.0 %copy-start.6 = (f32[256,1024]{1,0:T(8,128)S(1)}, f32[256,1024]{1,0:T(8,128)}, u32[]{:S(2)}) copy-start(f32[256,1024]{1,0:T(8,128)} %copy-done.5) | copy-start | bytes 3145732
  82.1 49.9 %collective-permute-start.15 = (bf16[768,2048]{1,0:T(8,128)(2,1)S(1)}, bf16[768,2048]{1,0:T(8,128)(2,1)}, u32[]{:S(2)}, u32[]{:S(2)}) collective-permute-start(bf16[768,2048]{1,0:T(8,128)(2,1)S(1)} %get-tuple-element.65.own_a.refs_0_.refs_2_), channel_id=1, source_target_pairs={{0,6},{1,3},{2,4},{3,1},{4,2},{5,7},{6,0},{7,5},{8,14},{9,11},{10,... | collective-permute-start | bytes 9437192 | tf_op jit(solution)/shard_map/ppermute | solution.py:529
  83.3 48.6 %collective-permute-start.16 = (bf16[768,2048]{1,0:T(8,128)(2,1)}, bf16[768,2048]{1,0:T(8,128)(2,1)}, u32[]{:S(2)}, u32[]{:S(2)}) collective-permute-start(bf16[768,2048]{1,0:T(8,128)(2,1)} %get-tuple-element.66.own_b.refs_2_.refs_4_), channel_id=1, source_target_pairs={{0,24},{1,9},{2,26},{3,11},{4,28},{5,13},{6,30},{7,15},{8,16},{9,1... | collective-permute-start | bytes 9437192 | tf_op jit(solution)/shard_map/ppermute | solution.py:529
  84.7 23.0 %collective-permute-start.10 = (f32[256,1024]{1,0:T(8,128)S(1)}, f32[256,1024]{1,0:T(8,128)S(1)}, u32[]{:S(2)}, u32[]{:S(2)}) collective-permute-start(f32[256,1024]{1,0:T(8,128)S(1)} %copy-done.6), channel_id=1, source_target_pairs={{0,96},{1,33},{2,98},{3,35},{4,100},{5,37},{6,102},{7,39},{8,104},... | collective-permute-start | bytes 3145736 | tf_op jit(solution)/shard_map/ppermute | solution.py:534
  92.4 15.3 %copy-start.1 = (f32[256,1024]{1,0:T(8,128)S(1)}, f32[256,1024]{1,0:T(8,128)}, u32[]{:S(2)}) copy-start(f32[256,1024]{1,0:T(8,128)} %copy-done) | copy-start | bytes 3145732
  92.7 26.2 %collective-permute-start.20 = (f32[256,1024]{1,0:T(8,128)S(1)}, f32[256,1024]{1,0:T(8,128)S(1)}, u32[]{:S(2)}, u32[]{:S(2)}) collective-permute-start(f32[256,1024]{1,0:T(8,128)S(1)} %get-tuple-element.74), channel_id=1, source_target_pairs={{0,96},{1,33},{2,98},{3,35},{4,100},{5,37},{6,102},{7,39},{8,104},... | collective-permute-start | bytes 3145736 | tf_op jit(solution)/shard_map/ppermute | solution.py:534
  107.8 15.4 %collective-permute-start.11 = (f32[128,1024]{1,0:T(8,128)S(1)}, f32[128,1024]{1,0:T(8,128)S(1)}, u32[]{:S(2)}, u32[]{:S(2)}) collective-permute-start(f32[128,1024]{1,0:T(8,128)S(1)} %get-tuple-element.84), channel_id=1, source_target_pairs={{0,8},{1,25},{2,10},{3,27},{4,12},{5,29},{6,14},{7,31},{8,0},{9,17... | collective-permute-start | bytes 1572872 | tf_op jit(solution)/shard_map/ppermute | solution.py:534
  119.1 11.6 %collective-permute-start.21 = (f32[128,1024]{1,0:T(8,128)S(1)}, f32[128,1024]{1,0:T(8,128)S(1)}, u32[]{:S(2)}, u32[]{:S(2)}) collective-permute-start(f32[128,1024]{1,0:T(8,128)S(1)} %get-tuple-element.86), channel_id=1, source_target_pairs={{0,2},{1,7},{2,0},{3,5},{4,6},{5,3},{6,4},{7,1},{8,10},{9,15},{10,... | collective-permute-start | bytes 1572872 | tf_op jit(solution)/shard_map/ppermute | solution.py:534
  124.0 18.3 %collective-permute-start.12 = (f32[64,1024]{1,0:T(8,128)}, f32[64,1024]{1,0:T(8,128)}, u32[]{:S(2)}, u32[]{:S(2)}) collective-permute-start(f32[64,1024]{1,0:T(8,128)} %get-tuple-element.87), channel_id=1, source_target_pairs={{0,24},{1,9},{2,26},{3,11},{4,28},{5,13},{6,30},{7,15},{8,16},{9,1... | collective-permute-start | bytes 786440 | tf_op jit(solution)/shard_map/ppermute | solution.py:534
  131.6 8.5 %collective-permute-start.22 = (f32[64,1024]{1,0:T(8,128)}, f32[64,1024]{1,0:T(8,128)}, u32[]{:S(2)}, u32[]{:S(2)}) collective-permute-start(f32[64,1024]{1,0:T(8,128)} %get-tuple-element.89), channel_id=1, source_target_pairs={{0,6},{1,3},{2,4},{3,1},{4,2},{5,7},{6,0},{7,5},{8,14},{9,11},{10,... | collective-permute-start | bytes 786440 | tf_op jit(solution)/shard_map/ppermute | solution.py:534
  131.9 8.2 %copy-start.4 = (f32[64,1024]{1,0:T(8,128)S(1)}, f32[64,1024]{1,0:T(8,128)}, u32[]{:S(2)}) copy-start(f32[64,1024]{1,0:T(8,128)} %get-tuple-element.90.keep) | copy-start | bytes 786436
  131.9 19.8 %copy-start.7 = (bf16[16,2048]{1,0:T(8,128)(2,1)S(1)}, bf16[16,2048]{1,0:T(8,128)(2,1)}, u32[]{:S(2)}) copy-start(bf16[16,2048]{1,0:T(8,128)(2,1)} %param.7) | copy-start | bytes 196612
  141.1 5.3 %collective-permute-start.23 = (f32[32,1024]{1,0:T(8,128)S(1)}, f32[32,1024]{1,0:T(8,128)S(1)}, u32[]{:S(2)}, u32[]{:S(2)}) collective-permute-start(f32[32,1024]{1,0:T(8,128)S(1)} %get-tuple-element.76), channel_id=1, source_target_pairs={{0,8},{1,25},{2,10},{3,27},{4,12},{5,29},{6,14},{7,31},{8,0},{9,17... | collective-permute-start | bytes 393224 | tf_op jit(solution)/shard_map/ppermute | solution.py:534
  143.2 5.1 %collective-permute-start.17 = (f32[32,1024]{1,0:T(8,128)S(1)}, f32[32,1024]{1,0:T(8,128)S(1)}, u32[]{:S(2)}, u32[]{:S(2)}) collective-permute-start(f32[32,1024]{1,0:T(8,128)S(1)} %get-tuple-element.69), channel_id=1, source_target_pairs={{0,2},{1,7},{2,0},{3,5},{4,6},{5,3},{6,4},{7,1},{8,10},{9,15},{10,... | collective-permute-start | bytes 393224 | tf_op jit(solution)/shard_map/ppermute | solution.py:534
  146.5 3.6 %collective-permute-start.24 = (f32[16,1024]{1,0:T(8,128)S(1)}, f32[16,1024]{1,0:T(8,128)S(1)}, u32[]{:S(2)}, u32[]{:S(2)}) collective-permute-start(f32[16,1024]{1,0:T(8,128)S(1)} %slice_add_fusion.8), channel_id=1, source_target_pairs={{0,24},{1,9},{2,26},{3,11},{4,28},{5,13},{6,30},{7,15},{8,16},{9,1... | collective-permute-start | bytes 196616 | tf_op jit(solution)/shard_map/ppermute | solution.py:534
  148.4 3.3 %collective-permute-start.18 = (f32[16,1024]{1,0:T(8,128)S(1)}, f32[16,1024]{1,0:T(8,128)S(1)}, u32[]{:S(2)}, u32[]{:S(2)}) collective-permute-start(f32[16,1024]{1,0:T(8,128)S(1)} %slice_add_fusion.10), channel_id=1, source_target_pairs={{0,6},{1,3},{2,4},{3,1},{4,2},{5,7},{6,0},{7,5},{8,14},{9,11},{10,... | collective-permute-start | bytes 196616 | tf_op jit(solution)/shard_map/ppermute | solution.py:534
  152.4 20.5 %collective-permute-start.25 = (f32[32,2048]{1,0:T(8,128)S(1)}, f32[32,2048]{1,0:T(8,128)S(1)}, u32[]{:S(2)}, u32[]{:S(2)}) collective-permute-start(f32[32,2048]{1,0:T(8,128)S(1)} %solve0.1.refs_0_), channel_id=1, source_target_pairs={{0,1},{2,3},{4,5},{6,7},{8,9},{10,11},{12,13},{14,15},{16,17},{18,... | collective-permute-start | bytes 786440 | tf_op jit(solution)/shard_map/ppermute | solution.py:591

commit v11 on v6

--- a/solution.py
+++ b/solution.py
@@ -46,17 +46,18 @@
     return both[:rows] + both[rows:] + dot(high, b_low)
 
 
-def strip_copies(chips, pieces, lower, below, sems):
+def strip_copies(chips, pieces, lower, below, sems, spans):
     own_a, got_a, own_b, got_b = pieces
     half = lower.shape[0] // 2
     cut = STRIP // 2
     groups = ([], [], [])
 
     def add(group, source, start, count, target, to):
+        cols = pl.ds(*spans[group])
         groups[group].append(
             pltpu.make_async_copy(
-                source.at[pl.ds(start, count)],
-                target.at[pl.ds(pl.multiple_of(to, cut), count)],
+                source.at[pl.ds(start, count), cols],
+                target.at[pl.ds(pl.multiple_of(to, cut), count), cols],
                 sems.at[group],
             )
         )
@@ -87,7 +88,8 @@
 def grow_kernel(chips, own_a, got_a, own_b, got_b, out_high, out_low, token, lower, sems):
     slab = lower.shape[0]
     half = slab // 2
-    even, odd, _ = strip_copies(chips, (own_a, got_a, own_b, got_b), lower, None, sems)
+    spans = ((0, slab), (0, slab), (0, slab))
+    even, odd, _ = strip_copies(chips, (own_a, got_a, own_b, got_b), lower, None, sems, spans)
     start_all(even)
     start_all(odd)
     del token
@@ -188,7 +190,8 @@
 
     @pl.when(active)
     def _():
-        even, odd, below = strip_copies(chips, pieces, factor, under, strip_sems)
+        spans = ((BLOCK, slab - BLOCK), (half + BLOCK, half - BLOCK), (0, slab))
+        even, odd, below = strip_copies(chips, pieces, factor, under, strip_sems, spans)
         inverse = inverse_copies(inv_high, inv_low, high, low, sems)
         order = [inverse[0], even, *inverse[1:], odd, below] if first else [below, *inverse, even, odd]
         for copies in order:
@@ -212,9 +215,9 @@
 
         def before_update(b):
             if b == 0:
-                wait_for(factor.at[:half], strip_sems.at[0])
+                wait_for(factor.at[:half, BLOCK:], strip_sems.at[0])
             if b == inner:
-                wait_for(factor.at[half:], strip_sems.at[1])
+                wait_for(factor.at[half:, half + BLOCK :], strip_sems.at[1])
 
         solve_block(slab // BLOCK, pending, factor, high, low, out, wait, before_update, after)
 
@@ -529,7 +532,13 @@
 
     got = lax.ppermute(strip, EVERY, to_first)
     held, token = small_call(pair_kernel, "pair", [(2 * STRIP, width)], [], flags, strip, got)
-    got = lax.ppermute(held, EVERY, flip_pairs("z", (3, 3)))
+    needed = [
+        (chip_index(start, y, x, c), chip_index(3 - start, y, x, c))
+        for start, c in ((0, 0), (1, 0), (1, 1), (2, 1), (3, 1))
+        for y in range(SIDE)
+        for x in range(SIDE)
+    ]
+    got = lax.ppermute(held, EVERY, needed)
     send0, token = half_product(0, 0, token, "send0")
     held, token = small_call(
         choose_kernel, "choose", [(2 * STRIP, width)], [], flags, held, got, token=token

time: 175 us -> 172 us (0.983)
  waiting for transfers between devices: 90 us -> 84.4 us
  starting transfers between devices: 20.9 us -> 23.2 us
    ppermute x1, waiting for transfers between devices: 5.21 us -> 1.62 us  [per_device(): got = lax.ppermute(held, EVERY, needed)]
    ppermute x12, waiting for transfers between devices: 57.9 us -> 55.1 us  [sum_step(): lax.ppermute(send, EVERY, partner_pairs(PARTS[n][2][step // 2], step % 2...]
    ppermute x8, waiting for transfers between devices: 0.49 us -> 3 us  [gather_step(): lax.ppermute(held[n], EVERY, partner_pairs(GATHER[n][step // 2], step % 2...]
    ppermute x1, starting transfers between devices: 0.09 us -> 1.87 us  [per_device(): got = lax.ppermute(held, EVERY, flip_pairs('z', (1, 1)))]
  transfers between devices with their start and end apart: 24 -> 24, of which waited for: 16 -> 16; matrix products, arithmetic and copies ran while one was open for 3% -> 3% of each run, Pallas kernels for 24% -> 25%
where the time goes in v11:
time: 172 us
  waiting for transfers between devices  84.4 us (49%)
  Pallas kernels  54.7 us (32%)
  starting transfers between devices  23.2 us (13%)
  other arithmetic  5.39 us (3%)
  local copies, waits for them, and re-layouts  3.32 us (2%)
    ppermute x12, waiting for transfers between devices, sum_step(): lax.ppermute(send, EVERY, partner_pairs(PARTS[n][2][step // 2], step % 2...  55.1 us
    pallas_call x4, Pallas kernels, product(): pl.pallas_call(functools.partial(product_kernel, parts, half), out_shape=...  32.8 us
    ppermute x1, waiting for transfers between devices, per_device(): other = lax.ppermute(first, 'pcol', [(0, 1)])  13 us
    ppermute x1, waiting for transfers between devices, per_device(): got = lax.ppermute(held, EVERY, flip_pairs('z', (1, 1)))  10.7 us
    ppermute x12, starting transfers between devices, sum_step(): lax.ppermute(send, EVERY, partner_pairs(PARTS[n][2][step // 2], step % 2...  9 us
    pallas_call x1, Pallas kernels, grow(): pl.pallas_call(grow_kernel, out_shape=(inverse, inverse, TOKEN), in_specs...  7.29 us
    pallas_call x2, Pallas kernels, solve_call(): pl.pallas_call(functools.partial(solve_kernel, first), out_shape=jax.Shap...  6.81 us
    ppermute x8, starting transfers between devices, gather_step(): lax.ppermute(held[n], EVERY, partner_pairs(GATHER[n][step // 2], step % 2...  6.45 us
  transfers between devices with their start and end apart: 24, of which 16 were waited for; matrix products, arithmetic and copies ran while one was open for 3% of the time, Pallas kernels for 25%

profile of v11, /device:TPU:1, one launch (start us, length us, event | category | flops | bytes accessed | tf_op | source)
XLA Modules:
  0.0 171.6 jit_solution(9563520476138837838)
XLA Ops:
  0.0 3.3 %collective-permute-start = (bf16[64,2048]{1,0:T(8,128)(2,1)}, bf16[64,2048]{1,0:T(8,128)(2,1)S(1)}, u32[]{:S(2)}, u32[]{:S(2)}) collective-permute-start(bf16[64,2048]{1,0:T(8,128)(2,1)} %bitcast.10), channel_id=1, source_target_pairs={{1,0},{3,2},{5,4},{7,6},{9,8},{11,10},{13,12},{15,14},{17,16},{19,... | collective-permute-start | bytes 786440 | tf_op jit(solution)/shard_map/ppermute | solution.py:533
  3.7 1.0 collective-permute-done.got
  4.7 0.9 copy-done.2
  5.6 0.6 pair.1
  6.2 1.3 collective-permute-start.1
  7.6 0.1 add.166
  7.7 0.1 add.170
  7.9 7.9 %send0.1 = (f32[512,1024]{1,0:T(8,128)S(1)}, f32[8,128]{1,0:T(8,128)S(1)}) custom-call(s32[128]{0:T(128)S(1)} %pad_add_fusion.3.order, bf16[3,1024,1024]{2,1,0:T(8,128)(2,1)} %left.7, bf16[3,2048,1024]{2,1,0:T(8,128)(2,1)} %right.7, f32[8,128]{1,0:T(8,128)S(1)} %get-tuple-element.42._), custom_call_target="tpu_custom_call" | custom-call | flops 3221225472 | bytes 11534336 | tf_op jit(solution)/shard_map/send0/pallas_call | solution.py:310
  15.7 1.6 collective-permute-done.1.got
  17.4 0.6 choose.1
  18.0 1.9 %collective-permute-start.2 = (bf16[128,2048]{1,0:T(8,128)(2,1)S(1)}, bf16[128,2048]{1,0:T(8,128)(2,1)S(1)}, u32[]{:S(2)}, u32[]{:S(2)}) collective-permute-start(bf16[128,2048]{1,0:T(8,128)(2,1)S(1)} %get-tuple-element.44.held), channel_id=1, source_target_pairs={{0,32},{1,33},{2,34},{3,35},{4,36},{5,37},{6,38},{7,39},{8,40},{9,... | collective-permute-start | bytes 1572872 | tf_op jit(solution)/shard_map/ppermute | solution.py:546
  19.8 10.7 %collective-permute-done.2.got = bf16[128,2048]{1,0:T(8,128)(2,1)S(1)} collective-permute-done((bf16[128,2048]{1,0:T(8,128)(2,1)S(1)}, bf16[128,2048]{1,0:T(8,128)(2,1)S(1)}, u32[]{:S(2)}, u32[]{:S(2)}) %collective-permute-start.2) | collective-permute-done | bytes 524320 | tf_op jit(solution)/shard_map/ppermute | solution.py:546
  30.5 1.6 pack.1
  32.1 2.8 %collective-permute-start.3 = (bf16[96,2048]{1,0:T(8,128)(2,1)S(1)}, bf16[96,2048]{1,0:T(8,128)(2,1)S(1)}, u32[]{:S(2)}, u32[]{:S(2)}) collective-permute-start(bf16[96,2048]{1,0:T(8,128)(2,1)S(1)} %get-tuple-element.46.held_a), channel_id=1, source_target_pairs={{0,8},{1,25},{2,10},{3,27},{4,12},{5,29},{6,14},{7,31},{8,0},{9,17... | collective-permute-start | bytes 1179656 | tf_op jit(solution)/shard_map/ppermute | solution.py:526
  34.9 2.5 %collective-permute-start.4 = (bf16[96,2048]{1,0:T(8,128)(2,1)S(1)}, bf16[96,2048]{1,0:T(8,128)(2,1)S(1)}, u32[]{:S(2)}, u32[]{:S(2)}) collective-permute-start(bf16[96,2048]{1,0:T(8,128)(2,1)S(1)} %get-tuple-element.47.held_b), channel_id=1, source_target_pairs={{0,2},{1,7},{2,0},{3,5},{4,6},{5,3},{6,4},{7,1},{8,10},{9,15},{10,... | collective-permute-start | bytes 1179656 | tf_op jit(solution)/shard_map/ppermute | solution.py:526
  37.4 2.8 %collective-permute-start.5 = (f32[512,1024]{1,0:T(8,128)S(1)}, f32[512,1024]{1,0:T(8,128)S(1)}, u32[]{:S(2)}, u32[]{:S(2)}) collective-permute-start(f32[512,1024]{1,0:T(8,128)S(1)} %get-tuple-element.52), channel_id=1, source_target_pairs={{0,32},{1,97},{2,34},{3,99},{4,36},{5,101},{6,38},{7,103},{8,40},{... | collective-permute-start | bytes 6291464 | tf_op jit(solution)/shard_map/ppermute | solution.py:531
  40.2 9.2 %send1.1 = (f32[512,1024]{1,0:T(8,128)}, f32[8,128]{1,0:T(8,128)S(1)}) custom-call(s32[128]{0:T(128)S(1)} %pad_add_fusion.3.order, bf16[3,1024,1024]{2,1,0:T(8,128)(2,1)} %left.7, bf16[3,2048,1024]{2,1,0:T(8,128)(2,1)} %right.7, f32[8,128]{1,0:T(8,128)S(1)} %get-tuple-element.48._), custom_call_target="tpu_custom_call" | custom-call | flops 3221225472 | bytes 11534336 | tf_op jit(solution)/shard_map/send1/pallas_call | solution.py:310
  49.4 1.6 join.3
  51.0 0.1 collective-permute-start.6
  51.1 0.1 collective-permute-start.7
  51.2 0.3 collective-permute-start.14
  51.4 7.9 %keep0.1 = (f32[512,1024]{1,0:T(8,128)S(1)}, f32[8,128]{1,0:T(8,128)S(1)}) custom-call(s32[128]{0:T(128)S(1)} %pad_add_fusion.3.order, bf16[3,1024,1024]{2,1,0:T(8,128)(2,1)} %left.7, bf16[3,2048,1024]{2,1,0:T(8,128)(2,1)} %right.7, f32[8,128]{1,0:T(8,128)S(1)} %get-tuple-element.50._), custom_call_target="tpu_custom_call" | custom-call | flops 3221225472 | bytes 11534336 | tf_op jit(solution)/shard_map/keep0/pallas_call | solution.py:310
  59.3 2.9 %collective-permute-done.6.got_a = bf16[192,2048]{1,0:T(8,128)(2,1)S(1)} collective-permute-done((bf16[192,2048]{1,0:T(8,128)(2,1)S(1)}, bf16[192,2048]{1,0:T(8,128)(2,1)S(1)}, u32[]{:S(2)}, u32[]{:S(2)}) %collective-permute-start.6) | collective-permute-done | bytes 786464 | tf_op jit(solution)/shard_map/ppermute | solution.py:526
  62.2 0.1 collective-permute-done.7.got_b
  62.3 0.5 join.4
  62.8 0.3 collective-permute-start.12
  63.1 0.5 collective-permute-start.13
  63.6 0.3 collective-permute-done.5.got
  63.9 0.3 add.236
  64.2 1.0 copy-done
  65.2 1.0 copy-done.3
  66.1 7.9 %keep1.1 = (f32[512,1024]{1,0:T(8,128)S(1)}, f32[8,128]{1,0:T(8,128)S(1)}) custom-call(s32[128]{0:T(128)S(1)} %pad_add_fusion.3.order, bf16[3,1024,1024]{2,1,0:T(8,128)(2,1)} %left.7, bf16[3,2048,1024]{2,1,0:T(8,128)(2,1)} %right.7, f32[8,128]{1,0:T(8,128)S(1)} %get-tuple-element.61._), custom_call_target="tpu_custom_call" | custom-call | flops 3221225472 | bytes 11534336 | tf_op jit(solution)/shard_map/keep1/pallas_call | solution.py:310
  74.0 12.1 %collective-permute-done.14.got = f32[512,1024]{1,0:T(8,128)S(1)} collective-permute-done((f32[512,1024]{1,0:T(8,128)}, f32[512,1024]{1,0:T(8,128)S(1)}, u32[]{:S(2)}, u32[]{:S(2)}) %collective-permute-start.14) | collective-permute-done | bytes 2097184 | tf_op jit(solution)/shard_map/ppermute | solution.py:531
  86.1 0.3 add.237
  86.4 2.4 %join.5 = (bf16[768,2048]{1,0:T(8,128)(2,1)S(1)}, bf16[768,2048]{1,0:T(8,128)(2,1)}, f32[8,128]{1,0:T(8,128)}) custom-call(bf16[384,2048]{1,0:T(8,128)(2,1)S(1)} %get-tuple-element.59.held_a, bf16[384,2048]{1,0:T(8,128)(2,1)S(1)} %collective-permute-done.12.got_a, bf16[384,2048]{1,0:T(8,128)(2,1)S(1)} %get-tuple-element.60.held_b, ...), custom_call_target="tpu_custom_call" | custom-call | tf_op jit(solution)/shard_map/join/pallas_call | solution.py:452
  88.8 0.1 collective-permute-start.15
  88.9 0.1 collective-permute-start.16
  89.0 1.0 collective-permute-start.8
  89.9 0.6 collective-permute-start.18
  90.5 12.6 %collective-permute-done.8 = f32[256,1024]{1,0:T(8,128)S(1)} collective-permute-done((f32[256,1024]{1,0:T(8,128)S(1)}, f32[256,1024]{1,0:T(8,128)S(1)}, u32[]{:S(2)}, u32[]{:S(2)}) %collective-permute-start.8) | collective-permute-done | bytes 1048608 | tf_op jit(solution)/shard_map/ppermute | solution.py:531
  103.1 1.1 slice_add_fusion.3
  104.3 0.5 collective-permute-start.9
  104.8 9.6 %collective-permute-done.18 = f32[256,1024]{1,0:T(8,128)S(1)} collective-permute-done((f32[256,1024]{1,0:T(8,128)S(1)}, f32[256,1024]{1,0:T(8,128)S(1)}, u32[]{:S(2)}, u32[]{:S(2)}) %collective-permute-start.18) | collective-permute-done | bytes 1048608 | tf_op jit(solution)/shard_map/ppermute | solution.py:531
  114.3 1.1 slice_add_fusion.1
  115.5 0.6 collective-permute-start.19
  116.3 3.5 %collective-permute-done.9 = f32[128,1024]{1,0:T(8,128)} collective-permute-done((f32[128,1024]{1,0:T(8,128)}, f32[128,1024]{1,0:T(8,128)}, u32[]{:S(2)}, u32[]{:S(2)}) %collective-permute-start.9) | collective-permute-done | bytes 524320 | tf_op jit(solution)/shard_map/ppermute | solution.py:531
  119.8 1.3 slice_add_fusion.7
  121.0 0.2 collective-permute-start.10
  121.3 9.7 %collective-permute-done.19 = f32[128,1024]{1,0:T(8,128)} collective-permute-done((f32[128,1024]{1,0:T(8,128)}, f32[128,1024]{1,0:T(8,128)}, u32[]{:S(2)}, u32[]{:S(2)}) %collective-permute-start.19) | collective-permute-done | bytes 524320 | tf_op jit(solution)/shard_map/ppermute | solution.py:531
  131.0 1.3 slice_add_fusion.5
  132.2 0.1 collective-permute-start.20
  132.5 1.6 collective-permute-done.10
  134.1 0.8 collective-permute-start.11
  134.9 2.9 %collective-permute-done.20 = f32[64,1024]{1,0:T(8,128)S(1)} collective-permute-done((f32[64,1024]{1,0:T(8,128)S(1)}, f32[64,1024]{1,0:T(8,128)S(1)}, u32[]{:S(2)}, u32[]{:S(2)}) %collective-permute-start.20) | collective-permute-done | bytes 262176 | tf_op jit(solution)/shard_map/ppermute | solution.py:531
  137.8 0.9 collective-permute-start.21
  138.7 7.3 %grow_inverse.1 = (bf16[4,512,512]{2,1,0:T(8,128)(2,1)S(1)}, bf16[4,512,512]{2,1,0:T(8,128)(2,1)S(1)}, f32[8,128]{1,0:T(8,128)S(1)}) custom-call(s32[32]{0:T(128)S(1)} %pad_add_fusion.1.chips, bf16[768,2048]{1,0:T(8,128)(2,1)S(1)} %get-tuple-element.66.own_a.refs_0_.refs_2_, bf16[768,2048]{1,0:T(8,128)(2,1)} %collective-permute-done.15.got_a.refs_1_.refs_3_, ...), custom_call_target="tpu_custom_call" | custom-call | flops 4000000000 | bytes 8388608 | tf_op jit(solution)/shard_map/grow_inverse/pallas_call | solution.py:147
  146.1 0.9 collective-permute-start.22
  147.0 0.2 collective-permute-start.17
  147.3 2.0 %collective-permute-done.22 = f32[16,1024]{1,0:T(8,128)S(1)} collective-permute-done((f32[16,1024]{1,0:T(8,128)S(1)}, f32[16,1024]{1,0:T(8,128)S(1)}, u32[]{:S(2)}, u32[]{:S(2)}) %collective-permute-start.22) | collective-permute-done | bytes 65568 | tf_op jit(solution)/shard_map/ppermute | solution.py:531
  149.3 1.0 collective-permute-done.17
  150.3 0.7 solve0.1.refs_0_
  151.0 1.3 collective-permute-start.23
  152.3 13.0 %collective-permute-done.23.refs_1_ = f32[32,2048]{1,0:T(8,128)S(1)} collective-permute-done((f32[32,2048]{1,0:T(8,128)S(1)}, f32[32,2048]{1,0:T(8,128)S(1)}, u32[]{:S(2)}, u32[]{:S(2)}) %collective-permute-start.23) | collective-permute-done | bytes 262176 | tf_op jit(solution)/shard_map/ppermute | solution.py:590
  165.3 6.1 %solve1.1 = f32[16,2048]{1,0:T(8,128)} custom-call(s32[1]{0:T(128)} %bitcast.core, s32[32]{0:T(128)S(1)} %pad_add_fusion.1.chips, f32[16,2048]{1,0:T(8,128)S(1)} %maximum_subtract_fusion.right, f32[32,2048]{1,0:T(8,128)S(1)} %solve0.1.refs_0_, f32[32,2048]{1,0:T(8,128)S(1)} %collective-permute-done.23.refs_1_, ...), custom_call_target="tpu_custom_call" | custom-call | tf_op jit(solution)/shard_map/solve1/pallas_call | solution.py:234
  (35 shorter events, 0.9 us)
Async XLA Ops:
  0.0 4.7 %collective-permute-start = (bf16[64,2048]{1,0:T(8,128)(2,1)}, bf16[64,2048]{1,0:T(8,128)(2,1)S(1)}, u32[]{:S(2)}, u32[]{:S(2)}) collective-permute-start(bf16[64,2048]{1,0:T(8,128)(2,1)} %bitcast.10), channel_id=1, source_target_pairs={{1,0},{3,2},{5,4},{7,6},{9,8},{11,10},{13,12},{15,14},{17,16},{19,... | collective-permute-start | bytes 786440 | tf_op jit(solution)/shard_map/ppermute | solution.py:533
  4.7 0.9 copy-start.2
  6.2 11.1 %collective-permute-start.1 = (bf16[128,2048]{1,0:T(8,128)(2,1)S(1)}, bf16[128,2048]{1,0:T(8,128)(2,1)S(1)}, u32[]{:S(2)}, u32[]{:S(2)}) collective-permute-start(bf16[128,2048]{1,0:T(8,128)(2,1)S(1)} %get-tuple-element.41.held), channel_id=1, source_target_pairs={{0,96},{2,98},{4,100},{6,102},{8,104},{10,106},{12,108},{14,110},{... | collective-permute-start | bytes 1572872 | tf_op jit(solution)/shard_map/ppermute | solution.py:541
  18.0 12.6 %collective-permute-start.2 = (bf16[128,2048]{1,0:T(8,128)(2,1)S(1)}, bf16[128,2048]{1,0:T(8,128)(2,1)S(1)}, u32[]{:S(2)}, u32[]{:S(2)}) collective-permute-start(bf16[128,2048]{1,0:T(8,128)(2,1)S(1)} %get-tuple-element.44.held), channel_id=1, source_target_pairs={{0,32},{1,33},{2,34},{3,35},{4,36},{5,37},{6,38},{7,39},{8,40},{9,... | collective-permute-start | bytes 1572872 | tf_op jit(solution)/shard_map/ppermute | solution.py:546
  32.1 17.3 %collective-permute-start.3 = (bf16[96,2048]{1,0:T(8,128)(2,1)S(1)}, bf16[96,2048]{1,0:T(8,128)(2,1)S(1)}, u32[]{:S(2)}, u32[]{:S(2)}) collective-permute-start(bf16[96,2048]{1,0:T(8,128)(2,1)S(1)} %get-tuple-element.46.held_a), channel_id=1, source_target_pairs={{0,8},{1,25},{2,10},{3,27},{4,12},{5,29},{6,14},{7,31},{8,0},{9,17... | collective-permute-start | bytes 1179656 | tf_op jit(solution)/shard_map/ppermute | solution.py:526
  34.9 14.5 %collective-permute-start.4 = (bf16[96,2048]{1,0:T(8,128)(2,1)S(1)}, bf16[96,2048]{1,0:T(8,128)(2,1)S(1)}, u32[]{:S(2)}, u32[]{:S(2)}) collective-permute-start(bf16[96,2048]{1,0:T(8,128)(2,1)S(1)} %get-tuple-element.47.held_b), channel_id=1, source_target_pairs={{0,2},{1,7},{2,0},{3,5},{4,6},{5,3},{6,4},{7,1},{8,10},{9,15},{10,... | collective-permute-start | bytes 1179656 | tf_op jit(solution)/shard_map/ppermute | solution.py:526
  37.4 26.5 %collective-permute-start.5 = (f32[512,1024]{1,0:T(8,128)S(1)}, f32[512,1024]{1,0:T(8,128)S(1)}, u32[]{:S(2)}, u32[]{:S(2)}) collective-permute-start(f32[512,1024]{1,0:T(8,128)S(1)} %get-tuple-element.52), channel_id=1, source_target_pairs={{0,32},{1,97},{2,34},{3,99},{4,36},{5,101},{6,38},{7,103},{8,40},{... | collective-permute-start | bytes 6291464 | tf_op jit(solution)/shard_map/ppermute | solution.py:531
  51.0 11.2 %collective-permute-start.6 = (bf16[192,2048]{1,0:T(8,128)(2,1)S(1)}, bf16[192,2048]{1,0:T(8,128)(2,1)S(1)}, u32[]{:S(2)}, u32[]{:S(2)}) collective-permute-start(bf16[192,2048]{1,0:T(8,128)(2,1)S(1)} %get-tuple-element.53.held_a), channel_id=1, source_target_pairs={{0,24},{1,9},{2,26},{3,11},{4,28},{5,13},{6,30},{7,15},{8,16},{9,1... | collective-permute-start | bytes 2359304 | tf_op jit(solution)/shard_map/ppermute | solution.py:526
  51.1 11.2 %collective-permute-start.7 = (bf16[192,2048]{1,0:T(8,128)(2,1)S(1)}, bf16[192,2048]{1,0:T(8,128)(2,1)S(1)}, u32[]{:S(2)}, u32[]{:S(2)}) collective-permute-start(bf16[192,2048]{1,0:T(8,128)(2,1)S(1)} %get-tuple-element.54.held_b), channel_id=1, source_target_pairs={{0,6},{1,3},{2,4},{3,1},{4,2},{5,7},{6,0},{7,5},{8,14},{9,11},{10,... | collective-permute-start | bytes 2359304 | tf_op jit(solution)/shard_map/ppermute | solution.py:526
  51.2 34.9 %collective-permute-start.14 = (f32[512,1024]{1,0:T(8,128)}, f32[512,1024]{1,0:T(8,128)S(1)}, u32[]{:S(2)}, u32[]{:S(2)}) collective-permute-start(f32[512,1024]{1,0:T(8,128)} %get-tuple-element.63), channel_id=1, source_target_pairs={{0,32},{1,97},{2,34},{3,99},{4,36},{5,101},{6,38},{7,103},{8,40},{... | collective-permute-start | bytes 6291464 | tf_op jit(solution)/shard_map/ppermute | solution.py:531
  62.8 23.6 %collective-permute-start.12 = (bf16[384,2048]{1,0:T(8,128)(2,1)S(1)}, bf16[384,2048]{1,0:T(8,128)(2,1)S(1)}, u32[]{:S(2)}, u32[]{:S(2)}) collective-permute-start(bf16[384,2048]{1,0:T(8,128)(2,1)S(1)} %get-tuple-element.59.held_a), channel_id=1, source_target_pairs={{0,2},{1,7},{2,0},{3,5},{4,6},{5,3},{6,4},{7,1},{8,10},{9,15},{10,... | collective-permute-start | bytes 4718600 | tf_op jit(solution)/shard_map/ppermute | solution.py:526
  63.1 23.3 %collective-permute-start.13 = (bf16[384,2048]{1,0:T(8,128)(2,1)S(1)}, bf16[384,2048]{1,0:T(8,128)(2,1)S(1)}, u32[]{:S(2)}, u32[]{:S(2)}) collective-permute-start(bf16[384,2048]{1,0:T(8,128)(2,1)S(1)} %get-tuple-element.60.held_b), channel_id=1, source_target_pairs={{0,8},{1,25},{2,10},{3,27},{4,12},{5,29},{6,14},{7,31},{8,0},{9,17... | collective-permute-start | bytes 4718600 | tf_op jit(solution)/shard_map/ppermute | solution.py:526
  64.2 1.0 copy-start
  65.2 1.0 copy-start.3
  86.4 2.6 %copy-start.4 = (f32[256,1024]{1,0:T(8,128)S(1)}, f32[256,1024]{1,0:T(8,128)}, u32[]{:S(2)}) copy-start(f32[256,1024]{1,0:T(8,128)} %copy-done.3) | copy-start | bytes 3145732
  86.4 16.7 %copy-start.1 = (f32[256,1024]{1,0:T(8,128)S(1)}, f32[256,1024]{1,0:T(8,128)}, u32[]{:S(2)}) copy-start(f32[256,1024]{1,0:T(8,128)} %copy-done) | copy-start | bytes 3145732
  88.8 49.9 %collective-permute-start.15 = (bf16[768,2048]{1,0:T(8,128)(2,1)S(1)}, bf16[768,2048]{1,0:T(8,128)(2,1)}, u32[]{:S(2)}, u32[]{:S(2)}) collective-permute-start(bf16[768,2048]{1,0:T(8,128)(2,1)S(1)} %get-tuple-element.66.own_a.refs_0_.refs_2_), channel_id=1, source_target_pairs={{0,6},{1,3},{2,4},{3,1},{4,2},{5,7},{6,0},{7,5},{8,14},{9,11},{10,... | collective-permute-start | bytes 9437192 | tf_op jit(solution)/shard_map/ppermute | solution.py:526
  88.9 49.9 %collective-permute-start.16 = (bf16[768,2048]{1,0:T(8,128)(2,1)}, bf16[768,2048]{1,0:T(8,128)(2,1)}, u32[]{:S(2)}, u32[]{:S(2)}) collective-permute-start(bf16[768,2048]{1,0:T(8,128)(2,1)} %get-tuple-element.67.own_b.refs_2_.refs_4_), channel_id=1, source_target_pairs={{0,24},{1,9},{2,26},{3,11},{4,28},{5,13},{6,30},{7,15},{8,16},{9,1... | collective-permute-start | bytes 9437192 | tf_op jit(solution)/shard_map/ppermute | solution.py:526
  89.0 14.1 %collective-permute-start.8 = (f32[256,1024]{1,0:T(8,128)S(1)}, f32[256,1024]{1,0:T(8,128)S(1)}, u32[]{:S(2)}, u32[]{:S(2)}) collective-permute-start(f32[256,1024]{1,0:T(8,128)S(1)} %copy-done.4), channel_id=1, source_target_pairs={{0,96},{1,33},{2,98},{3,35},{4,100},{5,37},{6,102},{7,39},{8,104},... | collective-permute-start | bytes 3145736 | tf_op jit(solution)/shard_map/ppermute | solution.py:531
  89.9 24.4 %collective-permute-start.18 = (f32[256,1024]{1,0:T(8,128)S(1)}, f32[256,1024]{1,0:T(8,128)S(1)}, u32[]{:S(2)}, u32[]{:S(2)}) collective-permute-start(f32[256,1024]{1,0:T(8,128)S(1)} %get-tuple-element.72), channel_id=1, source_target_pairs={{0,96},{1,33},{2,98},{3,35},{4,100},{5,37},{6,102},{7,39},{8,104},... | collective-permute-start | bytes 3145736 | tf_op jit(solution)/shard_map/ppermute | solution.py:531
  104.3 15.5 %collective-permute-start.9 = (f32[128,1024]{1,0:T(8,128)}, f32[128,1024]{1,0:T(8,128)}, u32[]{:S(2)}, u32[]{:S(2)}) collective-permute-start(f32[128,1024]{1,0:T(8,128)} %get-tuple-element.82), channel_id=1, source_target_pairs={{0,8},{1,25},{2,10},{3,27},{4,12},{5,29},{6,14},{7,31},{8,0},{9,17... | collective-permute-start | bytes 1572872 | tf_op jit(solution)/shard_map/ppermute | solution.py:531
  115.5 15.5 %collective-permute-start.19 = (f32[128,1024]{1,0:T(8,128)}, f32[128,1024]{1,0:T(8,128)}, u32[]{:S(2)}, u32[]{:S(2)}) collective-permute-start(f32[128,1024]{1,0:T(8,128)} %get-tuple-element.84), channel_id=1, source_target_pairs={{0,2},{1,7},{2,0},{3,5},{4,6},{5,3},{6,4},{7,1},{8,10},{9,15},{10,... | collective-permute-start | bytes 1572872 | tf_op jit(solution)/shard_map/ppermute | solution.py:531
  121.0 13.1 %collective-permute-start.10 = (f32[64,1024]{1,0:T(8,128)S(1)}, f32[64,1024]{1,0:T(8,128)S(1)}, u32[]{:S(2)}, u32[]{:S(2)}) collective-permute-start(f32[64,1024]{1,0:T(8,128)S(1)} %get-tuple-element.86), channel_id=1, source_target_pairs={{0,24},{1,9},{2,26},{3,11},{4,28},{5,13},{6,30},{7,15},{8,16},{9,1... | collective-permute-start | bytes 786440 | tf_op jit(solution)/shard_map/ppermute | solution.py:531
  132.2 5.5 %collective-permute-start.20 = (f32[64,1024]{1,0:T(8,128)S(1)}, f32[64,1024]{1,0:T(8,128)S(1)}, u32[]{:S(2)}, u32[]{:S(2)}) collective-permute-start(f32[64,1024]{1,0:T(8,128)S(1)} %get-tuple-element.88), channel_id=1, source_target_pairs={{0,6},{1,3},{2,4},{3,1},{4,2},{5,7},{6,0},{7,5},{8,14},{9,11},{10,... | collective-permute-start | bytes 786440 | tf_op jit(solution)/shard_map/ppermute | solution.py:531
  134.1 12.9 %collective-permute-start.11 = (f32[32,1024]{1,0:T(8,128)S(1)}, f32[32,1024]{1,0:T(8,128)S(1)}, u32[]{:S(2)}, u32[]{:S(2)}) collective-permute-start(f32[32,1024]{1,0:T(8,128)S(1)} %get-tuple-element.89), channel_id=1, source_target_pairs={{0,2},{1,7},{2,0},{3,5},{4,6},{5,3},{6,4},{7,1},{8,10},{9,15},{10,... | collective-permute-start | bytes 393224 | tf_op jit(solution)/shard_map/ppermute | solution.py:531
  137.8 12.4 %copy-start.5 = (bf16[16,2048]{1,0:T(8,128)(2,1)S(1)}, bf16[16,2048]{1,0:T(8,128)(2,1)}, u32[]{:S(2)}) copy-start(bf16[16,2048]{1,0:T(8,128)(2,1)} %param.7) | copy-start | bytes 196612
  137.8 8.2 %collective-permute-start.21 = (f32[32,1024]{1,0:T(8,128)S(1)}, f32[32,1024]{1,0:T(8,128)S(1)}, u32[]{:S(2)}, u32[]{:S(2)}) collective-permute-start(f32[32,1024]{1,0:T(8,128)S(1)} %get-tuple-element.91), channel_id=1, source_target_pairs={{0,8},{1,25},{2,10},{3,27},{4,12},{5,29},{6,14},{7,31},{8,0},{9,17... | collective-permute-start | bytes 393224 | tf_op jit(solution)/shard_map/ppermute | solution.py:531
  146.1 3.2 %collective-permute-start.22 = (f32[16,1024]{1,0:T(8,128)S(1)}, f32[16,1024]{1,0:T(8,128)S(1)}, u32[]{:S(2)}, u32[]{:S(2)}) collective-permute-start(f32[16,1024]{1,0:T(8,128)S(1)} %get-tuple-element.74), channel_id=1, source_target_pairs={{0,24},{1,9},{2,26},{3,11},{4,28},{5,13},{6,30},{7,15},{8,16},{9,1... | collective-permute-start | bytes 196616 | tf_op jit(solution)/shard_map/ppermute | solution.py:531
  147.0 3.2 %collective-permute-start.17 = (f32[16,1024]{1,0:T(8,128)S(1)}, f32[16,1024]{1,0:T(8,128)S(1)}, u32[]{:S(2)}, u32[]{:S(2)}) collective-permute-start(f32[16,1024]{1,0:T(8,128)S(1)} %get-tuple-element.70), channel_id=1, source_target_pairs={{0,6},{1,3},{2,4},{3,1},{4,2},{5,7},{6,0},{7,5},{8,14},{9,11},{10,... | collective-permute-start | bytes 196616 | tf_op jit(solution)/shard_map/ppermute | solution.py:531
  151.0 14.3 %collective-permute-start.23 = (f32[32,2048]{1,0:T(8,128)S(1)}, f32[32,2048]{1,0:T(8,128)S(1)}, u32[]{:S(2)}, u32[]{:S(2)}) collective-permute-start(f32[32,2048]{1,0:T(8,128)S(1)} %solve0.1.refs_0_), channel_id=1, source_target_pairs={{0,1},{2,3},{4,5},{6,7},{8,9},{10,11},{12,13},{14,15},{16,17},{18,... | collective-permute-start | bytes 786440 | tf_op jit(solution)/shard_map/ppermute | solution.py:590
